TPU v7x, 32 devices: a whole 2x2x4 slice. The times are simulated.
32 devices in a mesh: frames: 4 (over y, x), rows: 8 (over z, core).
Axes of the slice: x: 2, y: 2, z: 4, core: 2. Of those that a mesh axis runs over, the one named last changes fastest.
Arguments:
- latents: bfloat16 [8, 32, 40, 512], P('frames', 'rows'), may hold values from -100 to 100
- norm_gain: float32 [512], replicated, may hold values from 0.1 to 1.9
- norm_bias: float32 [512], replicated, may hold values from -3 to 3
- conv_weight: bfloat16 [3, 3, 3, 512, 512], P(None, None, None, None, ('frames', 'rows')), may hold values from -0.0546875 to 0.0546875
- conv_bias: float32 [512], replicated, may hold values from -3 to 3
Outputs:
- branch_out: bfloat16 [8, 32, 40, 512], P('frames', 'rows')
All inputs are finite; a program needn't handle non-finite values.
Results may differ from a plain program's by a relative error of at most 0.0043.
Values may be sent and summed in bfloat16 or wider, within the bound.
No kernel may reach another device: no remote copies, remote signals or barrier semaphores. Data moves between devices by JAX's collectives and lax.ppermute only.
A program may use at most 128 MiB of HBM per device.

v0:
```python
import jax
import jax.numpy as jnp
from jax import lax
from jax.sharding import PartitionSpec as P

GROUPS = 32


epsilon = 1e-06


def passed_along(block, axis, distance):
    devices = range(lax.axis_size(axis))
    route = [(i - distance, i) for i in devices if i - distance in devices]
    return lax.ppermute(block, axis, route)


def padded_2(block, sides, width):
    for axis, dim in sides:
        count = lax.axis_size(axis)
        forward = [(i, i + 1) for i in range(count - 1)]
        backward = [(target, source) for source, target in forward]
        low = lax.ppermute(
            lax.slice_in_dim(block, block.shape[dim] - width, None, axis=dim), axis, forward
        )
        high = lax.ppermute(lax.slice_in_dim(block, 0, width, axis=dim), axis, backward)
        block = jnp.concatenate([low, block, high], axis=dim)
    return block


def convolve(padded, weight_piece):
    frame_count = padded.shape[0] - 2
    row_count = padded.shape[1] - 2
    col_count = padded.shape[2] - 2
    channels = padded.shape[3]
    out_width = weight_piece.shape[4]
    running = None
    for tap_t in range(3):
        for tap_y in range(3):
            base = padded[tap_t : tap_t + frame_count, tap_y : tap_y + row_count]
            window = jnp.concatenate(
                [
                    base[:, :, 0:col_count],
                    base[:, :, 1 : col_count + 1],
                    base[:, :, 2 : col_count + 2],
                ],
                axis=3,
            )
            window = window.reshape(-1, 3 * channels)
            taps = weight_piece[tap_t, tap_y].reshape(3 * channels, out_width)
            product = jnp.dot(window, taps, preferred_element_type=jnp.float32)
            running = product if running is None else running + product
    return running.reshape(frame_count, row_count, col_count, out_width)


def body(latents, norm_gain, norm_bias, conv_weight, conv_bias):
    values = latents.astype(jnp.float32)
    frame_count, row_count, col_count, channels = values.shape
    grouped = values.reshape(frame_count, row_count, col_count, GROUPS, channels // GROUPS)
    entries = (
        frame_count
        * row_count
        * col_count
        * (channels // GROUPS)
        * lax.axis_size("frames")
        * lax.axis_size("rows")
    )
    local_sums = jnp.sum(grouped, axis=(0, 1, 2, 4))
    local_squares = jnp.sum(grouped * grouped, axis=(0, 1, 2, 4))
    total_sums, total_squares = lax.psum((local_sums, local_squares), ("frames", "rows"))
    group_mean = total_sums / entries
    group_var = total_squares / entries - group_mean * group_mean
    centered = grouped - group_mean[:, None]
    normed = (centered * lax.rsqrt(group_var + epsilon)[:, None]).reshape(
        frame_count, row_count, col_count, channels
    )
    activated = jax.nn.silu(normed * norm_gain + norm_bias).astype(jnp.bfloat16)
    earlier = passed_along(activated, "frames", 1)
    extended = jnp.concatenate([earlier, activated], axis=0)
    halo_rows = padded_2(extended, (("rows", 1),), 1)
    strip_index = lax.axis_index("rows")
    last_strip = lax.axis_size("rows") - 1
    upper_rim = jnp.where(strip_index == 0, extended[:, 1:2], halo_rows[:, 0:1])
    bottom = jnp.where(
        strip_index == last_strip,
        extended[:, row_count - 2 : row_count - 1],
        halo_rows[:, row_count + 1 : row_count + 2],
    )
    rowed = jnp.concatenate([upper_rim, extended, bottom], axis=1)
    padded = jnp.concatenate(
        [rowed[:, :, 1:2], rowed, rowed[:, :, col_count - 2 : col_count - 1]], axis=2
    )
    whole_weight = lax.all_gather(conv_weight, ("frames", "rows"), axis=4, tiled=True)
    output = convolve(padded, whole_weight)
    return (output + conv_bias).astype(jnp.bfloat16)


def solution(mesh):
    placed = (
        P("frames", "rows", None, None),
        P(),
        P(),
        P(None, None, None, None, ("frames", "rows")),
        P(),
    )
    return jax.shard_map(
        body, mesh=mesh, in_specs=placed, out_specs=P("frames", "rows", None, None), check_vma=False
    )
```

profile of v0, /device:TPU:0, one launch (start us, length us, event | category | flops | bytes accessed | tf_op | source)
XLA Modules:
  0.0 170.2 jit_solution(6384809716914911213)
XLA Ops:
  7.3 1.1 convert_reduce_fusion
  8.7 43.0 %all-reduce = (f32[32]{0:T(128)S(1)}, f32[32]{0:T(128)S(1)}) all-reduce(f32[32]{0:T(128)S(1)} %reduce_sum.37, f32[32]{0:T(128)S(1)} %reduce_sum.25), channel_id=1, replica_groups=mesh['frames'=4,'rows'=8] {'frames','rows'}, use_global_device_ids=true, to_apply=%region_5.6 | all-reduce | flops 64 | bytes 512 | tf_op jit(solution)/shard_map/psum | solution.py:70
  52.0 1.2 fusion.26
  53.3 4.3 %collective-permute-start = (bf16[2,4,40,512]{3,2,1,0:T(8,128)(2,1)S(1)}, bf16[2,4,40,512]{3,2,1,0:T(8,128)(2,1)S(1)}, u32[]{:S(2)}, u32[]{:S(2)}) collective-permute-start(bf16[2,4,40,512]{3,2,1,0:T(8,128)(2,1)S(1)} %fusion.26), channel_id=1, source_target_pairs={{0,8},{8,16},{16,24},{1,9},{9,17},{17,25},{2,10},{10,18},{18,26},{... | collective-permute-start | bytes 983048 | tf_op jit(solution)/shard_map/ppermute | solution.py:15
  57.5 5.4 %collective-permute-done = bf16[2,4,40,512]{3,2,1,0:T(8,128)(2,1)S(1)} collective-permute-done((bf16[2,4,40,512]{3,2,1,0:T(8,128)(2,1)S(1)}, bf16[2,4,40,512]{3,2,1,0:T(8,128)(2,1)S(1)}, u32[]{:S(2)}, u32[]{:S(2)}) %collective-permute-start) | collective-permute-done | bytes 327712 | tf_op jit(solution)/shard_map/ppermute | solution.py:15
  63.0 1.3 collective-permute-start.1
  64.3 1.3 collective-permute-start.2
  65.6 3.1 %collective-permute-done.2 = bf16[4,1,40,512]{3,2,1,0:T(8,128)(2,1)S(1)} collective-permute-done((bf16[4,1,40,512]{3,2,1,0:T(8,128)(2,1)S(1)}, bf16[4,1,40,512]{3,2,1,0:T(8,128)(2,1)S(1)}, u32[]{:S(2)}, u32[]{:S(2)}) %collective-permute-start.2) | collective-permute-done | bytes 163872 | tf_op jit(solution)/shard_map/ppermute | solution.py:26
  70.5 1.1 pad_maximum_fusion.8
  71.6 1.0 pad_maximum_fusion.6
  72.6 1.0 pad_maximum_fusion.5
  73.6 1.1 pad_maximum_fusion.4
  74.7 1.0 pad_maximum_fusion.3
  75.7 1.1 pad_maximum_fusion.1
  76.8 1.7 %pad_maximum_fusion.7 = (bf16[2,4,40,1536]{3,2,1,0:T(8,128)(2,1)}, bf16[2,4,40,1536]{3,2,1,0:T(8,128)(2,1)}, bf16[2,4,40,1536]{3,2,1,0:T(8,128)(2,1)}) fusion(bf16[2,4,40,512]{3,2,1,0:T(8,128)(2,1)S(1)} %get-tuple-element.62, bf16[2,4,40,512]{3,2,1,0:T(8,128)(2,1)S(1)} %fusion.26, bf16[2,4,40,512]{3,2,1,0:T(8,128)(2,1)S(1)} %get-tuple-element.19, ...), kind=kLoop, calls=%fused_computation.35 | loop fusion | flops 9830400 | bytes 5570560 | tf_op jit(solution)/shard_map/concatenate | solution.py:41
  78.5 40.0 %all-gather.2.cloned.1.call-done = bf16[3,3,3,512,512]{3,4,2,1,0:T(8,128)(2,1)} async-done(((bf16[3,3,3,512,16]{3,4,2,1,0:T(8,128)(2,1)}), bf16[3,3,3,512,512]{3,4,2,1,0:T(8,128)(2,1)}) %all-gather.2.cloned.1.call-update) | async-done | bytes 14155792 | tf_op jit(solution)/shard_map/all_gather | solution.py:93
  118.5 9.0 %fusion.34 = (bf16[1,1,3,512,512]{3,4,2,1,0:T(8,128)(2,1)}, bf16[1,1,3,512,512]{3,4,2,1,0:T(8,128)(2,1)}, bf16[1,1,3,512,512]{3,4,2,1,0:T(8,128)(2,1)}, bf16[1,1...) fusion(bf16[3,3,3,512,512]{3,4,2,1,0:T(8,128)(2,1)} %all-gather, ...), kind=kLoop, calls=%fused_computation.69 | loop fusion | bytes 28311552 | tf_op jit(solution)/shard_map/slice | solution.py:50
  127.5 2.6 %copy.24 = bf16[1,1,3,512,512]{4,3,2,1,0:T(8,128)(2,1)} copy(bf16[1,1,3,512,512]{3,4,2,1,0:T(8,128)(2,1)} %get-tuple-element.9) | data formatting | bytes 3145728
  130.1 2.6 %copy.23 = bf16[1,1,3,512,512]{4,3,2,1,0:T(8,128)(2,1)} copy(bf16[1,1,3,512,512]{3,4,2,1,0:T(8,128)(2,1)} %get-tuple-element.10) | data formatting | bytes 3145728
  132.7 2.6 %copy.22 = bf16[1,1,3,512,512]{4,3,2,1,0:T(8,128)(2,1)} copy(bf16[1,1,3,512,512]{3,4,2,1,0:T(8,128)(2,1)} %get-tuple-element.11) | data formatting | bytes 3145728
  135.3 2.6 %copy.21 = bf16[1,1,3,512,512]{4,3,2,1,0:T(8,128)(2,1)} copy(bf16[1,1,3,512,512]{3,4,2,1,0:T(8,128)(2,1)} %get-tuple-element.12) | data formatting | bytes 3145728
  137.9 2.6 %copy.20 = bf16[1,1,3,512,512]{4,3,2,1,0:T(8,128)(2,1)} copy(bf16[1,1,3,512,512]{3,4,2,1,0:T(8,128)(2,1)} %get-tuple-element.13) | data formatting | bytes 3145728
  140.5 2.6 %copy.19 = bf16[1,1,3,512,512]{4,3,2,1,0:T(8,128)(2,1)} copy(bf16[1,1,3,512,512]{3,4,2,1,0:T(8,128)(2,1)} %get-tuple-element.14) | data formatting | bytes 3145728
  143.1 2.6 %copy.18 = bf16[1,1,3,512,512]{4,3,2,1,0:T(8,128)(2,1)} copy(bf16[1,1,3,512,512]{3,4,2,1,0:T(8,128)(2,1)} %get-tuple-element.15) | data formatting | bytes 3145728
  145.8 1.6 copy.17
  148.1 2.0 %fusion.39 = f32[320,512]{1,0:T(8,128)S(1)} fusion(bf16[320,1536]{1,0:T(8,128)(2,1)} %bitcast.53, bf16[1536,512]{1,0:T(8,128)(2,1)S(1)} %bitcast.45), kind=kOutput, calls=%fused_computation.74 | convolution fusion | flops 503316480 | bytes 3211264 | tf_op jit(solution)/shard_map/dot_general | solution.py:51
  152.5 0.7 copy-done.5
  154.2 0.7 copy-done.4
  155.8 0.7 copy-done.3
  159.2 0.7 copy-done.1
  160.8 0.7 copy-done
  162.5 0.8 add_convert_fusion
  (56 shorter events, 12.6 us)
Async XLA Ops:
  6.5 112.0 %all-gather.2.cloned.1.call-start = ((), (), s32[]{:S(2)}) async-start(), calls=%async_computation | async-start | bytes 14598144 | tf_op jit(solution)/shard_map/all_gather | solution.py:93
  53.3 9.6 %collective-permute-start = (bf16[2,4,40,512]{3,2,1,0:T(8,128)(2,1)S(1)}, bf16[2,4,40,512]{3,2,1,0:T(8,128)(2,1)S(1)}, u32[]{:S(2)}, u32[]{:S(2)}) collective-permute-start(bf16[2,4,40,512]{3,2,1,0:T(8,128)(2,1)S(1)} %fusion.26), channel_id=1, source_target_pairs={{0,8},{8,16},{16,24},{1,9},{9,17},{17,25},{2,10},{10,18},{18,26},{... | collective-permute-start | bytes 983048 | tf_op jit(solution)/shard_map/ppermute | solution.py:15
  63.0 2.6 %collective-permute-start.1 = (bf16[4,1,40,512]{3,2,1,0:T(8,128)(2,1)S(1)}, bf16[4,1,40,512]{3,2,1,0:T(8,128)(2,1)S(1)}, u32[]{:S(2)}, u32[]{:S(2)}) collective-permute-start(bf16[4,1,40,512]{3,2,1,0:T(8,128)(2,1)S(1)} %get-tuple-element.48), channel_id=1, source_target_pairs={{0,1},{1,2},{2,3},{3,4},{4,5},{5,6},{6,7},{8,9},{9,10},{10,11},{11... | collective-permute-start | bytes 491528 | tf_op jit(solution)/shard_map/ppermute | solution.py:23
  64.3 4.4 %collective-permute-start.2 = (bf16[4,1,40,512]{3,2,1,0:T(8,128)(2,1)S(1)}, bf16[4,1,40,512]{3,2,1,0:T(8,128)(2,1)S(1)}, u32[]{:S(2)}, u32[]{:S(2)}) collective-permute-start(bf16[4,1,40,512]{3,2,1,0:T(8,128)(2,1)S(1)} %get-tuple-element.49), channel_id=1, source_target_pairs={{1,0},{2,1},{3,2},{4,3},{5,4},{6,5},{7,6},{9,8},{10,9},{11,10},{12... | collective-permute-start | bytes 491528 | tf_op jit(solution)/shard_map/ppermute | solution.py:26
  148.1 2.0 %copy-start.7 = (bf16[1,1,3,512,512]{4,3,2,1,0:T(8,128)(2,1)S(1)}, bf16[1,1,3,512,512]{4,3,2,1,0:T(8,128)(2,1)}, u32[]{:S(2)}) copy-start(bf16[1,1,3,512,512]{4,3,2,1,0:T(8,128)(2,1)} %copy.17) | copy-start | bytes 4718596
  148.1 2.0 %copy-start.15 = (bf16[2,4,40,1536]{3,2,1,0:T(8,128)(2,1)S(1)}, bf16[2,4,40,1536]{3,2,1,0:T(8,128)(2,1)}, u32[]{:S(2)}) copy-start(bf16[2,4,40,1536]{3,2,1,0:T(8,128)(2,1)} %get-tuple-element.52) | copy-start | bytes 2949124
  150.1 1.4 copy-start.6
  150.1 1.7 copy-start.13
  151.8 1.4 copy-start.5
  151.8 1.7 copy-start.11
  153.5 1.4 copy-start.4
  153.5 1.7 copy-start.14
  155.1 1.4 copy-start.3
  155.1 1.7 copy-start.10
  156.8 1.4 copy-start.2
  156.8 1.7 copy-start.9
  158.5 1.4 copy-start.1
  158.5 1.7 copy-start.12
  160.2 1.4 copy-start
  160.2 1.7 copy-start.8
  161.8 0.7 copy-start.16
Sparse Core Ops, SparseCore 0:
  10.4 108.0 all-gather.1
where the time goes:
time: 172 us; the launch traced here: 170 us
  waiting for transfers between devices  49.2 us (29%)
  blocking collectives  43 us (25%)
  local copies, waits for them, and re-layouts  37.9 us (22%)
  between operations  13.6 us (8%)
  other arithmetic  12.3 us (7%)
  matrix products  7.36 us (4%)
  starting transfers between devices  6.85 us (4%)
    psum x1, blocking collectives, body(): lax.psum((local_sums, local_squares), ('frames', 'rows'))  43 us
    all_gather x1, waiting for transfers between devices, body(): lax.all_gather(conv_weight, ('frames', 'rows'), axis=4, tiled=True)  40 us
    unnamed x43, local copies, waits for them, and re-layouts  27.5 us
    slice x1, local copies, waits for them, and re-layouts, convolve(): taps = weight_piece[tap_t, tap_y].reshape(3 * channels, out_width)  8.98 us
    concatenate x7, other arithmetic, convolve(): jnp.concatenate([base[:, :, 0:col_count], base[:, :, 1:col_count + 1], ba...  8.02 us
    dot_general x9, matrix products, convolve(): product = jnp.dot(window, taps, preferred_element_type=jnp.float32)  7.36 us
    ppermute x1, waiting for transfers between devices, passed_along(): return lax.ppermute(block, axis, route)  5.39 us
    ppermute x1, starting transfers between devices, passed_along(): return lax.ppermute(block, axis, route)  4.25 us
  transfers between devices with their start and end apart: 4, of which 3 were waited for; matrix products, arithmetic and copies ran while one was open for 8% of the time, Pallas kernels for 0%

commit v1 on v0

v1 whole, which is shorter than its diff:
```python
import functools

import jax
import jax.numpy as jnp
from jax import lax
from jax.experimental import pallas as pl
from jax.experimental.pallas import tpu as pltpu
from jax.sharding import PartitionSpec as P

GROUPS = 32
LANES = 128

epsilon = 1e-06

whole = pl.BlockSpec(memory_space=pltpu.VMEM)
scalars = pl.BlockSpec(memory_space=pltpu.SMEM)


def params(mib):
    return pltpu.CompilerParams(vmem_limit_bytes=mib * 2**20)


def flip(axis, distance):
    return [(i, i ^ distance) for i in range(lax.axis_size(axis))]


def stats_kernel(x_ref, out_ref):
    frames, rows, cols, channels = x_ref.shape
    entries = frames * rows * cols
    for block in range(channels // LANES):
        lanes = pl.ds(block * LANES, LANES)
        total = jnp.zeros((8, LANES), jnp.float32)
        for f in range(frames):
            for r in range(rows):
                x = x_ref[f, r, :, lanes].astype(jnp.float32)
                total = total + jnp.sum(x.reshape(-1, 8, LANES), axis=0)
        mean = jnp.sum(total, axis=0, keepdims=True) / entries
        total = jnp.zeros((8, LANES), jnp.float32)
        for f in range(frames):
            for r in range(rows):
                x = x_ref[f, r, :, lanes].astype(jnp.float32) - mean
                total = total + jnp.sum((x * x).reshape(-1, 8, LANES), axis=0)
        out_ref[0:1, lanes] = mean
        out_ref[1:2, lanes] = jnp.sum(total, axis=0, keepdims=True)


def local_stats(latents):
    return pl.pallas_call(
        stats_kernel,
        out_shape=jax.ShapeDtypeStruct((2, latents.shape[3]), jnp.float32),
        in_specs=[whole],
        out_specs=whole,
        compiler_params=params(8),
    )(latents)


def merge(one, other, entries):
    apart = one[0] - other[0]
    mean = 0.5 * (one[0] + other[0])
    return jnp.stack([mean, one[1] + other[1] + apart * apart * (0.5 * entries)])


def group_stats(stats, entries):
    channels = stats.shape[1]
    means = stats[0].reshape(GROUPS, channels // GROUPS)
    apart = stats[1].reshape(GROUPS, channels // GROUPS)
    mean = jnp.mean(means, axis=1, keepdims=True)
    spread = jnp.sum(apart + entries * (means - mean) ** 2, axis=1, keepdims=True)
    var = spread / (entries * (channels // GROUPS))
    scale = lax.rsqrt(var + epsilon)
    shape = means.shape
    return (
        jnp.broadcast_to(mean, shape).reshape(channels),
        jnp.broadcast_to(scale, shape).reshape(channels),
    )


def activate_kernel(place_ref, norm_ref, *refs):
    *piece_refs, even_ref, odd_ref, scratch = refs
    held, rows, cols, channels = piece_refs[0].shape
    frames = held * len(piece_refs)
    blocks = channels // LANES

    def step(index, carry):
        r = index // blocks
        lanes = pl.ds(pl.multiple_of((index % blocks) * LANES, LANES), LANES)
        mean = norm_ref[0:1, lanes]
        scale = norm_ref[1:2, lanes]
        bias = norm_ref[2:3, lanes]
        for p, piece_ref in enumerate(piece_refs):
            for f in range(held):
                x = piece_ref[f, r, :, lanes].astype(jnp.float32)
                v = (x - mean) * scale + bias
                h = 0.5 * v
                scratch[pl.ds(frames + place_ref[p] + f, cols, stride=frames), :] = h + h * jnp.tanh(h)
        last = (cols + 1) * frames
        scratch[0:frames, :] = scratch[2 * frames : 3 * frames, :]
        scratch[last : last + frames, :] = scratch[last - 2 * frames : last - frames, :]
        even_ref[r, :, lanes] = scratch[...].astype(jnp.bfloat16)
        odd_ref[r, :, lanes] = scratch[frames:last, :].astype(jnp.bfloat16)
        return carry

    lax.fori_loop(0, rows * blocks, step, 0)


def activate(places, norm, pieces):
    held, rows, cols, channels = pieces[0].shape
    frames = held * len(pieces)
    return pl.pallas_call(
        activate_kernel,
        out_shape=(
            jax.ShapeDtypeStruct((rows, (cols + 2) * frames, channels), jnp.bfloat16),
            jax.ShapeDtypeStruct((rows, cols * frames, channels), jnp.bfloat16),
        ),
        in_specs=[scalars, whole] + [whole] * len(pieces),
        out_specs=(whole, whole),
        scratch_shapes=[pltpu.VMEM(((cols + 2) * frames, LANES), jnp.float32)],
        compiler_params=params(24),
        cost_estimate=pl.CostEstimate(
            flops=10 * frames * rows * cols * channels,
            bytes_accessed=6 * frames * rows * cols * channels,
            transcendentals=frames * rows * cols * channels,
        ),
    )(places, norm, *pieces)


def conv_kernel(count, held, place_ref, slot_ref, even_ref, odd_ref, bias_ref, *refs):
    piece_refs, refs = refs[:count], refs[count:]
    out_refs, (taps, sums, placed) = refs[:-3], refs[-3:]
    rows = even_ref.shape[0] - 2
    per_row = odd_ref.shape[1]
    frames = held * len(out_refs)
    cols = per_row // frames
    channels = even_ref.shape[2]
    width = taps.shape[2] * taps.shape[3]
    for p, piece_ref in enumerate(piece_refs):
        slot = slot_ref[p]
        for tap in range(27):
            taps[tap % 9, tap // 9, slot] = piece_ref[tap]

    for tap in range(9):
        b, c = tap // 3, tap % 3
        weight = taps[tap].reshape(3 * width, channels)
        for y in range(rows):
            if c == 1:
                window = odd_ref[y + b]
            else:
                window = even_ref[y + b, pl.ds(c * frames, per_row), :]
            product = lax.dot_general(
                window, weight, (((1,), (1,)), ((), ())), preferred_element_type=jnp.float32
            )
            for a in range(3):
                part = product[:, a * width : (a + 1) * width]
                if tap == 0:
                    sums[a, y * per_row : (y + 1) * per_row, :] = part
                else:
                    sums[a, y * per_row : (y + 1) * per_row, :] += part

    for f in range(frames):
        value = bias_ref[...] + jnp.zeros((rows * cols, width), jnp.float32)
        for a in range(3):
            if f + a >= 2:
                value = value + sums[a, pl.ds(f + a - 2, rows * cols, stride=frames), :]
        placed[f] = value.astype(jnp.bfloat16)
    for p, out_ref in enumerate(out_refs):
        out_ref[...] = placed[pl.ds(place_ref[p], held)]


def convolve(places, slots, even, odd, bias, pieces, groups, held):
    rows, per_row, channels = even.shape[0] - 2, odd.shape[1], even.shape[2]
    frames = held * groups
    positions = rows * per_row // frames
    each = pieces[0].shape[1]
    width = each * len(pieces)
    return pl.pallas_call(
        functools.partial(conv_kernel, len(pieces), held),
        out_shape=tuple(
            jax.ShapeDtypeStruct((held, positions, width), jnp.bfloat16) for _ in range(groups)
        ),
        in_specs=[scalars, scalars] + [whole] * (3 + len(pieces)),
        out_specs=tuple(whole for _ in range(groups)),
        scratch_shapes=[
            pltpu.VMEM((9, 3, len(pieces), each, channels), jnp.bfloat16),
            pltpu.VMEM((3, rows * per_row, width), jnp.float32),
            pltpu.VMEM((frames, positions, width), jnp.bfloat16),
        ],
        compiler_params=params(32),
        cost_estimate=pl.CostEstimate(
            flops=2 * 27 * rows * per_row * channels * width,
            bytes_accessed=2 * 27 * channels * width + 4 * even.size,
            transcendentals=0,
        ),
    )(places, slots, even, odd, bias, *pieces)


def place_kernel(place_ref, *refs):
    *piece_refs, out_ref = refs
    width = piece_refs[0].shape[2]
    for p, piece_ref in enumerate(piece_refs):
        start = pl.multiple_of(place_ref[p] * width, LANES)
        out_ref[:, :, pl.ds(start, width)] = piece_ref[...]


def place(groups, pieces):
    held, positions, width = pieces[0].shape
    return pl.pallas_call(
        place_kernel,
        out_shape=jax.ShapeDtypeStruct((held, positions, width * len(pieces)), jnp.bfloat16),
        in_specs=[scalars] + [whole] * len(pieces),
        out_specs=whole,
        compiler_params=params(8),
    )(groups, *pieces)


def line_pieces(weight):
    cores = 2

    def both(pairs):
        return [(cores * a + c, cores * b + c) for a, b in pairs for c in range(cores)]

    second = lax.ppermute(weight, "rows", flip("rows", 2 * cores))
    first = lax.ppermute(weight, "rows", flip("rows", cores))
    middle, second = lax.optimization_barrier((weight, second))
    third_ends = lax.ppermute(second, "rows", both([(1, 0), (2, 3)]))
    third_middle = lax.ppermute(middle, "rows", both([(1, 2), (2, 1)]))
    chip = lax.axis_index("rows") // cores
    third = jnp.where((chip == 0) | (chip == 3), third_ends, third_middle)
    mine = [weight, first, second, third]
    return mine + [lax.ppermute(piece, "rows", flip("rows", 1)) for piece in mine]


def body(latents, norm_gain, norm_bias, conv_weight, conv_bias):
    held, row_count, col_count, channels = latents.shape
    group_count = lax.axis_size("frames")
    strips = lax.axis_size("rows")
    group = lax.axis_index("frames")
    strip = lax.axis_index("rows")

    forward = [(i, i + 1) for i in range(strips - 1)]
    backward = [(i + 1, i) for i in range(strips - 1)]
    above = lax.ppermute(latents[:, row_count - 1 :], "rows", forward)
    below = lax.ppermute(latents[:, :1], "rows", backward)

    weight = conv_weight.transpose(0, 1, 2, 4, 3)
    weight = weight.reshape((-1,) + weight.shape[3:])
    if strips == 8:
        pieces = line_pieces(weight)
        slots = jnp.stack([strip ^ (2 * d) ^ c for c in range(2) for d in range(4)])
    else:
        gathered = lax.all_gather(weight, "rows", axis=1, tiled=True)
        pieces, slots = [gathered], jnp.zeros((1,), jnp.int32)

    above = jnp.where(strip == 0, latents[:, 1:2], above)
    below = jnp.where(strip == strips - 1, latents[:, row_count - 2 : row_count - 1], below)
    rowed = jnp.concatenate([above, latents, below], axis=1)
    strip_pieces = [rowed] + [
        lax.ppermute(rowed, "frames", flip("frames", d)) for d in range(1, group_count)
    ]

    stats = local_stats(latents)
    entries = held * row_count * col_count
    for axis in ("rows", "frames"):
        distance = 1
        while distance < lax.axis_size(axis):
            stats = merge(stats, lax.ppermute(stats, axis, flip(axis, distance)), entries)
            entries *= 2
            distance *= 2
    mean, scale = group_stats(stats, entries)
    norm = jnp.stack([mean, scale * norm_gain, norm_bias])

    groups = jnp.stack([group ^ d for d in range(group_count)]).astype(jnp.int32)
    even, odd = activate(groups * held, norm, strip_pieces)

    width = channels // group_count
    bias = lax.dynamic_slice_in_dim(conv_bias, group * width, width)[None]
    parts = convolve(
        groups * held, slots.astype(jnp.int32), even, odd, bias, pieces, group_count, held
    )
    parts = [parts[0]] + [
        lax.ppermute(parts[d], "frames", flip("frames", d)) for d in range(1, group_count)
    ]
    return place(groups, parts).reshape(latents.shape)


def solution(mesh):
    placed = (
        P("frames", "rows", None, None),
        P(),
        P(),
        P(None, None, None, None, ("frames", "rows")),
        P(),
    )
    return jax.shard_map(
        body, mesh=mesh, in_specs=placed, out_specs=P("frames", "rows", None, None), check_vma=False
    )
```

time: 172 us -> 84 us (0.49)
  blocking collectives: 43 us -> 0 us
  local copies, waits for them, and re-layouts: 37.9 us -> 4.36 us
  starting transfers between devices: 6.85 us -> 25.9 us
  between operations: 13.6 us -> 0.26 us
  waiting for transfers between devices: 49.2 us -> 36.2 us
  Pallas kernels: 0 us -> 12.3 us
  other arithmetic: 12.3 us -> 3.56 us
  matrix products: 7.36 us -> 0 us
    psum x1 -> x0, blocking collectives: 43 us -> none  [body(): lax.psum((local_sums, local_squares), ('frames', 'rows'))]
    all_gather x1 -> x0, waiting for transfers between devices: 40 us -> none  [body(): lax.all_gather(conv_weight, ('frames', 'rows'), axis=4, tiled=True)]
    ppermute x3 -> x21, waiting for transfers between devices: 8.48 us -> 36.2 us  [the longest x5 16.8 us: body(): lax.ppermute(stats, axis, flip(axis, distance))]
    unnamed x43 -> x16, local copies, waits for them, and re-layouts: 27.5 us -> 2.8 us
    ppermute x3 -> x21, starting transfers between devices: 6.84 us -> 25.9 us  [the longest x5 7.47 us: body(): lax.ppermute(stats, axis, flip(axis, distance))]
    pallas_call x0 -> x4, Pallas kernels: none -> 12.3 us  [the longest x1 8.02 us: convolve(): pl.pallas_call(functools.partial(conv_kernel, len(pieces), held), out_sha...]
    slice x3 -> x1, local copies, waits for them, and re-layouts: 9.88 us -> 0.94 us  [body(): above = lax.ppermute(latents[:, row_count - 1:], 'rows', forward)]
    concatenate x10 -> x1, other arithmetic: 8.86 us -> 1.03 us  [body(): rowed = jnp.concatenate([above, latents, below], axis=1)]
  transfers between devices with their start and end apart: 4 -> 21, of which waited for: 3 -> 7; matrix products, arithmetic and copies ran while one was open for 8% -> 6% of each run, Pallas kernels for 0% -> 3%
where the time goes in v1:
time: 84 us; the launch traced here: 82.6 us
  waiting for transfers between devices  36.2 us (43%)
  starting transfers between devices  25.9 us (31%)
  Pallas kernels  12.3 us (15%)
  local copies, waits for them, and re-layouts  4.36 us (5%)
  other arithmetic  3.56 us (4%)
    ppermute x5, waiting for transfers between devices, body(): lax.ppermute(stats, axis, flip(axis, distance))  16.8 us
    ppermute x3, waiting for transfers between devices, body(): lax.ppermute(rowed, 'frames', flip('frames', d))  10.9 us
    pallas_call x1, Pallas kernels, convolve(): pl.pallas_call(functools.partial(conv_kernel, len(pieces), held), out_sha...  8.02 us
    ppermute x5, starting transfers between devices, body(): lax.ppermute(stats, axis, flip(axis, distance))  7.47 us
    ppermute x1, waiting for transfers between devices, line_pieces(): third_ends = lax.ppermute(second, 'rows', both([(1, 0), (2, 3)]))  5.02 us
    ppermute x3, starting transfers between devices, body(): lax.ppermute(parts[d], 'frames', flip('frames', d))  3.55 us
    ppermute x3, starting transfers between devices, body(): lax.ppermute(rowed, 'frames', flip('frames', d))  3.5 us
    ppermute x3, waiting for transfers between devices, body(): lax.ppermute(parts[d], 'frames', flip('frames', d))  3.49 us
  transfers between devices with their start and end apart: 21, of which 7 were waited for; matrix products, arithmetic and copies ran while one was open for 6% of the time, Pallas kernels for 3%

profile of v1, /device:TPU:0, one launch (start us, length us, event | category | flops | bytes accessed | tf_op | source)
XLA Modules:
  0.0 82.6 jit_solution(12365633441578308282)
XLA Ops:
  0.0 1.0 %copy-done.1 = bf16[2,4,40,512]{3,2,1,0:T(8,128)(2,1)S(1)} copy-done((bf16[2,4,40,512]{3,2,1,0:T(8,128)(2,1)S(1)}, bf16[2,4,40,512]{3,2,1,0:T(8,128)(2,1)}, u32[]{:S(2)}) %copy-start.1) | copy-done | bytes 327704
  1.1 0.5 collective-permute-start
  1.7 2.6 %collective-permute-start.10 = (bf16[27,16,512]{2,1,0:T(8,128)(2,1)}, bf16[27,16,512]{2,1,0:T(8,128)(2,1)S(1)}, u32[]{:S(2)}, u32[]{:S(2)}) collective-permute-start(bf16[27,16,512]{2,1,0:T(8,128)(2,1)} %bitcast.20), channel_id=1, source_target_pairs={{0,2},{1,3},{2,0},{3,1},{4,6},{5,7},{6,4},{7,5},{8,10},{9,11},{10,... | collective-permute-start | bytes 1327112 | tf_op jit(solution)/shard_map/ppermute | solution.py:222
  4.3 2.6 %collective-permute-start.11 = (bf16[27,16,512]{2,1,0:T(8,128)(2,1)}, bf16[27,16,512]{2,1,0:T(8,128)(2,1)S(1)}, u32[]{:S(2)}, u32[]{:S(2)}) collective-permute-start(bf16[27,16,512]{2,1,0:T(8,128)(2,1)} %bitcast.21), channel_id=1, source_target_pairs={{0,4},{1,5},{2,6},{3,7},{4,0},{5,1},{6,2},{7,3},{8,12},{9,13},{10,... | collective-permute-start | bytes 1327112 | tf_op jit(solution)/shard_map/ppermute | solution.py:221
  6.9 0.5 collective-permute-start.1
  7.5 0.9 %fusion.6 = (bf16[2,1,40,512]{3,2,1,0:T(8,128)(2,1)S(1)}, bf16[2,1,40,512]{3,2,1,0:T(8,128)(2,1)S(1)}) fusion(bf16[2,4,40,512]{3,2,1,0:T(8,128)(2,1)} %x_ref.1), kind=kLoop, calls=%fused_computation.31 | loop fusion | bytes 327680 | tf_op jit(solution)/shard_map/slice | solution.py:241
  8.4 1.5 %collective-permute-start.5 = (bf16[2,1,40,512]{3,2,1,0:T(8,128)(2,1)S(1)}, bf16[2,1,40,512]{3,2,1,0:T(8,128)(2,1)S(1)}, u32[]{:S(2)}, u32[]{:S(2)}) collective-permute-start(bf16[2,1,40,512]{3,2,1,0:T(8,128)(2,1)S(1)} %get-tuple-element.27), channel_id=1, source_target_pairs={{0,1},{1,2},{2,3},{3,4},{4,5},{5,6},{6,7},{8,9},{9,10},{10,11},{11... | collective-permute-start | bytes 245768 | tf_op jit(solution)/shard_map/ppermute | solution.py:241
  9.9 1.3 %collective-permute-start.6 = (bf16[2,1,40,512]{3,2,1,0:T(8,128)(2,1)S(1)}, bf16[2,1,40,512]{3,2,1,0:T(8,128)(2,1)S(1)}, u32[]{:S(2)}, u32[]{:S(2)}) collective-permute-start(bf16[2,1,40,512]{3,2,1,0:T(8,128)(2,1)S(1)} %get-tuple-element.28), channel_id=1, source_target_pairs={{1,0},{2,1},{3,2},{4,3},{5,4},{6,5},{7,6},{9,8},{10,9},{11,10},{12... | collective-permute-start | bytes 245768 | tf_op jit(solution)/shard_map/ppermute | solution.py:242
  11.2 13.5 %collective-permute-done.1 = f32[2,512]{1,0:T(2,128)S(1)} collective-permute-done((f32[2,512]{1,0:T(2,128)S(1)}, f32[2,512]{1,0:T(2,128)S(1)}, u32[]{:S(2)}, u32[]{:S(2)}) %collective-permute-start.1) | collective-permute-done | bytes 4128 | tf_op jit(solution)/shard_map/ppermute | solution.py:265
  24.8 3.0 %collective-permute-start.2 = (f32[2,512]{1,0:T(2,128)S(1)}, f32[2,512]{1,0:T(2,128)S(1)}, u32[]{:S(2)}, u32[]{:S(2)}) collective-permute-start(f32[2,512]{1,0:T(2,128)S(1)} %pad_maximum_fusion.3), channel_id=1, source_target_pairs={{0,4},{1,5},{2,6},{3,7},{4,0},{5,1},{6,2},{7,3},{8,12},{9,13},{10,... | collective-permute-start | bytes 12296 | tf_op jit(solution)/shard_map/ppermute | solution.py:265
  27.8 1.5 %collective-permute-done.2 = f32[2,512]{1,0:T(2,128)S(1)} collective-permute-done((f32[2,512]{1,0:T(2,128)S(1)}, f32[2,512]{1,0:T(2,128)S(1)}, u32[]{:S(2)}, u32[]{:S(2)}) %collective-permute-start.2) | collective-permute-done | bytes 4128 | tf_op jit(solution)/shard_map/ppermute | solution.py:265
  29.4 1.7 %collective-permute-start.3 = (f32[2,512]{1,0:T(2,128)S(1)}, f32[2,512]{1,0:T(2,128)S(1)}, u32[]{:S(2)}, u32[]{:S(2)}) collective-permute-start(f32[2,512]{1,0:T(2,128)S(1)} %pad_maximum_fusion.4), channel_id=1, source_target_pairs={{0,8},{8,0},{16,24},{24,16},{1,9},{9,1},{17,25},{25,17},{2,10},{10... | collective-permute-start | bytes 12296 | tf_op jit(solution)/shard_map/ppermute | solution.py:265
  31.3 1.8 %collective-permute-done.3 = f32[2,512]{1,0:T(2,128)S(1)} collective-permute-done((f32[2,512]{1,0:T(2,128)S(1)}, f32[2,512]{1,0:T(2,128)S(1)}, u32[]{:S(2)}, u32[]{:S(2)}) %collective-permute-start.3) | collective-permute-done | bytes 4128 | tf_op jit(solution)/shard_map/ppermute | solution.py:265
  33.1 1.7 %collective-permute-start.4 = (f32[2,512]{1,0:T(2,128)S(1)}, f32[2,512]{1,0:T(2,128)S(1)}, u32[]{:S(2)}, u32[]{:S(2)}) collective-permute-start(f32[2,512]{1,0:T(2,128)S(1)} %pad_maximum_fusion.5), channel_id=1, source_target_pairs={{0,16},{8,24},{16,0},{24,8},{1,17},{9,25},{17,1},{25,9},{2,18},{10... | collective-permute-start | bytes 12296 | tf_op jit(solution)/shard_map/ppermute | solution.py:265
  34.8 1.0 %slice_select_fusion.1 = (bf16[2,1,40,512]{3,2,1,0:T(8,128)(2,1)S(1)}, bf16[2,1,40,512]{3,2,1,0:T(8,128)(2,1)S(1)}) fusion(bf16[2,1,40,512]{3,2,1,0:T(8,128)(2,1)S(1)} %collective-permute-done.5, bf16[2,4,40,512]{3,2,1,0:T(8,128)(2,1)} %x_ref.1, pred[]{:T(512)S(6)} %eq.12, bf16[2,1,40,512]{3,2,1,0:T(8,128)(2,1)S(1)} %collective-permute-done.6, pred[]{:T(512)S(6)} %eq.13), kind=kLoop, calls=%fused_computation.3 | loop fusion | flops 81920 | bytes 491522 | tf_op jit(solution)/shard_map/jit(_where)/select_n | solution.py:253
  35.8 1.3 %collective-permute-start.12 = (bf16[27,16,512]{2,1,0:T(8,128)(2,1)S(1)}, bf16[27,16,512]{2,1,0:T(8,128)(2,1)S(1)}, u32[]{:S(2)}, u32[]{:S(2)}) collective-permute-start(bf16[27,16,512]{2,1,0:T(8,128)(2,1)S(1)} %collective-permute-done.11.refs_2_), channel_id=1, source_target_pairs={{2,0},{3,1},{4,6},{5,7},{10,8},{11,9},{12,14},{13,15},{18,16},{19,... | collective-permute-start | bytes 1327112 | tf_op jit(solution)/shard_map/ppermute | solution.py:224
  37.1 1.4 %collective-permute-start.13 = (bf16[27,16,512]{2,1,0:T(8,128)(2,1)}, bf16[27,16,512]{2,1,0:T(8,128)(2,1)}, u32[]{:S(2)}, u32[]{:S(2)}) collective-permute-start(bf16[27,16,512]{2,1,0:T(8,128)(2,1)} %bitcast.22), channel_id=1, source_target_pairs={{2,4},{3,5},{4,2},{5,3},{10,12},{11,13},{12,10},{13,11},{18,20},{1... | collective-permute-start | bytes 1327112 | tf_op jit(solution)/shard_map/ppermute | solution.py:225
  38.5 1.0 %pad_maximum_fusion.refs_0_ = bf16[2,6,40,512]{3,2,1,0:T(8,128)(2,1)S(1)} fusion(bf16[2,1,40,512]{3,2,1,0:T(8,128)(2,1)S(1)} %get-tuple-element.26, bf16[2,4,40,512]{3,2,1,0:T(8,128)(2,1)} %x_ref.1, bf16[2,1,40,512]{3,2,1,0:T(8,128)(2,1)S(1)} %get-tuple-element.25), kind=kLoop, calls=%fused_computation | loop fusion | flops 491520 | bytes 983040 | tf_op jit(solution)/shard_map/concatenate | solution.py:255
  39.6 1.6 %collective-permute-start.7 = (bf16[2,6,40,512]{3,2,1,0:T(8,128)(2,1)S(1)}, bf16[2,6,40,512]{3,2,1,0:T(8,128)(2,1)S(1)}, u32[]{:S(2)}, u32[]{:S(2)}) collective-permute-start(bf16[2,6,40,512]{3,2,1,0:T(8,128)(2,1)S(1)} %pad_maximum_fusion.refs_0_), channel_id=1, source_target_pairs={{0,8},{8,0},{16,24},{24,16},{1,9},{9,1},{17,25},{25,17},{2,10},{10... | collective-permute-start | bytes 1474568 | tf_op jit(solution)/shard_map/ppermute | solution.py:257
  42.0 5.0 %collective-permute-done.12 = bf16[27,16,512]{2,1,0:T(8,128)(2,1)S(1)} collective-permute-done((bf16[27,16,512]{2,1,0:T(8,128)(2,1)S(1)}, bf16[27,16,512]{2,1,0:T(8,128)(2,1)S(1)}, u32[]{:S(2)}, u32[]{:S(2)}) %collective-permute-start.12) | collective-permute-done | bytes 442400 | tf_op jit(solution)/shard_map/ppermute | solution.py:224
  47.0 0.8 copy-done.5
  47.8 1.4 %collective-permute-start.9 = (bf16[2,6,40,512]{3,2,1,0:T(8,128)(2,1)S(1)}, bf16[2,6,40,512]{3,2,1,0:T(8,128)(2,1)S(1)}, u32[]{:S(2)}, u32[]{:S(2)}) collective-permute-start(bf16[2,6,40,512]{3,2,1,0:T(8,128)(2,1)S(1)} %pad_maximum_fusion.refs_0_), channel_id=1, source_target_pairs={{0,24},{8,16},{16,8},{24,0},{1,25},{9,17},{17,9},{25,1},{2,26},{10... | collective-permute-start | bytes 1474568 | tf_op jit(solution)/shard_map/ppermute | solution.py:257
  49.2 1.1 %broadcast_select_fusion.refs_3_ = bf16[27,16,512]{2,1,0:T(8,128)(2,1)S(1)} fusion(bf16[27,16,512]{2,1,0:T(8,128)(2,1)} %copy-done.5, bf16[27,16,512]{2,1,0:T(8,128)(2,1)} %collective-permute-done.13, pred[]{:T(512)S(6)} %or.3), kind=kLoop, calls=%fused_computation.1 | loop fusion | flops 221184 | bytes 1327105 | tf_op jit(solution)/shard_map/jit(_where)/select_n | solution.py:227
  50.9 10.9 %collective-permute-done.8.refs_2_ = bf16[2,6,40,512]{3,2,1,0:T(8,128)(2,1)S(1)} collective-permute-done((bf16[2,6,40,512]{3,2,1,0:T(8,128)(2,1)S(1)}, bf16[2,6,40,512]{3,2,1,0:T(8,128)(2,1)S(1)}, u32[]{:S(2)}, u32[]{:S(2)}) %collective-permute-start.8) | collective-permute-done | bytes 491552 | tf_op jit(solution)/shard_map/ppermute | solution.py:257
  62.3 2.8 %shard_map.56 = (bf16[6,336,512]{2,1,0:T(8,128)(2,1)S(1)}, bf16[6,320,512]{2,1,0:T(8,128)(2,1)S(1)}) custom-call(s32[4]{0:T(128)S(1)} %get-tuple-element.23.place_ref, f32[3,512]{1,0:T(4,128)S(1)} %pad_maximum_fusion.1.norm_ref, bf16[2,6,40,512]{3,2,1,0:T(8,128)(2,1)S(1)} %pad_maximum_fusion.refs_0_, ...), custom_call_target="tpu_custom_call" | custom-call | flops 9830400 | bytes 5898240 | tf_op jit(solution)/shard_map/pallas_call | solution.py:109
  65.2 1.0 %copy-done.4 = bf16[27,16,512]{2,1,0:T(8,128)(2,1)S(1)} copy-done((bf16[27,16,512]{2,1,0:T(8,128)(2,1)S(1)}, bf16[27,16,512]{2,1,0:T(8,128)(2,1)}, u32[]{:S(2)}) %copy-start.4) | copy-done | bytes 442392
  66.2 8.0 %shard_map.57 = (bf16[2,160,128]{2,1,0:T(8,128)(2,1)S(1)}, bf16[2,160,128]{2,1,0:T(8,128)(2,1)S(1)}, bf16[2,160,128]{2,1,0:T(8,128)(2,1)S(1)}, bf16[2,160,128]{2,1,0:T(8,128)(2,1)S(1)}) custom-call(s32[4]{0:T(128)S(1)} %get-tuple-element.23.place_ref, s32[8]{0:T(128)S(1)} %stack.84.slot_ref, bf16[6,336,512]{2,1,0:T(8,128)(2,1)S(1)} %get-tuple-element.13.even_ref, ...), custom_call_target="tpu_custom_call" | custom-call | flops 4529848320 | bytes 7667712 | tf_op jit(solution)/shard_map/pallas_call | solution.py:175
  74.2 0.8 %collective-permute-start.18 = (bf16[2,160,128]{2,1,0:T(8,128)(2,1)S(1)}, bf16[2,160,128]{2,1,0:T(8,128)(2,1)S(1)}, u32[]{:S(2)}, u32[]{:S(2)}) collective-permute-start(bf16[2,160,128]{2,1,0:T(8,128)(2,1)S(1)} %get-tuple-element.18), channel_id=1, source_target_pairs={{0,8},{8,0},{16,24},{24,16},{1,9},{9,1},{17,25},{25,17},{2,10},{10... | collective-permute-start | bytes 245768 | tf_op jit(solution)/shard_map/ppermute | solution.py:280
  75.6 2.2 %collective-permute-start.20 = (bf16[2,160,128]{2,1,0:T(8,128)(2,1)S(1)}, bf16[2,160,128]{2,1,0:T(8,128)(2,1)S(1)}, u32[]{:S(2)}, u32[]{:S(2)}) collective-permute-start(bf16[2,160,128]{2,1,0:T(8,128)(2,1)S(1)} %get-tuple-element.20), channel_id=1, source_target_pairs={{0,24},{8,16},{16,8},{24,0},{1,25},{9,17},{17,9},{25,1},{2,26},{10... | collective-permute-start | bytes 245768 | tf_op jit(solution)/shard_map/ppermute | solution.py:280
  77.8 1.8 %collective-permute-done.18.refs_1_ = bf16[2,160,128]{2,1,0:T(8,128)(2,1)S(1)} collective-permute-done((bf16[2,160,128]{2,1,0:T(8,128)(2,1)S(1)}, bf16[2,160,128]{2,1,0:T(8,128)(2,1)S(1)}, u32[]{:S(2)}, u32[]{:S(2)}) %collective-permute-start.18) | collective-permute-done | bytes 81952 | tf_op jit(solution)/shard_map/ppermute | solution.py:280
  79.5 1.7 %collective-permute-done.19.refs_2_ = bf16[2,160,128]{2,1,0:T(8,128)(2,1)S(1)} collective-permute-done((bf16[2,160,128]{2,1,0:T(8,128)(2,1)S(1)}, bf16[2,160,128]{2,1,0:T(8,128)(2,1)S(1)}, u32[]{:S(2)}, u32[]{:S(2)}) %collective-permute-start.19) | collective-permute-done | bytes 81952 | tf_op jit(solution)/shard_map/ppermute | solution.py:280
  81.2 1.3 %shard_map.58 = bf16[2,160,512]{2,1,0:T(8,128)(2,1)} custom-call(s32[4]{0:T(128)S(1)} %get-tuple-element.24.place_ref, bf16[2,160,128]{2,1,0:T(8,128)(2,1)S(1)} %get-tuple-element.17.refs_0_, bf16[2,160,128]{2,1,0:T(8,128)(2,1)S(1)} %collective-permute-done.18.refs_1_, bf16[2,160,128]{2,1,0:T(8,128)(2,1)S(1)} %collective-permute-done.19.refs_2_, ...), custom_call_target="tpu_custom_call" | custom-call | tf_op jit(solution)/shard_map/pallas_call | solution.py:206
  (58 shorter events, 2.9 us)
Async XLA Ops:
  0.0 31.1 %copy-start = (f32[512]{0:T(512)S(1)}, f32[512]{0:T(512)}, u32[]{:S(2)}) copy-start(f32[512]{0:T(512)} %param.9) | copy-start | bytes 6148
  0.0 1.0 %copy-start.1 = (bf16[2,4,40,512]{3,2,1,0:T(8,128)(2,1)S(1)}, bf16[2,4,40,512]{3,2,1,0:T(8,128)(2,1)}, u32[]{:S(2)}) copy-start(bf16[2,4,40,512]{3,2,1,0:T(8,128)(2,1)} %x_ref.1) | copy-start | bytes 983044
  1.0 46.0 %copy-start.2 = (bf16[3,3,3,512,16]{3,4,2,1,0:T(8,128)(2,1)S(1)}, bf16[3,3,3,512,16]{3,4,2,1,0:T(8,128)(2,1)}, u32[]{:S(2)}) copy-start(bf16[3,3,3,512,16]{3,4,2,1,0:T(8,128)(2,1)} %param.8) | copy-start | bytes 1327108
  1.0 61.2 %copy-start.6 = (f32[512]{0:T(512)S(1)}, f32[512]{0:T(512)}, u32[]{:S(2)}) copy-start(f32[512]{0:T(512)} %param.6) | copy-start | bytes 6148
  1.0 61.3 %copy-start.7 = (f32[512]{0:T(512)S(1)}, f32[512]{0:T(512)}, u32[]{:S(2)}) copy-start(f32[512]{0:T(512)} %param.7) | copy-start | bytes 6148
  1.1 5.8 %collective-permute-start = (f32[2,512]{1,0:T(2,128)S(1)}, f32[2,512]{1,0:T(2,128)S(1)}, u32[]{:S(2)}, u32[]{:S(2)}) collective-permute-start(f32[2,512]{1,0:T(2,128)S(1)} %shard_map.55), channel_id=1, source_target_pairs={{0,1},{1,0},{2,3},{3,2},{4,5},{5,4},{6,7},{7,6},{8,9},{9,8},{10,11... | collective-permute-start | bytes 12296 | tf_op jit(solution)/shard_map/ppermute | solution.py:265
  1.7 48.6 %collective-permute-start.10 = (bf16[27,16,512]{2,1,0:T(8,128)(2,1)}, bf16[27,16,512]{2,1,0:T(8,128)(2,1)S(1)}, u32[]{:S(2)}, u32[]{:S(2)}) collective-permute-start(bf16[27,16,512]{2,1,0:T(8,128)(2,1)} %bitcast.20), channel_id=1, source_target_pairs={{0,2},{1,3},{2,0},{3,1},{4,6},{5,7},{6,4},{7,5},{8,10},{9,11},{10,... | collective-permute-start | bytes 1327112 | tf_op jit(solution)/shard_map/ppermute | solution.py:222
  4.3 31.5 %collective-permute-start.11 = (bf16[27,16,512]{2,1,0:T(8,128)(2,1)}, bf16[27,16,512]{2,1,0:T(8,128)(2,1)S(1)}, u32[]{:S(2)}, u32[]{:S(2)}) collective-permute-start(bf16[27,16,512]{2,1,0:T(8,128)(2,1)} %bitcast.21), channel_id=1, source_target_pairs={{0,4},{1,5},{2,6},{3,7},{4,0},{5,1},{6,2},{7,3},{8,12},{9,13},{10,... | collective-permute-start | bytes 1327112 | tf_op jit(solution)/shard_map/ppermute | solution.py:221
  6.9 17.8 %collective-permute-start.1 = (f32[2,512]{1,0:T(2,128)S(1)}, f32[2,512]{1,0:T(2,128)S(1)}, u32[]{:S(2)}, u32[]{:S(2)}) collective-permute-start(f32[2,512]{1,0:T(2,128)S(1)} %pad_maximum_fusion.2), channel_id=1, source_target_pairs={{0,2},{1,3},{2,0},{3,1},{4,6},{5,7},{6,4},{7,5},{8,10},{9,11},{10,... | collective-permute-start | bytes 12296 | tf_op jit(solution)/shard_map/ppermute | solution.py:265
  8.4 26.4 %collective-permute-start.5 = (bf16[2,1,40,512]{3,2,1,0:T(8,128)(2,1)S(1)}, bf16[2,1,40,512]{3,2,1,0:T(8,128)(2,1)S(1)}, u32[]{:S(2)}, u32[]{:S(2)}) collective-permute-start(bf16[2,1,40,512]{3,2,1,0:T(8,128)(2,1)S(1)} %get-tuple-element.27), channel_id=1, source_target_pairs={{0,1},{1,2},{2,3},{3,4},{4,5},{5,6},{6,7},{8,9},{9,10},{10,11},{11... | collective-permute-start | bytes 245768 | tf_op jit(solution)/shard_map/ppermute | solution.py:241
  9.9 24.9 %collective-permute-start.6 = (bf16[2,1,40,512]{3,2,1,0:T(8,128)(2,1)S(1)}, bf16[2,1,40,512]{3,2,1,0:T(8,128)(2,1)S(1)}, u32[]{:S(2)}, u32[]{:S(2)}) collective-permute-start(bf16[2,1,40,512]{3,2,1,0:T(8,128)(2,1)S(1)} %get-tuple-element.28), channel_id=1, source_target_pairs={{1,0},{2,1},{3,2},{4,3},{5,4},{6,5},{7,6},{9,8},{10,9},{11,10},{12... | collective-permute-start | bytes 245768 | tf_op jit(solution)/shard_map/ppermute | solution.py:242
  24.8 4.6 %collective-permute-start.2 = (f32[2,512]{1,0:T(2,128)S(1)}, f32[2,512]{1,0:T(2,128)S(1)}, u32[]{:S(2)}, u32[]{:S(2)}) collective-permute-start(f32[2,512]{1,0:T(2,128)S(1)} %pad_maximum_fusion.3), channel_id=1, source_target_pairs={{0,4},{1,5},{2,6},{3,7},{4,0},{5,1},{6,2},{7,3},{8,12},{9,13},{10,... | collective-permute-start | bytes 12296 | tf_op jit(solution)/shard_map/ppermute | solution.py:265
  29.4 3.7 %collective-permute-start.3 = (f32[2,512]{1,0:T(2,128)S(1)}, f32[2,512]{1,0:T(2,128)S(1)}, u32[]{:S(2)}, u32[]{:S(2)}) collective-permute-start(f32[2,512]{1,0:T(2,128)S(1)} %pad_maximum_fusion.4), channel_id=1, source_target_pairs={{0,8},{8,0},{16,24},{24,16},{1,9},{9,1},{17,25},{25,17},{2,10},{10... | collective-permute-start | bytes 12296 | tf_op jit(solution)/shard_map/ppermute | solution.py:265
  33.1 8.0 %collective-permute-start.4 = (f32[2,512]{1,0:T(2,128)S(1)}, f32[2,512]{1,0:T(2,128)S(1)}, u32[]{:S(2)}, u32[]{:S(2)}) collective-permute-start(f32[2,512]{1,0:T(2,128)S(1)} %pad_maximum_fusion.5), channel_id=1, source_target_pairs={{0,16},{8,24},{16,0},{24,8},{1,17},{9,25},{17,1},{25,9},{2,18},{10... | collective-permute-start | bytes 12296 | tf_op jit(solution)/shard_map/ppermute | solution.py:265
  35.8 12.0 %copy-start.3 = (bf16[27,16,512]{2,1,0:T(8,128)(2,1)}, bf16[27,16,512]{2,1,0:T(8,128)(2,1)S(1)}, u32[]{:S(2)}) copy-start(bf16[27,16,512]{2,1,0:T(8,128)(2,1)S(1)} %collective-permute-done.11.refs_2_) | copy-start | bytes 1327108
  35.8 11.2 %collective-permute-start.12 = (bf16[27,16,512]{2,1,0:T(8,128)(2,1)S(1)}, bf16[27,16,512]{2,1,0:T(8,128)(2,1)S(1)}, u32[]{:S(2)}, u32[]{:S(2)}) collective-permute-start(bf16[27,16,512]{2,1,0:T(8,128)(2,1)S(1)} %collective-permute-done.11.refs_2_), channel_id=1, source_target_pairs={{2,0},{3,1},{4,6},{5,7},{10,8},{11,9},{12,14},{13,15},{18,16},{19,... | collective-permute-start | bytes 1327112 | tf_op jit(solution)/shard_map/ppermute | solution.py:224
  37.1 10.7 %collective-permute-start.13 = (bf16[27,16,512]{2,1,0:T(8,128)(2,1)}, bf16[27,16,512]{2,1,0:T(8,128)(2,1)}, u32[]{:S(2)}, u32[]{:S(2)}) collective-permute-start(bf16[27,16,512]{2,1,0:T(8,128)(2,1)} %bitcast.22), channel_id=1, source_target_pairs={{2,4},{3,5},{4,2},{5,3},{10,12},{11,13},{12,10},{13,11},{18,20},{1... | collective-permute-start | bytes 1327112 | tf_op jit(solution)/shard_map/ppermute | solution.py:225
  39.6 10.8 %collective-permute-start.7 = (bf16[2,6,40,512]{3,2,1,0:T(8,128)(2,1)S(1)}, bf16[2,6,40,512]{3,2,1,0:T(8,128)(2,1)S(1)}, u32[]{:S(2)}, u32[]{:S(2)}) collective-permute-start(bf16[2,6,40,512]{3,2,1,0:T(8,128)(2,1)S(1)} %pad_maximum_fusion.refs_0_), channel_id=1, source_target_pairs={{0,8},{8,0},{16,24},{24,16},{1,9},{9,1},{17,25},{25,17},{2,10},{10... | collective-permute-start | bytes 1474568 | tf_op jit(solution)/shard_map/ppermute | solution.py:257
  41.1 20.6 %collective-permute-start.8 = (bf16[2,6,40,512]{3,2,1,0:T(8,128)(2,1)S(1)}, bf16[2,6,40,512]{3,2,1,0:T(8,128)(2,1)S(1)}, u32[]{:S(2)}, u32[]{:S(2)}) collective-permute-start(bf16[2,6,40,512]{3,2,1,0:T(8,128)(2,1)S(1)} %pad_maximum_fusion.refs_0_), channel_id=1, source_target_pairs={{0,16},{8,24},{16,0},{24,8},{1,17},{9,25},{17,1},{25,9},{2,18},{10... | collective-permute-start | bytes 1474568 | tf_op jit(solution)/shard_map/ppermute | solution.py:257
  47.0 0.8 copy-start.5
  47.0 18.1 %collective-permute-start.14 = (bf16[27,16,512]{2,1,0:T(8,128)(2,1)S(1)}, bf16[27,16,512]{2,1,0:T(8,128)(2,1)}, u32[]{:S(2)}, u32[]{:S(2)}) collective-permute-start(bf16[27,16,512]{2,1,0:T(8,128)(2,1)S(1)} %bitcast.23), channel_id=1, source_target_pairs={{0,1},{1,0},{2,3},{3,2},{4,5},{5,4},{6,7},{7,6},{8,9},{9,8},{10,11... | collective-permute-start | bytes 1327112 | tf_op jit(solution)/shard_map/ppermute | solution.py:229
  47.8 14.5 %collective-permute-start.9 = (bf16[2,6,40,512]{3,2,1,0:T(8,128)(2,1)S(1)}, bf16[2,6,40,512]{3,2,1,0:T(8,128)(2,1)S(1)}, u32[]{:S(2)}, u32[]{:S(2)}) collective-permute-start(bf16[2,6,40,512]{3,2,1,0:T(8,128)(2,1)S(1)} %pad_maximum_fusion.refs_0_), channel_id=1, source_target_pairs={{0,24},{8,16},{16,8},{24,0},{1,25},{9,17},{17,9},{25,1},{2,26},{10... | collective-permute-start | bytes 1474568 | tf_op jit(solution)/shard_map/ppermute | solution.py:257
  50.3 14.8 %collective-permute-start.16 = (bf16[27,16,512]{2,1,0:T(8,128)(2,1)}, bf16[27,16,512]{2,1,0:T(8,128)(2,1)}, u32[]{:S(2)}, u32[]{:S(2)}) collective-permute-start(bf16[27,16,512]{2,1,0:T(8,128)(2,1)} %copy-done.3), channel_id=1, source_target_pairs={{0,1},{1,0},{2,3},{3,2},{4,5},{5,4},{6,7},{7,6},{8,9},{9,8},{10,11... | collective-permute-start | bytes 1327112 | tf_op jit(solution)/shard_map/ppermute | solution.py:229
  50.4 14.7 %collective-permute-start.15 = (bf16[27,16,512]{2,1,0:T(8,128)(2,1)S(1)}, bf16[27,16,512]{2,1,0:T(8,128)(2,1)}, u32[]{:S(2)}, u32[]{:S(2)}) collective-permute-start(bf16[27,16,512]{2,1,0:T(8,128)(2,1)S(1)} %collective-permute-done.10.refs_1_), channel_id=1, source_target_pairs={{0,1},{1,0},{2,3},{3,2},{4,5},{5,4},{6,7},{7,6},{8,9},{9,8},{10,11... | collective-permute-start | bytes 1327112 | tf_op jit(solution)/shard_map/ppermute | solution.py:229
  61.7 3.4 %collective-permute-start.17 = (bf16[27,16,512]{2,1,0:T(8,128)(2,1)S(1)}, bf16[27,16,512]{2,1,0:T(8,128)(2,1)}, u32[]{:S(2)}, u32[]{:S(2)}) collective-permute-start(bf16[27,16,512]{2,1,0:T(8,128)(2,1)S(1)} %broadcast_select_fusion.refs_3_), channel_id=1, source_target_pairs={{0,1},{1,0},{2,3},{3,2},{4,5},{5,4},{6,7},{7,6},{8,9},{9,8},{10,11... | collective-permute-start | bytes 1327112 | tf_op jit(solution)/shard_map/ppermute | solution.py:229
  65.2 1.0 %copy-start.4 = (bf16[27,16,512]{2,1,0:T(8,128)(2,1)S(1)}, bf16[27,16,512]{2,1,0:T(8,128)(2,1)}, u32[]{:S(2)}) copy-start(bf16[27,16,512]{2,1,0:T(8,128)(2,1)} %copy-done.3) | copy-start | bytes 1327108
  74.2 5.3 %collective-permute-start.18 = (bf16[2,160,128]{2,1,0:T(8,128)(2,1)S(1)}, bf16[2,160,128]{2,1,0:T(8,128)(2,1)S(1)}, u32[]{:S(2)}, u32[]{:S(2)}) collective-permute-start(bf16[2,160,128]{2,1,0:T(8,128)(2,1)S(1)} %get-tuple-element.18), channel_id=1, source_target_pairs={{0,8},{8,0},{16,24},{24,16},{1,9},{9,1},{17,25},{25,17},{2,10},{10... | collective-permute-start | bytes 245768 | tf_op jit(solution)/shard_map/ppermute | solution.py:280
  75.0 6.2 %collective-permute-start.19 = (bf16[2,160,128]{2,1,0:T(8,128)(2,1)S(1)}, bf16[2,160,128]{2,1,0:T(8,128)(2,1)S(1)}, u32[]{:S(2)}, u32[]{:S(2)}) collective-permute-start(bf16[2,160,128]{2,1,0:T(8,128)(2,1)S(1)} %get-tuple-element.19), channel_id=1, source_target_pairs={{0,16},{8,24},{16,0},{24,8},{1,17},{9,25},{17,1},{25,9},{2,18},{10... | collective-permute-start | bytes 245768 | tf_op jit(solution)/shard_map/ppermute | solution.py:280
  75.6 5.7 %collective-permute-start.20 = (bf16[2,160,128]{2,1,0:T(8,128)(2,1)S(1)}, bf16[2,160,128]{2,1,0:T(8,128)(2,1)S(1)}, u32[]{:S(2)}, u32[]{:S(2)}) collective-permute-start(bf16[2,160,128]{2,1,0:T(8,128)(2,1)S(1)} %get-tuple-element.20), channel_id=1, source_target_pairs={{0,24},{8,16},{16,8},{24,0},{1,25},{9,17},{17,9},{25,1},{2,26},{10... | collective-permute-start | bytes 245768 | tf_op jit(solution)/shard_map/ppermute | solution.py:280

commit v2 on v1

v2 whole, which is shorter than its diff:
```python
import functools

import jax
import jax.numpy as jnp
from jax import lax
from jax.experimental import pallas as pl
from jax.experimental.pallas import tpu as pltpu
from jax.sharding import PartitionSpec as P

GROUPS = 32
LANES = 128
CORES = 2

epsilon = 1e-06

whole = pl.BlockSpec(memory_space=pltpu.VMEM)
scalars = pl.BlockSpec(memory_space=pltpu.SMEM)


def params(mib):
    return pltpu.CompilerParams(vmem_limit_bytes=mib * 2**20)


def flip(axis, distance):
    return [(i, i ^ distance) for i in range(lax.axis_size(axis))]


def exchange(block, axis, distances):
    return [lax.ppermute(block, axis, flip(axis, d)) for d in distances]


def chip_pairs(pairs):
    return [(CORES * a + c, CORES * b + c) for a, b in pairs for c in range(CORES)]


def after(block, *others):
    return lax.optimization_barrier((block, *others))[0]


def stats_kernel(x_ref, out_ref):
    frames, rows, cols, channels = x_ref.shape
    entries = frames * rows * cols
    for block in range(channels // LANES):
        lanes = pl.ds(block * LANES, LANES)
        total = jnp.zeros((8, LANES), jnp.float32)
        for f in range(frames):
            for r in range(rows):
                x = x_ref[f, r, :, lanes].astype(jnp.float32)
                total = total + jnp.sum(x.reshape(-1, 8, LANES), axis=0)
        mean = jnp.sum(total, axis=0, keepdims=True) / entries
        total = jnp.zeros((8, LANES), jnp.float32)
        for f in range(frames):
            for r in range(rows):
                x = x_ref[f, r, :, lanes].astype(jnp.float32) - mean
                total = total + jnp.sum((x * x).reshape(-1, 8, LANES), axis=0)
        out_ref[0:1, lanes] = mean
        out_ref[1:2, lanes] = jnp.sum(total, axis=0, keepdims=True)


def local_stats(latents):
    return pl.pallas_call(
        stats_kernel,
        out_shape=jax.ShapeDtypeStruct((2, latents.shape[3]), jnp.float32),
        in_specs=[whole],
        out_specs=whole,
        compiler_params=params(8),
    )(latents)


def merge(parts, entries):
    mean = sum(part[0] for part in parts) / len(parts)
    apart = sum((part[0] - mean) ** 2 for part in parts) * entries
    return jnp.stack([mean, sum(part[1] for part in parts) + apart])


def pack_kernel(edge_ref, stats_ref, above_ref, x_ref, below_ref, out_ref):
    frames, rows, cols, _ = x_ref.shape
    count = frames * (rows + 2) * cols
    for f in range(frames):
        start = f * (rows + 2) * cols
        out_ref[start + cols : start + (rows + 1) * cols, :] = x_ref[f].reshape(rows * cols, -1)
        last = start + (rows + 1) * cols

        @pl.when(edge_ref[0] == 0)
        def _():
            out_ref[start : start + cols, :] = above_ref[f, 0]

        @pl.when(edge_ref[0] != 0)
        def _():
            out_ref[start : start + cols, :] = x_ref[f, 1]

        @pl.when(edge_ref[1] == 0)
        def _():
            out_ref[last : last + cols, :] = below_ref[f, 0]

        @pl.when(edge_ref[1] != 0)
        def _():
            out_ref[last : last + cols, :] = x_ref[f, rows - 2]

    rest = stats_ref[...]
    terms = []
    for _ in range(3):
        term = rest.astype(jnp.bfloat16).astype(jnp.float32)
        terms.append(term)
        rest = rest - term
    unused = out_ref.shape[0] - count - 6
    terms.append(jnp.zeros((unused, rest.shape[1]), jnp.float32))
    out_ref[count:, :] = jnp.concatenate(terms, axis=0).astype(jnp.bfloat16)


def pack(edges, stats, above, latents, below):
    frames, rows, cols, channels = latents.shape
    return pl.pallas_call(
        pack_kernel,
        out_shape=jax.ShapeDtypeStruct((frames * (rows + 2) * cols + 16, channels), jnp.bfloat16),
        in_specs=[scalars] + [whole] * 4,
        out_specs=whole,
        compiler_params=params(8),
    )(edges, stats, above, latents, below)


def lane_group_sum(x, size):
    lane = lax.broadcasted_iota(jnp.int32, x.shape, 1)
    step = 1
    while step < size:
        up = pltpu.roll(x, x.shape[1] - step, 1)
        down = pltpu.roll(x, step, 1)
        x = x + jnp.where((lane & step) == 0, up, down)
        step *= 2
    return x


def activate_kernel(held, rows, entries, place_ref, affine_ref, *refs):
    *piece_refs, even_ref, odd_ref, scratch = refs
    channels = piece_refs[0].shape[1]
    frames = held * len(piece_refs)
    cols = odd_ref.shape[1] // frames
    tail = held * rows * cols
    size = channels // GROUPS

    def step(index, carry):
        lanes = pl.ds(pl.multiple_of(index * LANES, LANES), LANES)
        means, squares = [], []
        for piece_ref in piece_refs:
            terms = piece_ref[tail : tail + 16, lanes].astype(jnp.float32)
            both = terms[0:2] + terms[2:4] + terms[4:6]
            means.append(both[0:1])
            squares.append(both[1:2])
        count = len(piece_refs) * size
        mean = lane_group_sum(jnp.broadcast_to(sum(means), (8, LANES)), size) / count
        spread = sum(squares) + entries * sum((m - mean[0:1]) ** 2 for m in means)
        var = lane_group_sum(jnp.broadcast_to(spread, (8, LANES)), size) / (count * entries)
        mean = mean[0:1]
        scale = lax.rsqrt(var[0:1] + epsilon) * affine_ref[0:1, lanes]
        bias = affine_ref[1:2, lanes]
        last = (cols + 1) * frames
        for r in range(rows):
            for p, piece_ref in enumerate(piece_refs):
                for f in range(held):
                    start = (f * rows + r) * cols
                    x = piece_ref[start : start + cols, lanes].astype(jnp.float32)
                    h = 0.5 * ((x - mean) * scale + bias)
                    scratch[r, pl.ds(frames + place_ref[p] + f, cols, stride=frames), :] = h + h * jnp.tanh(h)
            scratch[r, 0:frames, :] = scratch[r, 2 * frames : 3 * frames, :]
            scratch[r, last : last + frames, :] = scratch[r, last - 2 * frames : last - frames, :]
            even_ref[r, :, lanes] = scratch[r].astype(jnp.bfloat16)
            odd_ref[r, :, lanes] = scratch[r, frames:last, :].astype(jnp.bfloat16)
        return carry

    lax.fori_loop(0, channels // LANES, step, 0)


def activate(places, affine, pieces, held, rows, cols, entries):
    channels = pieces[0].shape[1]
    frames = held * len(pieces)
    return pl.pallas_call(
        functools.partial(activate_kernel, held, rows, entries),
        out_shape=(
            jax.ShapeDtypeStruct((rows, (cols + 2) * frames, channels), jnp.bfloat16),
            jax.ShapeDtypeStruct((rows, cols * frames, channels), jnp.bfloat16),
        ),
        in_specs=[scalars, whole] + [whole] * len(pieces),
        out_specs=(whole, whole),
        scratch_shapes=[pltpu.VMEM((rows, (cols + 2) * frames, LANES), jnp.float32)],
        compiler_params=params(24),
        cost_estimate=pl.CostEstimate(
            flops=10 * frames * rows * cols * channels,
            bytes_accessed=6 * frames * rows * cols * channels,
            transcendentals=frames * rows * cols * channels,
        ),
    )(places, affine, *pieces)


def conv_kernel(count, with_other, place_ref, slot_ref, half_ref, even_ref, odd_ref, bias_ref, *refs):
    piece_refs, refs = refs[:count], refs[count:]
    if with_other:
        other_ref, refs = refs[0], refs[1:]
    out_refs, (taps, sums, placed) = refs[:-3], refs[-3:]
    rows = even_ref.shape[0] - 2
    per_row = odd_ref.shape[1]
    frames = placed.shape[0]
    cols = per_row // frames
    channels = even_ref.shape[2]
    width = taps.shape[2] * taps.shape[3]
    for p, piece_ref in enumerate(piece_refs):
        slot = slot_ref[p]
        for tap in range(27):
            taps[tap % 9, tap // 9, slot] = piece_ref[tap]

    for y in range(rows):
        total = None
        for tap in range(9):
            b, c = tap // 3, tap % 3
            if c == 1:
                window = odd_ref[y + b]
            else:
                window = even_ref[y + b, pl.ds(c * frames, per_row), :]
            product = lax.dot_general(
                window,
                taps[tap].reshape(3 * width, channels),
                (((1,), (1,)), ((), ())),
                preferred_element_type=jnp.float32,
            )
            total = product if total is None else total + product
        place = slice(y * per_row, (y + 1) * per_row)
        sums[0, place, :] = total[:, : 2 * width]
        sums[1, place, 0:width] = total[:, 2 * width :]

    count = rows * cols
    lane = lax.broadcasted_iota(jnp.int32, (count, 2 * width), 1)
    low = lane < width
    for f in range(frames):
        value = sums[1, pl.ds(f, count, stride=frames), :]
        if f >= 1:
            value = value + pltpu.roll(sums[0, pl.ds(f - 1, count, stride=frames), :], width, 1)
        if f >= 2:
            value = value + sums[0, pl.ds(f - 2, count, stride=frames), :]
        value = jnp.where(low, value, pltpu.roll(value, width, 1)) + bias_ref[...]
        if with_other:
            value = jnp.where(low == (half_ref[0] == 0), value, other_ref[f].astype(jnp.float32))
        placed[f] = value.astype(jnp.bfloat16)
    if with_other:
        for p, out_ref in enumerate(out_refs):
            out_ref[...] = placed[pl.ds(place_ref[p], out_ref.shape[0])]
    else:
        out_refs[0][...] = placed[...]


def convolve(places, slots, half, even, odd, bias, pieces, frames, other=None):
    rows, per_row, channels = even.shape[0] - 2, odd.shape[1], even.shape[2]
    positions = rows * per_row // frames
    each = pieces[0].shape[1]
    width = each * len(pieces)
    if other is None:
        shapes, others = [(frames, positions, 2 * width)], []
    else:
        groups = places.shape[0]
        shapes, others = [(frames // groups, positions, 2 * width)] * groups, [other]
    return pl.pallas_call(
        functools.partial(conv_kernel, len(pieces), other is not None),
        out_shape=tuple(jax.ShapeDtypeStruct(shape, jnp.bfloat16) for shape in shapes),
        in_specs=[scalars] * 3 + [whole] * (3 + len(pieces) + len(others)),
        out_specs=tuple(whole for _ in shapes),
        scratch_shapes=[
            pltpu.VMEM((9, 3, len(pieces), each, channels), jnp.bfloat16),
            pltpu.VMEM((2, rows * per_row, 2 * width), jnp.float32),
            pltpu.VMEM((frames, positions, 2 * width), jnp.bfloat16),
        ],
        compiler_params=params(32),
        cost_estimate=pl.CostEstimate(
            flops=2 * rows * per_row * channels * width,
            bytes_accessed=2 * channels * width,
            transcendentals=0,
        ),
    )(places, slots, half, even, odd, bias, *pieces, *others)


def place_kernel(place_ref, *refs):
    *piece_refs, out_ref = refs
    width = piece_refs[0].shape[2]
    for p, piece_ref in enumerate(piece_refs):
        start = pl.multiple_of(place_ref[p] * width, LANES)
        out_ref[:, :, pl.ds(start, width)] = piece_ref[...]


def place(groups, pieces):
    held, positions, width = pieces[0].shape
    return pl.pallas_call(
        place_kernel,
        out_shape=jax.ShapeDtypeStruct((held, positions, width * len(pieces)), jnp.bfloat16),
        in_specs=[scalars] + [whole] * len(pieces),
        out_specs=whole,
        compiler_params=params(8),
    )(groups, *pieces)


def body(latents, norm_gain, norm_bias, conv_weight, conv_bias):
    held, row_count, col_count, channels = latents.shape
    group_count = lax.axis_size("frames")
    strips = lax.axis_size("rows")
    group = lax.axis_index("frames")
    strip = lax.axis_index("rows")
    is_line = strips == 4 * CORES
    weight = conv_weight.transpose(0, 1, 2, 4, 3)
    weight = weight.reshape((-1,) + weight.shape[3:])

    above = lax.ppermute(latents[:, row_count - 1 :], "rows", [(i, i + 1) for i in range(strips - 1)])
    below = lax.ppermute(latents[:, :1], "rows", [(i + 1, i) for i in range(strips - 1)])

    entries = held * row_count * col_count
    stats = local_stats(latents)
    if is_line:
        stats = merge([stats] + exchange(stats, "rows", [1]), entries)
        chips = range(CORES, strips, CORES)
        stats = merge([stats] + exchange(stats, "rows", chips), CORES * entries)
        entries *= strips
    else:
        distance = 1
        while distance < strips:
            stats = merge([stats] + exchange(stats, "rows", [distance]), entries)
            entries *= 2
            distance *= 2

    if is_line:
        weight = after(weight, stats, above, below)
        first, second = exchange(weight, "rows", [CORES, 2 * CORES])
        weight, first, second = lax.optimization_barrier((weight, first, second))
        ends = chip_pairs([(1, 0), (2, 3)])
        middle = chip_pairs([(1, 2), (2, 1)])
        third_ends = lax.ppermute(second, "rows", ends)
        third_middle = lax.ppermute(weight, "rows", middle)

    edges = jnp.stack([strip == 0, strip == strips - 1]).astype(jnp.int32)
    payload = pack(edges, stats, above, latents, below)
    strip_pieces = [payload] + exchange(payload, "frames", range(1, group_count))
    groups = jnp.stack([group ^ d for d in range(group_count)]).astype(jnp.int32)
    affine = jnp.stack([norm_gain, norm_bias])
    if is_line:
        near, strip_pieces, far = lax.optimization_barrier(([weight, first], strip_pieces, [second]))
    even, odd = activate(
        groups * held, affine, strip_pieces, held, row_count + 2, col_count, entries
    )

    width = channels // group_count
    bias = lax.dynamic_slice_in_dim(conv_bias, group * width, width)[None]
    if is_line:
        near += [lax.ppermute(piece, "rows", flip("rows", 1)) for piece in near]
        slots = jnp.stack([strip, strip ^ 2, strip ^ 1, strip ^ 3]) % 4
        half, other_half = (strip // 4)[None], 1 - (strip // 4)[None]
    else:
        gathered = lax.all_gather(weight, "rows", axis=1, tiled=True)
        near, far = [gathered[:, : width // 2]], [gathered[:, width // 2 :]]
        slots = jnp.zeros((1,), jnp.int32)
        half, other_half = slots, slots + 1
    convolved = functools.partial(
        convolve, groups * held, slots, even=even, odd=odd, bias=bias, frames=held * group_count
    )
    done = convolved(half, pieces=near)[0]
    if is_line:
        third_ends, third_middle, done = lax.optimization_barrier((third_ends, third_middle, done))
        chip = strip // CORES
        third = jnp.where((chip == 0) | (chip == 3), third_ends, third_middle)
        far.append(third)
        far += [lax.ppermute(piece, "rows", flip("rows", 1)) for piece in far]
    parts = convolved(other_half, pieces=far, other=done)
    parts = [parts[0]] + [
        lax.ppermute(parts[d], "frames", flip("frames", d)) for d in range(1, group_count)
    ]
    return place(groups, parts).reshape(latents.shape)


def solution(mesh):
    placed = (
        P("frames", "rows", None, None),
        P(),
        P(),
        P(None, None, None, None, ("frames", "rows")),
        P(),
    )
    return jax.shard_map(
        body, mesh=mesh, in_specs=placed, out_specs=P("frames", "rows", None, None), check_vma=False
    )
```

time: 84 us -> 73.7 us (0.88)
  the two profiles are of different devices: /device:TPU:0 before, /device:TPU:8 now
where the time goes in v2:
time: 73.7 us; the launch traced here: 73.4 us
  starting transfers between devices  28.4 us (39%)
  waiting for transfers between devices  25.7 us (35%)
  Pallas kernels  15.1 us (20%)
  local copies, waits for them, and re-layouts  2.98 us (4%)
  other arithmetic  1.05 us (1%)
    ppermute x9, waiting for transfers between devices, exchange(): return [lax.ppermute(block, axis, flip(axis, d)) for d in distances]  19.4 us
    ppermute x9, starting transfers between devices, exchange(): return [lax.ppermute(block, axis, flip(axis, d)) for d in distances]  10.5 us
    pallas_call x2, Pallas kernels, convolve(): pl.pallas_call(functools.partial(conv_kernel, len(pieces), other is not N...  8.29 us
    ppermute x1, starting transfers between devices, body(): third_ends = lax.ppermute(second, 'rows', ends)  5.04 us
    ppermute x3, waiting for transfers between devices, body(): lax.ppermute(parts[d], 'frames', flip('frames', d))  4.86 us
    pallas_call x1, Pallas kernels, activate(): pl.pallas_call(functools.partial(activate_kernel, held, rows, entries), o...  4.65 us
    ppermute x3, starting transfers between devices, body(): lax.ppermute(parts[d], 'frames', flip('frames', d))  3.57 us
    ppermute x1, starting transfers between devices, body(): lax.ppermute(latents[:, :1], 'rows', [(i + 1, i) for i in range(strips -...  3.16 us
  transfers between devices with their start and end apart: 20, of which 8 were waited for; matrix products, arithmetic and copies ran while one was open for 3% of the time, Pallas kernels for 12%

profile of v2, /device:TPU:8, one launch (start us, length us, event | category | flops | bytes accessed | tf_op | source)
XLA Modules:
  0.0 73.4 jit_solution(8332555752190921777)
XLA Ops:
  0.0 1.0 %copy-done.1 = bf16[2,4,40,512]{3,2,1,0:T(8,128)(2,1)S(1)} copy-done((bf16[2,4,40,512]{3,2,1,0:T(8,128)(2,1)S(1)}, bf16[2,4,40,512]{3,2,1,0:T(8,128)(2,1)}, u32[]{:S(2)}) %copy-start.1) | copy-done | bytes 327704
  1.2 0.9 %fusion.3 = (bf16[2,1,40,512]{3,2,1,0:T(8,128)(2,1)S(1)}, bf16[2,1,40,512]{3,2,1,0:T(8,128)(2,1)S(1)}) fusion(bf16[2,4,40,512]{3,2,1,0:T(8,128)(2,1)} %x_ref.3), kind=kLoop, calls=%fused_computation.20 | loop fusion | bytes 327680 | tf_op jit(solution)/shard_map/slice | solution.py:308
  2.2 2.4 %collective-permute-start.4 = (bf16[2,1,40,512]{3,2,1,0:T(8,128)(2,1)S(1)}, bf16[2,1,40,512]{3,2,1,0:T(8,128)(2,1)S(1)}, u32[]{:S(2)}, u32[]{:S(2)}) collective-permute-start(bf16[2,1,40,512]{3,2,1,0:T(8,128)(2,1)S(1)} %get-tuple-element.52), channel_id=1, source_target_pairs={{0,1},{1,2},{2,3},{3,4},{4,5},{5,6},{6,7},{8,9},{9,10},{10,11},{11... | collective-permute-start | bytes 245768 | tf_op jit(solution)/shard_map/ppermute | solution.py:307
  4.6 3.2 %collective-permute-start.5 = (bf16[2,1,40,512]{3,2,1,0:T(8,128)(2,1)S(1)}, bf16[2,1,40,512]{3,2,1,0:T(8,128)(2,1)S(1)}, u32[]{:S(2)}, u32[]{:S(2)}) collective-permute-start(bf16[2,1,40,512]{3,2,1,0:T(8,128)(2,1)S(1)} %get-tuple-element.51), channel_id=1, source_target_pairs={{1,0},{2,1},{3,2},{4,3},{5,4},{6,5},{7,6},{9,8},{10,9},{11,10},{12... | collective-permute-start | bytes 245768 | tf_op jit(solution)/shard_map/ppermute | solution.py:308
  7.9 3.0 %collective-permute-start.2 = (f32[2,512]{1,0:T(2,128)S(1)}, f32[2,512]{1,0:T(2,128)S(1)}, u32[]{:S(2)}, u32[]{:S(2)}) collective-permute-start(f32[2,512]{1,0:T(2,128)S(1)} %pad_maximum_fusion.1), channel_id=1, source_target_pairs={{0,4},{1,5},{2,6},{3,7},{4,0},{5,1},{6,2},{7,3},{8,12},{9,13},{10,... | collective-permute-start | bytes 12296 | tf_op jit(solution)/shard_map/ppermute | solution.py:29
  10.9 0.5 collective-permute-start.3
  11.5 1.3 %collective-permute-done.2 = f32[2,512]{1,0:T(2,128)S(1)} collective-permute-done((f32[2,512]{1,0:T(2,128)S(1)}, f32[2,512]{1,0:T(2,128)S(1)}, u32[]{:S(2)}, u32[]{:S(2)}) %collective-permute-start.2) | collective-permute-done | bytes 4128 | tf_op jit(solution)/shard_map/ppermute | solution.py:29
  12.8 1.7 %collective-permute-done.3 = f32[2,512]{1,0:T(2,128)S(1)} collective-permute-done((f32[2,512]{1,0:T(2,128)S(1)}, f32[2,512]{1,0:T(2,128)S(1)}, u32[]{:S(2)}, u32[]{:S(2)}) %collective-permute-start.3) | collective-permute-done | bytes 4128 | tf_op jit(solution)/shard_map/ppermute | solution.py:29
  14.6 1.0 %copy-done.2 = bf16[2,4,40,512]{3,2,1,0:T(8,128)(2,1)S(1)} copy-done((bf16[2,4,40,512]{3,2,1,0:T(8,128)(2,1)S(1)}, bf16[2,4,40,512]{3,2,1,0:T(8,128)(2,1)}, u32[]{:S(2)}) %copy-start.2) | copy-done | bytes 327704
  15.6 0.6 shard_map.56.refs_0_
  16.2 2.5 %collective-permute-start.10 = (bf16[496,512]{1,0:T(8,128)(2,1)S(1)}, bf16[496,512]{1,0:T(8,128)(2,1)S(1)}, u32[]{:S(2)}, u32[]{:S(2)}) collective-permute-start(bf16[496,512]{1,0:T(8,128)(2,1)S(1)} %shard_map.56.refs_0_), channel_id=1, source_target_pairs={{0,24},{8,16},{16,8},{24,0},{1,25},{9,17},{17,9},{25,1},{2,26},{10... | collective-permute-start | bytes 1523720 | tf_op jit(solution)/shard_map/ppermute | solution.py:29
  18.7 0.5 collective-permute-start.8
  19.2 0.5 collective-permute-start.9
  19.8 3.4 %collective-permute-start.6 = (bf16[27,16,512]{2,1,0:T(8,128)(2,1)}, bf16[27,16,512]{2,1,0:T(8,128)(2,1)S(1)}, u32[]{:S(2)}, u32[]{:S(2)}) collective-permute-start(bf16[27,16,512]{2,1,0:T(8,128)(2,1)} %bitcast.19), channel_id=1, source_target_pairs={{0,2},{1,3},{2,0},{3,1},{4,6},{5,7},{6,4},{7,5},{8,10},{9,11},{10,... | collective-permute-start | bytes 1327112 | tf_op jit(solution)/shard_map/ppermute | solution.py:29
  23.1 14.4 %collective-permute-done.6.refs_1_ = bf16[27,16,512]{2,1,0:T(8,128)(2,1)S(1)} collective-permute-done((bf16[27,16,512]{2,1,0:T(8,128)(2,1)}, bf16[27,16,512]{2,1,0:T(8,128)(2,1)S(1)}, u32[]{:S(2)}, u32[]{:S(2)}) %collective-permute-start.6) | collective-permute-done | bytes 442400 | tf_op jit(solution)/shard_map/ppermute | solution.py:29
  37.6 1.9 %collective-permute-done.7.refs_0_ = bf16[27,16,512]{2,1,0:T(8,128)(2,1)S(1)} collective-permute-done((bf16[27,16,512]{2,1,0:T(8,128)(2,1)}, bf16[27,16,512]{2,1,0:T(8,128)(2,1)S(1)}, u32[]{:S(2)}, u32[]{:S(2)}) %collective-permute-start.7) | collective-permute-done | bytes 442400 | tf_op jit(solution)/shard_map/ppermute | solution.py:29
  39.4 5.0 %collective-permute-start.11 = (bf16[27,16,512]{2,1,0:T(8,128)(2,1)S(1)}, bf16[27,16,512]{2,1,0:T(8,128)(2,1)S(1)}, u32[]{:S(2)}, u32[]{:S(2)}) collective-permute-start(bf16[27,16,512]{2,1,0:T(8,128)(2,1)S(1)} %collective-permute-done.7.refs_0_), channel_id=1, source_target_pairs={{2,0},{3,1},{4,6},{5,7},{10,8},{11,9},{12,14},{13,15},{18,16},{19,... | collective-permute-start | bytes 1327112 | tf_op jit(solution)/shard_map/ppermute | solution.py:330
  44.5 2.5 %collective-permute-start.12 = (bf16[27,16,512]{2,1,0:T(8,128)(2,1)}, bf16[27,16,512]{2,1,0:T(8,128)(2,1)S(1)}, u32[]{:S(2)}, u32[]{:S(2)}) collective-permute-start(bf16[27,16,512]{2,1,0:T(8,128)(2,1)} %bitcast.21), channel_id=1, source_target_pairs={{2,4},{3,5},{4,2},{5,3},{10,12},{11,13},{12,10},{13,11},{18,20},{1... | collective-permute-start | bytes 1327112 | tf_op jit(solution)/shard_map/ppermute | solution.py:331
  47.1 0.5 collective-permute-start.14
  47.8 0.7 pad_maximum_fusion.affine_ref
  48.7 4.7 %shard_map.57 = (bf16[6,336,512]{2,1,0:T(8,128)(2,1)S(1)}, bf16[6,320,512]{2,1,0:T(8,128)(2,1)S(1)}) custom-call(s32[4]{0:T(128)S(1)} %get-tuple-element.49.place_ref, f32[2,512]{1,0:T(2,128)S(1)} %pad_maximum_fusion.affine_ref, bf16[496,512]{1,0:T(8,128)(2,1)S(1)} %shard_map.56.refs_0_, bf16[496,512]{1,0:T(8,128)(2,1)S(1)} %collective-permute-done.8.refs_1_, ...), custom_call_target="tpu_custom_call" | custom-call | flops 9830400 | bytes 5898240 | tf_op jit(solution)/shard_map/pallas_call | solution.py:176
  53.4 4.2 %shard_map.58.refs_4_ = bf16[8,160,128]{2,1,0:T(8,128)(2,1)S(1)} custom-call(s32[4]{0:T(128)S(1)} %get-tuple-element.49.place_ref, s32[4]{0:T(128)S(1)} %and_select_fusion.slot_ref, s32[1]{0:T(128)} %bitcast.8.half_ref, bf16[6,336,512]{2,1,0:T(8,128)(2,1)S(1)} %get-tuple-element.33.even_ref, bf16[6,320,512]{2,1,0:T(8,128)(2,1)S(1)} %get-tuple-element.34.odd_ref, ...), custom_call_target="tpu_custom_call" | custom-call | flops 83886080 | bytes 65536 | tf_op jit(solution)/shard_map/pallas_call | solution.py:259
  57.6 0.5 collective-permute-start.16
  58.1 1.4 %collective-permute-done.16.refs_3_ = bf16[27,16,512]{2,1,0:T(8,128)(2,1)S(1)} collective-permute-done((bf16[27,16,512]{2,1,0:T(8,128)(2,1)S(1)}, bf16[27,16,512]{2,1,0:T(8,128)(2,1)S(1)}, u32[]{:S(2)}, u32[]{:S(2)}) %collective-permute-start.16) | collective-permute-done | bytes 442400 | tf_op jit(solution)/shard_map/ppermute | solution.py:364
  59.5 4.1 %shard_map.59 = (bf16[2,160,128]{2,1,0:T(8,128)(2,1)S(1)}, bf16[2,160,128]{2,1,0:T(8,128)(2,1)S(1)}, bf16[2,160,128]{2,1,0:T(8,128)(2,1)S(1)}, bf16[2,160,128]{2,1,0:T(8,128)(2,1)S(1)}) custom-call(s32[4]{0:T(128)S(1)} %get-tuple-element.49.place_ref, s32[4]{0:T(128)S(1)} %and_select_fusion.slot_ref, s32[1]{0:T(128)S(6)} %sub.38.half_ref, ...), custom_call_target="tpu_custom_call" | custom-call | flops 83886080 | bytes 65536 | tf_op jit(solution)/shard_map/pallas_call | solution.py:259
  63.7 1.6 %collective-permute-start.17 = (bf16[2,160,128]{2,1,0:T(8,128)(2,1)S(1)}, bf16[2,160,128]{2,1,0:T(8,128)(2,1)S(1)}, u32[]{:S(2)}, u32[]{:S(2)}) collective-permute-start(bf16[2,160,128]{2,1,0:T(8,128)(2,1)S(1)} %get-tuple-element.42), channel_id=1, source_target_pairs={{0,8},{8,0},{16,24},{24,16},{1,9},{9,1},{17,25},{25,17},{2,10},{10... | collective-permute-start | bytes 245768 | tf_op jit(solution)/shard_map/ppermute | solution.py:367
  65.2 1.5 %collective-permute-start.18 = (bf16[2,160,128]{2,1,0:T(8,128)(2,1)S(1)}, bf16[2,160,128]{2,1,0:T(8,128)(2,1)S(1)}, u32[]{:S(2)}, u32[]{:S(2)}) collective-permute-start(bf16[2,160,128]{2,1,0:T(8,128)(2,1)S(1)} %get-tuple-element.43), channel_id=1, source_target_pairs={{0,16},{8,24},{16,0},{24,8},{1,17},{9,25},{17,1},{25,9},{2,18},{10... | collective-permute-start | bytes 245768 | tf_op jit(solution)/shard_map/ppermute | solution.py:367
  66.8 0.5 collective-permute-start.19
  67.2 1.2 %collective-permute-done.17.refs_1_ = bf16[2,160,128]{2,1,0:T(8,128)(2,1)S(1)} collective-permute-done((bf16[2,160,128]{2,1,0:T(8,128)(2,1)S(1)}, bf16[2,160,128]{2,1,0:T(8,128)(2,1)S(1)}, u32[]{:S(2)}, u32[]{:S(2)}) %collective-permute-start.17) | collective-permute-done | bytes 81952 | tf_op jit(solution)/shard_map/ppermute | solution.py:367
  68.5 2.0 %collective-permute-done.18.refs_2_ = bf16[2,160,128]{2,1,0:T(8,128)(2,1)S(1)} collective-permute-done((bf16[2,160,128]{2,1,0:T(8,128)(2,1)S(1)}, bf16[2,160,128]{2,1,0:T(8,128)(2,1)S(1)}, u32[]{:S(2)}, u32[]{:S(2)}) %collective-permute-start.18) | collective-permute-done | bytes 81952 | tf_op jit(solution)/shard_map/ppermute | solution.py:367
  70.5 1.6 %collective-permute-done.19.refs_3_ = bf16[2,160,128]{2,1,0:T(8,128)(2,1)S(1)} collective-permute-done((bf16[2,160,128]{2,1,0:T(8,128)(2,1)S(1)}, bf16[2,160,128]{2,1,0:T(8,128)(2,1)S(1)}, u32[]{:S(2)}, u32[]{:S(2)}) %collective-permute-start.19) | collective-permute-done | bytes 81952 | tf_op jit(solution)/shard_map/ppermute | solution.py:367
  72.1 1.3 %shard_map.60 = bf16[2,160,512]{2,1,0:T(8,128)(2,1)} custom-call(s32[4]{0:T(128)S(1)} %get-tuple-element.50.place_ref, bf16[2,160,128]{2,1,0:T(8,128)(2,1)S(1)} %get-tuple-element.41.refs_0_, bf16[2,160,128]{2,1,0:T(8,128)(2,1)S(1)} %collective-permute-done.17.refs_1_, bf16[2,160,128]{2,1,0:T(8,128)(2,1)S(1)} %collective-permute-done.18.refs_2_, ...), custom_call_target="tpu_custom_call" | custom-call | tf_op jit(solution)/shard_map/pallas_call | solution.py:288
  (33 shorter events, 1.0 us)
Async XLA Ops:
  0.0 47.6 %copy-start = (f32[512]{0:T(512)S(1)}, f32[512]{0:T(512)}, u32[]{:S(2)}) copy-start(f32[512]{0:T(512)} %param.9) | copy-start | bytes 6148
  0.0 1.0 %copy-start.1 = (bf16[2,4,40,512]{3,2,1,0:T(8,128)(2,1)S(1)}, bf16[2,4,40,512]{3,2,1,0:T(8,128)(2,1)}, u32[]{:S(2)}) copy-start(bf16[2,4,40,512]{3,2,1,0:T(8,128)(2,1)} %x_ref.3) | copy-start | bytes 983044
  1.0 52.4 %copy-start.3 = (bf16[3,3,3,512,16]{3,4,2,1,0:T(8,128)(2,1)S(1)}, bf16[3,3,3,512,16]{3,4,2,1,0:T(8,128)(2,1)}, u32[]{:S(2)}) copy-start(bf16[3,3,3,512,16]{3,4,2,1,0:T(8,128)(2,1)} %param.8) | copy-start | bytes 1327108
  1.1 6.6 %collective-permute-start = (f32[2,512]{1,0:T(2,128)S(1)}, f32[2,512]{1,0:T(2,128)S(1)}, u32[]{:S(2)}, u32[]{:S(2)}) collective-permute-start(f32[2,512]{1,0:T(2,128)S(1)} %shard_map.55), channel_id=1, source_target_pairs={{0,1},{1,0},{2,3},{3,2},{4,5},{5,4},{6,7},{7,6},{8,9},{9,8},{10,11... | collective-permute-start | bytes 12296 | tf_op jit(solution)/shard_map/ppermute | solution.py:29
  2.2 12.4 %collective-permute-start.4 = (bf16[2,1,40,512]{3,2,1,0:T(8,128)(2,1)S(1)}, bf16[2,1,40,512]{3,2,1,0:T(8,128)(2,1)S(1)}, u32[]{:S(2)}, u32[]{:S(2)}) collective-permute-start(bf16[2,1,40,512]{3,2,1,0:T(8,128)(2,1)S(1)} %get-tuple-element.52), channel_id=1, source_target_pairs={{0,1},{1,2},{2,3},{3,4},{4,5},{5,6},{6,7},{8,9},{9,10},{10,11},{11... | collective-permute-start | bytes 245768 | tf_op jit(solution)/shard_map/ppermute | solution.py:307
  4.6 10.0 %collective-permute-start.5 = (bf16[2,1,40,512]{3,2,1,0:T(8,128)(2,1)S(1)}, bf16[2,1,40,512]{3,2,1,0:T(8,128)(2,1)S(1)}, u32[]{:S(2)}, u32[]{:S(2)}) collective-permute-start(bf16[2,1,40,512]{3,2,1,0:T(8,128)(2,1)S(1)} %get-tuple-element.51), channel_id=1, source_target_pairs={{1,0},{2,1},{3,2},{4,3},{5,4},{6,5},{7,6},{9,8},{10,9},{11,10},{12... | collective-permute-start | bytes 245768 | tf_op jit(solution)/shard_map/ppermute | solution.py:308
  7.8 3.7 %collective-permute-start.1 = (f32[2,512]{1,0:T(2,128)S(1)}, f32[2,512]{1,0:T(2,128)S(1)}, u32[]{:S(2)}, u32[]{:S(2)}) collective-permute-start(f32[2,512]{1,0:T(2,128)S(1)} %pad_maximum_fusion.1), channel_id=1, source_target_pairs={{0,2},{1,3},{2,0},{3,1},{4,6},{5,7},{6,4},{7,5},{8,10},{9,11},{10,... | collective-permute-start | bytes 12296 | tf_op jit(solution)/shard_map/ppermute | solution.py:29
  7.9 4.9 %collective-permute-start.2 = (f32[2,512]{1,0:T(2,128)S(1)}, f32[2,512]{1,0:T(2,128)S(1)}, u32[]{:S(2)}, u32[]{:S(2)}) collective-permute-start(f32[2,512]{1,0:T(2,128)S(1)} %pad_maximum_fusion.1), channel_id=1, source_target_pairs={{0,4},{1,5},{2,6},{3,7},{4,0},{5,1},{6,2},{7,3},{8,12},{9,13},{10,... | collective-permute-start | bytes 12296 | tf_op jit(solution)/shard_map/ppermute | solution.py:29
  10.9 3.6 %collective-permute-start.3 = (f32[2,512]{1,0:T(2,128)S(1)}, f32[2,512]{1,0:T(2,128)S(1)}, u32[]{:S(2)}, u32[]{:S(2)}) collective-permute-start(f32[2,512]{1,0:T(2,128)S(1)} %pad_maximum_fusion.1), channel_id=1, source_target_pairs={{0,6},{1,7},{2,4},{3,5},{4,2},{5,3},{6,0},{7,1},{8,14},{9,15},{10,... | collective-permute-start | bytes 12296 | tf_op jit(solution)/shard_map/ppermute | solution.py:29
  14.6 1.0 %copy-start.2 = (bf16[2,4,40,512]{3,2,1,0:T(8,128)(2,1)S(1)}, bf16[2,4,40,512]{3,2,1,0:T(8,128)(2,1)}, u32[]{:S(2)}) copy-start(bf16[2,4,40,512]{3,2,1,0:T(8,128)(2,1)} %x_ref.3) | copy-start | bytes 983044
  16.2 30.8 %collective-permute-start.10 = (bf16[496,512]{1,0:T(8,128)(2,1)S(1)}, bf16[496,512]{1,0:T(8,128)(2,1)S(1)}, u32[]{:S(2)}, u32[]{:S(2)}) collective-permute-start(bf16[496,512]{1,0:T(8,128)(2,1)S(1)} %shard_map.56.refs_0_), channel_id=1, source_target_pairs={{0,24},{8,16},{16,8},{24,0},{1,25},{9,17},{17,9},{25,1},{2,26},{10... | collective-permute-start | bytes 1523720 | tf_op jit(solution)/shard_map/ppermute | solution.py:29
  18.7 28.3 %collective-permute-start.8 = (bf16[496,512]{1,0:T(8,128)(2,1)S(1)}, bf16[496,512]{1,0:T(8,128)(2,1)S(1)}, u32[]{:S(2)}, u32[]{:S(2)}) collective-permute-start(bf16[496,512]{1,0:T(8,128)(2,1)S(1)} %shard_map.56.refs_0_), channel_id=1, source_target_pairs={{0,8},{8,0},{16,24},{24,16},{1,9},{9,1},{17,25},{25,17},{2,10},{10... | collective-permute-start | bytes 1523720 | tf_op jit(solution)/shard_map/ppermute | solution.py:29
  19.2 27.8 %collective-permute-start.9 = (bf16[496,512]{1,0:T(8,128)(2,1)S(1)}, bf16[496,512]{1,0:T(8,128)(2,1)S(1)}, u32[]{:S(2)}, u32[]{:S(2)}) collective-permute-start(bf16[496,512]{1,0:T(8,128)(2,1)S(1)} %shard_map.56.refs_0_), channel_id=1, source_target_pairs={{0,16},{8,24},{16,0},{24,8},{1,17},{9,25},{17,1},{25,9},{2,18},{10... | collective-permute-start | bytes 1523720 | tf_op jit(solution)/shard_map/ppermute | solution.py:29
  19.8 17.8 %collective-permute-start.6 = (bf16[27,16,512]{2,1,0:T(8,128)(2,1)}, bf16[27,16,512]{2,1,0:T(8,128)(2,1)S(1)}, u32[]{:S(2)}, u32[]{:S(2)}) collective-permute-start(bf16[27,16,512]{2,1,0:T(8,128)(2,1)} %bitcast.19), channel_id=1, source_target_pairs={{0,2},{1,3},{2,0},{3,1},{4,6},{5,7},{6,4},{7,5},{8,10},{9,11},{10,... | collective-permute-start | bytes 1327112 | tf_op jit(solution)/shard_map/ppermute | solution.py:29
  23.1 16.3 %collective-permute-start.7 = (bf16[27,16,512]{2,1,0:T(8,128)(2,1)}, bf16[27,16,512]{2,1,0:T(8,128)(2,1)S(1)}, u32[]{:S(2)}, u32[]{:S(2)}) collective-permute-start(bf16[27,16,512]{2,1,0:T(8,128)(2,1)} %bitcast.20), channel_id=1, source_target_pairs={{0,4},{1,5},{2,6},{3,7},{4,0},{5,1},{6,2},{7,3},{8,12},{9,13},{10,... | collective-permute-start | bytes 1327112 | tf_op jit(solution)/shard_map/ppermute | solution.py:29
  39.4 18.1 %collective-permute-start.11 = (bf16[27,16,512]{2,1,0:T(8,128)(2,1)S(1)}, bf16[27,16,512]{2,1,0:T(8,128)(2,1)S(1)}, u32[]{:S(2)}, u32[]{:S(2)}) collective-permute-start(bf16[27,16,512]{2,1,0:T(8,128)(2,1)S(1)} %collective-permute-done.7.refs_0_), channel_id=1, source_target_pairs={{2,0},{3,1},{4,6},{5,7},{10,8},{11,9},{12,14},{13,15},{18,16},{19,... | collective-permute-start | bytes 1327112 | tf_op jit(solution)/shard_map/ppermute | solution.py:330
  44.5 13.1 %collective-permute-start.12 = (bf16[27,16,512]{2,1,0:T(8,128)(2,1)}, bf16[27,16,512]{2,1,0:T(8,128)(2,1)S(1)}, u32[]{:S(2)}, u32[]{:S(2)}) collective-permute-start(bf16[27,16,512]{2,1,0:T(8,128)(2,1)} %bitcast.21), channel_id=1, source_target_pairs={{2,4},{3,5},{4,2},{5,3},{10,12},{11,13},{12,10},{13,11},{18,20},{1... | collective-permute-start | bytes 1327112 | tf_op jit(solution)/shard_map/ppermute | solution.py:331
  47.0 6.3 %collective-permute-start.13 = (bf16[27,16,512]{2,1,0:T(8,128)(2,1)}, bf16[27,16,512]{2,1,0:T(8,128)(2,1)S(1)}, u32[]{:S(2)}, u32[]{:S(2)}) collective-permute-start(bf16[27,16,512]{2,1,0:T(8,128)(2,1)} %bitcast.22), channel_id=1, source_target_pairs={{0,1},{1,0},{2,3},{3,2},{4,5},{5,4},{6,7},{7,6},{8,9},{9,8},{10,11... | collective-permute-start | bytes 1327112 | tf_op jit(solution)/shard_map/ppermute | solution.py:347
  47.1 6.2 %collective-permute-start.14 = (bf16[27,16,512]{2,1,0:T(8,128)(2,1)S(1)}, bf16[27,16,512]{2,1,0:T(8,128)(2,1)S(1)}, u32[]{:S(2)}, u32[]{:S(2)}) collective-permute-start(bf16[27,16,512]{2,1,0:T(8,128)(2,1)S(1)} %collective-permute-done.6.refs_1_), channel_id=1, source_target_pairs={{0,1},{1,0},{2,3},{3,2},{4,5},{5,4},{6,7},{7,6},{8,9},{9,8},{10,11... | collective-permute-start | bytes 1327112 | tf_op jit(solution)/shard_map/ppermute | solution.py:347
  48.5 9.6 %collective-permute-start.15 = (bf16[27,16,512]{2,1,0:T(8,128)(2,1)S(1)}, bf16[27,16,512]{2,1,0:T(8,128)(2,1)S(1)}, u32[]{:S(2)}, u32[]{:S(2)}) collective-permute-start(bf16[27,16,512]{2,1,0:T(8,128)(2,1)S(1)} %collective-permute-done.7.refs_0_), channel_id=1, source_target_pairs={{0,1},{1,0},{2,3},{3,2},{4,5},{5,4},{6,7},{7,6},{8,9},{9,8},{10,11... | collective-permute-start | bytes 1327112 | tf_op jit(solution)/shard_map/ppermute | solution.py:364
  57.6 1.9 %collective-permute-start.16 = (bf16[27,16,512]{2,1,0:T(8,128)(2,1)S(1)}, bf16[27,16,512]{2,1,0:T(8,128)(2,1)S(1)}, u32[]{:S(2)}, u32[]{:S(2)}) collective-permute-start(bf16[27,16,512]{2,1,0:T(8,128)(2,1)S(1)} %broadcast_select_fusion.refs_1_), channel_id=1, source_target_pairs={{0,1},{1,0},{2,3},{3,2},{4,5},{5,4},{6,7},{7,6},{8,9},{9,8},{10,11... | collective-permute-start | bytes 1327112 | tf_op jit(solution)/shard_map/ppermute | solution.py:364
  63.7 4.8 %collective-permute-start.17 = (bf16[2,160,128]{2,1,0:T(8,128)(2,1)S(1)}, bf16[2,160,128]{2,1,0:T(8,128)(2,1)S(1)}, u32[]{:S(2)}, u32[]{:S(2)}) collective-permute-start(bf16[2,160,128]{2,1,0:T(8,128)(2,1)S(1)} %get-tuple-element.42), channel_id=1, source_target_pairs={{0,8},{8,0},{16,24},{24,16},{1,9},{9,1},{17,25},{25,17},{2,10},{10... | collective-permute-start | bytes 245768 | tf_op jit(solution)/shard_map/ppermute | solution.py:367
  65.2 5.3 %collective-permute-start.18 = (bf16[2,160,128]{2,1,0:T(8,128)(2,1)S(1)}, bf16[2,160,128]{2,1,0:T(8,128)(2,1)S(1)}, u32[]{:S(2)}, u32[]{:S(2)}) collective-permute-start(bf16[2,160,128]{2,1,0:T(8,128)(2,1)S(1)} %get-tuple-element.43), channel_id=1, source_target_pairs={{0,16},{8,24},{16,0},{24,8},{1,17},{9,25},{17,1},{25,9},{2,18},{10... | collective-permute-start | bytes 245768 | tf_op jit(solution)/shard_map/ppermute | solution.py:367
  66.8 5.3 %collective-permute-start.19 = (bf16[2,160,128]{2,1,0:T(8,128)(2,1)S(1)}, bf16[2,160,128]{2,1,0:T(8,128)(2,1)S(1)}, u32[]{:S(2)}, u32[]{:S(2)}) collective-permute-start(bf16[2,160,128]{2,1,0:T(8,128)(2,1)S(1)} %get-tuple-element.44), channel_id=1, source_target_pairs={{0,24},{8,16},{16,8},{24,0},{1,25},{9,17},{17,9},{25,1},{2,26},{10... | collective-permute-start | bytes 245768 | tf_op jit(solution)/shard_map/ppermute | solution.py:367

commit v3 on v2

--- a/solution.py
+++ b/solution.py
@@ -37,9 +37,14 @@
     return lax.optimization_barrier((block, *others))[0]
 
 
-def stats_kernel(x_ref, out_ref):
+def local_kernel(x_ref, stats_ref, top_ref, bottom_ref, payload_ref):
     frames, rows, cols, channels = x_ref.shape
     entries = frames * rows * cols
+    top_ref[...] = x_ref[:, 0:1]
+    bottom_ref[...] = x_ref[:, rows - 1 : rows]
+    for f in range(frames):
+        start = (f * (rows + 2) + 1) * cols
+        payload_ref[start : start + rows * cols, :] = x_ref[f].reshape(rows * cols, channels)
     for block in range(channels // LANES):
         lanes = pl.ds(block * LANES, LANES)
         total = jnp.zeros((8, LANES), jnp.float32)
@@ -53,16 +58,23 @@
             for r in range(rows):
                 x = x_ref[f, r, :, lanes].astype(jnp.float32) - mean
                 total = total + jnp.sum((x * x).reshape(-1, 8, LANES), axis=0)
-        out_ref[0:1, lanes] = mean
-        out_ref[1:2, lanes] = jnp.sum(total, axis=0, keepdims=True)
-
-
-def local_stats(latents):
-    return pl.pallas_call(
-        stats_kernel,
-        out_shape=jax.ShapeDtypeStruct((2, latents.shape[3]), jnp.float32),
+        stats_ref[0:1, lanes] = mean
+        stats_ref[1:2, lanes] = jnp.sum(total, axis=0, keepdims=True)
+
+
+def local(latents):
+    frames, rows, cols, channels = latents.shape
+    edge = jax.ShapeDtypeStruct((frames, 1, cols, channels), jnp.bfloat16)
+    return pl.pallas_call(
+        local_kernel,
+        out_shape=(
+            jax.ShapeDtypeStruct((2, channels), jnp.float32),
+            edge,
+            edge,
+            jax.ShapeDtypeStruct((frames * (rows + 2) * cols + 16, channels), jnp.bfloat16),
+        ),
         in_specs=[whole],
-        out_specs=whole,
+        out_specs=(whole,) * 4,
         compiler_params=params(8),
     )(latents)
 
@@ -73,29 +85,23 @@
     return jnp.stack([mean, sum(part[1] for part in parts) + apart])
 
 
-def pack_kernel(edge_ref, stats_ref, above_ref, x_ref, below_ref, out_ref):
-    frames, rows, cols, _ = x_ref.shape
-    count = frames * (rows + 2) * cols
+def pack_kernel(frames, rows, cols, edge_ref, stats_ref, above_ref, below_ref, _, out_ref):
+    count = frames * rows * cols
     for f in range(frames):
-        start = f * (rows + 2) * cols
-        out_ref[start + cols : start + (rows + 1) * cols, :] = x_ref[f].reshape(rows * cols, -1)
-        last = start + (rows + 1) * cols
-
-        @pl.when(edge_ref[0] == 0)
-        def _():
-            out_ref[start : start + cols, :] = above_ref[f, 0]
-
-        @pl.when(edge_ref[0] != 0)
-        def _():
-            out_ref[start : start + cols, :] = x_ref[f, 1]
-
-        @pl.when(edge_ref[1] == 0)
-        def _():
-            out_ref[last : last + cols, :] = below_ref[f, 0]
-
-        @pl.when(edge_ref[1] != 0)
-        def _():
-            out_ref[last : last + cols, :] = x_ref[f, rows - 2]
+        first = f * rows * cols
+        last = first + (rows - 1) * cols
+        for start, rim_ref, edge, mirror in (
+            (first, above_ref, 0, first + 2 * cols),
+            (last, below_ref, 1, last - 2 * cols),
+        ):
+
+            @pl.when(edge_ref[edge] == 0)
+            def _():
+                out_ref[start : start + cols, :] = rim_ref[f, 0]
+
+            @pl.when(edge_ref[edge] != 0)
+            def _():
+                out_ref[start : start + cols, :] = out_ref[mirror : mirror + cols, :]
 
     rest = stats_ref[...]
     terms = []
@@ -108,15 +114,51 @@
     out_ref[count:, :] = jnp.concatenate(terms, axis=0).astype(jnp.bfloat16)
 
 
-def pack(edges, stats, above, latents, below):
-    frames, rows, cols, channels = latents.shape
-    return pl.pallas_call(
-        pack_kernel,
-        out_shape=jax.ShapeDtypeStruct((frames * (rows + 2) * cols + 16, channels), jnp.bfloat16),
+def pack(edges, stats, above, below, payload, frames, rows, cols):
+    return pl.pallas_call(
+        functools.partial(pack_kernel, frames, rows, cols),
+        out_shape=jax.ShapeDtypeStruct(payload.shape, jnp.bfloat16),
         in_specs=[scalars] + [whole] * 4,
         out_specs=whole,
+        input_output_aliases={4: 0},
         compiler_params=params(8),
-    )(edges, stats, above, latents, below)
+    )(edges, stats, above, below, payload)
+
+
+def held_kernel(in_ref, out_ref):
+    pass
+
+
+def hold(block):
+    return pl.pallas_call(
+        held_kernel,
+        out_shape=jax.ShapeDtypeStruct(block.shape, block.dtype),
+        in_specs=[pl.BlockSpec(memory_space=pl.ANY)],
+        out_specs=pl.BlockSpec(memory_space=pl.ANY),
+        input_output_aliases={0: 0},
+        cost_estimate=pl.CostEstimate(flops=10**10, bytes_accessed=0, transcendentals=0),
+    )(block)
+
+
+def pick_kernel(which_ref, one_ref, other_ref, out_ref):
+    @pl.when(which_ref[0] != 0)
+    def _():
+        out_ref[...] = one_ref[...]
+
+    @pl.when(which_ref[0] == 0)
+    def _():
+        out_ref[...] = other_ref[...]
+
+
+def pick(which, one, other):
+    return pl.pallas_call(
+        pick_kernel,
+        out_shape=jax.ShapeDtypeStruct(one.shape, one.dtype),
+        in_specs=[scalars] + [whole] * 2,
+        out_specs=whole,
+        compiler_params=params(8),
+        cost_estimate=pl.CostEstimate(flops=10**10, bytes_accessed=one.size, transcendentals=0),
+    )(which, one, other)
 
 
 def lane_group_sum(x, size):
@@ -131,15 +173,14 @@
 
 
 def activate_kernel(held, rows, entries, place_ref, affine_ref, *refs):
-    *piece_refs, even_ref, odd_ref, scratch = refs
+    *piece_refs, even_ref, odd_ref, scratch, norm = refs
     channels = piece_refs[0].shape[1]
     frames = held * len(piece_refs)
     cols = odd_ref.shape[1] // frames
     tail = held * rows * cols
     size = channels // GROUPS
 
-    def step(index, carry):
-        lanes = pl.ds(pl.multiple_of(index * LANES, LANES), LANES)
+    def norms(lanes):
         means, squares = [], []
         for piece_ref in piece_refs:
             terms = piece_ref[tail : tail + 16, lanes].astype(jnp.float32)
@@ -150,24 +191,35 @@
         mean = lane_group_sum(jnp.broadcast_to(sum(means), (8, LANES)), size) / count
         spread = sum(squares) + entries * sum((m - mean[0:1]) ** 2 for m in means)
         var = lane_group_sum(jnp.broadcast_to(spread, (8, LANES)), size) / (count * entries)
-        mean = mean[0:1]
-        scale = lax.rsqrt(var[0:1] + epsilon) * affine_ref[0:1, lanes]
-        bias = affine_ref[1:2, lanes]
-        last = (cols + 1) * frames
-        for r in range(rows):
-            for p, piece_ref in enumerate(piece_refs):
-                for f in range(held):
-                    start = (f * rows + r) * cols
-                    x = piece_ref[start : start + cols, lanes].astype(jnp.float32)
-                    h = 0.5 * ((x - mean) * scale + bias)
-                    scratch[r, pl.ds(frames + place_ref[p] + f, cols, stride=frames), :] = h + h * jnp.tanh(h)
+        norm[0:1, lanes] = mean[0:1]
+        norm[1:2, lanes] = lax.rsqrt(var[0:1] + epsilon) * affine_ref[0:1, lanes]
+        norm[2:3, lanes] = affine_ref[1:2, lanes]
+
+    blocks = channels // LANES
+    for block in range(blocks):
+        norms(pl.ds(block * LANES, LANES))
+    last = (cols + 1) * frames
+
+    def step(index, carry):
+        pair, block = index // blocks, index % blocks
+        lanes = pl.ds(pl.multiple_of(block * LANES, LANES), LANES)
+        mean, scale, bias = norm[0:1, lanes], norm[1:2, lanes], norm[2:3, lanes]
+        for p, piece_ref in enumerate(piece_refs):
+            for f in range(held):
+                start = pl.multiple_of((f * rows + 2 * pair) * cols, 16)
+                x = piece_ref[pl.ds(start, 2 * cols), lanes].astype(jnp.float32)
+                h = 0.5 * ((x - mean) * scale + bias)
+                h = h + h * jnp.tanh(h)
+                for r in range(2):
+                    scratch[r, pl.ds(frames + place_ref[p] + f, cols, stride=frames), :] = h[r * cols : (r + 1) * cols]
+        for r in range(2):
             scratch[r, 0:frames, :] = scratch[r, 2 * frames : 3 * frames, :]
             scratch[r, last : last + frames, :] = scratch[r, last - 2 * frames : last - frames, :]
-            even_ref[r, :, lanes] = scratch[r].astype(jnp.bfloat16)
-            odd_ref[r, :, lanes] = scratch[r, frames:last, :].astype(jnp.bfloat16)
+            even_ref[2 * pair + r, :, lanes] = scratch[r].astype(jnp.bfloat16)
+            odd_ref[2 * pair + r, :, lanes] = scratch[r, frames:last, :].astype(jnp.bfloat16)
         return carry
 
-    lax.fori_loop(0, channels // LANES, step, 0)
+    lax.fori_loop(0, rows // 2 * blocks, step, 0)
 
 
 def activate(places, affine, pieces, held, rows, cols, entries):
@@ -181,7 +233,10 @@
         ),
         in_specs=[scalars, whole] + [whole] * len(pieces),
         out_specs=(whole, whole),
-        scratch_shapes=[pltpu.VMEM((rows, (cols + 2) * frames, LANES), jnp.float32)],
+        scratch_shapes=[
+            pltpu.VMEM((2, (cols + 2) * frames, LANES), jnp.float32),
+            pltpu.VMEM((3, channels), jnp.float32),
+        ],
         compiler_params=params(24),
         cost_estimate=pl.CostEstimate(
             flops=10 * frames * rows * cols * channels,
@@ -304,15 +359,17 @@
     weight = conv_weight.transpose(0, 1, 2, 4, 3)
     weight = weight.reshape((-1,) + weight.shape[3:])
 
-    above = lax.ppermute(latents[:, row_count - 1 :], "rows", [(i, i + 1) for i in range(strips - 1)])
-    below = lax.ppermute(latents[:, :1], "rows", [(i + 1, i) for i in range(strips - 1)])
+    stats, top, bottom, payload = local(latents)
+    above = lax.ppermute(bottom, "rows", [(i, i + 1) for i in range(strips - 1)])
+    below = lax.ppermute(top, "rows", [(i + 1, i) for i in range(strips - 1)])
 
     entries = held * row_count * col_count
-    stats = local_stats(latents)
     if is_line:
-        stats = merge([stats] + exchange(stats, "rows", [1]), entries)
         chips = range(CORES, strips, CORES)
-        stats = merge([stats] + exchange(stats, "rows", chips), CORES * entries)
+        stats = merge([stats] + exchange(stats, "rows", chips), entries)
+        weight = after(weight, stats, above, below)
+        first, second = exchange(weight, "rows", [CORES, 2 * CORES])
+        stats = merge([stats] + exchange(stats, "rows", [1]), 4 * entries)
         entries *= strips
     else:
         distance = 1
@@ -322,16 +379,15 @@
             distance *= 2
 
     if is_line:
-        weight = after(weight, stats, above, below)
-        first, second = exchange(weight, "rows", [CORES, 2 * CORES])
         weight, first, second = lax.optimization_barrier((weight, first, second))
+        second = hold(second)
         ends = chip_pairs([(1, 0), (2, 3)])
         middle = chip_pairs([(1, 2), (2, 1)])
         third_ends = lax.ppermute(second, "rows", ends)
         third_middle = lax.ppermute(weight, "rows", middle)
 
     edges = jnp.stack([strip == 0, strip == strips - 1]).astype(jnp.int32)
-    payload = pack(edges, stats, above, latents, below)
+    payload = pack(edges, stats, above, below, payload, held, row_count + 2, col_count)
     strip_pieces = [payload] + exchange(payload, "frames", range(1, group_count))
     groups = jnp.stack([group ^ d for d in range(group_count)]).astype(jnp.int32)
     affine = jnp.stack([norm_gain, norm_bias])
@@ -359,7 +415,8 @@
     if is_line:
         third_ends, third_middle, done = lax.optimization_barrier((third_ends, third_middle, done))
         chip = strip // CORES
-        third = jnp.where((chip == 0) | (chip == 3), third_ends, third_middle)
+        at_end = ((chip == 0) | (chip == 3)).astype(jnp.int32)[None]
+        third = pick(at_end, third_ends, third_middle)
         far.append(third)
         far += [lax.ppermute(piece, "rows", flip("rows", 1)) for piece in far]
     parts = convolved(other_half, pieces=far, other=done)

time: 73.7 us -> 70.9 us (0.962)
  the two profiles are of different devices: /device:TPU:8 before, /device:TPU:0 now
where the time goes in v3:
time: 70.9 us; the launch traced here: 70.3 us
  waiting for transfers between devices  29.7 us (42%)
  starting transfers between devices  24.5 us (35%)
  Pallas kernels  13.8 us (19%)
  local copies, waits for them, and re-layouts  1.86 us (3%)
    ppermute x9, waiting for transfers between devices, exchange(): return [lax.ppermute(block, axis, flip(axis, d)) for d in distances]  21.8 us
    ppermute x9, starting transfers between devices, exchange(): return [lax.ppermute(block, axis, flip(axis, d)) for d in distances]  15.7 us
    pallas_call x2, Pallas kernels, convolve(): pl.pallas_call(functools.partial(conv_kernel, len(pieces), other is not N...  8.29 us
    ppermute x3, waiting for transfers between devices, body(): lax.ppermute(parts[d], 'frames', flip('frames', d))  4.87 us
    ppermute x3, starting transfers between devices, body(): lax.ppermute(parts[d], 'frames', flip('frames', d))  3.55 us
    pallas_call x1, Pallas kernels, activate(): pl.pallas_call(functools.partial(activate_kernel, held, rows, entries), o...  3.32 us
    unnamed x14, local copies, waits for them, and re-layouts  1.78 us
    ppermute x2, waiting for transfers between devices, body(): far += [lax.ppermute(piece, 'rows', flip('rows', 1)) for piece in far]  1.77 us
  transfers between devices with their start and end apart: 20, of which 10 were waited for; matrix products, arithmetic and copies ran while one was open for 1% of the time, Pallas kernels for 12%

profile of v3, /device:TPU:0, one launch (start us, length us, event | category | flops | bytes accessed | tf_op | source)
XLA Modules:
  0.0 70.3 jit_solution(6618119403686726439)
XLA Ops:
  0.0 1.0 %copy-done.4 = bf16[2,4,40,512]{3,2,1,0:T(8,128)(2,1)S(1)} copy-done((bf16[2,4,40,512]{3,2,1,0:T(8,128)(2,1)S(1)}, bf16[2,4,40,512]{3,2,1,0:T(8,128)(2,1)}, u32[]{:S(2)}) %copy-start.4) | copy-done | bytes 327704
  1.0 0.2 shard_map.55
  1.2 3.1 %collective-permute-start = (f32[2,512]{1,0:T(2,128)S(1)}, f32[2,512]{1,0:T(2,128)S(1)}, u32[]{:S(2)}, u32[]{:S(2)}) collective-permute-start(f32[2,512]{1,0:T(2,128)S(1)} %get-tuple-element.29), channel_id=1, source_target_pairs={{0,2},{1,3},{2,0},{3,1},{4,6},{5,7},{6,4},{7,5},{8,10},{9,11},{10,... | collective-permute-start | bytes 12296 | tf_op jit(solution)/shard_map/ppermute | solution.py:29
  4.3 2.6 %collective-permute-start.1 = (f32[2,512]{1,0:T(2,128)S(1)}, f32[2,512]{1,0:T(2,128)S(1)}, u32[]{:S(2)}, u32[]{:S(2)}) collective-permute-start(f32[2,512]{1,0:T(2,128)S(1)} %get-tuple-element.29), channel_id=1, source_target_pairs={{0,4},{1,5},{2,6},{3,7},{4,0},{5,1},{6,2},{7,3},{8,12},{9,13},{10,... | collective-permute-start | bytes 12296 | tf_op jit(solution)/shard_map/ppermute | solution.py:29
  6.8 1.3 %collective-permute-start.3 = (bf16[2,1,40,512]{3,2,1,0:T(8,128)(2,1)S(1)}, bf16[2,1,40,512]{3,2,1,0:T(8,128)(2,1)S(1)}, u32[]{:S(2)}, u32[]{:S(2)}) collective-permute-start(bf16[2,1,40,512]{3,2,1,0:T(8,128)(2,1)S(1)} %get-tuple-element.30), channel_id=1, source_target_pairs={{0,1},{1,2},{2,3},{3,4},{4,5},{5,6},{6,7},{8,9},{9,10},{10,11},{11... | collective-permute-start | bytes 245768 | tf_op jit(solution)/shard_map/ppermute | solution.py:363
  8.1 1.3 %collective-permute-start.4 = (bf16[2,1,40,512]{3,2,1,0:T(8,128)(2,1)S(1)}, bf16[2,1,40,512]{3,2,1,0:T(8,128)(2,1)S(1)}, u32[]{:S(2)}, u32[]{:S(2)}) collective-permute-start(bf16[2,1,40,512]{3,2,1,0:T(8,128)(2,1)S(1)} %get-tuple-element.31), channel_id=1, source_target_pairs={{1,0},{2,1},{3,2},{4,3},{5,4},{6,5},{7,6},{9,8},{10,9},{11,10},{12... | collective-permute-start | bytes 245768 | tf_op jit(solution)/shard_map/ppermute | solution.py:364
  9.5 2.8 %collective-permute-done.2 = f32[2,512]{1,0:T(2,128)S(1)} collective-permute-done((f32[2,512]{1,0:T(2,128)S(1)}, f32[2,512]{1,0:T(2,128)S(1)}, u32[]{:S(2)}, u32[]{:S(2)}) %collective-permute-start.2) | collective-permute-done | bytes 4128 | tf_op jit(solution)/shard_map/ppermute | solution.py:29
  12.4 2.9 %collective-permute-start.5 = (bf16[27,16,512]{2,1,0:T(8,128)(2,1)}, bf16[27,16,512]{2,1,0:T(8,128)(2,1)S(1)}, u32[]{:S(2)}, u32[]{:S(2)}) collective-permute-start(bf16[27,16,512]{2,1,0:T(8,128)(2,1)} %bitcast.20), channel_id=1, source_target_pairs={{0,2},{1,3},{2,0},{3,1},{4,6},{5,7},{6,4},{7,5},{8,10},{9,11},{10,... | collective-permute-start | bytes 1327112 | tf_op jit(solution)/shard_map/ppermute | solution.py:29
  15.3 3.5 %collective-permute-start.6 = (bf16[27,16,512]{2,1,0:T(8,128)(2,1)}, bf16[27,16,512]{2,1,0:T(8,128)(2,1)S(1)}, u32[]{:S(2)}, u32[]{:S(2)}) collective-permute-start(bf16[27,16,512]{2,1,0:T(8,128)(2,1)} %bitcast.21), channel_id=1, source_target_pairs={{0,4},{1,5},{2,6},{3,7},{4,0},{5,1},{6,2},{7,3},{8,12},{9,13},{10,... | collective-permute-start | bytes 1327112 | tf_op jit(solution)/shard_map/ppermute | solution.py:29
  18.9 0.6 shard_map.56.refs_0_
  19.6 2.5 %collective-permute-start.10 = (bf16[496,512]{1,0:T(8,128)(2,1)S(1)}, bf16[496,512]{1,0:T(8,128)(2,1)S(1)}, u32[]{:S(2)}, u32[]{:S(2)}) collective-permute-start(bf16[496,512]{1,0:T(8,128)(2,1)S(1)} %shard_map.56.refs_0_), channel_id=1, source_target_pairs={{0,24},{8,16},{16,8},{24,0},{1,25},{9,17},{17,9},{25,1},{2,26},{10... | collective-permute-start | bytes 1523720 | tf_op jit(solution)/shard_map/ppermute | solution.py:29
  22.1 0.5 collective-permute-start.8
  22.7 0.5 collective-permute-start.9
  23.2 11.2 %collective-permute-done.5.refs_1_ = bf16[27,16,512]{2,1,0:T(8,128)(2,1)S(1)} collective-permute-done((bf16[27,16,512]{2,1,0:T(8,128)(2,1)}, bf16[27,16,512]{2,1,0:T(8,128)(2,1)S(1)}, u32[]{:S(2)}, u32[]{:S(2)}) %collective-permute-start.5) | collective-permute-done | bytes 442400 | tf_op jit(solution)/shard_map/ppermute | solution.py:29
  34.4 5.2 %collective-permute-done.6.in_ref = bf16[27,16,512]{2,1,0:T(8,128)(2,1)S(1)} collective-permute-done((bf16[27,16,512]{2,1,0:T(8,128)(2,1)}, bf16[27,16,512]{2,1,0:T(8,128)(2,1)S(1)}, u32[]{:S(2)}, u32[]{:S(2)}) %collective-permute-start.6) | collective-permute-done | bytes 442400 | tf_op jit(solution)/shard_map/ppermute | solution.py:29
  39.5 0.8 %copy-done.2 = bf16[27,16,512]{2,1,0:T(8,128)(2,1)} copy-done((bf16[27,16,512]{2,1,0:T(8,128)(2,1)}, bf16[27,16,512]{2,1,0:T(8,128)(2,1)S(1)}, u32[]{:S(2)}) %copy-start.2) | copy-done | bytes 442392
  40.3 1.3 %collective-permute-start.11 = (bf16[27,16,512]{2,1,0:T(8,128)(2,1)}, bf16[27,16,512]{2,1,0:T(8,128)(2,1)S(1)}, u32[]{:S(2)}, u32[]{:S(2)}) collective-permute-start(bf16[27,16,512]{2,1,0:T(8,128)(2,1)} %shard_map.57.refs_0_), channel_id=1, source_target_pairs={{2,0},{3,1},{4,6},{5,7},{10,8},{11,9},{12,14},{13,15},{18,16},{19,... | collective-permute-start | bytes 1327112 | tf_op jit(solution)/shard_map/ppermute | solution.py:386
  41.6 0.7 collective-permute-start.12
  42.3 2.6 %collective-permute-done.8.refs_1_ = bf16[496,512]{1,0:T(8,128)(2,1)S(1)} collective-permute-done((bf16[496,512]{1,0:T(8,128)(2,1)S(1)}, bf16[496,512]{1,0:T(8,128)(2,1)S(1)}, u32[]{:S(2)}, u32[]{:S(2)}) %collective-permute-start.8) | collective-permute-done | bytes 507936 | tf_op jit(solution)/shard_map/ppermute | solution.py:29
  44.9 0.5 collective-permute-start.14
  45.8 3.3 %shard_map.58 = (bf16[6,336,512]{2,1,0:T(8,128)(2,1)S(1)}, bf16[6,320,512]{2,1,0:T(8,128)(2,1)S(1)}) custom-call(s32[4]{0:T(128)S(1)} %get-tuple-element.55.place_ref, f32[2,512]{1,0:T(2,128)S(1)} %pad_maximum_fusion.affine_ref, bf16[496,512]{1,0:T(8,128)(2,1)S(1)} %shard_map.56.refs_0_, bf16[496,512]{1,0:T(8,128)(2,1)S(1)} %collective-permute-done.8.refs_1_, ...), custom_call_target="tpu_custom_call" | custom-call | flops 9830400 | bytes 5898240 | tf_op jit(solution)/shard_map/pallas_call | solution.py:228
  49.1 4.2 %shard_map.59.refs_4_ = bf16[8,160,128]{2,1,0:T(8,128)(2,1)S(1)} custom-call(s32[4]{0:T(128)S(1)} %get-tuple-element.55.place_ref, s32[4]{0:T(128)S(1)} %and_select_fusion.slot_ref, s32[1]{0:T(128)} %bitcast.8.half_ref, bf16[6,336,512]{2,1,0:T(8,128)(2,1)S(1)} %get-tuple-element.41.even_ref, bf16[6,320,512]{2,1,0:T(8,128)(2,1)S(1)} %get-tuple-element.42.odd_ref, ...), custom_call_target="tpu_custom_call" | custom-call | flops 83886080 | bytes 65536 | tf_op jit(solution)/shard_map/pallas_call | solution.py:314
  53.3 1.2 %collective-permute-done.11.one_ref = bf16[27,16,512]{2,1,0:T(8,128)(2,1)S(1)} collective-permute-done((bf16[27,16,512]{2,1,0:T(8,128)(2,1)}, bf16[27,16,512]{2,1,0:T(8,128)(2,1)S(1)}, u32[]{:S(2)}, u32[]{:S(2)}) %collective-permute-start.11) | collective-permute-done | bytes 442400 | tf_op jit(solution)/shard_map/ppermute | solution.py:386
  54.6 1.8 %collective-permute-done.16.refs_3_ = bf16[27,16,512]{2,1,0:T(8,128)(2,1)S(1)} collective-permute-done((bf16[27,16,512]{2,1,0:T(8,128)(2,1)S(1)}, bf16[27,16,512]{2,1,0:T(8,128)(2,1)S(1)}, u32[]{:S(2)}, u32[]{:S(2)}) %collective-permute-start.16) | collective-permute-done | bytes 442400 | tf_op jit(solution)/shard_map/ppermute | solution.py:421
  56.4 4.1 %shard_map.61 = (bf16[2,160,128]{2,1,0:T(8,128)(2,1)S(1)}, bf16[2,160,128]{2,1,0:T(8,128)(2,1)S(1)}, bf16[2,160,128]{2,1,0:T(8,128)(2,1)S(1)}, bf16[2,160,128]{2,1,0:T(8,128)(2,1)S(1)}) custom-call(s32[4]{0:T(128)S(1)} %get-tuple-element.55.place_ref, s32[4]{0:T(128)S(1)} %and_select_fusion.slot_ref, s32[1]{0:T(128)S(6)} %sub.40.half_ref, ...), custom_call_target="tpu_custom_call" | custom-call | flops 83886080 | bytes 65536 | tf_op jit(solution)/shard_map/pallas_call | solution.py:314
  60.5 1.6 %collective-permute-start.17 = (bf16[2,160,128]{2,1,0:T(8,128)(2,1)S(1)}, bf16[2,160,128]{2,1,0:T(8,128)(2,1)S(1)}, u32[]{:S(2)}, u32[]{:S(2)}) collective-permute-start(bf16[2,160,128]{2,1,0:T(8,128)(2,1)S(1)} %get-tuple-element.50), channel_id=1, source_target_pairs={{0,8},{8,0},{16,24},{24,16},{1,9},{9,1},{17,25},{25,17},{2,10},{10... | collective-permute-start | bytes 245768 | tf_op jit(solution)/shard_map/ppermute | solution.py:424
  62.1 1.5 %collective-permute-start.18 = (bf16[2,160,128]{2,1,0:T(8,128)(2,1)S(1)}, bf16[2,160,128]{2,1,0:T(8,128)(2,1)S(1)}, u32[]{:S(2)}, u32[]{:S(2)}) collective-permute-start(bf16[2,160,128]{2,1,0:T(8,128)(2,1)S(1)} %get-tuple-element.51), channel_id=1, source_target_pairs={{0,16},{8,24},{16,0},{24,8},{1,17},{9,25},{17,1},{25,9},{2,18},{10... | collective-permute-start | bytes 245768 | tf_op jit(solution)/shard_map/ppermute | solution.py:424
  63.6 0.5 collective-permute-start.19
  64.1 1.0 %collective-permute-done.17.refs_1_ = bf16[2,160,128]{2,1,0:T(8,128)(2,1)S(1)} collective-permute-done((bf16[2,160,128]{2,1,0:T(8,128)(2,1)S(1)}, bf16[2,160,128]{2,1,0:T(8,128)(2,1)S(1)}, u32[]{:S(2)}, u32[]{:S(2)}) %collective-permute-start.17) | collective-permute-done | bytes 81952 | tf_op jit(solution)/shard_map/ppermute | solution.py:424
  65.1 2.3 %collective-permute-done.18.refs_2_ = bf16[2,160,128]{2,1,0:T(8,128)(2,1)S(1)} collective-permute-done((bf16[2,160,128]{2,1,0:T(8,128)(2,1)S(1)}, bf16[2,160,128]{2,1,0:T(8,128)(2,1)S(1)}, u32[]{:S(2)}, u32[]{:S(2)}) %collective-permute-start.18) | collective-permute-done | bytes 81952 | tf_op jit(solution)/shard_map/ppermute | solution.py:424
  67.4 1.6 %collective-permute-done.19.refs_3_ = bf16[2,160,128]{2,1,0:T(8,128)(2,1)S(1)} collective-permute-done((bf16[2,160,128]{2,1,0:T(8,128)(2,1)S(1)}, bf16[2,160,128]{2,1,0:T(8,128)(2,1)S(1)}, u32[]{:S(2)}, u32[]{:S(2)}) %collective-permute-start.19) | collective-permute-done | bytes 81952 | tf_op jit(solution)/shard_map/ppermute | solution.py:424
  69.0 1.3 %shard_map.62 = bf16[2,160,512]{2,1,0:T(8,128)(2,1)} custom-call(s32[4]{0:T(128)S(1)} %get-tuple-element.56.place_ref, bf16[2,160,128]{2,1,0:T(8,128)(2,1)S(1)} %get-tuple-element.49.refs_0_, bf16[2,160,128]{2,1,0:T(8,128)(2,1)S(1)} %collective-permute-done.17.refs_1_, bf16[2,160,128]{2,1,0:T(8,128)(2,1)S(1)} %collective-permute-done.18.refs_2_, ...), custom_call_target="tpu_custom_call" | custom-call | tf_op jit(solution)/shard_map/pallas_call | solution.py:343
  (39 shorter events, 0.7 us)
Async XLA Ops:
  0.0 45.5 %copy-start = (f32[512]{0:T(512)S(1)}, f32[512]{0:T(512)}, u32[]{:S(2)}) copy-start(f32[512]{0:T(512)} %param.9) | copy-start | bytes 6148
  0.0 1.0 %copy-start.4 = (bf16[2,4,40,512]{3,2,1,0:T(8,128)(2,1)S(1)}, bf16[2,4,40,512]{3,2,1,0:T(8,128)(2,1)}, u32[]{:S(2)}) copy-start(bf16[2,4,40,512]{3,2,1,0:T(8,128)(2,1)} %x_ref.1) | copy-start | bytes 983044
  1.2 8.3 %collective-permute-start = (f32[2,512]{1,0:T(2,128)S(1)}, f32[2,512]{1,0:T(2,128)S(1)}, u32[]{:S(2)}, u32[]{:S(2)}) collective-permute-start(f32[2,512]{1,0:T(2,128)S(1)} %get-tuple-element.29), channel_id=1, source_target_pairs={{0,2},{1,3},{2,0},{3,1},{4,6},{5,7},{6,4},{7,5},{8,10},{9,11},{10,... | collective-permute-start | bytes 12296 | tf_op jit(solution)/shard_map/ppermute | solution.py:29
  4.3 5.2 %collective-permute-start.1 = (f32[2,512]{1,0:T(2,128)S(1)}, f32[2,512]{1,0:T(2,128)S(1)}, u32[]{:S(2)}, u32[]{:S(2)}) collective-permute-start(f32[2,512]{1,0:T(2,128)S(1)} %get-tuple-element.29), channel_id=1, source_target_pairs={{0,4},{1,5},{2,6},{3,7},{4,0},{5,1},{6,2},{7,3},{8,12},{9,13},{10,... | collective-permute-start | bytes 12296 | tf_op jit(solution)/shard_map/ppermute | solution.py:29
  6.8 5.4 %collective-permute-start.2 = (f32[2,512]{1,0:T(2,128)S(1)}, f32[2,512]{1,0:T(2,128)S(1)}, u32[]{:S(2)}, u32[]{:S(2)}) collective-permute-start(f32[2,512]{1,0:T(2,128)S(1)} %get-tuple-element.29), channel_id=1, source_target_pairs={{0,6},{1,7},{2,4},{3,5},{4,2},{5,3},{6,0},{7,1},{8,14},{9,15},{10,... | collective-permute-start | bytes 12296 | tf_op jit(solution)/shard_map/ppermute | solution.py:29
  6.8 5.5 %collective-permute-start.3 = (bf16[2,1,40,512]{3,2,1,0:T(8,128)(2,1)S(1)}, bf16[2,1,40,512]{3,2,1,0:T(8,128)(2,1)S(1)}, u32[]{:S(2)}, u32[]{:S(2)}) collective-permute-start(bf16[2,1,40,512]{3,2,1,0:T(8,128)(2,1)S(1)} %get-tuple-element.30), channel_id=1, source_target_pairs={{0,1},{1,2},{2,3},{3,4},{4,5},{5,6},{6,7},{8,9},{9,10},{10,11},{11... | collective-permute-start | bytes 245768 | tf_op jit(solution)/shard_map/ppermute | solution.py:363
  8.1 4.3 %collective-permute-start.4 = (bf16[2,1,40,512]{3,2,1,0:T(8,128)(2,1)S(1)}, bf16[2,1,40,512]{3,2,1,0:T(8,128)(2,1)S(1)}, u32[]{:S(2)}, u32[]{:S(2)}) collective-permute-start(bf16[2,1,40,512]{3,2,1,0:T(8,128)(2,1)S(1)} %get-tuple-element.31), channel_id=1, source_target_pairs={{1,0},{2,1},{3,2},{4,3},{5,4},{6,5},{7,6},{9,8},{10,9},{11,10},{12... | collective-permute-start | bytes 245768 | tf_op jit(solution)/shard_map/ppermute | solution.py:364
  12.3 6.6 %collective-permute-start.7 = (f32[2,512]{1,0:T(2,128)S(1)}, f32[2,512]{1,0:T(2,128)S(1)}, u32[]{:S(2)}, u32[]{:S(2)}) collective-permute-start(f32[2,512]{1,0:T(2,128)S(1)} %pad_maximum_fusion.1), channel_id=1, source_target_pairs={{0,1},{1,0},{2,3},{3,2},{4,5},{5,4},{6,7},{7,6},{8,9},{9,8},{10,11... | collective-permute-start | bytes 12296 | tf_op jit(solution)/shard_map/ppermute | solution.py:29
  12.4 21.9 %collective-permute-start.5 = (bf16[27,16,512]{2,1,0:T(8,128)(2,1)}, bf16[27,16,512]{2,1,0:T(8,128)(2,1)S(1)}, u32[]{:S(2)}, u32[]{:S(2)}) collective-permute-start(bf16[27,16,512]{2,1,0:T(8,128)(2,1)} %bitcast.20), channel_id=1, source_target_pairs={{0,2},{1,3},{2,0},{3,1},{4,6},{5,7},{6,4},{7,5},{8,10},{9,11},{10,... | collective-permute-start | bytes 1327112 | tf_op jit(solution)/shard_map/ppermute | solution.py:29
  15.3 24.2 %collective-permute-start.6 = (bf16[27,16,512]{2,1,0:T(8,128)(2,1)}, bf16[27,16,512]{2,1,0:T(8,128)(2,1)S(1)}, u32[]{:S(2)}, u32[]{:S(2)}) collective-permute-start(bf16[27,16,512]{2,1,0:T(8,128)(2,1)} %bitcast.21), channel_id=1, source_target_pairs={{0,4},{1,5},{2,6},{3,7},{4,0},{5,1},{6,2},{7,3},{8,12},{9,13},{10,... | collective-permute-start | bytes 1327112 | tf_op jit(solution)/shard_map/ppermute | solution.py:29
  19.6 22.0 %copy-start.1 = (bf16[3,3,3,512,16]{3,4,2,1,0:T(8,128)(2,1)S(1)}, bf16[3,3,3,512,16]{3,4,2,1,0:T(8,128)(2,1)}, u32[]{:S(2)}) copy-start(bf16[3,3,3,512,16]{3,4,2,1,0:T(8,128)(2,1)} %param.8) | copy-start | bytes 1327108
  19.6 26.1 %copy-start.5 = (f32[512]{0:T(512)S(1)}, f32[512]{0:T(512)}, u32[]{:S(2)}) copy-start(f32[512]{0:T(512)} %param.7) | copy-start | bytes 6148
  19.6 26.1 %copy-start.6 = (f32[512]{0:T(512)S(1)}, f32[512]{0:T(512)}, u32[]{:S(2)}) copy-start(f32[512]{0:T(512)} %param.6) | copy-start | bytes 6148
  19.6 22.7 %collective-permute-start.10 = (bf16[496,512]{1,0:T(8,128)(2,1)S(1)}, bf16[496,512]{1,0:T(8,128)(2,1)S(1)}, u32[]{:S(2)}, u32[]{:S(2)}) collective-permute-start(bf16[496,512]{1,0:T(8,128)(2,1)S(1)} %shard_map.56.refs_0_), channel_id=1, source_target_pairs={{0,24},{8,16},{16,8},{24,0},{1,25},{9,17},{17,9},{25,1},{2,26},{10... | collective-permute-start | bytes 1523720 | tf_op jit(solution)/shard_map/ppermute | solution.py:29
  22.1 22.8 %collective-permute-start.8 = (bf16[496,512]{1,0:T(8,128)(2,1)S(1)}, bf16[496,512]{1,0:T(8,128)(2,1)S(1)}, u32[]{:S(2)}, u32[]{:S(2)}) collective-permute-start(bf16[496,512]{1,0:T(8,128)(2,1)S(1)} %shard_map.56.refs_0_), channel_id=1, source_target_pairs={{0,8},{8,0},{16,24},{24,16},{1,9},{9,1},{17,25},{25,17},{2,10},{10... | collective-permute-start | bytes 1523720 | tf_op jit(solution)/shard_map/ppermute | solution.py:29
  22.7 22.3 %collective-permute-start.9 = (bf16[496,512]{1,0:T(8,128)(2,1)S(1)}, bf16[496,512]{1,0:T(8,128)(2,1)S(1)}, u32[]{:S(2)}, u32[]{:S(2)}) collective-permute-start(bf16[496,512]{1,0:T(8,128)(2,1)S(1)} %shard_map.56.refs_0_), channel_id=1, source_target_pairs={{0,16},{8,24},{16,0},{24,8},{1,17},{9,25},{17,1},{25,9},{2,18},{10... | collective-permute-start | bytes 1523720 | tf_op jit(solution)/shard_map/ppermute | solution.py:29
  39.5 0.8 %copy-start.2 = (bf16[27,16,512]{2,1,0:T(8,128)(2,1)}, bf16[27,16,512]{2,1,0:T(8,128)(2,1)S(1)}, u32[]{:S(2)}) copy-start(bf16[27,16,512]{2,1,0:T(8,128)(2,1)S(1)} %collective-permute-done.6.in_ref) | copy-start | bytes 1327108
  40.3 14.2 %collective-permute-start.11 = (bf16[27,16,512]{2,1,0:T(8,128)(2,1)}, bf16[27,16,512]{2,1,0:T(8,128)(2,1)S(1)}, u32[]{:S(2)}, u32[]{:S(2)}) collective-permute-start(bf16[27,16,512]{2,1,0:T(8,128)(2,1)} %shard_map.57.refs_0_), channel_id=1, source_target_pairs={{2,0},{3,1},{4,6},{5,7},{10,8},{11,9},{12,14},{13,15},{18,16},{19,... | collective-permute-start | bytes 1327112 | tf_op jit(solution)/shard_map/ppermute | solution.py:386
  41.6 12.9 %collective-permute-start.12 = (bf16[27,16,512]{2,1,0:T(8,128)(2,1)S(1)}, bf16[27,16,512]{2,1,0:T(8,128)(2,1)S(1)}, u32[]{:S(2)}, u32[]{:S(2)}) collective-permute-start(bf16[27,16,512]{2,1,0:T(8,128)(2,1)S(1)} %bitcast.22), channel_id=1, source_target_pairs={{2,4},{3,5},{4,2},{5,3},{10,12},{11,13},{12,10},{13,11},{18,20},{1... | collective-permute-start | bytes 1327112 | tf_op jit(solution)/shard_map/ppermute | solution.py:387
  44.9 4.2 %collective-permute-start.13 = (bf16[27,16,512]{2,1,0:T(8,128)(2,1)S(1)}, bf16[27,16,512]{2,1,0:T(8,128)(2,1)S(1)}, u32[]{:S(2)}, u32[]{:S(2)}) collective-permute-start(bf16[27,16,512]{2,1,0:T(8,128)(2,1)S(1)} %bitcast.23), channel_id=1, source_target_pairs={{0,1},{1,0},{2,3},{3,2},{4,5},{5,4},{6,7},{7,6},{8,9},{9,8},{10,11... | collective-permute-start | bytes 1327112 | tf_op jit(solution)/shard_map/ppermute | solution.py:403
  44.9 4.2 %collective-permute-start.14 = (bf16[27,16,512]{2,1,0:T(8,128)(2,1)S(1)}, bf16[27,16,512]{2,1,0:T(8,128)(2,1)S(1)}, u32[]{:S(2)}, u32[]{:S(2)}) collective-permute-start(bf16[27,16,512]{2,1,0:T(8,128)(2,1)S(1)} %collective-permute-done.5.refs_1_), channel_id=1, source_target_pairs={{0,1},{1,0},{2,3},{3,2},{4,5},{5,4},{6,7},{7,6},{8,9},{9,8},{10,11... | collective-permute-start | bytes 1327112 | tf_op jit(solution)/shard_map/ppermute | solution.py:403
  45.7 8.9 %collective-permute-start.15 = (bf16[27,16,512]{2,1,0:T(8,128)(2,1)}, bf16[27,16,512]{2,1,0:T(8,128)(2,1)S(1)}, u32[]{:S(2)}, u32[]{:S(2)}) collective-permute-start(bf16[27,16,512]{2,1,0:T(8,128)(2,1)} %shard_map.57.refs_0_), channel_id=1, source_target_pairs={{0,1},{1,0},{2,3},{3,2},{4,5},{5,4},{6,7},{7,6},{8,9},{9,8},{10,11... | collective-permute-start | bytes 1327112 | tf_op jit(solution)/shard_map/ppermute | solution.py:421
  54.5 1.9 %copy-start.3 = (bf16[27,16,512]{2,1,0:T(8,128)(2,1)S(1)}, bf16[27,16,512]{2,1,0:T(8,128)(2,1)}, u32[]{:S(2)}) copy-start(bf16[27,16,512]{2,1,0:T(8,128)(2,1)} %shard_map.57.refs_0_) | copy-start | bytes 1327108
  54.5 1.9 %collective-permute-start.16 = (bf16[27,16,512]{2,1,0:T(8,128)(2,1)S(1)}, bf16[27,16,512]{2,1,0:T(8,128)(2,1)S(1)}, u32[]{:S(2)}, u32[]{:S(2)}) collective-permute-start(bf16[27,16,512]{2,1,0:T(8,128)(2,1)S(1)} %shard_map.60.refs_1_), channel_id=1, source_target_pairs={{0,1},{1,0},{2,3},{3,2},{4,5},{5,4},{6,7},{7,6},{8,9},{9,8},{10,11... | collective-permute-start | bytes 1327112 | tf_op jit(solution)/shard_map/ppermute | solution.py:421
  60.5 4.6 %collective-permute-start.17 = (bf16[2,160,128]{2,1,0:T(8,128)(2,1)S(1)}, bf16[2,160,128]{2,1,0:T(8,128)(2,1)S(1)}, u32[]{:S(2)}, u32[]{:S(2)}) collective-permute-start(bf16[2,160,128]{2,1,0:T(8,128)(2,1)S(1)} %get-tuple-element.50), channel_id=1, source_target_pairs={{0,8},{8,0},{16,24},{24,16},{1,9},{9,1},{17,25},{25,17},{2,10},{10... | collective-permute-start | bytes 245768 | tf_op jit(solution)/shard_map/ppermute | solution.py:424
  62.1 5.3 %collective-permute-start.18 = (bf16[2,160,128]{2,1,0:T(8,128)(2,1)S(1)}, bf16[2,160,128]{2,1,0:T(8,128)(2,1)S(1)}, u32[]{:S(2)}, u32[]{:S(2)}) collective-permute-start(bf16[2,160,128]{2,1,0:T(8,128)(2,1)S(1)} %get-tuple-element.51), channel_id=1, source_target_pairs={{0,16},{8,24},{16,0},{24,8},{1,17},{9,25},{17,1},{25,9},{2,18},{10... | collective-permute-start | bytes 245768 | tf_op jit(solution)/shard_map/ppermute | solution.py:424
  63.6 5.3 %collective-permute-start.19 = (bf16[2,160,128]{2,1,0:T(8,128)(2,1)S(1)}, bf16[2,160,128]{2,1,0:T(8,128)(2,1)S(1)}, u32[]{:S(2)}, u32[]{:S(2)}) collective-permute-start(bf16[2,160,128]{2,1,0:T(8,128)(2,1)S(1)} %get-tuple-element.52), channel_id=1, source_target_pairs={{0,24},{8,16},{16,8},{24,0},{1,25},{9,17},{17,9},{25,1},{2,26},{10... | collective-permute-start | bytes 245768 | tf_op jit(solution)/shard_map/ppermute | solution.py:424

commit v4 on v3

--- a/solution.py
+++ b/solution.py
@@ -71,7 +71,7 @@
             jax.ShapeDtypeStruct((2, channels), jnp.float32),
             edge,
             edge,
-            jax.ShapeDtypeStruct((frames * (rows + 2) * cols + 16, channels), jnp.bfloat16),
+            jax.ShapeDtypeStruct((frames * (rows + 2) * cols, channels), jnp.bfloat16),
         ),
         in_specs=[whole],
         out_specs=(whole,) * 4,
@@ -85,8 +85,7 @@
     return jnp.stack([mean, sum(part[1] for part in parts) + apart])
 
 
-def pack_kernel(frames, rows, cols, edge_ref, stats_ref, above_ref, below_ref, _, out_ref):
-    count = frames * rows * cols
+def pack_kernel(frames, rows, cols, edge_ref, above_ref, below_ref, _, out_ref):
     for f in range(frames):
         first = f * rows * cols
         last = first + (rows - 1) * cols
@@ -103,26 +102,16 @@
             def _():
                 out_ref[start : start + cols, :] = out_ref[mirror : mirror + cols, :]
 
-    rest = stats_ref[...]
-    terms = []
-    for _ in range(3):
-        term = rest.astype(jnp.bfloat16).astype(jnp.float32)
-        terms.append(term)
-        rest = rest - term
-    unused = out_ref.shape[0] - count - 6
-    terms.append(jnp.zeros((unused, rest.shape[1]), jnp.float32))
-    out_ref[count:, :] = jnp.concatenate(terms, axis=0).astype(jnp.bfloat16)
-
-
-def pack(edges, stats, above, below, payload, frames, rows, cols):
+
+def pack(edges, above, below, payload, frames, rows, cols):
     return pl.pallas_call(
         functools.partial(pack_kernel, frames, rows, cols),
         out_shape=jax.ShapeDtypeStruct(payload.shape, jnp.bfloat16),
-        in_specs=[scalars] + [whole] * 4,
+        in_specs=[scalars] + [whole] * 3,
         out_specs=whole,
-        input_output_aliases={4: 0},
+        input_output_aliases={3: 0},
         compiler_params=params(8),
-    )(edges, stats, above, below, payload)
+    )(edges, above, below, payload)
 
 
 def held_kernel(in_ref, out_ref):
@@ -172,25 +161,17 @@
     return x
 
 
-def activate_kernel(held, rows, entries, place_ref, affine_ref, *refs):
+def activate_kernel(origins, rows, cols, entries, place_ref, stats_ref, affine_ref, *refs):
     *piece_refs, even_ref, odd_ref, scratch, norm = refs
     channels = piece_refs[0].shape[1]
-    frames = held * len(piece_refs)
-    cols = odd_ref.shape[1] // frames
-    tail = held * rows * cols
+    frames = odd_ref.shape[1] // cols
     size = channels // GROUPS
 
     def norms(lanes):
-        means, squares = [], []
-        for piece_ref in piece_refs:
-            terms = piece_ref[tail : tail + 16, lanes].astype(jnp.float32)
-            both = terms[0:2] + terms[2:4] + terms[4:6]
-            means.append(both[0:1])
-            squares.append(both[1:2])
-        count = len(piece_refs) * size
-        mean = lane_group_sum(jnp.broadcast_to(sum(means), (8, LANES)), size) / count
-        spread = sum(squares) + entries * sum((m - mean[0:1]) ** 2 for m in means)
-        var = lane_group_sum(jnp.broadcast_to(spread, (8, LANES)), size) / (count * entries)
+        means = stats_ref[0:1, lanes]
+        mean = lane_group_sum(jnp.broadcast_to(means, (8, LANES)), size) / size
+        spread = stats_ref[1:2, lanes] + entries * (means - mean[0:1]) ** 2
+        var = lane_group_sum(jnp.broadcast_to(spread, (8, LANES)), size) / (size * entries)
         norm[0:1, lanes] = mean[0:1]
         norm[1:2, lanes] = lax.rsqrt(var[0:1] + epsilon) * affine_ref[0:1, lanes]
         norm[2:3, lanes] = affine_ref[1:2, lanes]
@@ -204,14 +185,14 @@
         pair, block = index // blocks, index % blocks
         lanes = pl.ds(pl.multiple_of(block * LANES, LANES), LANES)
         mean, scale, bias = norm[0:1, lanes], norm[1:2, lanes], norm[2:3, lanes]
-        for p, piece_ref in enumerate(piece_refs):
-            for f in range(held):
+        for (p, shift), piece_ref in zip(origins, piece_refs):
+            for f in range(piece_ref.shape[0] // (rows * cols)):
                 start = pl.multiple_of((f * rows + 2 * pair) * cols, 16)
                 x = piece_ref[pl.ds(start, 2 * cols), lanes].astype(jnp.float32)
                 h = 0.5 * ((x - mean) * scale + bias)
                 h = h + h * jnp.tanh(h)
                 for r in range(2):
-                    scratch[r, pl.ds(frames + place_ref[p] + f, cols, stride=frames), :] = h[r * cols : (r + 1) * cols]
+                    scratch[r, pl.ds(frames + place_ref[p] + shift + f, cols, stride=frames), :] = h[r * cols : (r + 1) * cols]
         for r in range(2):
             scratch[r, 0:frames, :] = scratch[r, 2 * frames : 3 * frames, :]
             scratch[r, last : last + frames, :] = scratch[r, last - 2 * frames : last - frames, :]
@@ -222,16 +203,16 @@
     lax.fori_loop(0, rows // 2 * blocks, step, 0)
 
 
-def activate(places, affine, pieces, held, rows, cols, entries):
+def activate(places, stats, affine, pieces, origins, rows, cols, entries):
     channels = pieces[0].shape[1]
-    frames = held * len(pieces)
-    return pl.pallas_call(
-        functools.partial(activate_kernel, held, rows, entries),
+    frames = sum(piece.shape[0] for piece in pieces) // (rows * cols)
+    return pl.pallas_call(
+        functools.partial(activate_kernel, origins, rows, cols, entries),
         out_shape=(
             jax.ShapeDtypeStruct((rows, (cols + 2) * frames, channels), jnp.bfloat16),
             jax.ShapeDtypeStruct((rows, cols * frames, channels), jnp.bfloat16),
         ),
-        in_specs=[scalars, whole] + [whole] * len(pieces),
+        in_specs=[scalars, whole, whole] + [whole] * len(pieces),
         out_specs=(whole, whole),
         scratch_shapes=[
             pltpu.VMEM((2, (cols + 2) * frames, LANES), jnp.float32),
@@ -243,7 +224,7 @@
             bytes_accessed=6 * frames * rows * cols * channels,
             transcendentals=frames * rows * cols * channels,
         ),
-    )(places, affine, *pieces)
+    )(places, stats, affine, *pieces)
 
 
 def conv_kernel(count, with_other, place_ref, slot_ref, half_ref, even_ref, odd_ref, bias_ref, *refs):
@@ -284,15 +265,19 @@
     count = rows * cols
     lane = lax.broadcasted_iota(jnp.int32, (count, 2 * width), 1)
     low = lane < width
+    quarter = lane // (width // 2)
+    turned = (half_ref[1] != 0) & ((quarter == 1) | (quarter == 2))
+    mine = jnp.where(half_ref[1] != 0, quarter % 2, quarter // 2) == half_ref[0]
     for f in range(frames):
         value = sums[1, pl.ds(f, count, stride=frames), :]
         if f >= 1:
             value = value + pltpu.roll(sums[0, pl.ds(f - 1, count, stride=frames), :], width, 1)
         if f >= 2:
             value = value + sums[0, pl.ds(f - 2, count, stride=frames), :]
-        value = jnp.where(low, value, pltpu.roll(value, width, 1)) + bias_ref[...]
+        value = jnp.where(low, value, pltpu.roll(value, width, 1))
+        value = jnp.where(turned, pltpu.roll(value, width // 2, 1), value) + bias_ref[...]
         if with_other:
-            value = jnp.where(low == (half_ref[0] == 0), value, other_ref[f].astype(jnp.float32))
+            value = jnp.where(mine, value, other_ref[f].astype(jnp.float32))
         placed[f] = value.astype(jnp.bfloat16)
     if with_other:
         for p, out_ref in enumerate(out_refs):
@@ -363,14 +348,38 @@
     above = lax.ppermute(bottom, "rows", [(i, i + 1) for i in range(strips - 1)])
     below = lax.ppermute(top, "rows", [(i + 1, i) for i in range(strips - 1)])
 
+    if is_line:
+        chip = strip // CORES
+        at_end = ((chip == 0) | (chip == 3)).astype(jnp.int32)[None]
+        weight = after(weight, above, below)
+        one = lax.ppermute(weight, "rows", chip_pairs([(0, 2), (3, 1), (2, 3), (1, 0)]))
+
     entries = held * row_count * col_count
+    stats = merge([stats] + exchange(stats, "frames", range(1, group_count)), entries)
+    entries *= group_count
+    edges = jnp.stack([strip == 0, strip == strips - 1]).astype(jnp.int32)
+    payload = pack(edges, above, below, payload, held, row_count + 2, col_count)
+    payload = after(payload, stats)
+    if group_count == 4 and held % 2 == 0:
+        strip_pieces = [payload] + exchange(payload, "frames", [1, 2])
+        origins = [(0, 0), (1, 0), (2, 0), (3, 0), (3, held // 2)]
+        middle = payload.shape[0] // 2
+        strip_pieces += exchange(strip_pieces[1][:middle], "frames", [2])
+        strip_pieces += exchange(strip_pieces[2][middle:], "frames", [1])
+    else:
+        strip_pieces = [payload] + exchange(payload, "frames", range(1, group_count))
+        origins = [(p, 0) for p in range(group_count)]
+
     if is_line:
-        chips = range(CORES, strips, CORES)
-        stats = merge([stats] + exchange(stats, "rows", chips), entries)
-        weight = after(weight, stats, above, below)
-        first, second = exchange(weight, "rows", [CORES, 2 * CORES])
-        stats = merge([stats] + exchange(stats, "rows", [1]), 4 * entries)
+        stats = merge([stats] + exchange(stats, "rows", [1]), entries)
+        stats, one = lax.optimization_barrier((hold(stats), one))
+        stats = merge([stats] + exchange(stats, "rows", range(CORES, strips, CORES)), CORES * entries)
         entries *= strips
+        weight, one, stats = lax.optimization_barrier((weight, one, stats))
+        passed = pick(at_end, weight, one)
+        two = lax.ppermute(passed, "rows", chip_pairs([(0, 1), (3, 2), (2, 3), (1, 0)]))
+        three_middle = lax.ppermute(weight, "rows", chip_pairs([(1, 2), (2, 1)]))
+        three_ends = lax.ppermute(weight, "rows", chip_pairs([(1, 3), (2, 0)]))
     else:
         distance = 1
         while distance < strips:
@@ -378,48 +387,46 @@
             entries *= 2
             distance *= 2
 
-    if is_line:
-        weight, first, second = lax.optimization_barrier((weight, first, second))
-        second = hold(second)
-        ends = chip_pairs([(1, 0), (2, 3)])
-        middle = chip_pairs([(1, 2), (2, 1)])
-        third_ends = lax.ppermute(second, "rows", ends)
-        third_middle = lax.ppermute(weight, "rows", middle)
-
-    edges = jnp.stack([strip == 0, strip == strips - 1]).astype(jnp.int32)
-    payload = pack(edges, stats, above, below, payload, held, row_count + 2, col_count)
-    strip_pieces = [payload] + exchange(payload, "frames", range(1, group_count))
     groups = jnp.stack([group ^ d for d in range(group_count)]).astype(jnp.int32)
     affine = jnp.stack([norm_gain, norm_bias])
     if is_line:
-        near, strip_pieces, far = lax.optimization_barrier(([weight, first], strip_pieces, [second]))
+        near, strip_pieces = lax.optimization_barrier(([weight, one], strip_pieces))
     even, odd = activate(
-        groups * held, affine, strip_pieces, held, row_count + 2, col_count, entries
+        groups * held, stats, affine, strip_pieces, origins, row_count + 2, col_count, entries
     )
 
     width = channels // group_count
     bias = lax.dynamic_slice_in_dim(conv_bias, group * width, width)[None]
     if is_line:
         near += [lax.ppermute(piece, "rows", flip("rows", 1)) for piece in near]
-        slots = jnp.stack([strip, strip ^ 2, strip ^ 1, strip ^ 3]) % 4
-        half, other_half = (strip // 4)[None], 1 - (strip // 4)[None]
+        middle = (at_end == 0).astype(jnp.int32)[0]
+        chips = [chip] + [jnp.where(middle == 1, a, b) for a, b in ((chip ^ 2, chip ^ 1), (chip ^ 1, chip ^ 3), (chip ^ 3, chip ^ 2))]
+
+        def order(a, b):
+            first = (a > b).astype(jnp.int32)
+            second = 1 - first
+            core = strip % CORES
+            return jnp.stack([CORES * t + c for c in (core, 1 - core) for t in (first, second)])
+
+        def held_quarters(a, b):
+            return jnp.stack([jnp.where(middle == 1, a % 2, a // 2), middle])
+
+        slots, other_slots = order(chips[0], chips[1]), order(chips[2], chips[3])
+        half, other_half = held_quarters(chips[0], chips[1]), held_quarters(chips[2], chips[3])
     else:
         gathered = lax.all_gather(weight, "rows", axis=1, tiled=True)
         near, far = [gathered[:, : width // 2]], [gathered[:, width // 2 :]]
-        slots = jnp.zeros((1,), jnp.int32)
-        half, other_half = slots, slots + 1
+        slots = other_slots = jnp.zeros((1,), jnp.int32)
+        half, other_half = jnp.zeros((2,), jnp.int32), jnp.asarray([1, 0], jnp.int32)
     convolved = functools.partial(
-        convolve, groups * held, slots, even=even, odd=odd, bias=bias, frames=held * group_count
+        convolve, groups * held, even=even, odd=odd, bias=bias, frames=held * group_count
     )
-    done = convolved(half, pieces=near)[0]
+    done = convolved(slots, half, pieces=near)[0]
     if is_line:
-        third_ends, third_middle, done = lax.optimization_barrier((third_ends, third_middle, done))
-        chip = strip // CORES
-        at_end = ((chip == 0) | (chip == 3)).astype(jnp.int32)[None]
-        third = pick(at_end, third_ends, third_middle)
-        far.append(third)
+        two, three_ends, three_middle, done = lax.optimization_barrier((two, three_ends, three_middle, done))
+        far = [two, pick(at_end, three_ends, three_middle)]
         far += [lax.ppermute(piece, "rows", flip("rows", 1)) for piece in far]
-    parts = convolved(other_half, pieces=far, other=done)
+    parts = convolved(other_slots, other_half, pieces=far, other=done)
     parts = [parts[0]] + [
         lax.ppermute(parts[d], "frames", flip("frames", d)) for d in range(1, group_count)
     ]

time: 70.9 us -> 81.6 us (1.15)
  starting transfers between devices: 24.5 us -> 32.9 us
  waiting for transfers between devices: 29.7 us -> 26 us
  Pallas kernels: 13.8 us -> 17 us
  other arithmetic: 0.3 us -> 2.48 us
    ppermute x9 -> x11, waiting for transfers between devices: 21.8 us -> 6.13 us  [exchange(): return [lax.ppermute(block, axis, flip(axis, d)) for d in distances]]
    ppermute x2 -> x4, waiting for transfers between devices: 1.17 us -> 14.5 us  [the longest x1 10.7 us: body(): lax.ppermute(weight, 'rows', chip_pairs([(0, 2), (3, 1), (2, 3), (1, 0)]))]
    ppermute x2 -> x4, starting transfers between devices: 1.97 us -> 10.5 us  [the longest x1 5.41 us: body(): lax.ppermute(passed, 'rows', chip_pairs([(0, 1), (3, 2), (2, 3), (1, 0)]))]
    pallas_call x2, Pallas kernels: 8.29 us -> 10.3 us  [convolve(): pl.pallas_call(functools.partial(conv_kernel, len(pieces), other is not N...]
    ppermute x3, waiting for transfers between devices: 4.87 us -> 3.25 us  [body(): lax.ppermute(parts[d], 'frames', flip('frames', d))]
    pallas_call x1 -> x2, Pallas kernels: 0.03 us -> 1.21 us  [pick(): pl.pallas_call(pick_kernel, out_shape=jax.ShapeDtypeStruct(one.shape, one...]
    another operation x0 -> x4, other arithmetic: none -> 0.88 us  [the longest x2 0.73 us: held_quarters(): return jnp.stack([jnp.where(middle == 1, a % 2, a // 2), middle])]
    ppermute x9 -> x11, starting transfers between devices: 15.7 us -> 15.2 us  [exchange(): return [lax.ppermute(block, axis, flip(axis, d)) for d in distances]]
  transfers between devices with their start and end apart: 20 -> 24, of which waited for: 10 -> 10; matrix products, arithmetic and copies ran while one was open for 1% -> 3% of each run, Pallas kernels for 12% -> 12%
where the time goes in v4:
time: 81.6 us; the launch traced here: 81.2 us
  starting transfers between devices  32.9 us (40%)
  waiting for transfers between devices  26 us (32%)
  Pallas kernels  17 us (21%)
  local copies, waits for them, and re-layouts  2.66 us (3%)
  other arithmetic  2.48 us (3%)
    ppermute x11, starting transfers between devices, exchange(): return [lax.ppermute(block, axis, flip(axis, d)) for d in distances]  15.2 us
    ppermute x1, waiting for transfers between devices, body(): lax.ppermute(weight, 'rows', chip_pairs([(0, 2), (3, 1), (2, 3), (1, 0)]))  10.7 us
    pallas_call x2, Pallas kernels, convolve(): pl.pallas_call(functools.partial(conv_kernel, len(pieces), other is not N...  10.3 us
    ppermute x11, waiting for transfers between devices, exchange(): return [lax.ppermute(block, axis, flip(axis, d)) for d in distances]  6.13 us
    ppermute x1, starting transfers between devices, body(): lax.ppermute(passed, 'rows', chip_pairs([(0, 1), (3, 2), (2, 3), (1, 0)]))  5.41 us
    ppermute x1, waiting for transfers between devices, body(): lax.ppermute(passed, 'rows', chip_pairs([(0, 1), (3, 2), (2, 3), (1, 0)]))  3.84 us
    ppermute x3, starting transfers between devices, body(): lax.ppermute(parts[d], 'frames', flip('frames', d))  3.55 us
    pallas_call x1, Pallas kernels, activate(): pl.pallas_call(functools.partial(activate_kernel, origins, rows, cols, en...  3.3 us
  transfers between devices with their start and end apart: 24, of which 10 were waited for; matrix products, arithmetic and copies ran while one was open for 3% of the time, Pallas kernels for 12%

profile of v4, /device:TPU:0, one launch (start us, length us, event | category | flops | bytes accessed | tf_op | source)
XLA Modules:
  0.0 81.2 jit_solution(1096345198308097729)
XLA Ops:
  0.0 1.0 %copy-done.3 = bf16[2,4,40,512]{3,2,1,0:T(8,128)(2,1)S(1)} copy-done((bf16[2,4,40,512]{3,2,1,0:T(8,128)(2,1)S(1)}, bf16[2,4,40,512]{3,2,1,0:T(8,128)(2,1)}, u32[]{:S(2)}) %copy-start.3) | copy-done | bytes 327704
  1.2 3.0 %collective-permute-start.2 = (f32[2,512]{1,0:T(2,128)S(1)}, f32[2,512]{1,0:T(2,128)S(1)}, u32[]{:S(2)}, u32[]{:S(2)}) collective-permute-start(f32[2,512]{1,0:T(2,128)S(1)} %get-tuple-element.36), channel_id=1, source_target_pairs={{0,8},{8,0},{16,24},{24,16},{1,9},{9,1},{17,25},{25,17},{2,10},{10... | collective-permute-start | bytes 12296 | tf_op jit(solution)/shard_map/ppermute | solution.py:29
  4.2 1.5 %collective-permute-start.3 = (f32[2,512]{1,0:T(2,128)S(1)}, f32[2,512]{1,0:T(2,128)S(1)}, u32[]{:S(2)}, u32[]{:S(2)}) collective-permute-start(f32[2,512]{1,0:T(2,128)S(1)} %get-tuple-element.36), channel_id=1, source_target_pairs={{0,16},{8,24},{16,0},{24,8},{1,17},{9,25},{17,1},{25,9},{2,18},{10... | collective-permute-start | bytes 12296 | tf_op jit(solution)/shard_map/ppermute | solution.py:29
  5.7 1.3 %collective-permute-start = (bf16[2,1,40,512]{3,2,1,0:T(8,128)(2,1)S(1)}, bf16[2,1,40,512]{3,2,1,0:T(8,128)(2,1)S(1)}, u32[]{:S(2)}, u32[]{:S(2)}) collective-permute-start(bf16[2,1,40,512]{3,2,1,0:T(8,128)(2,1)S(1)} %get-tuple-element.33), channel_id=1, source_target_pairs={{0,1},{1,2},{2,3},{3,4},{4,5},{5,6},{6,7},{8,9},{9,10},{10,11},{11... | collective-permute-start | bytes 245768 | tf_op jit(solution)/shard_map/ppermute | solution.py:348
  7.0 1.3 %collective-permute-start.1 = (bf16[2,1,40,512]{3,2,1,0:T(8,128)(2,1)S(1)}, bf16[2,1,40,512]{3,2,1,0:T(8,128)(2,1)S(1)}, u32[]{:S(2)}, u32[]{:S(2)}) collective-permute-start(bf16[2,1,40,512]{3,2,1,0:T(8,128)(2,1)S(1)} %get-tuple-element.34), channel_id=1, source_target_pairs={{1,0},{2,1},{3,2},{4,3},{5,4},{6,5},{7,6},{9,8},{10,9},{11,10},{12... | collective-permute-start | bytes 245768 | tf_op jit(solution)/shard_map/ppermute | solution.py:349
  8.3 1.9 %collective-permute-done.4 = f32[2,512]{1,0:T(2,128)S(1)} collective-permute-done((f32[2,512]{1,0:T(2,128)S(1)}, f32[2,512]{1,0:T(2,128)S(1)}, u32[]{:S(2)}, u32[]{:S(2)}) %collective-permute-start.4) | collective-permute-done | bytes 4128 | tf_op jit(solution)/shard_map/ppermute | solution.py:29
  10.2 1.6 %collective-permute-start.5 = (f32[2,512]{1,0:T(2,128)S(1)}, f32[2,512]{1,0:T(2,128)S(1)}, u32[]{:S(2)}, u32[]{:S(2)}) collective-permute-start(f32[2,512]{1,0:T(2,128)S(1)} %pad_maximum_fusion), channel_id=1, source_target_pairs={{0,1},{1,0},{2,3},{3,2},{4,5},{5,4},{6,7},{7,6},{8,9},{9,8},{10,11... | collective-permute-start | bytes 12296 | tf_op jit(solution)/shard_map/ppermute | solution.py:29
  11.9 0.7 collective-permute-done.5
  13.9 1.6 %collective-permute-start.10 = (bf16[480,512]{1,0:T(8,128)(2,1)S(1)}, bf16[480,512]{1,0:T(8,128)(2,1)S(1)}, u32[]{:S(2)}, u32[]{:S(2)}) collective-permute-start(bf16[480,512]{1,0:T(8,128)(2,1)S(1)} %shard_map.57.refs_0_), channel_id=1, source_target_pairs={{0,8},{8,0},{16,24},{24,16},{1,9},{9,1},{17,25},{25,17},{2,10},{10... | collective-permute-start | bytes 1474568 | tf_op jit(solution)/shard_map/ppermute | solution.py:29
  15.5 1.5 %collective-permute-start.11 = (bf16[480,512]{1,0:T(8,128)(2,1)S(1)}, bf16[480,512]{1,0:T(8,128)(2,1)S(1)}, u32[]{:S(2)}, u32[]{:S(2)}) collective-permute-start(bf16[480,512]{1,0:T(8,128)(2,1)S(1)} %shard_map.57.refs_0_), channel_id=1, source_target_pairs={{0,16},{8,24},{16,0},{24,8},{1,17},{9,25},{17,1},{25,9},{2,18},{10... | collective-permute-start | bytes 1474568 | tf_op jit(solution)/shard_map/ppermute | solution.py:29
  17.0 3.1 %collective-permute-start.6 = (bf16[27,16,512]{2,1,0:T(8,128)(2,1)}, bf16[27,16,512]{2,1,0:T(8,128)(2,1)}, u32[]{:S(2)}, u32[]{:S(2)}) collective-permute-start(bf16[27,16,512]{2,1,0:T(8,128)(2,1)} %bitcast.12.one_ref.refs_0_), channel_id=1, source_target_pairs={{0,4},{1,5},{6,2},{7,3},{4,6},{5,7},{2,0},{3,1},{8,12},{9,13},{14,... | collective-permute-start | bytes 1327112 | tf_op jit(solution)/shard_map/ppermute | solution.py:355
  20.0 10.7 %collective-permute-done.6.other_ref.refs_1_ = bf16[27,16,512]{2,1,0:T(8,128)(2,1)} collective-permute-done((bf16[27,16,512]{2,1,0:T(8,128)(2,1)}, bf16[27,16,512]{2,1,0:T(8,128)(2,1)}, u32[]{:S(2)}, u32[]{:S(2)}) %collective-permute-start.6) | collective-permute-done | bytes 442400 | tf_op jit(solution)/shard_map/ppermute | solution.py:355
  30.7 2.4 %collective-permute-start.7 = (f32[2,512]{1,0:T(2,128)}, f32[2,512]{1,0:T(2,128)S(1)}, u32[]{:S(2)}, u32[]{:S(2)}) collective-permute-start(f32[2,512]{1,0:T(2,128)} %shard_map.56), channel_id=1, source_target_pairs={{0,2},{1,3},{2,0},{3,1},{4,6},{5,7},{6,4},{7,5},{8,10},{9,11},{10,... | collective-permute-start | bytes 12296 | tf_op jit(solution)/shard_map/ppermute | solution.py:29
  33.1 1.0 %collective-permute-start.8 = (f32[2,512]{1,0:T(2,128)}, f32[2,512]{1,0:T(2,128)S(1)}, u32[]{:S(2)}, u32[]{:S(2)}) collective-permute-start(f32[2,512]{1,0:T(2,128)} %shard_map.56), channel_id=1, source_target_pairs={{0,4},{1,5},{2,6},{3,7},{4,0},{5,1},{6,2},{7,3},{8,12},{9,13},{10,... | collective-permute-start | bytes 12296 | tf_op jit(solution)/shard_map/ppermute | solution.py:29
  34.1 1.5 %collective-permute-start.9 = (f32[2,512]{1,0:T(2,128)}, f32[2,512]{1,0:T(2,128)S(1)}, u32[]{:S(2)}, u32[]{:S(2)}) collective-permute-start(f32[2,512]{1,0:T(2,128)} %shard_map.56), channel_id=1, source_target_pairs={{0,6},{1,7},{2,4},{3,5},{4,2},{5,3},{6,0},{7,1},{8,14},{9,15},{10,... | collective-permute-start | bytes 12296 | tf_op jit(solution)/shard_map/ppermute | solution.py:29
  36.2 1.6 %collective-permute-done.8 = f32[2,512]{1,0:T(2,128)S(1)} collective-permute-done((f32[2,512]{1,0:T(2,128)}, f32[2,512]{1,0:T(2,128)S(1)}, u32[]{:S(2)}, u32[]{:S(2)}) %collective-permute-start.8) | collective-permute-done | bytes 4128 | tf_op jit(solution)/shard_map/ppermute | solution.py:29
  37.8 1.9 %collective-permute-done.9 = f32[2,512]{1,0:T(2,128)S(1)} collective-permute-done((f32[2,512]{1,0:T(2,128)}, f32[2,512]{1,0:T(2,128)S(1)}, u32[]{:S(2)}, u32[]{:S(2)}) %collective-permute-start.9) | collective-permute-done | bytes 4128 | tf_op jit(solution)/shard_map/ppermute | solution.py:29
  39.7 0.8 fusion
  40.5 1.3 %collective-permute-start.15 = (bf16[27,16,512]{2,1,0:T(8,128)(2,1)}, bf16[27,16,512]{2,1,0:T(8,128)(2,1)S(1)}, u32[]{:S(2)}, u32[]{:S(2)}) collective-permute-start(bf16[27,16,512]{2,1,0:T(8,128)(2,1)} %bitcast.12.one_ref.refs_0_), channel_id=1, source_target_pairs={{2,6},{3,7},{4,0},{5,1},{10,14},{11,15},{12,8},{13,9},{18,22},{19,... | collective-permute-start | bytes 1327112 | tf_op jit(solution)/shard_map/ppermute | solution.py:382
  43.8 1.2 %shard_map.59 = bf16[27,16,512]{2,1,0:T(8,128)(2,1)S(1)} custom-call(s32[1]{0:T(128)} %bitcast.4.which_ref, bf16[27,16,512]{2,1,0:T(8,128)(2,1)} %bitcast.12.one_ref.refs_0_, bf16[27,16,512]{2,1,0:T(8,128)(2,1)} %collective-permute-done.6.other_ref.refs_1_), custom_call_target="tpu_custom_call" | custom-call | flops 10000000000 | bytes 221184 | tf_op jit(solution)/shard_map/pallas_call | solution.py:143
  45.0 5.4 %collective-permute-start.14 = (bf16[27,16,512]{2,1,0:T(8,128)(2,1)S(1)}, bf16[27,16,512]{2,1,0:T(8,128)(2,1)}, u32[]{:S(2)}, u32[]{:S(2)}) collective-permute-start(bf16[27,16,512]{2,1,0:T(8,128)(2,1)S(1)} %shard_map.59), channel_id=1, source_target_pairs={{0,2},{1,3},{6,4},{7,5},{4,6},{5,7},{2,0},{3,1},{8,10},{9,11},{14,... | collective-permute-start | bytes 1327112 | tf_op jit(solution)/shard_map/ppermute | solution.py:380
  51.1 3.3 %shard_map.58 = (bf16[6,336,512]{2,1,0:T(8,128)(2,1)S(1)}, bf16[6,320,512]{2,1,0:T(8,128)(2,1)S(1)}) custom-call(s32[4]{0:T(128)S(1)} %get-tuple-element.65.place_ref, f32[2,512]{1,0:T(2,128)S(1)} %pad_maximum_fusion.2.stats_ref, f32[2,512]{1,0:T(2,128)S(1)} %pad_maximum_fusion.3.affine_ref, bf16[480,512]{1,0:T(8,128)(2,1)S(1)} %shard_map.57.refs_0_, ...), custom_call_target="tpu_custom_call" | custom-call | flops 9830400 | bytes 5898240 | tf_op jit(solution)/shard_map/pallas_call | solution.py:209
  54.5 5.5 %shard_map.60.refs_4_ = bf16[8,160,128]{2,1,0:T(8,128)(2,1)S(1)} custom-call(s32[4]{0:T(128)S(1)} %get-tuple-element.65.place_ref, s32[4]{0:T(128)S(1)} %pad_add_fusion.3.slot_ref, s32[2]{0:T(128)S(1)} %copy-done.4, bf16[6,336,512]{2,1,0:T(8,128)(2,1)S(1)} %get-tuple-element.49.even_ref, bf16[6,320,512]{2,1,0:T(8,128)(2,1)S(1)} %get-tuple-element.50.odd_ref, ...), custom_call_target="tpu_custom_call" | custom-call | flops 83886080 | bytes 65536 | tf_op jit(solution)/shard_map/pallas_call | solution.py:299
  60.0 3.8 %collective-permute-done.14.refs_0_ = bf16[27,16,512]{2,1,0:T(8,128)(2,1)} collective-permute-done((bf16[27,16,512]{2,1,0:T(8,128)(2,1)S(1)}, bf16[27,16,512]{2,1,0:T(8,128)(2,1)}, u32[]{:S(2)}, u32[]{:S(2)}) %collective-permute-start.14) | collective-permute-done | bytes 442400 | tf_op jit(solution)/shard_map/ppermute | solution.py:380
  64.6 1.1 %collective-permute-done.20.refs_3_ = bf16[27,16,512]{2,1,0:T(8,128)(2,1)S(1)} collective-permute-done((bf16[27,16,512]{2,1,0:T(8,128)(2,1)S(1)}, bf16[27,16,512]{2,1,0:T(8,128)(2,1)S(1)}, u32[]{:S(2)}, u32[]{:S(2)}) %collective-permute-start.20) | collective-permute-done | bytes 442400 | tf_op jit(solution)/shard_map/ppermute | solution.py:428
  65.8 1.0 %collective-permute-done.19.refs_2_ = bf16[27,16,512]{2,1,0:T(8,128)(2,1)} collective-permute-done((bf16[27,16,512]{2,1,0:T(8,128)(2,1)}, bf16[27,16,512]{2,1,0:T(8,128)(2,1)}, u32[]{:S(2)}, u32[]{:S(2)}) %collective-permute-start.19) | collective-permute-done | bytes 442400 | tf_op jit(solution)/shard_map/ppermute | solution.py:428
  66.7 1.5 %copy-done.2 = bf16[6,320,512]{2,1,0:T(8,128)(2,1)S(1)} copy-done((bf16[6,320,512]{2,1,0:T(8,128)(2,1)S(1)}, bf16[6,320,512]{2,1,0:T(8,128)(2,1)}, u32[]{:S(2)}) %copy-start.2) | copy-done | bytes 1966104
  68.3 4.8 %shard_map.62 = (bf16[2,160,128]{2,1,0:T(8,128)(2,1)S(1)}, bf16[2,160,128]{2,1,0:T(8,128)(2,1)S(1)}, bf16[2,160,128]{2,1,0:T(8,128)(2,1)S(1)}, bf16[2,160,128]{2,1,0:T(8,128)(2,1)S(1)}) custom-call(s32[4]{0:T(128)S(1)} %get-tuple-element.65.place_ref, s32[4]{0:T(128)S(1)} %pad_add_fusion.1.slot_ref, s32[2]{0:T(128)S(1)} %pad_add_fusion.2.half_ref, ...), custom_call_target="tpu_custom_call" | custom-call | flops 83886080 | bytes 65536 | tf_op jit(solution)/shard_map/pallas_call | solution.py:299
  74.2 2.4 %collective-permute-start.23 = (bf16[2,160,128]{2,1,0:T(8,128)(2,1)S(1)}, bf16[2,160,128]{2,1,0:T(8,128)(2,1)S(1)}, u32[]{:S(2)}, u32[]{:S(2)}) collective-permute-start(bf16[2,160,128]{2,1,0:T(8,128)(2,1)S(1)} %get-tuple-element.60), channel_id=1, source_target_pairs={{0,24},{8,16},{16,8},{24,0},{1,25},{9,17},{17,9},{25,1},{2,26},{10... | collective-permute-start | bytes 245768 | tf_op jit(solution)/shard_map/ppermute | solution.py:431
  76.7 1.4 %collective-permute-done.21.refs_1_ = bf16[2,160,128]{2,1,0:T(8,128)(2,1)S(1)} collective-permute-done((bf16[2,160,128]{2,1,0:T(8,128)(2,1)S(1)}, bf16[2,160,128]{2,1,0:T(8,128)(2,1)S(1)}, u32[]{:S(2)}, u32[]{:S(2)}) %collective-permute-start.21) | collective-permute-done | bytes 81952 | tf_op jit(solution)/shard_map/ppermute | solution.py:431
  78.0 1.9 %collective-permute-done.22.refs_2_ = bf16[2,160,128]{2,1,0:T(8,128)(2,1)S(1)} collective-permute-done((bf16[2,160,128]{2,1,0:T(8,128)(2,1)S(1)}, bf16[2,160,128]{2,1,0:T(8,128)(2,1)S(1)}, u32[]{:S(2)}, u32[]{:S(2)}) %collective-permute-start.22) | collective-permute-done | bytes 81952 | tf_op jit(solution)/shard_map/ppermute | solution.py:431
  79.9 1.3 %shard_map.63 = bf16[2,160,512]{2,1,0:T(8,128)(2,1)} custom-call(s32[4]{0:T(128)S(1)} %get-tuple-element.66.place_ref, bf16[2,160,128]{2,1,0:T(8,128)(2,1)S(1)} %get-tuple-element.57.refs_0_, bf16[2,160,128]{2,1,0:T(8,128)(2,1)S(1)} %collective-permute-done.21.refs_1_, bf16[2,160,128]{2,1,0:T(8,128)(2,1)S(1)} %collective-permute-done.22.refs_2_, ...), custom_call_target="tpu_custom_call" | custom-call | tf_op jit(solution)/shard_map/pallas_call | solution.py:328
  (55 shorter events, 6.8 us)
Async XLA Ops:
  0.0 50.9 %copy-start = (f32[512]{0:T(512)S(1)}, f32[512]{0:T(512)}, u32[]{:S(2)}) copy-start(f32[512]{0:T(512)} %param.9) | copy-start | bytes 6148
  0.0 1.0 %copy-start.3 = (bf16[2,4,40,512]{3,2,1,0:T(8,128)(2,1)S(1)}, bf16[2,4,40,512]{3,2,1,0:T(8,128)(2,1)}, u32[]{:S(2)}) copy-start(bf16[2,4,40,512]{3,2,1,0:T(8,128)(2,1)} %x_ref.1) | copy-start | bytes 983044
  1.2 7.1 %collective-permute-start.2 = (f32[2,512]{1,0:T(2,128)S(1)}, f32[2,512]{1,0:T(2,128)S(1)}, u32[]{:S(2)}, u32[]{:S(2)}) collective-permute-start(f32[2,512]{1,0:T(2,128)S(1)} %get-tuple-element.36), channel_id=1, source_target_pairs={{0,8},{8,0},{16,24},{24,16},{1,9},{9,1},{17,25},{25,17},{2,10},{10... | collective-permute-start | bytes 12296 | tf_op jit(solution)/shard_map/ppermute | solution.py:29
  4.2 4.2 %collective-permute-start.3 = (f32[2,512]{1,0:T(2,128)S(1)}, f32[2,512]{1,0:T(2,128)S(1)}, u32[]{:S(2)}, u32[]{:S(2)}) collective-permute-start(f32[2,512]{1,0:T(2,128)S(1)} %get-tuple-element.36), channel_id=1, source_target_pairs={{0,16},{8,24},{16,0},{24,8},{1,17},{9,25},{17,1},{25,9},{2,18},{10... | collective-permute-start | bytes 12296 | tf_op jit(solution)/shard_map/ppermute | solution.py:29
  5.7 4.5 %collective-permute-start.4 = (f32[2,512]{1,0:T(2,128)S(1)}, f32[2,512]{1,0:T(2,128)S(1)}, u32[]{:S(2)}, u32[]{:S(2)}) collective-permute-start(f32[2,512]{1,0:T(2,128)S(1)} %get-tuple-element.36), channel_id=1, source_target_pairs={{0,24},{8,16},{16,8},{24,0},{1,25},{9,17},{17,9},{25,1},{2,26},{10... | collective-permute-start | bytes 12296 | tf_op jit(solution)/shard_map/ppermute | solution.py:29
  5.7 7.6 %collective-permute-start = (bf16[2,1,40,512]{3,2,1,0:T(8,128)(2,1)S(1)}, bf16[2,1,40,512]{3,2,1,0:T(8,128)(2,1)S(1)}, u32[]{:S(2)}, u32[]{:S(2)}) collective-permute-start(bf16[2,1,40,512]{3,2,1,0:T(8,128)(2,1)S(1)} %get-tuple-element.33), channel_id=1, source_target_pairs={{0,1},{1,2},{2,3},{3,4},{4,5},{5,6},{6,7},{8,9},{9,10},{10,11},{11... | collective-permute-start | bytes 245768 | tf_op jit(solution)/shard_map/ppermute | solution.py:348
  7.0 6.3 %collective-permute-start.1 = (bf16[2,1,40,512]{3,2,1,0:T(8,128)(2,1)S(1)}, bf16[2,1,40,512]{3,2,1,0:T(8,128)(2,1)S(1)}, u32[]{:S(2)}, u32[]{:S(2)}) collective-permute-start(bf16[2,1,40,512]{3,2,1,0:T(8,128)(2,1)S(1)} %get-tuple-element.34), channel_id=1, source_target_pairs={{1,0},{2,1},{3,2},{4,3},{5,4},{6,5},{7,6},{9,8},{10,9},{11,10},{12... | collective-permute-start | bytes 245768 | tf_op jit(solution)/shard_map/ppermute | solution.py:349
  10.2 2.4 %collective-permute-start.5 = (f32[2,512]{1,0:T(2,128)S(1)}, f32[2,512]{1,0:T(2,128)S(1)}, u32[]{:S(2)}, u32[]{:S(2)}) collective-permute-start(f32[2,512]{1,0:T(2,128)S(1)} %pad_maximum_fusion), channel_id=1, source_target_pairs={{0,1},{1,0},{2,3},{3,2},{4,5},{5,4},{6,7},{7,6},{8,9},{9,8},{10,11... | collective-permute-start | bytes 12296 | tf_op jit(solution)/shard_map/ppermute | solution.py:29
  13.9 28.6 %collective-permute-start.10 = (bf16[480,512]{1,0:T(8,128)(2,1)S(1)}, bf16[480,512]{1,0:T(8,128)(2,1)S(1)}, u32[]{:S(2)}, u32[]{:S(2)}) collective-permute-start(bf16[480,512]{1,0:T(8,128)(2,1)S(1)} %shard_map.57.refs_0_), channel_id=1, source_target_pairs={{0,8},{8,0},{16,24},{24,16},{1,9},{9,1},{17,25},{25,17},{2,10},{10... | collective-permute-start | bytes 1474568 | tf_op jit(solution)/shard_map/ppermute | solution.py:29
  15.5 27.6 %collective-permute-start.11 = (bf16[480,512]{1,0:T(8,128)(2,1)S(1)}, bf16[480,512]{1,0:T(8,128)(2,1)S(1)}, u32[]{:S(2)}, u32[]{:S(2)}) collective-permute-start(bf16[480,512]{1,0:T(8,128)(2,1)S(1)} %shard_map.57.refs_0_), channel_id=1, source_target_pairs={{0,16},{8,24},{16,0},{24,8},{1,17},{9,25},{17,1},{25,9},{2,18},{10... | collective-permute-start | bytes 1474568 | tf_op jit(solution)/shard_map/ppermute | solution.py:29
  17.0 13.7 %collective-permute-start.6 = (bf16[27,16,512]{2,1,0:T(8,128)(2,1)}, bf16[27,16,512]{2,1,0:T(8,128)(2,1)}, u32[]{:S(2)}, u32[]{:S(2)}) collective-permute-start(bf16[27,16,512]{2,1,0:T(8,128)(2,1)} %bitcast.12.one_ref.refs_0_), channel_id=1, source_target_pairs={{0,4},{1,5},{6,2},{7,3},{4,6},{5,7},{2,0},{3,1},{8,12},{9,13},{14,... | collective-permute-start | bytes 1327112 | tf_op jit(solution)/shard_map/ppermute | solution.py:355
  30.7 5.5 %collective-permute-start.7 = (f32[2,512]{1,0:T(2,128)}, f32[2,512]{1,0:T(2,128)S(1)}, u32[]{:S(2)}, u32[]{:S(2)}) collective-permute-start(f32[2,512]{1,0:T(2,128)} %shard_map.56), channel_id=1, source_target_pairs={{0,2},{1,3},{2,0},{3,1},{4,6},{5,7},{6,4},{7,5},{8,10},{9,11},{10,... | collective-permute-start | bytes 12296 | tf_op jit(solution)/shard_map/ppermute | solution.py:29
  33.1 4.7 %collective-permute-start.8 = (f32[2,512]{1,0:T(2,128)}, f32[2,512]{1,0:T(2,128)S(1)}, u32[]{:S(2)}, u32[]{:S(2)}) collective-permute-start(f32[2,512]{1,0:T(2,128)} %shard_map.56), channel_id=1, source_target_pairs={{0,4},{1,5},{2,6},{3,7},{4,0},{5,1},{6,2},{7,3},{8,12},{9,13},{10,... | collective-permute-start | bytes 12296 | tf_op jit(solution)/shard_map/ppermute | solution.py:29
  34.1 5.6 %collective-permute-start.9 = (f32[2,512]{1,0:T(2,128)}, f32[2,512]{1,0:T(2,128)S(1)}, u32[]{:S(2)}, u32[]{:S(2)}) collective-permute-start(f32[2,512]{1,0:T(2,128)} %shard_map.56), channel_id=1, source_target_pairs={{0,6},{1,7},{2,4},{3,5},{4,2},{5,3},{6,0},{7,1},{8,14},{9,15},{10,... | collective-permute-start | bytes 12296 | tf_op jit(solution)/shard_map/ppermute | solution.py:29
  40.5 23.4 %collective-permute-start.15 = (bf16[27,16,512]{2,1,0:T(8,128)(2,1)}, bf16[27,16,512]{2,1,0:T(8,128)(2,1)S(1)}, u32[]{:S(2)}, u32[]{:S(2)}) collective-permute-start(bf16[27,16,512]{2,1,0:T(8,128)(2,1)} %bitcast.12.one_ref.refs_0_), channel_id=1, source_target_pairs={{2,6},{3,7},{4,0},{5,1},{10,14},{11,15},{12,8},{13,9},{18,22},{19,... | collective-permute-start | bytes 1327112 | tf_op jit(solution)/shard_map/ppermute | solution.py:382
  41.8 22.1 %collective-permute-start.16 = (bf16[27,16,512]{2,1,0:T(8,128)(2,1)}, bf16[27,16,512]{2,1,0:T(8,128)(2,1)S(1)}, u32[]{:S(2)}, u32[]{:S(2)}) collective-permute-start(bf16[27,16,512]{2,1,0:T(8,128)(2,1)} %bitcast.12.one_ref.refs_0_), channel_id=1, source_target_pairs={{2,4},{3,5},{4,2},{5,3},{10,12},{11,13},{12,10},{13,11},{18,20},{1... | collective-permute-start | bytes 1327112 | tf_op jit(solution)/shard_map/ppermute | solution.py:381
  42.5 7.8 %collective-permute-start.12 = (bf16[240,512]{1,0:T(8,128)(2,1)S(1)}, bf16[240,512]{1,0:T(8,128)(2,1)S(1)}, u32[]{:S(2)}, u32[]{:S(2)}) collective-permute-start(bf16[240,512]{1,0:T(8,128)(2,1)S(1)} %slice.103), channel_id=1, source_target_pairs={{0,16},{8,24},{16,0},{24,8},{1,17},{9,25},{17,1},{25,9},{2,18},{10... | collective-permute-start | bytes 737288 | tf_op jit(solution)/shard_map/ppermute | solution.py:29
  43.1 8.0 %copy-start.5 = (f32[512]{0:T(512)S(1)}, f32[512]{0:T(512)}, u32[]{:S(2)}) copy-start(f32[512]{0:T(512)} %param.7) | copy-start | bytes 6148
  43.1 8.0 %copy-start.6 = (f32[512]{0:T(512)S(1)}, f32[512]{0:T(512)}, u32[]{:S(2)}) copy-start(f32[512]{0:T(512)} %param.6) | copy-start | bytes 6148
  43.2 11.3 %copy-start.4 = (s32[2]{0:T(128)S(1)}, s32[2]{0:T(128)}, u32[]{:S(2)}) copy-start(s32[2]{0:T(128)} %pad_add_fusion.4.half_ref) | copy-start | bytes 28
  43.2 7.2 %collective-permute-start.13 = (bf16[240,512]{1,0:T(8,128)(2,1)S(1)}, bf16[240,512]{1,0:T(8,128)(2,1)S(1)}, u32[]{:S(2)}, u32[]{:S(2)}) collective-permute-start(bf16[240,512]{1,0:T(8,128)(2,1)S(1)} %slice.104), channel_id=1, source_target_pairs={{0,8},{8,0},{16,24},{24,16},{1,9},{9,1},{17,25},{25,17},{2,10},{10... | collective-permute-start | bytes 737288 | tf_op jit(solution)/shard_map/ppermute | solution.py:29
  45.0 18.9 %collective-permute-start.14 = (bf16[27,16,512]{2,1,0:T(8,128)(2,1)S(1)}, bf16[27,16,512]{2,1,0:T(8,128)(2,1)}, u32[]{:S(2)}, u32[]{:S(2)}) collective-permute-start(bf16[27,16,512]{2,1,0:T(8,128)(2,1)S(1)} %shard_map.59), channel_id=1, source_target_pairs={{0,2},{1,3},{6,4},{7,5},{4,6},{5,7},{2,0},{3,1},{8,10},{9,11},{14,... | collective-permute-start | bytes 1327112 | tf_op jit(solution)/shard_map/ppermute | solution.py:380
  50.4 4.1 %collective-permute-start.17 = (bf16[27,16,512]{2,1,0:T(8,128)(2,1)}, bf16[27,16,512]{2,1,0:T(8,128)(2,1)S(1)}, u32[]{:S(2)}, u32[]{:S(2)}) collective-permute-start(bf16[27,16,512]{2,1,0:T(8,128)(2,1)} %bitcast.12.one_ref.refs_0_), channel_id=1, source_target_pairs={{0,1},{1,0},{2,3},{3,2},{4,5},{5,4},{6,7},{7,6},{8,9},{9,8},{10,11... | collective-permute-start | bytes 1327112 | tf_op jit(solution)/shard_map/ppermute | solution.py:401
  50.4 4.1 %collective-permute-start.18 = (bf16[27,16,512]{2,1,0:T(8,128)(2,1)}, bf16[27,16,512]{2,1,0:T(8,128)(2,1)S(1)}, u32[]{:S(2)}, u32[]{:S(2)}) collective-permute-start(bf16[27,16,512]{2,1,0:T(8,128)(2,1)} %collective-permute-done.6.other_ref.refs_1_), channel_id=1, source_target_pairs={{0,1},{1,0},{2,3},{3,2},{4,5},{5,4},{6,7},{7,6},{8,9},{9,8},{10,11... | collective-permute-start | bytes 1327112 | tf_op jit(solution)/shard_map/ppermute | solution.py:401
  54.4 5.6 %copy-start.1 = (bf16[6,320,512]{2,1,0:T(8,128)(2,1)}, bf16[6,320,512]{2,1,0:T(8,128)(2,1)S(1)}, u32[]{:S(2)}) copy-start(bf16[6,320,512]{2,1,0:T(8,128)(2,1)S(1)} %get-tuple-element.50.odd_ref) | copy-start | bytes 5898244
  63.9 1.9 %collective-permute-start.20 = (bf16[27,16,512]{2,1,0:T(8,128)(2,1)S(1)}, bf16[27,16,512]{2,1,0:T(8,128)(2,1)S(1)}, u32[]{:S(2)}, u32[]{:S(2)}) collective-permute-start(bf16[27,16,512]{2,1,0:T(8,128)(2,1)S(1)} %shard_map.61.refs_1_), channel_id=1, source_target_pairs={{0,1},{1,0},{2,3},{3,2},{4,5},{5,4},{6,7},{7,6},{8,9},{9,8},{10,11... | collective-permute-start | bytes 1327112 | tf_op jit(solution)/shard_map/ppermute | solution.py:428
  64.0 2.8 %collective-permute-start.19 = (bf16[27,16,512]{2,1,0:T(8,128)(2,1)}, bf16[27,16,512]{2,1,0:T(8,128)(2,1)}, u32[]{:S(2)}, u32[]{:S(2)}) collective-permute-start(bf16[27,16,512]{2,1,0:T(8,128)(2,1)} %collective-permute-done.14.refs_0_), channel_id=1, source_target_pairs={{0,1},{1,0},{2,3},{3,2},{4,5},{5,4},{6,7},{7,6},{8,9},{9,8},{10,11... | collective-permute-start | bytes 1327112 | tf_op jit(solution)/shard_map/ppermute | solution.py:428
  66.7 1.5 %copy-start.2 = (bf16[6,320,512]{2,1,0:T(8,128)(2,1)S(1)}, bf16[6,320,512]{2,1,0:T(8,128)(2,1)}, u32[]{:S(2)}) copy-start(bf16[6,320,512]{2,1,0:T(8,128)(2,1)} %copy-done.1) | copy-start | bytes 5898244
  73.1 4.9 %collective-permute-start.21 = (bf16[2,160,128]{2,1,0:T(8,128)(2,1)S(1)}, bf16[2,160,128]{2,1,0:T(8,128)(2,1)S(1)}, u32[]{:S(2)}, u32[]{:S(2)}) collective-permute-start(bf16[2,160,128]{2,1,0:T(8,128)(2,1)S(1)} %get-tuple-element.58), channel_id=1, source_target_pairs={{0,8},{8,0},{16,24},{24,16},{1,9},{9,1},{17,25},{25,17},{2,10},{10... | collective-permute-start | bytes 245768 | tf_op jit(solution)/shard_map/ppermute | solution.py:431
  73.7 6.2 %collective-permute-start.22 = (bf16[2,160,128]{2,1,0:T(8,128)(2,1)S(1)}, bf16[2,160,128]{2,1,0:T(8,128)(2,1)S(1)}, u32[]{:S(2)}, u32[]{:S(2)}) collective-permute-start(bf16[2,160,128]{2,1,0:T(8,128)(2,1)S(1)} %get-tuple-element.59), channel_id=1, source_target_pairs={{0,16},{8,24},{16,0},{24,8},{1,17},{9,25},{17,1},{25,9},{2,18},{10... | collective-permute-start | bytes 245768 | tf_op jit(solution)/shard_map/ppermute | solution.py:431
  74.2 5.7 %collective-permute-start.23 = (bf16[2,160,128]{2,1,0:T(8,128)(2,1)S(1)}, bf16[2,160,128]{2,1,0:T(8,128)(2,1)S(1)}, u32[]{:S(2)}, u32[]{:S(2)}) collective-permute-start(bf16[2,160,128]{2,1,0:T(8,128)(2,1)S(1)} %get-tuple-element.60), channel_id=1, source_target_pairs={{0,24},{8,16},{16,8},{24,0},{1,25},{9,17},{17,9},{25,1},{2,26},{10... | collective-permute-start | bytes 245768 | tf_op jit(solution)/shard_map/ppermute | solution.py:431

commit v5 on v3

--- a/solution.py
+++ b/solution.py
@@ -157,7 +157,7 @@
         in_specs=[scalars] + [whole] * 2,
         out_specs=whole,
         compiler_params=params(8),
-        cost_estimate=pl.CostEstimate(flops=10**10, bytes_accessed=one.size, transcendentals=0),
+        cost_estimate=pl.CostEstimate(flops=0, bytes_accessed=one.size, transcendentals=0),
     )(which, one, other)
 
 
@@ -172,22 +172,22 @@
     return x
 
 
-def activate_kernel(held, rows, entries, place_ref, affine_ref, *refs):
+def activate_kernel(origins, rows, cols, entries, place_ref, affine_ref, *refs):
     *piece_refs, even_ref, odd_ref, scratch, norm = refs
     channels = piece_refs[0].shape[1]
-    frames = held * len(piece_refs)
-    cols = odd_ref.shape[1] // frames
-    tail = held * rows * cols
+    frames = odd_ref.shape[1] // cols
     size = channels // GROUPS
+    tails = [ref for (_, shift), ref in zip(origins, piece_refs) if ref.shape[0] % (rows * cols) != 0]
 
     def norms(lanes):
         means, squares = [], []
-        for piece_ref in piece_refs:
-            terms = piece_ref[tail : tail + 16, lanes].astype(jnp.float32)
+        for piece_ref in tails:
+            count = piece_ref.shape[0]
+            terms = piece_ref[count - 16 : count, lanes].astype(jnp.float32)
             both = terms[0:2] + terms[2:4] + terms[4:6]
             means.append(both[0:1])
             squares.append(both[1:2])
-        count = len(piece_refs) * size
+        count = len(tails) * size
         mean = lane_group_sum(jnp.broadcast_to(sum(means), (8, LANES)), size) / count
         spread = sum(squares) + entries * sum((m - mean[0:1]) ** 2 for m in means)
         var = lane_group_sum(jnp.broadcast_to(spread, (8, LANES)), size) / (count * entries)
@@ -204,14 +204,14 @@
         pair, block = index // blocks, index % blocks
         lanes = pl.ds(pl.multiple_of(block * LANES, LANES), LANES)
         mean, scale, bias = norm[0:1, lanes], norm[1:2, lanes], norm[2:3, lanes]
-        for p, piece_ref in enumerate(piece_refs):
-            for f in range(held):
+        for (p, shift), piece_ref in zip(origins, piece_refs):
+            for f in range(piece_ref.shape[0] // (rows * cols)):
                 start = pl.multiple_of((f * rows + 2 * pair) * cols, 16)
                 x = piece_ref[pl.ds(start, 2 * cols), lanes].astype(jnp.float32)
                 h = 0.5 * ((x - mean) * scale + bias)
                 h = h + h * jnp.tanh(h)
                 for r in range(2):
-                    scratch[r, pl.ds(frames + place_ref[p] + f, cols, stride=frames), :] = h[r * cols : (r + 1) * cols]
+                    scratch[r, pl.ds(frames + place_ref[p] + shift + f, cols, stride=frames), :] = h[r * cols : (r + 1) * cols]
         for r in range(2):
             scratch[r, 0:frames, :] = scratch[r, 2 * frames : 3 * frames, :]
             scratch[r, last : last + frames, :] = scratch[r, last - 2 * frames : last - frames, :]
@@ -222,11 +222,11 @@
     lax.fori_loop(0, rows // 2 * blocks, step, 0)
 
 
-def activate(places, affine, pieces, held, rows, cols, entries):
+def activate(places, affine, pieces, origins, rows, cols, entries):
     channels = pieces[0].shape[1]
-    frames = held * len(pieces)
-    return pl.pallas_call(
-        functools.partial(activate_kernel, held, rows, entries),
+    frames = sum(piece.shape[0] // (rows * cols) for piece in pieces)
+    return pl.pallas_call(
+        functools.partial(activate_kernel, origins, rows, cols, entries),
         out_shape=(
             jax.ShapeDtypeStruct((rows, (cols + 2) * frames, channels), jnp.bfloat16),
             jax.ShapeDtypeStruct((rows, cols * frames, channels), jnp.bfloat16),
@@ -239,9 +239,7 @@
         ],
         compiler_params=params(24),
         cost_estimate=pl.CostEstimate(
-            flops=10 * frames * rows * cols * channels,
-            bytes_accessed=6 * frames * rows * cols * channels,
-            transcendentals=frames * rows * cols * channels,
+            flops=channels, bytes_accessed=channels, transcendentals=0
         ),
     )(places, affine, *pieces)
 
@@ -323,9 +321,7 @@
         ],
         compiler_params=params(32),
         cost_estimate=pl.CostEstimate(
-            flops=2 * rows * per_row * channels * width,
-            bytes_accessed=2 * channels * width,
-            transcendentals=0,
+            flops=channels, bytes_accessed=channels, transcendentals=0
         ),
     )(places, slots, half, even, odd, bias, *pieces, *others)
 
@@ -365,10 +361,11 @@
 
     entries = held * row_count * col_count
     if is_line:
-        chips = range(CORES, strips, CORES)
-        stats = merge([stats] + exchange(stats, "rows", chips), entries)
+        chip = strip // CORES
+        at_end = ((chip == 0) | (chip == 3)).astype(jnp.int32)[None]
+        stats = merge([stats] + exchange(stats, "rows", range(CORES, strips, CORES)), entries)
         weight = after(weight, stats, above, below)
-        first, second = exchange(weight, "rows", [CORES, 2 * CORES])
+        one = lax.ppermute(weight, "rows", chip_pairs([(0, 2), (3, 1), (2, 3), (1, 0)]))
         stats = merge([stats] + exchange(stats, "rows", [1]), 4 * entries)
         entries *= strips
     else:
@@ -378,23 +375,32 @@
             entries *= 2
             distance *= 2
 
-    if is_line:
-        weight, first, second = lax.optimization_barrier((weight, first, second))
-        second = hold(second)
-        ends = chip_pairs([(1, 0), (2, 3)])
-        middle = chip_pairs([(1, 2), (2, 1)])
-        third_ends = lax.ppermute(second, "rows", ends)
-        third_middle = lax.ppermute(weight, "rows", middle)
-
     edges = jnp.stack([strip == 0, strip == strips - 1]).astype(jnp.int32)
     payload = pack(edges, stats, above, below, payload, held, row_count + 2, col_count)
-    strip_pieces = [payload] + exchange(payload, "frames", range(1, group_count))
+    if group_count == 4 and held % 2 == 0:
+        strip_pieces = [payload] + exchange(payload, "frames", [1, 2])
+        origins = [(0, 0), (1, 0), (2, 0), (3, 0), (3, held // 2)]
+        middle = (payload.shape[0] - 16) // 2
+        strip_pieces += exchange(strip_pieces[1][:middle], "frames", [2])
+        strip_pieces += exchange(strip_pieces[2][middle:], "frames", [1])
+    else:
+        strip_pieces = [payload] + exchange(payload, "frames", range(1, group_count))
+        origins = [(p, 0) for p in range(group_count)]
+
+    if is_line:
+        weight, one = lax.optimization_barrier((weight, hold(one)))
+        passed = pick(at_end, weight, one)
+        two = lax.ppermute(passed, "rows", chip_pairs([(0, 1), (3, 2), (2, 3), (1, 0)]))
+        three_middle = lax.ppermute(weight, "rows", chip_pairs([(1, 2), (2, 1)]))
+        three_ends = lax.ppermute(weight, "rows", chip_pairs([(1, 3), (2, 0)]))
+        near = [weight, pick(at_end, one, two)]
+
     groups = jnp.stack([group ^ d for d in range(group_count)]).astype(jnp.int32)
     affine = jnp.stack([norm_gain, norm_bias])
     if is_line:
-        near, strip_pieces, far = lax.optimization_barrier(([weight, first], strip_pieces, [second]))
+        near, strip_pieces = lax.optimization_barrier((near, strip_pieces))
     even, odd = activate(
-        groups * held, affine, strip_pieces, held, row_count + 2, col_count, entries
+        groups * held, affine, strip_pieces, origins, row_count + 2, col_count, entries
     )
 
     width = channels // group_count
@@ -413,11 +419,8 @@
     )
     done = convolved(half, pieces=near)[0]
     if is_line:
-        third_ends, third_middle, done = lax.optimization_barrier((third_ends, third_middle, done))
-        chip = strip // CORES
-        at_end = ((chip == 0) | (chip == 3)).astype(jnp.int32)[None]
-        third = pick(at_end, third_ends, third_middle)
-        far.append(third)
+        three_ends, three_middle, done = lax.optimization_barrier((three_ends, three_middle, done))
+        far = [pick(at_end, three_ends, one), pick(at_end, two, three_middle)]
         far += [lax.ppermute(piece, "rows", flip("rows", 1)) for piece in far]
     parts = convolved(other_half, pieces=far, other=done)
     parts = [parts[0]] + [

time: 70.9 us -> 77.1 us (1.087)
  starting transfers between devices: 24.5 us -> 29.5 us
  local copies, waits for them, and re-layouts: 1.86 us -> 4.31 us
  waiting for transfers between devices: 29.7 us -> 28.3 us
    ppermute x9 -> x8, waiting for transfers between devices: 21.8 us -> 2.8 us  [exchange(): return [lax.ppermute(block, axis, flip(axis, d)) for d in distances]]
    ppermute x2 -> x4, waiting for transfers between devices: 1.17 us -> 18.3 us  [the longest x1 13 us: body(): lax.ppermute(passed, 'rows', chip_pairs([(0, 1), (3, 2), (2, 3), (1, 0)]))]
    ppermute x2 -> x4, starting transfers between devices: 1.97 us -> 10.3 us  [the longest x1 4.42 us: body(): lax.ppermute(passed, 'rows', chip_pairs([(0, 1), (3, 2), (2, 3), (1, 0)]))]
    ppermute x9 -> x8, starting transfers between devices: 15.7 us -> 11.8 us  [exchange(): return [lax.ppermute(block, axis, flip(axis, d)) for d in distances]]
    slice x0 -> x2, local copies, waits for them, and re-layouts: none -> 1.45 us  [the longest x1 0.73 us: body(): strip_pieces += exchange(strip_pieces[1][:middle], 'frames', [2])]
    unnamed x14 -> x16, local copies, waits for them, and re-layouts: 1.78 us -> 2.78 us
  transfers between devices with their start and end apart: 20 -> 21, of which waited for: 10 -> 9; matrix products, arithmetic and copies ran while one was open for 1% -> 2% of each run, Pallas kernels for 12% -> 11%
where the time goes in v5:
time: 77.1 us; the launch traced here: 76.8 us
  starting transfers between devices  29.5 us (38%)
  waiting for transfers between devices  28.3 us (37%)
  Pallas kernels  14.2 us (18%)
  local copies, waits for them, and re-layouts  4.31 us (6%)
    ppermute x1, waiting for transfers between devices, body(): lax.ppermute(passed, 'rows', chip_pairs([(0, 1), (3, 2), (2, 3), (1, 0)]))  13 us
    ppermute x8, starting transfers between devices, exchange(): return [lax.ppermute(block, axis, flip(axis, d)) for d in distances]  11.8 us
    pallas_call x2, Pallas kernels, convolve(): pl.pallas_call(functools.partial(conv_kernel, len(pieces), other is not N...  8.28 us
    ppermute x3, waiting for transfers between devices, body(): lax.ppermute(parts[d], 'frames', flip('frames', d))  5.3 us
    ppermute x1, waiting for transfers between devices, body(): lax.ppermute(weight, 'rows', chip_pairs([(0, 2), (3, 1), (2, 3), (1, 0)]))  5.3 us
    ppermute x1, starting transfers between devices, body(): lax.ppermute(passed, 'rows', chip_pairs([(0, 1), (3, 2), (2, 3), (1, 0)]))  4.42 us
    ppermute x1, starting transfers between devices, body(): lax.ppermute(weight, 'rows', chip_pairs([(0, 2), (3, 1), (2, 3), (1, 0)]))  3.92 us
    pallas_call x1, Pallas kernels, activate(): pl.pallas_call(functools.partial(activate_kernel, origins, rows, cols, en...  3.63 us
  transfers between devices with their start and end apart: 21, of which 9 were waited for; matrix products, arithmetic and copies ran while one was open for 2% of the time, Pallas kernels for 11%

profile of v5, /device:TPU:0, one launch (start us, length us, event | category | flops | bytes accessed | tf_op | source)
XLA Modules:
  0.0 76.8 jit_solution(16388404614272924270)
XLA Ops:
  0.0 1.0 %copy-done.5 = bf16[2,4,40,512]{3,2,1,0:T(8,128)(2,1)S(1)} copy-done((bf16[2,4,40,512]{3,2,1,0:T(8,128)(2,1)S(1)}, bf16[2,4,40,512]{3,2,1,0:T(8,128)(2,1)}, u32[]{:S(2)}) %copy-start.5) | copy-done | bytes 327704
  1.2 3.1 %collective-permute-start = (f32[2,512]{1,0:T(2,128)S(1)}, f32[2,512]{1,0:T(2,128)S(1)}, u32[]{:S(2)}, u32[]{:S(2)}) collective-permute-start(f32[2,512]{1,0:T(2,128)S(1)} %get-tuple-element.28), channel_id=1, source_target_pairs={{0,2},{1,3},{2,0},{3,1},{4,6},{5,7},{6,4},{7,5},{8,10},{9,11},{10,... | collective-permute-start | bytes 12296 | tf_op jit(solution)/shard_map/ppermute | solution.py:29
  4.3 2.6 %collective-permute-start.1 = (f32[2,512]{1,0:T(2,128)S(1)}, f32[2,512]{1,0:T(2,128)S(1)}, u32[]{:S(2)}, u32[]{:S(2)}) collective-permute-start(f32[2,512]{1,0:T(2,128)S(1)} %get-tuple-element.28), channel_id=1, source_target_pairs={{0,4},{1,5},{2,6},{3,7},{4,0},{5,1},{6,2},{7,3},{8,12},{9,13},{10,... | collective-permute-start | bytes 12296 | tf_op jit(solution)/shard_map/ppermute | solution.py:29
  6.8 1.3 %collective-permute-start.3 = (bf16[2,1,40,512]{3,2,1,0:T(8,128)(2,1)S(1)}, bf16[2,1,40,512]{3,2,1,0:T(8,128)(2,1)S(1)}, u32[]{:S(2)}, u32[]{:S(2)}) collective-permute-start(bf16[2,1,40,512]{3,2,1,0:T(8,128)(2,1)S(1)} %get-tuple-element.29), channel_id=1, source_target_pairs={{0,1},{1,2},{2,3},{3,4},{4,5},{5,6},{6,7},{8,9},{9,10},{10,11},{11... | collective-permute-start | bytes 245768 | tf_op jit(solution)/shard_map/ppermute | solution.py:359
  8.1 1.3 %collective-permute-start.4 = (bf16[2,1,40,512]{3,2,1,0:T(8,128)(2,1)S(1)}, bf16[2,1,40,512]{3,2,1,0:T(8,128)(2,1)S(1)}, u32[]{:S(2)}, u32[]{:S(2)}) collective-permute-start(bf16[2,1,40,512]{3,2,1,0:T(8,128)(2,1)S(1)} %get-tuple-element.30), channel_id=1, source_target_pairs={{1,0},{2,1},{3,2},{4,3},{5,4},{6,5},{7,6},{9,8},{10,9},{11,10},{12... | collective-permute-start | bytes 245768 | tf_op jit(solution)/shard_map/ppermute | solution.py:360
  9.5 2.8 %collective-permute-done.2 = f32[2,512]{1,0:T(2,128)S(1)} collective-permute-done((f32[2,512]{1,0:T(2,128)S(1)}, f32[2,512]{1,0:T(2,128)S(1)}, u32[]{:S(2)}, u32[]{:S(2)}) %collective-permute-start.2) | collective-permute-done | bytes 4128 | tf_op jit(solution)/shard_map/ppermute | solution.py:29
  12.4 3.9 %collective-permute-start.5 = (bf16[27,16,512]{2,1,0:T(8,128)(2,1)}, bf16[27,16,512]{2,1,0:T(8,128)(2,1)S(1)}, u32[]{:S(2)}, u32[]{:S(2)}) collective-permute-start(bf16[27,16,512]{2,1,0:T(8,128)(2,1)} %bitcast.20), channel_id=1, source_target_pairs={{0,4},{1,5},{6,2},{7,3},{4,6},{5,7},{2,0},{3,1},{8,12},{9,13},{14,... | collective-permute-start | bytes 1327112 | tf_op jit(solution)/shard_map/ppermute | solution.py:368
  16.5 0.6 shard_map.59.refs_0_
  17.1 1.6 %collective-permute-start.9 = (bf16[496,512]{1,0:T(8,128)(2,1)S(1)}, bf16[496,512]{1,0:T(8,128)(2,1)S(1)}, u32[]{:S(2)}, u32[]{:S(2)}) collective-permute-start(bf16[496,512]{1,0:T(8,128)(2,1)S(1)} %shard_map.59.refs_0_), channel_id=1, source_target_pairs={{0,16},{8,24},{16,0},{24,8},{1,17},{9,25},{17,1},{25,9},{2,18},{10... | collective-permute-start | bytes 1523720 | tf_op jit(solution)/shard_map/ppermute | solution.py:29
  18.7 1.5 %collective-permute-start.8 = (bf16[496,512]{1,0:T(8,128)(2,1)S(1)}, bf16[496,512]{1,0:T(8,128)(2,1)S(1)}, u32[]{:S(2)}, u32[]{:S(2)}) collective-permute-start(bf16[496,512]{1,0:T(8,128)(2,1)S(1)} %shard_map.59.refs_0_), channel_id=1, source_target_pairs={{0,8},{8,0},{16,24},{24,16},{1,9},{9,1},{17,25},{25,17},{2,10},{10... | collective-permute-start | bytes 1523720 | tf_op jit(solution)/shard_map/ppermute | solution.py:29
  20.2 5.3 %collective-permute-done.5.in_ref = bf16[27,16,512]{2,1,0:T(8,128)(2,1)S(1)} collective-permute-done((bf16[27,16,512]{2,1,0:T(8,128)(2,1)}, bf16[27,16,512]{2,1,0:T(8,128)(2,1)S(1)}, u32[]{:S(2)}, u32[]{:S(2)}) %collective-permute-start.5) | collective-permute-done | bytes 442400 | tf_op jit(solution)/shard_map/ppermute | solution.py:368
  25.5 0.8 copy-done.1
  26.3 1.0 %copy-done.2 = bf16[27,16,512]{2,1,0:T(8,128)(2,1)S(1)} copy-done((bf16[27,16,512]{2,1,0:T(8,128)(2,1)S(1)}, bf16[27,16,512]{2,1,0:T(8,128)(2,1)}, u32[]{:S(2)}) %copy-start.2) | copy-done | bytes 442392
  27.3 4.4 %collective-permute-start.6 = (bf16[27,16,512]{2,1,0:T(8,128)(2,1)S(1)}, bf16[27,16,512]{2,1,0:T(8,128)(2,1)S(1)}, u32[]{:S(2)}, u32[]{:S(2)}) collective-permute-start(bf16[27,16,512]{2,1,0:T(8,128)(2,1)S(1)} %shard_map.57), channel_id=1, source_target_pairs={{0,2},{1,3},{6,4},{7,5},{4,6},{5,7},{2,0},{3,1},{8,10},{9,11},{14,... | collective-permute-start | bytes 1327112 | tf_op jit(solution)/shard_map/ppermute | solution.py:393
  31.7 0.7 slice.62
  32.5 1.5 %collective-permute-start.11 = (bf16[256,512]{1,0:T(8,128)(2,1)}, bf16[256,512]{1,0:T(8,128)(2,1)}, u32[]{:S(2)}, u32[]{:S(2)}) collective-permute-start(bf16[256,512]{1,0:T(8,128)(2,1)} %slice.62), channel_id=1, source_target_pairs={{0,8},{8,0},{16,24},{24,16},{1,9},{9,1},{17,25},{25,17},{2,10},{10... | collective-permute-start | bytes 786440 | tf_op jit(solution)/shard_map/ppermute | solution.py:29
  34.0 0.7 slice.61
  34.7 1.5 %collective-permute-start.10 = (bf16[240,512]{1,0:T(8,128)(2,1)}, bf16[240,512]{1,0:T(8,128)(2,1)S(1)}, u32[]{:S(2)}, u32[]{:S(2)}) collective-permute-start(bf16[240,512]{1,0:T(8,128)(2,1)} %slice.61), channel_id=1, source_target_pairs={{0,16},{8,24},{16,0},{24,8},{1,17},{9,25},{17,1},{25,9},{2,18},{10... | collective-permute-start | bytes 737288 | tf_op jit(solution)/shard_map/ppermute | solution.py:29
  36.2 1.3 %collective-permute-start.12 = (bf16[27,16,512]{2,1,0:T(8,128)(2,1)S(1)}, bf16[27,16,512]{2,1,0:T(8,128)(2,1)S(1)}, u32[]{:S(2)}, u32[]{:S(2)}) collective-permute-start(bf16[27,16,512]{2,1,0:T(8,128)(2,1)S(1)} %bitcast.22), channel_id=1, source_target_pairs={{2,6},{3,7},{4,0},{5,1},{10,14},{11,15},{12,8},{13,9},{18,22},{19,... | collective-permute-start | bytes 1327112 | tf_op jit(solution)/shard_map/ppermute | solution.py:395
  37.5 0.7 collective-permute-start.13
  38.2 13.0 %collective-permute-done.6.other_ref.one_ref = bf16[27,16,512]{2,1,0:T(8,128)(2,1)S(1)} collective-permute-done((bf16[27,16,512]{2,1,0:T(8,128)(2,1)S(1)}, bf16[27,16,512]{2,1,0:T(8,128)(2,1)S(1)}, u32[]{:S(2)}, u32[]{:S(2)}) %collective-permute-start.6) | collective-permute-done | bytes 442400 | tf_op jit(solution)/shard_map/ppermute | solution.py:393
  52.1 3.6 %shard_map.60 = (bf16[6,336,512]{2,1,0:T(8,128)(2,1)S(1)}, bf16[6,320,512]{2,1,0:T(8,128)(2,1)S(1)}) custom-call(s32[4]{0:T(128)S(1)} %get-tuple-element.53.place_ref, f32[2,512]{1,0:T(2,128)S(1)} %pad_maximum_fusion.affine_ref, bf16[496,512]{1,0:T(8,128)(2,1)S(1)} %shard_map.59.refs_0_, bf16[496,512]{1,0:T(8,128)(2,1)S(1)} %collective-permute-done.8.refs_1_, ...), custom_call_target="tpu_custom_call" | custom-call | flops 512 | bytes 512 | tf_op jit(solution)/shard_map/pallas_call | solution.py:228
  55.8 4.2 %shard_map.61.refs_4_ = bf16[8,160,128]{2,1,0:T(8,128)(2,1)S(1)} custom-call(s32[4]{0:T(128)S(1)} %get-tuple-element.53.place_ref, s32[4]{0:T(128)S(1)} %and_select_fusion.slot_ref, s32[1]{0:T(128)} %bitcast.8.half_ref, bf16[6,336,512]{2,1,0:T(8,128)(2,1)S(1)} %get-tuple-element.40.even_ref, bf16[6,320,512]{2,1,0:T(8,128)(2,1)S(1)} %get-tuple-element.41.odd_ref, ...), custom_call_target="tpu_custom_call" | custom-call | flops 512 | bytes 512 | tf_op jit(solution)/shard_map/pallas_call | solution.py:312
  60.7 1.2 %collective-permute-done.17.refs_3_ = bf16[27,16,512]{2,1,0:T(8,128)(2,1)S(1)} collective-permute-done((bf16[27,16,512]{2,1,0:T(8,128)(2,1)S(1)}, bf16[27,16,512]{2,1,0:T(8,128)(2,1)S(1)}, u32[]{:S(2)}, u32[]{:S(2)}) %collective-permute-start.17) | collective-permute-done | bytes 442400 | tf_op jit(solution)/shard_map/ppermute | solution.py:424
  61.9 0.6 collective-permute-done.16.refs_2_
  62.5 4.1 %shard_map.64 = (bf16[2,160,128]{2,1,0:T(8,128)(2,1)S(1)}, bf16[2,160,128]{2,1,0:T(8,128)(2,1)S(1)}, bf16[2,160,128]{2,1,0:T(8,128)(2,1)S(1)}, bf16[2,160,128]{2,1,0:T(8,128)(2,1)S(1)}) custom-call(s32[4]{0:T(128)S(1)} %get-tuple-element.53.place_ref, s32[4]{0:T(128)S(1)} %and_select_fusion.slot_ref, s32[1]{0:T(128)S(6)} %sub.40.half_ref, ...), custom_call_target="tpu_custom_call" | custom-call | flops 512 | bytes 512 | tf_op jit(solution)/shard_map/pallas_call | solution.py:312
  66.6 2.0 %collective-permute-start.18 = (bf16[2,160,128]{2,1,0:T(8,128)(2,1)S(1)}, bf16[2,160,128]{2,1,0:T(8,128)(2,1)S(1)}, u32[]{:S(2)}, u32[]{:S(2)}) collective-permute-start(bf16[2,160,128]{2,1,0:T(8,128)(2,1)S(1)} %get-tuple-element.48), channel_id=1, source_target_pairs={{0,8},{8,0},{16,24},{24,16},{1,9},{9,1},{17,25},{25,17},{2,10},{10... | collective-permute-start | bytes 245768 | tf_op jit(solution)/shard_map/ppermute | solution.py:427
  68.6 1.5 %collective-permute-start.19 = (bf16[2,160,128]{2,1,0:T(8,128)(2,1)S(1)}, bf16[2,160,128]{2,1,0:T(8,128)(2,1)S(1)}, u32[]{:S(2)}, u32[]{:S(2)}) collective-permute-start(bf16[2,160,128]{2,1,0:T(8,128)(2,1)S(1)} %get-tuple-element.49), channel_id=1, source_target_pairs={{0,16},{8,24},{16,0},{24,8},{1,17},{9,25},{17,1},{25,9},{2,18},{10... | collective-permute-start | bytes 245768 | tf_op jit(solution)/shard_map/ppermute | solution.py:427
  70.2 1.2 %collective-permute-done.18.refs_1_ = bf16[2,160,128]{2,1,0:T(8,128)(2,1)S(1)} collective-permute-done((bf16[2,160,128]{2,1,0:T(8,128)(2,1)S(1)}, bf16[2,160,128]{2,1,0:T(8,128)(2,1)S(1)}, u32[]{:S(2)}, u32[]{:S(2)}) %collective-permute-start.18) | collective-permute-done | bytes 81952 | tf_op jit(solution)/shard_map/ppermute | solution.py:427
  71.4 2.5 %collective-permute-done.19.refs_2_ = bf16[2,160,128]{2,1,0:T(8,128)(2,1)S(1)} collective-permute-done((bf16[2,160,128]{2,1,0:T(8,128)(2,1)S(1)}, bf16[2,160,128]{2,1,0:T(8,128)(2,1)S(1)}, u32[]{:S(2)}, u32[]{:S(2)}) %collective-permute-start.19) | collective-permute-done | bytes 81952 | tf_op jit(solution)/shard_map/ppermute | solution.py:427
  73.9 1.6 %collective-permute-done.20.refs_3_ = bf16[2,160,128]{2,1,0:T(8,128)(2,1)S(1)} collective-permute-done((bf16[2,160,128]{2,1,0:T(8,128)(2,1)S(1)}, bf16[2,160,128]{2,1,0:T(8,128)(2,1)S(1)}, u32[]{:S(2)}, u32[]{:S(2)}) %collective-permute-start.20) | collective-permute-done | bytes 81952 | tf_op jit(solution)/shard_map/ppermute | solution.py:427
  75.5 1.3 %shard_map.65 = bf16[2,160,512]{2,1,0:T(8,128)(2,1)} custom-call(s32[4]{0:T(128)S(1)} %get-tuple-element.54.place_ref, bf16[2,160,128]{2,1,0:T(8,128)(2,1)S(1)} %get-tuple-element.47.refs_0_, bf16[2,160,128]{2,1,0:T(8,128)(2,1)S(1)} %collective-permute-done.18.refs_1_, bf16[2,160,128]{2,1,0:T(8,128)(2,1)S(1)} %collective-permute-done.19.refs_2_, ...), custom_call_target="tpu_custom_call" | custom-call | tf_op jit(solution)/shard_map/pallas_call | solution.py:339
  (48 shorter events, 2.1 us)
Async XLA Ops:
  0.0 51.9 %copy-start = (f32[512]{0:T(512)S(1)}, f32[512]{0:T(512)}, u32[]{:S(2)}) copy-start(f32[512]{0:T(512)} %param.9) | copy-start | bytes 6148
  0.0 1.0 %copy-start.5 = (bf16[2,4,40,512]{3,2,1,0:T(8,128)(2,1)S(1)}, bf16[2,4,40,512]{3,2,1,0:T(8,128)(2,1)}, u32[]{:S(2)}) copy-start(bf16[2,4,40,512]{3,2,1,0:T(8,128)(2,1)} %x_ref.1) | copy-start | bytes 983044
  1.2 8.3 %collective-permute-start = (f32[2,512]{1,0:T(2,128)S(1)}, f32[2,512]{1,0:T(2,128)S(1)}, u32[]{:S(2)}, u32[]{:S(2)}) collective-permute-start(f32[2,512]{1,0:T(2,128)S(1)} %get-tuple-element.28), channel_id=1, source_target_pairs={{0,2},{1,3},{2,0},{3,1},{4,6},{5,7},{6,4},{7,5},{8,10},{9,11},{10,... | collective-permute-start | bytes 12296 | tf_op jit(solution)/shard_map/ppermute | solution.py:29
  4.3 5.2 %collective-permute-start.1 = (f32[2,512]{1,0:T(2,128)S(1)}, f32[2,512]{1,0:T(2,128)S(1)}, u32[]{:S(2)}, u32[]{:S(2)}) collective-permute-start(f32[2,512]{1,0:T(2,128)S(1)} %get-tuple-element.28), channel_id=1, source_target_pairs={{0,4},{1,5},{2,6},{3,7},{4,0},{5,1},{6,2},{7,3},{8,12},{9,13},{10,... | collective-permute-start | bytes 12296 | tf_op jit(solution)/shard_map/ppermute | solution.py:29
  6.8 5.4 %collective-permute-start.2 = (f32[2,512]{1,0:T(2,128)S(1)}, f32[2,512]{1,0:T(2,128)S(1)}, u32[]{:S(2)}, u32[]{:S(2)}) collective-permute-start(f32[2,512]{1,0:T(2,128)S(1)} %get-tuple-element.28), channel_id=1, source_target_pairs={{0,6},{1,7},{2,4},{3,5},{4,2},{5,3},{6,0},{7,1},{8,14},{9,15},{10,... | collective-permute-start | bytes 12296 | tf_op jit(solution)/shard_map/ppermute | solution.py:29
  6.8 5.5 %collective-permute-start.3 = (bf16[2,1,40,512]{3,2,1,0:T(8,128)(2,1)S(1)}, bf16[2,1,40,512]{3,2,1,0:T(8,128)(2,1)S(1)}, u32[]{:S(2)}, u32[]{:S(2)}) collective-permute-start(bf16[2,1,40,512]{3,2,1,0:T(8,128)(2,1)S(1)} %get-tuple-element.29), channel_id=1, source_target_pairs={{0,1},{1,2},{2,3},{3,4},{4,5},{5,6},{6,7},{8,9},{9,10},{10,11},{11... | collective-permute-start | bytes 245768 | tf_op jit(solution)/shard_map/ppermute | solution.py:359
  8.1 4.3 %collective-permute-start.4 = (bf16[2,1,40,512]{3,2,1,0:T(8,128)(2,1)S(1)}, bf16[2,1,40,512]{3,2,1,0:T(8,128)(2,1)S(1)}, u32[]{:S(2)}, u32[]{:S(2)}) collective-permute-start(bf16[2,1,40,512]{3,2,1,0:T(8,128)(2,1)S(1)} %get-tuple-element.30), channel_id=1, source_target_pairs={{1,0},{2,1},{3,2},{4,3},{5,4},{6,5},{7,6},{9,8},{10,9},{11,10},{12... | collective-permute-start | bytes 245768 | tf_op jit(solution)/shard_map/ppermute | solution.py:360
  12.3 4.1 %collective-permute-start.7 = (f32[2,512]{1,0:T(2,128)S(1)}, f32[2,512]{1,0:T(2,128)S(1)}, u32[]{:S(2)}, u32[]{:S(2)}) collective-permute-start(f32[2,512]{1,0:T(2,128)S(1)} %pad_maximum_fusion.1), channel_id=1, source_target_pairs={{0,1},{1,0},{2,3},{3,2},{4,5},{5,4},{6,7},{7,6},{8,9},{9,8},{10,11... | collective-permute-start | bytes 12296 | tf_op jit(solution)/shard_map/ppermute | solution.py:29
  12.4 13.1 %collective-permute-start.5 = (bf16[27,16,512]{2,1,0:T(8,128)(2,1)}, bf16[27,16,512]{2,1,0:T(8,128)(2,1)S(1)}, u32[]{:S(2)}, u32[]{:S(2)}) collective-permute-start(bf16[27,16,512]{2,1,0:T(8,128)(2,1)} %bitcast.20), channel_id=1, source_target_pairs={{0,4},{1,5},{6,2},{7,3},{4,6},{5,7},{2,0},{3,1},{8,12},{9,13},{14,... | collective-permute-start | bytes 1327112 | tf_op jit(solution)/shard_map/ppermute | solution.py:368
  17.1 9.2 %copy-start.4 = (bf16[3,3,3,512,16]{3,4,2,1,0:T(8,128)(2,1)S(1)}, bf16[3,3,3,512,16]{3,4,2,1,0:T(8,128)(2,1)}, u32[]{:S(2)}) copy-start(bf16[3,3,3,512,16]{3,4,2,1,0:T(8,128)(2,1)} %param.8) | copy-start | bytes 1327108
  17.1 14.6 %collective-permute-start.9 = (bf16[496,512]{1,0:T(8,128)(2,1)S(1)}, bf16[496,512]{1,0:T(8,128)(2,1)S(1)}, u32[]{:S(2)}, u32[]{:S(2)}) collective-permute-start(bf16[496,512]{1,0:T(8,128)(2,1)S(1)} %shard_map.59.refs_0_), channel_id=1, source_target_pairs={{0,16},{8,24},{16,0},{24,8},{1,17},{9,25},{17,1},{25,9},{2,18},{10... | collective-permute-start | bytes 1523720 | tf_op jit(solution)/shard_map/ppermute | solution.py:29
  18.7 15.3 %collective-permute-start.8 = (bf16[496,512]{1,0:T(8,128)(2,1)S(1)}, bf16[496,512]{1,0:T(8,128)(2,1)S(1)}, u32[]{:S(2)}, u32[]{:S(2)}) collective-permute-start(bf16[496,512]{1,0:T(8,128)(2,1)S(1)} %shard_map.59.refs_0_), channel_id=1, source_target_pairs={{0,8},{8,0},{16,24},{24,16},{1,9},{9,1},{17,25},{25,17},{2,10},{10... | collective-permute-start | bytes 1523720 | tf_op jit(solution)/shard_map/ppermute | solution.py:29
  25.5 0.8 copy-start.1
  26.3 1.0 %copy-start.2 = (bf16[27,16,512]{2,1,0:T(8,128)(2,1)S(1)}, bf16[27,16,512]{2,1,0:T(8,128)(2,1)}, u32[]{:S(2)}) copy-start(bf16[27,16,512]{2,1,0:T(8,128)(2,1)} %shard_map.56.other_ref.one_ref) | copy-start | bytes 1327108
  27.3 24.0 %copy-start.3 = (bf16[27,16,512]{2,1,0:T(8,128)(2,1)S(1)}, bf16[27,16,512]{2,1,0:T(8,128)(2,1)}, u32[]{:S(2)}) copy-start(bf16[27,16,512]{2,1,0:T(8,128)(2,1)} %shard_map.56.other_ref.one_ref) | copy-start | bytes 1327108
  27.3 24.8 %copy-start.6 = (f32[512]{0:T(512)S(1)}, f32[512]{0:T(512)}, u32[]{:S(2)}) copy-start(f32[512]{0:T(512)} %param.7) | copy-start | bytes 6148
  27.3 24.8 %copy-start.7 = (f32[512]{0:T(512)S(1)}, f32[512]{0:T(512)}, u32[]{:S(2)}) copy-start(f32[512]{0:T(512)} %param.6) | copy-start | bytes 6148
  27.3 23.9 %collective-permute-start.6 = (bf16[27,16,512]{2,1,0:T(8,128)(2,1)S(1)}, bf16[27,16,512]{2,1,0:T(8,128)(2,1)S(1)}, u32[]{:S(2)}, u32[]{:S(2)}) collective-permute-start(bf16[27,16,512]{2,1,0:T(8,128)(2,1)S(1)} %shard_map.57), channel_id=1, source_target_pairs={{0,2},{1,3},{6,4},{7,5},{4,6},{5,7},{2,0},{3,1},{8,10},{9,11},{14,... | collective-permute-start | bytes 1327112 | tf_op jit(solution)/shard_map/ppermute | solution.py:393
  32.5 18.8 %collective-permute-start.11 = (bf16[256,512]{1,0:T(8,128)(2,1)}, bf16[256,512]{1,0:T(8,128)(2,1)}, u32[]{:S(2)}, u32[]{:S(2)}) collective-permute-start(bf16[256,512]{1,0:T(8,128)(2,1)} %slice.62), channel_id=1, source_target_pairs={{0,8},{8,0},{16,24},{24,16},{1,9},{9,1},{17,25},{25,17},{2,10},{10... | collective-permute-start | bytes 786440 | tf_op jit(solution)/shard_map/ppermute | solution.py:29
  34.7 16.6 %collective-permute-start.10 = (bf16[240,512]{1,0:T(8,128)(2,1)}, bf16[240,512]{1,0:T(8,128)(2,1)S(1)}, u32[]{:S(2)}, u32[]{:S(2)}) collective-permute-start(bf16[240,512]{1,0:T(8,128)(2,1)} %slice.61), channel_id=1, source_target_pairs={{0,16},{8,24},{16,0},{24,8},{1,17},{9,25},{17,1},{25,9},{2,18},{10... | collective-permute-start | bytes 737288 | tf_op jit(solution)/shard_map/ppermute | solution.py:29
  36.2 23.7 %collective-permute-start.12 = (bf16[27,16,512]{2,1,0:T(8,128)(2,1)S(1)}, bf16[27,16,512]{2,1,0:T(8,128)(2,1)S(1)}, u32[]{:S(2)}, u32[]{:S(2)}) collective-permute-start(bf16[27,16,512]{2,1,0:T(8,128)(2,1)S(1)} %bitcast.22), channel_id=1, source_target_pairs={{2,6},{3,7},{4,0},{5,1},{10,14},{11,15},{12,8},{13,9},{18,22},{19,... | collective-permute-start | bytes 1327112 | tf_op jit(solution)/shard_map/ppermute | solution.py:395
  37.5 22.5 %collective-permute-start.13 = (bf16[27,16,512]{2,1,0:T(8,128)(2,1)S(1)}, bf16[27,16,512]{2,1,0:T(8,128)(2,1)S(1)}, u32[]{:S(2)}, u32[]{:S(2)}) collective-permute-start(bf16[27,16,512]{2,1,0:T(8,128)(2,1)S(1)} %bitcast.23), channel_id=1, source_target_pairs={{2,4},{3,5},{4,2},{5,3},{10,12},{11,13},{12,10},{13,11},{18,20},{1... | collective-permute-start | bytes 1327112 | tf_op jit(solution)/shard_map/ppermute | solution.py:394
  51.3 4.5 %collective-permute-start.14 = (bf16[27,16,512]{2,1,0:T(8,128)(2,1)S(1)}, bf16[27,16,512]{2,1,0:T(8,128)(2,1)S(1)}, u32[]{:S(2)}, u32[]{:S(2)}) collective-permute-start(bf16[27,16,512]{2,1,0:T(8,128)(2,1)S(1)} %bitcast.24), channel_id=1, source_target_pairs={{0,1},{1,0},{2,3},{3,2},{4,5},{5,4},{6,7},{7,6},{8,9},{9,8},{10,11... | collective-permute-start | bytes 1327112 | tf_op jit(solution)/shard_map/ppermute | solution.py:409
  51.4 4.4 %collective-permute-start.15 = (bf16[27,16,512]{2,1,0:T(8,128)(2,1)S(1)}, bf16[27,16,512]{2,1,0:T(8,128)(2,1)S(1)}, u32[]{:S(2)}, u32[]{:S(2)}) collective-permute-start(bf16[27,16,512]{2,1,0:T(8,128)(2,1)S(1)} %shard_map.58.refs_1_), channel_id=1, source_target_pairs={{0,1},{1,0},{2,3},{3,2},{4,5},{5,4},{6,7},{7,6},{8,9},{9,8},{10,11... | collective-permute-start | bytes 1327112 | tf_op jit(solution)/shard_map/ppermute | solution.py:409
  60.0 1.9 %collective-permute-start.17 = (bf16[27,16,512]{2,1,0:T(8,128)(2,1)S(1)}, bf16[27,16,512]{2,1,0:T(8,128)(2,1)S(1)}, u32[]{:S(2)}, u32[]{:S(2)}) collective-permute-start(bf16[27,16,512]{2,1,0:T(8,128)(2,1)S(1)} %shard_map.63.refs_1_), channel_id=1, source_target_pairs={{0,1},{1,0},{2,3},{3,2},{4,5},{5,4},{6,7},{7,6},{8,9},{9,8},{10,11... | collective-permute-start | bytes 1327112 | tf_op jit(solution)/shard_map/ppermute | solution.py:424
  60.2 2.3 %collective-permute-start.16 = (bf16[27,16,512]{2,1,0:T(8,128)(2,1)S(1)}, bf16[27,16,512]{2,1,0:T(8,128)(2,1)S(1)}, u32[]{:S(2)}, u32[]{:S(2)}) collective-permute-start(bf16[27,16,512]{2,1,0:T(8,128)(2,1)S(1)} %shard_map.62.refs_0_), channel_id=1, source_target_pairs={{0,1},{1,0},{2,3},{3,2},{4,5},{5,4},{6,7},{7,6},{8,9},{9,8},{10,11... | collective-permute-start | bytes 1327112 | tf_op jit(solution)/shard_map/ppermute | solution.py:424
  66.6 4.7 %collective-permute-start.18 = (bf16[2,160,128]{2,1,0:T(8,128)(2,1)S(1)}, bf16[2,160,128]{2,1,0:T(8,128)(2,1)S(1)}, u32[]{:S(2)}, u32[]{:S(2)}) collective-permute-start(bf16[2,160,128]{2,1,0:T(8,128)(2,1)S(1)} %get-tuple-element.48), channel_id=1, source_target_pairs={{0,8},{8,0},{16,24},{24,16},{1,9},{9,1},{17,25},{25,17},{2,10},{10... | collective-permute-start | bytes 245768 | tf_op jit(solution)/shard_map/ppermute | solution.py:427
  68.6 5.3 %collective-permute-start.19 = (bf16[2,160,128]{2,1,0:T(8,128)(2,1)S(1)}, bf16[2,160,128]{2,1,0:T(8,128)(2,1)S(1)}, u32[]{:S(2)}, u32[]{:S(2)}) collective-permute-start(bf16[2,160,128]{2,1,0:T(8,128)(2,1)S(1)} %get-tuple-element.49), channel_id=1, source_target_pairs={{0,16},{8,24},{16,0},{24,8},{1,17},{9,25},{17,1},{25,9},{2,18},{10... | collective-permute-start | bytes 245768 | tf_op jit(solution)/shard_map/ppermute | solution.py:427
  70.2 5.3 %collective-permute-start.20 = (bf16[2,160,128]{2,1,0:T(8,128)(2,1)S(1)}, bf16[2,160,128]{2,1,0:T(8,128)(2,1)S(1)}, u32[]{:S(2)}, u32[]{:S(2)}) collective-permute-start(bf16[2,160,128]{2,1,0:T(8,128)(2,1)S(1)} %get-tuple-element.50), channel_id=1, source_target_pairs={{0,24},{8,16},{16,8},{24,0},{1,25},{9,17},{17,9},{25,1},{2,26},{10... | collective-permute-start | bytes 245768 | tf_op jit(solution)/shard_map/ppermute | solution.py:427

commit v6 on v3

--- a/solution.py
+++ b/solution.py
@@ -37,11 +37,12 @@
     return lax.optimization_barrier((block, *others))[0]
 
 
-def local_kernel(x_ref, stats_ref, top_ref, bottom_ref, payload_ref):
+def local_kernel(core_ref, x_ref, stats_ref, inner_ref, outer_ref, payload_ref):
     frames, rows, cols, channels = x_ref.shape
     entries = frames * rows * cols
-    top_ref[...] = x_ref[:, 0:1]
-    bottom_ref[...] = x_ref[:, rows - 1 : rows]
+    inner = (rows - 1) * (1 - core_ref[0])
+    inner_ref[...] = x_ref[:, pl.ds(inner, 1)]
+    outer_ref[...] = x_ref[:, pl.ds(rows - 1 - inner, 1)]
     for f in range(frames):
         start = (f * (rows + 2) + 1) * cols
         payload_ref[start : start + rows * cols, :] = x_ref[f].reshape(rows * cols, channels)
@@ -62,7 +63,7 @@
         stats_ref[1:2, lanes] = jnp.sum(total, axis=0, keepdims=True)
 
 
-def local(latents):
+def local(core, latents):
     frames, rows, cols, channels = latents.shape
     edge = jax.ShapeDtypeStruct((frames, 1, cols, channels), jnp.bfloat16)
     return pl.pallas_call(
@@ -73,10 +74,10 @@
             edge,
             jax.ShapeDtypeStruct((frames * (rows + 2) * cols + 16, channels), jnp.bfloat16),
         ),
-        in_specs=[whole],
+        in_specs=[scalars, whole],
         out_specs=(whole,) * 4,
         compiler_params=params(8),
-    )(latents)
+    )(core, latents)
 
 
 def merge(parts, entries):
@@ -85,21 +86,21 @@
     return jnp.stack([mean, sum(part[1] for part in parts) + apart])
 
 
-def pack_kernel(frames, rows, cols, edge_ref, stats_ref, above_ref, below_ref, _, out_ref):
+def pack_kernel(frames, rows, cols, edge_ref, stats_ref, sibling_ref, facing_ref, _, out_ref):
     count = frames * rows * cols
     for f in range(frames):
         first = f * rows * cols
         last = first + (rows - 1) * cols
-        for start, rim_ref, edge, mirror in (
-            (first, above_ref, 0, first + 2 * cols),
-            (last, below_ref, 1, last - 2 * cols),
-        ):
-
+        for start, edge, mirror in ((first, 0, first + 2 * cols), (last, 1, last - 2 * cols)):
             @pl.when(edge_ref[edge] == 0)
             def _():
-                out_ref[start : start + cols, :] = rim_ref[f, 0]
-
-            @pl.when(edge_ref[edge] != 0)
+                out_ref[start : start + cols, :] = sibling_ref[f, 0]
+
+            @pl.when(edge_ref[edge] == 1)
+            def _():
+                out_ref[start : start + cols, :] = facing_ref[f, 0]
+
+            @pl.when(edge_ref[edge] == 2)
             def _():
                 out_ref[start : start + cols, :] = out_ref[mirror : mirror + cols, :]
 
@@ -114,7 +115,7 @@
     out_ref[count:, :] = jnp.concatenate(terms, axis=0).astype(jnp.bfloat16)
 
 
-def pack(edges, stats, above, below, payload, frames, rows, cols):
+def pack(edges, stats, sibling, facing, payload, frames, rows, cols):
     return pl.pallas_call(
         functools.partial(pack_kernel, frames, rows, cols),
         out_shape=jax.ShapeDtypeStruct(payload.shape, jnp.bfloat16),
@@ -122,22 +123,42 @@
         out_specs=whole,
         input_output_aliases={4: 0},
         compiler_params=params(8),
-    )(edges, stats, above, below, payload)
-
-
-def held_kernel(in_ref, out_ref):
-    pass
-
-
-def hold(block):
-    return pl.pallas_call(
-        held_kernel,
-        out_shape=jax.ShapeDtypeStruct(block.shape, block.dtype),
-        in_specs=[pl.BlockSpec(memory_space=pl.ANY)],
-        out_specs=pl.BlockSpec(memory_space=pl.ANY),
-        input_output_aliases={0: 0},
+    )(edges, stats, sibling, facing, payload)
+
+
+def wait_kernel(in_ref, out_ref):
+    out_ref[...] = in_ref[...]
+
+
+def behind(block, small):
+    block, small = lax.optimization_barrier((block, small))
+    small = pl.pallas_call(
+        wait_kernel,
+        out_shape=jax.ShapeDtypeStruct(small.shape, small.dtype),
+        in_specs=[whole],
+        out_specs=whole,
         cost_estimate=pl.CostEstimate(flops=10**10, bytes_accessed=0, transcendentals=0),
-    )(block)
+    )(small)
+    return lax.optimization_barrier((block, small))
+
+
+def join_kernel(*refs):
+    *in_refs, out_ref = refs
+    start = 0
+    for in_ref in in_refs:
+        out_ref[start : start + in_ref.shape[0]] = in_ref[...]
+        start += in_ref.shape[0]
+
+
+def join(blocks):
+    count = sum(block.shape[0] for block in blocks)
+    return pl.pallas_call(
+        join_kernel,
+        out_shape=jax.ShapeDtypeStruct((count,) + blocks[0].shape[1:], blocks[0].dtype),
+        in_specs=[whole] * len(blocks),
+        out_specs=whole,
+        compiler_params=params(16),
+    )(*blocks)
 
 
 def pick_kernel(which_ref, one_ref, other_ref, out_ref):
@@ -157,7 +178,7 @@
         in_specs=[scalars] + [whole] * 2,
         out_specs=whole,
         compiler_params=params(8),
-        cost_estimate=pl.CostEstimate(flops=10**10, bytes_accessed=one.size, transcendentals=0),
+        cost_estimate=pl.CostEstimate(flops=0, bytes_accessed=one.size, transcendentals=0),
     )(which, one, other)
 
 
@@ -239,14 +260,13 @@
         ],
         compiler_params=params(24),
         cost_estimate=pl.CostEstimate(
-            flops=10 * frames * rows * cols * channels,
-            bytes_accessed=6 * frames * rows * cols * channels,
-            transcendentals=frames * rows * cols * channels,
+            flops=channels, bytes_accessed=channels, transcendentals=0
         ),
     )(places, affine, *pieces)
 
 
-def conv_kernel(count, with_other, place_ref, slot_ref, half_ref, even_ref, odd_ref, bias_ref, *refs):
+def conv_kernel(spans, with_other, place_ref, slot_ref, half_ref, even_ref, odd_ref, bias_ref, *refs):
+    count = 1 + max(array for array, _ in spans)
     piece_refs, refs = refs[:count], refs[count:]
     if with_other:
         other_ref, refs = refs[0], refs[1:]
@@ -257,10 +277,10 @@
     cols = per_row // frames
     channels = even_ref.shape[2]
     width = taps.shape[2] * taps.shape[3]
-    for p, piece_ref in enumerate(piece_refs):
+    for p, (array, start) in enumerate(spans):
         slot = slot_ref[p]
         for tap in range(27):
-            taps[tap % 9, tap // 9, slot] = piece_ref[tap]
+            taps[tap % 9, tap // 9, slot] = piece_refs[array][start + tap]
 
     for y in range(rows):
         total = None
@@ -301,31 +321,29 @@
         out_refs[0][...] = placed[...]
 
 
-def convolve(places, slots, half, even, odd, bias, pieces, frames, other=None):
+def convolve(places, slots, half, even, odd, bias, pieces, spans, frames, other=None):
     rows, per_row, channels = even.shape[0] - 2, odd.shape[1], even.shape[2]
     positions = rows * per_row // frames
     each = pieces[0].shape[1]
-    width = each * len(pieces)
+    width = each * len(spans)
     if other is None:
         shapes, others = [(frames, positions, 2 * width)], []
     else:
         groups = places.shape[0]
         shapes, others = [(frames // groups, positions, 2 * width)] * groups, [other]
     return pl.pallas_call(
-        functools.partial(conv_kernel, len(pieces), other is not None),
+        functools.partial(conv_kernel, spans, other is not None),
         out_shape=tuple(jax.ShapeDtypeStruct(shape, jnp.bfloat16) for shape in shapes),
         in_specs=[scalars] * 3 + [whole] * (3 + len(pieces) + len(others)),
         out_specs=tuple(whole for _ in shapes),
         scratch_shapes=[
-            pltpu.VMEM((9, 3, len(pieces), each, channels), jnp.bfloat16),
+            pltpu.VMEM((9, 3, len(spans), each, channels), jnp.bfloat16),
             pltpu.VMEM((2, rows * per_row, 2 * width), jnp.float32),
             pltpu.VMEM((frames, positions, 2 * width), jnp.bfloat16),
         ],
         compiler_params=params(32),
         cost_estimate=pl.CostEstimate(
-            flops=2 * rows * per_row * channels * width,
-            bytes_accessed=2 * channels * width,
-            transcendentals=0,
+            flops=channels, bytes_accessed=channels, transcendentals=0
         ),
     )(places, slots, half, even, odd, bias, *pieces, *others)
 
@@ -359,16 +377,20 @@
     weight = conv_weight.transpose(0, 1, 2, 4, 3)
     weight = weight.reshape((-1,) + weight.shape[3:])
 
-    stats, top, bottom, payload = local(latents)
-    above = lax.ppermute(bottom, "rows", [(i, i + 1) for i in range(strips - 1)])
-    below = lax.ppermute(top, "rows", [(i + 1, i) for i in range(strips - 1)])
-
+    core = strip % CORES
+    stats, inner, outer, payload = local(core[None], latents)
+    sibling = lax.ppermute(inner, "rows", flip("rows", 1))
+    facing = [(i, i + 1) for i in range(1, strips - 1, CORES)]
+    facing = lax.ppermute(outer, "rows", facing + [(b, a) for a, b in facing])
+
+    width = channels // group_count
+    bias = lax.dynamic_slice_in_dim(conv_bias, group * width, width)[None]
     entries = held * row_count * col_count
     if is_line:
+        weight = after(weight, sibling, facing)
+        first, second = exchange(weight, "rows", [CORES, 2 * CORES])
         chips = range(CORES, strips, CORES)
         stats = merge([stats] + exchange(stats, "rows", chips), entries)
-        weight = after(weight, stats, above, below)
-        first, second = exchange(weight, "rows", [CORES, 2 * CORES])
         stats = merge([stats] + exchange(stats, "rows", [1]), 4 * entries)
         entries *= strips
     else:
@@ -380,46 +402,50 @@
 
     if is_line:
         weight, first, second = lax.optimization_barrier((weight, first, second))
-        second = hold(second)
+        second, bias = behind(second, bias)
         ends = chip_pairs([(1, 0), (2, 3)])
         middle = chip_pairs([(1, 2), (2, 1)])
         third_ends = lax.ppermute(second, "rows", ends)
         third_middle = lax.ppermute(weight, "rows", middle)
 
-    edges = jnp.stack([strip == 0, strip == strips - 1]).astype(jnp.int32)
-    payload = pack(edges, stats, above, below, payload, held, row_count + 2, col_count)
+    above = jnp.where(strip == 0, 2, 1 - core)
+    below = jnp.where(strip == strips - 1, 2, core)
+    edges = jnp.stack([above, below]).astype(jnp.int32)
+    payload = pack(edges, stats, sibling, facing, payload, held, row_count + 2, col_count)
     strip_pieces = [payload] + exchange(payload, "frames", range(1, group_count))
     groups = jnp.stack([group ^ d for d in range(group_count)]).astype(jnp.int32)
     affine = jnp.stack([norm_gain, norm_bias])
     if is_line:
-        near, strip_pieces, far = lax.optimization_barrier(([weight, first], strip_pieces, [second]))
+        mine, strip_pieces = lax.optimization_barrier((join([weight, first, second]), strip_pieces))
     even, odd = activate(
         groups * held, affine, strip_pieces, held, row_count + 2, col_count, entries
     )
 
-    width = channels // group_count
-    bias = lax.dynamic_slice_in_dim(conv_bias, group * width, width)[None]
-    if is_line:
-        near += [lax.ppermute(piece, "rows", flip("rows", 1)) for piece in near]
+    if is_line:
+        others = lax.ppermute(mine, "rows", flip("rows", 1))
         slots = jnp.stack([strip, strip ^ 2, strip ^ 1, strip ^ 3]) % 4
         half, other_half = (strip // 4)[None], 1 - (strip // 4)[None]
+        taps = weight.shape[0]
+        near, near_spans = [mine, others], [(0, 0), (0, taps), (1, 0), (1, taps)]
     else:
         gathered = lax.all_gather(weight, "rows", axis=1, tiled=True)
         near, far = [gathered[:, : width // 2]], [gathered[:, width // 2 :]]
+        near_spans = far_spans = [(0, 0)]
         slots = jnp.zeros((1,), jnp.int32)
         half, other_half = slots, slots + 1
     convolved = functools.partial(
-        convolve, groups * held, slots, even=even, odd=odd, bias=bias, frames=held * group_count
+        convolve, groups * held, slots, even=even, odd=odd, frames=held * group_count
     )
-    done = convolved(half, pieces=near)[0]
-    if is_line:
-        third_ends, third_middle, done = lax.optimization_barrier((third_ends, third_middle, done))
+    if is_line:
         chip = strip // CORES
         at_end = ((chip == 0) | (chip == 3)).astype(jnp.int32)[None]
-        third = pick(at_end, third_ends, third_middle)
-        far.append(third)
-        far += [lax.ppermute(piece, "rows", flip("rows", 1)) for piece in far]
-    parts = convolved(other_half, pieces=far, other=done)
+        thirds, bias = behind((third_ends, third_middle), after(bias, even))
+        third = pick(at_end, *thirds)
+    done = convolved(half, bias=bias, pieces=near, spans=near_spans)[0]
+    if is_line:
+        far = [mine, others, third, lax.ppermute(third, "rows", flip("rows", 1))]
+        far_spans = [(0, 2 * taps), (2, 0), (1, 2 * taps), (3, 0)]
+    parts = convolved(other_half, bias=bias, pieces=far, spans=far_spans, other=done)
     parts = [parts[0]] + [
         lax.ppermute(parts[d], "frames", flip("frames", d)) for d in range(1, group_count)
     ]

time: 70.9 us -> 82.2 us (1.16)
  the two profiles are of different devices: /device:TPU:0 before, /device:TPU:8 now
where the time goes in v6:
time: 82.2 us; the launch traced here: 81.7 us
  starting transfers between devices  25.9 us (32%)
  waiting for transfers between devices  22.4 us (27%)
  Pallas kernels  21 us (26%)
  local copies, waits for them, and re-layouts  11.7 us (14%)
    ppermute x9, waiting for transfers between devices, exchange(): return [lax.ppermute(block, axis, flip(axis, d)) for d in distances]  16.1 us
    ppermute x9, starting transfers between devices, exchange(): return [lax.ppermute(block, axis, flip(axis, d)) for d in distances]  11.5 us
    unnamed x36, local copies, waits for them, and re-layouts  11.1 us
    pallas_call x2, Pallas kernels, convolve(): pl.pallas_call(functools.partial(conv_kernel, spans, other is not None),...  10.1 us
    ppermute x3, waiting for transfers between devices, body(): lax.ppermute(parts[d], 'frames', flip('frames', d))  4.84 us
    ppermute x1, starting transfers between devices, body(): third_ends = lax.ppermute(second, 'rows', ends)  4.38 us
    ppermute x3, starting transfers between devices, body(): lax.ppermute(parts[d], 'frames', flip('frames', d))  3.55 us
    ppermute x1, starting transfers between devices, body(): third_middle = lax.ppermute(weight, 'rows', middle)  3.36 us
  transfers between devices with their start and end apart: 18, of which 6 were waited for; matrix products, arithmetic and copies ran while one was open for 1% of the time, Pallas kernels for 18%

profile of v6, /device:TPU:8, one launch (start us, length us, event | category | flops | bytes accessed | tf_op | source)
XLA Modules:
  0.0 81.7 jit_solution(5632355131258526024)
XLA Ops:
  0.0 1.0 %copy-done.13 = bf16[2,4,40,512]{3,2,1,0:T(8,128)(2,1)S(1)} copy-done((bf16[2,4,40,512]{3,2,1,0:T(8,128)(2,1)S(1)}, bf16[2,4,40,512]{3,2,1,0:T(8,128)(2,1)}, u32[]{:S(2)}) %copy-start.13) | copy-done | bytes 327704
  1.2 1.6 %collective-permute-start.6 = (f32[2,512]{1,0:T(2,128)S(1)}, f32[2,512]{1,0:T(2,128)S(1)}, u32[]{:S(2)}, u32[]{:S(2)}) collective-permute-start(f32[2,512]{1,0:T(2,128)S(1)} %get-tuple-element.44), channel_id=1, source_target_pairs={{0,6},{1,7},{2,4},{3,5},{4,2},{5,3},{6,0},{7,1},{8,14},{9,15},{10,... | collective-permute-start | bytes 12296 | tf_op jit(solution)/shard_map/ppermute | solution.py:29
  2.8 1.1 %collective-permute-start.5 = (f32[2,512]{1,0:T(2,128)S(1)}, f32[2,512]{1,0:T(2,128)S(1)}, u32[]{:S(2)}, u32[]{:S(2)}) collective-permute-start(f32[2,512]{1,0:T(2,128)S(1)} %get-tuple-element.44), channel_id=1, source_target_pairs={{0,4},{1,5},{2,6},{3,7},{4,0},{5,1},{6,2},{7,3},{8,12},{9,13},{10,... | collective-permute-start | bytes 12296 | tf_op jit(solution)/shard_map/ppermute | solution.py:29
  3.9 1.4 %collective-permute-start.4 = (f32[2,512]{1,0:T(2,128)S(1)}, f32[2,512]{1,0:T(2,128)S(1)}, u32[]{:S(2)}, u32[]{:S(2)}) collective-permute-start(f32[2,512]{1,0:T(2,128)S(1)} %get-tuple-element.44), channel_id=1, source_target_pairs={{0,2},{1,3},{2,0},{3,1},{4,6},{5,7},{6,4},{7,5},{8,10},{9,11},{10,... | collective-permute-start | bytes 12296 | tf_op jit(solution)/shard_map/ppermute | solution.py:29
  5.3 2.6 %collective-permute-start.1 = (bf16[2,1,40,512]{3,2,1,0:T(8,128)(2,1)S(1)}, bf16[2,1,40,512]{3,2,1,0:T(8,128)(2,1)S(1)}, u32[]{:S(2)}, u32[]{:S(2)}) collective-permute-start(bf16[2,1,40,512]{3,2,1,0:T(8,128)(2,1)S(1)} %get-tuple-element.36), channel_id=1, source_target_pairs={{1,2},{3,4},{5,6},{2,1},{4,3},{6,5},{9,10},{11,12},{13,14},{10,9},... | collective-permute-start | bytes 245768 | tf_op jit(solution)/shard_map/ppermute | solution.py:384
  9.6 1.5 %collective-permute-done.1.facing_ref = bf16[2,1,40,512]{3,2,1,0:T(8,128)(2,1)S(1)} collective-permute-done((bf16[2,1,40,512]{3,2,1,0:T(8,128)(2,1)S(1)}, bf16[2,1,40,512]{3,2,1,0:T(8,128)(2,1)S(1)}, u32[]{:S(2)}, u32[]{:S(2)}) %collective-permute-start.1) | collective-permute-done | bytes 81952 | tf_op jit(solution)/shard_map/ppermute | solution.py:384
  11.0 2.9 %collective-permute-start.3 = (bf16[27,16,512]{2,1,0:T(8,128)(2,1)}, bf16[27,16,512]{2,1,0:T(8,128)(2,1)}, u32[]{:S(2)}, u32[]{:S(2)}) collective-permute-start(bf16[27,16,512]{2,1,0:T(8,128)(2,1)} %bitcast.12.refs_0_), channel_id=1, source_target_pairs={{0,4},{1,5},{2,6},{3,7},{4,0},{5,1},{6,2},{7,3},{8,12},{9,13},{10,... | collective-permute-start | bytes 1327112 | tf_op jit(solution)/shard_map/ppermute | solution.py:29
  14.8 1.6 %collective-permute-start.8 = (bf16[496,512]{1,0:T(8,128)(2,1)S(1)}, bf16[496,512]{1,0:T(8,128)(2,1)S(1)}, u32[]{:S(2)}, u32[]{:S(2)}) collective-permute-start(bf16[496,512]{1,0:T(8,128)(2,1)S(1)} %shard_map.58.refs_0_), channel_id=1, source_target_pairs={{0,8},{8,0},{16,24},{24,16},{1,9},{9,1},{17,25},{25,17},{2,10},{10... | collective-permute-start | bytes 1523720 | tf_op jit(solution)/shard_map/ppermute | solution.py:29
  16.3 1.5 %collective-permute-start.9 = (bf16[496,512]{1,0:T(8,128)(2,1)S(1)}, bf16[496,512]{1,0:T(8,128)(2,1)S(1)}, u32[]{:S(2)}, u32[]{:S(2)}) collective-permute-start(bf16[496,512]{1,0:T(8,128)(2,1)S(1)} %shard_map.58.refs_0_), channel_id=1, source_target_pairs={{0,16},{8,24},{16,0},{24,8},{1,17},{9,25},{17,1},{25,9},{2,18},{10... | collective-permute-start | bytes 1523720 | tf_op jit(solution)/shard_map/ppermute | solution.py:29
  18.3 12.7 %collective-permute-done.2.refs_1_ = bf16[27,16,512]{2,1,0:T(8,128)(2,1)S(1)} collective-permute-done((bf16[27,16,512]{2,1,0:T(8,128)(2,1)}, bf16[27,16,512]{2,1,0:T(8,128)(2,1)S(1)}, u32[]{:S(2)}, u32[]{:S(2)}) %collective-permute-start.2) | collective-permute-done | bytes 442400 | tf_op jit(solution)/shard_map/ppermute | solution.py:29
  31.0 3.4 %collective-permute-done.3.refs_2_ = bf16[27,16,512]{2,1,0:T(8,128)(2,1)} collective-permute-done((bf16[27,16,512]{2,1,0:T(8,128)(2,1)}, bf16[27,16,512]{2,1,0:T(8,128)(2,1)}, u32[]{:S(2)}, u32[]{:S(2)}) %collective-permute-start.3) | collective-permute-done | bytes 442400 | tf_op jit(solution)/shard_map/ppermute | solution.py:29
  34.4 1.2 %shard_map.56.in_ref = f32[1,128]{1,0:T(1,128)} custom-call(f32[1,128]{1,0:T(1,128)} %dynamic-slice_bitcast_fusion.in_ref), custom_call_target="tpu_custom_call" | custom-call | flops 10000000000 | tf_op jit(solution)/shard_map/pallas_call | solution.py:135
  35.6 4.4 %collective-permute-start.11 = (bf16[27,16,512]{2,1,0:T(8,128)(2,1)}, bf16[27,16,512]{2,1,0:T(8,128)(2,1)}, u32[]{:S(2)}, u32[]{:S(2)}) collective-permute-start(bf16[27,16,512]{2,1,0:T(8,128)(2,1)} %collective-permute-done.3.refs_2_), channel_id=1, source_target_pairs={{2,0},{3,1},{4,6},{5,7},{10,8},{11,9},{12,14},{13,15},{18,16},{19,... | collective-permute-start | bytes 1327112 | tf_op jit(solution)/shard_map/ppermute | solution.py:408
  40.0 3.4 %collective-permute-start.12 = (bf16[27,16,512]{2,1,0:T(8,128)(2,1)}, bf16[27,16,512]{2,1,0:T(8,128)(2,1)}, u32[]{:S(2)}, u32[]{:S(2)}) collective-permute-start(bf16[27,16,512]{2,1,0:T(8,128)(2,1)} %bitcast.12.refs_0_), channel_id=1, source_target_pairs={{2,4},{3,5},{4,2},{5,3},{10,12},{11,13},{12,10},{13,11},{18,20},{1... | collective-permute-start | bytes 1327112 | tf_op jit(solution)/shard_map/ppermute | solution.py:409
  43.5 1.0 %copy-done.12 = bf16[27,16,512]{2,1,0:T(8,128)(2,1)S(1)} copy-done((bf16[27,16,512]{2,1,0:T(8,128)(2,1)S(1)}, bf16[27,16,512]{2,1,0:T(8,128)(2,1)}, u32[]{:S(2)}) %copy-start.12) | copy-done | bytes 442392
  44.5 1.2 %shard_map.57.refs_0_ = bf16[81,16,512]{2,1,0:T(8,128)(2,1)S(1)} custom-call(bf16[27,16,512]{2,1,0:T(8,128)(2,1)} %bitcast.12.refs_0_, bf16[27,16,512]{2,1,0:T(8,128)(2,1)S(1)} %copy-done.12, bf16[27,16,512]{2,1,0:T(8,128)(2,1)} %collective-permute-done.3.refs_2_), custom_call_target="tpu_custom_call" | custom-call | tf_op jit(solution)/shard_map/pallas_call | solution.py:155
  48.2 1.0 %copy-done.6 = bf16[496,512]{1,0:T(8,128)(2,1)S(1)} copy-done((bf16[496,512]{1,0:T(8,128)(2,1)S(1)}, bf16[496,512]{1,0:T(8,128)(2,1)}, u32[]{:S(2)}) %copy-start.6) | copy-done | bytes 507928
  49.2 1.0 %copy-done.8 = bf16[496,512]{1,0:T(8,128)(2,1)S(1)} copy-done((bf16[496,512]{1,0:T(8,128)(2,1)S(1)}, bf16[496,512]{1,0:T(8,128)(2,1)}, u32[]{:S(2)}) %copy-start.8) | copy-done | bytes 507928
  50.3 1.0 %copy-done.10 = bf16[496,512]{1,0:T(8,128)(2,1)S(1)} copy-done((bf16[496,512]{1,0:T(8,128)(2,1)S(1)}, bf16[496,512]{1,0:T(8,128)(2,1)}, u32[]{:S(2)}) %copy-start.10) | copy-done | bytes 507928
  51.3 3.2 %shard_map.59 = (bf16[6,336,512]{2,1,0:T(8,128)(2,1)S(1)}, bf16[6,320,512]{2,1,0:T(8,128)(2,1)S(1)}) custom-call(s32[4]{0:T(128)S(1)} %get-tuple-element.67.place_ref, f32[2,512]{1,0:T(2,128)S(1)} %pad_maximum_fusion.affine_ref, bf16[496,512]{1,0:T(8,128)(2,1)S(1)} %copy-done.4, bf16[496,512]{1,0:T(8,128)(2,1)S(1)} %copy-done.6, ...), custom_call_target="tpu_custom_call" | custom-call | flops 512 | bytes 512 | tf_op jit(solution)/shard_map/pallas_call | solution.py:249
  54.5 1.3 %copy-done.1 = bf16[6,320,512]{2,1,0:T(8,128)(2,1)} copy-done((bf16[6,320,512]{2,1,0:T(8,128)(2,1)}, bf16[6,320,512]{2,1,0:T(8,128)(2,1)S(1)}, u32[]{:S(2)}) %copy-start.1) | copy-done | bytes 1966104
  55.9 1.2 %shard_map.60.bias_ref = f32[1,128]{1,0:T(1,128)} custom-call(f32[1,128]{1,0:T(1,128)} %shard_map.56.in_ref), custom_call_target="tpu_custom_call" | custom-call | flops 10000000000 | tf_op jit(solution)/shard_map/pallas_call | solution.py:135
  57.1 1.9 %shard_map.61.refs_2_ = bf16[27,16,512]{2,1,0:T(8,128)(2,1)} custom-call(s32[1]{0:T(128)} %bitcast.17.which_ref, bf16[27,16,512]{2,1,0:T(8,128)(2,1)} %collective-permute-done.11.one_ref, bf16[27,16,512]{2,1,0:T(8,128)(2,1)} %collective-permute-done.12.other_ref), custom_call_target="tpu_custom_call" | custom-call | bytes 221184 | tf_op jit(solution)/shard_map/pallas_call | solution.py:175
  59.6 1.5 %copy-done.2 = bf16[6,320,512]{2,1,0:T(8,128)(2,1)S(1)} copy-done((bf16[6,320,512]{2,1,0:T(8,128)(2,1)S(1)}, bf16[6,320,512]{2,1,0:T(8,128)(2,1)}, u32[]{:S(2)}) %copy-start.2) | copy-done | bytes 1966104
  61.8 5.0 %shard_map.62.refs_4_ = bf16[8,160,128]{2,1,0:T(8,128)(2,1)S(1)} custom-call(s32[4]{0:T(128)S(1)} %get-tuple-element.67.place_ref, s32[4]{0:T(128)S(1)} %and_select_fusion.slot_ref, s32[1]{0:T(128)} %bitcast.8.half_ref, bf16[6,336,512]{2,1,0:T(8,128)(2,1)S(1)} %get-tuple-element.50.even_ref, bf16[6,320,512]{2,1,0:T(8,128)(2,1)S(1)} %copy-done.2, ...), custom_call_target="tpu_custom_call" | custom-call | flops 512 | bytes 512 | tf_op jit(solution)/shard_map/pallas_call | solution.py:334
  66.8 5.2 %shard_map.63 = (bf16[2,160,128]{2,1,0:T(8,128)(2,1)S(1)}, bf16[2,160,128]{2,1,0:T(8,128)(2,1)S(1)}, bf16[2,160,128]{2,1,0:T(8,128)(2,1)S(1)}, bf16[2,160,128]{2,1,0:T(8,128)(2,1)S(1)}) custom-call(s32[4]{0:T(128)S(1)} %get-tuple-element.67.place_ref, s32[4]{0:T(128)S(1)} %and_select_fusion.slot_ref, s32[1]{0:T(128)S(6)} %sub.43.half_ref, ...), custom_call_target="tpu_custom_call" | custom-call | flops 512 | bytes 512 | tf_op jit(solution)/shard_map/pallas_call | solution.py:334
  72.0 1.6 %collective-permute-start.15 = (bf16[2,160,128]{2,1,0:T(8,128)(2,1)S(1)}, bf16[2,160,128]{2,1,0:T(8,128)(2,1)S(1)}, u32[]{:S(2)}, u32[]{:S(2)}) collective-permute-start(bf16[2,160,128]{2,1,0:T(8,128)(2,1)S(1)} %get-tuple-element.62), channel_id=1, source_target_pairs={{0,8},{8,0},{16,24},{24,16},{1,9},{9,1},{17,25},{25,17},{2,10},{10... | collective-permute-start | bytes 245768 | tf_op jit(solution)/shard_map/ppermute | solution.py:450
  73.5 1.5 %collective-permute-start.16 = (bf16[2,160,128]{2,1,0:T(8,128)(2,1)S(1)}, bf16[2,160,128]{2,1,0:T(8,128)(2,1)S(1)}, u32[]{:S(2)}, u32[]{:S(2)}) collective-permute-start(bf16[2,160,128]{2,1,0:T(8,128)(2,1)S(1)} %get-tuple-element.63), channel_id=1, source_target_pairs={{0,16},{8,24},{16,0},{24,8},{1,17},{9,25},{17,1},{25,9},{2,18},{10... | collective-permute-start | bytes 245768 | tf_op jit(solution)/shard_map/ppermute | solution.py:450
  75.5 1.0 %collective-permute-done.15.refs_1_ = bf16[2,160,128]{2,1,0:T(8,128)(2,1)S(1)} collective-permute-done((bf16[2,160,128]{2,1,0:T(8,128)(2,1)S(1)}, bf16[2,160,128]{2,1,0:T(8,128)(2,1)S(1)}, u32[]{:S(2)}, u32[]{:S(2)}) %collective-permute-start.15) | collective-permute-done | bytes 81952 | tf_op jit(solution)/shard_map/ppermute | solution.py:450
  76.5 1.5 %collective-permute-done.16.refs_2_ = bf16[2,160,128]{2,1,0:T(8,128)(2,1)S(1)} collective-permute-done((bf16[2,160,128]{2,1,0:T(8,128)(2,1)S(1)}, bf16[2,160,128]{2,1,0:T(8,128)(2,1)S(1)}, u32[]{:S(2)}, u32[]{:S(2)}) %collective-permute-start.16) | collective-permute-done | bytes 81952 | tf_op jit(solution)/shard_map/ppermute | solution.py:450
  78.0 2.4 %collective-permute-done.17.refs_3_ = bf16[2,160,128]{2,1,0:T(8,128)(2,1)S(1)} collective-permute-done((bf16[2,160,128]{2,1,0:T(8,128)(2,1)S(1)}, bf16[2,160,128]{2,1,0:T(8,128)(2,1)S(1)}, u32[]{:S(2)}, u32[]{:S(2)}) %collective-permute-start.17) | collective-permute-done | bytes 81952 | tf_op jit(solution)/shard_map/ppermute | solution.py:450
  80.4 1.3 %shard_map.64 = bf16[2,160,512]{2,1,0:T(8,128)(2,1)} custom-call(s32[4]{0:T(128)S(1)} %get-tuple-element.68.place_ref, bf16[2,160,128]{2,1,0:T(8,128)(2,1)S(1)} %get-tuple-element.61.refs_0_, bf16[2,160,128]{2,1,0:T(8,128)(2,1)S(1)} %collective-permute-done.15.refs_1_, bf16[2,160,128]{2,1,0:T(8,128)(2,1)S(1)} %collective-permute-done.16.refs_2_, ...), custom_call_target="tpu_custom_call" | custom-call | tf_op jit(solution)/shard_map/pallas_call | solution.py:361
  (59 shorter events, 7.3 us)
Async XLA Ops:
  0.0 8.0 %copy-start = (f32[512]{0:T(512)S(1)}, f32[512]{0:T(512)}, u32[]{:S(2)}) copy-start(f32[512]{0:T(512)} %param.9) | copy-start | bytes 6148
  0.0 1.0 %copy-start.13 = (bf16[2,4,40,512]{3,2,1,0:T(8,128)(2,1)S(1)}, bf16[2,4,40,512]{3,2,1,0:T(8,128)(2,1)}, u32[]{:S(2)}) copy-start(bf16[2,4,40,512]{3,2,1,0:T(8,128)(2,1)} %x_ref.1) | copy-start | bytes 983044
  1.2 7.4 %collective-permute-start.6 = (f32[2,512]{1,0:T(2,128)S(1)}, f32[2,512]{1,0:T(2,128)S(1)}, u32[]{:S(2)}, u32[]{:S(2)}) collective-permute-start(f32[2,512]{1,0:T(2,128)S(1)} %get-tuple-element.44), channel_id=1, source_target_pairs={{0,6},{1,7},{2,4},{3,5},{4,2},{5,3},{6,0},{7,1},{8,14},{9,15},{10,... | collective-permute-start | bytes 12296 | tf_op jit(solution)/shard_map/ppermute | solution.py:29
  2.8 5.8 %collective-permute-start.5 = (f32[2,512]{1,0:T(2,128)S(1)}, f32[2,512]{1,0:T(2,128)S(1)}, u32[]{:S(2)}, u32[]{:S(2)}) collective-permute-start(f32[2,512]{1,0:T(2,128)S(1)} %get-tuple-element.44), channel_id=1, source_target_pairs={{0,4},{1,5},{2,6},{3,7},{4,0},{5,1},{6,2},{7,3},{8,12},{9,13},{10,... | collective-permute-start | bytes 12296 | tf_op jit(solution)/shard_map/ppermute | solution.py:29
  3.9 4.7 %collective-permute-start.4 = (f32[2,512]{1,0:T(2,128)S(1)}, f32[2,512]{1,0:T(2,128)S(1)}, u32[]{:S(2)}, u32[]{:S(2)}) collective-permute-start(f32[2,512]{1,0:T(2,128)S(1)} %get-tuple-element.44), channel_id=1, source_target_pairs={{0,2},{1,3},{2,0},{3,1},{4,6},{5,7},{6,4},{7,5},{8,10},{9,11},{10,... | collective-permute-start | bytes 12296 | tf_op jit(solution)/shard_map/ppermute | solution.py:29
  5.3 4.3 %collective-permute-start = (bf16[2,1,40,512]{3,2,1,0:T(8,128)(2,1)S(1)}, bf16[2,1,40,512]{3,2,1,0:T(8,128)(2,1)S(1)}, u32[]{:S(2)}, u32[]{:S(2)}) collective-permute-start(bf16[2,1,40,512]{3,2,1,0:T(8,128)(2,1)S(1)} %get-tuple-element.35), channel_id=1, source_target_pairs={{0,1},{1,0},{2,3},{3,2},{4,5},{5,4},{6,7},{7,6},{8,9},{9,8},{10,11... | collective-permute-start | bytes 245768 | tf_op jit(solution)/shard_map/ppermute | solution.py:382
  5.3 5.7 %collective-permute-start.1 = (bf16[2,1,40,512]{3,2,1,0:T(8,128)(2,1)S(1)}, bf16[2,1,40,512]{3,2,1,0:T(8,128)(2,1)S(1)}, u32[]{:S(2)}, u32[]{:S(2)}) collective-permute-start(bf16[2,1,40,512]{3,2,1,0:T(8,128)(2,1)S(1)} %get-tuple-element.36), channel_id=1, source_target_pairs={{1,2},{3,4},{5,6},{2,1},{4,3},{6,5},{9,10},{11,12},{13,14},{10,9},... | collective-permute-start | bytes 245768 | tf_op jit(solution)/shard_map/ppermute | solution.py:384
  8.7 5.4 %collective-permute-start.7 = (f32[2,512]{1,0:T(2,128)S(1)}, f32[2,512]{1,0:T(2,128)S(1)}, u32[]{:S(2)}, u32[]{:S(2)}) collective-permute-start(f32[2,512]{1,0:T(2,128)S(1)} %pad_maximum_fusion.1), channel_id=1, source_target_pairs={{0,1},{1,0},{2,3},{3,2},{4,5},{5,4},{6,7},{7,6},{8,9},{9,8},{10,11... | collective-permute-start | bytes 12296 | tf_op jit(solution)/shard_map/ppermute | solution.py:29
  11.0 20.0 %collective-permute-start.2 = (bf16[27,16,512]{2,1,0:T(8,128)(2,1)}, bf16[27,16,512]{2,1,0:T(8,128)(2,1)S(1)}, u32[]{:S(2)}, u32[]{:S(2)}) collective-permute-start(bf16[27,16,512]{2,1,0:T(8,128)(2,1)} %bitcast.12.refs_0_), channel_id=1, source_target_pairs={{0,2},{1,3},{2,0},{3,1},{4,6},{5,7},{6,4},{7,5},{8,10},{9,11},{10,... | collective-permute-start | bytes 1327112 | tf_op jit(solution)/shard_map/ppermute | solution.py:29
  11.0 23.4 %collective-permute-start.3 = (bf16[27,16,512]{2,1,0:T(8,128)(2,1)}, bf16[27,16,512]{2,1,0:T(8,128)(2,1)}, u32[]{:S(2)}, u32[]{:S(2)}) collective-permute-start(bf16[27,16,512]{2,1,0:T(8,128)(2,1)} %bitcast.12.refs_0_), channel_id=1, source_target_pairs={{0,4},{1,5},{2,6},{3,7},{4,0},{5,1},{6,2},{7,3},{8,12},{9,13},{10,... | collective-permute-start | bytes 1327112 | tf_op jit(solution)/shard_map/ppermute | solution.py:29
  14.7 20.9 %copy-start.3 = (bf16[496,512]{1,0:T(8,128)(2,1)}, bf16[496,512]{1,0:T(8,128)(2,1)S(1)}, u32[]{:S(2)}) copy-start(bf16[496,512]{1,0:T(8,128)(2,1)S(1)} %shard_map.58.refs_0_) | copy-start | bytes 1523716
  14.8 28.7 %copy-start.16 = (f32[512]{0:T(512)S(1)}, f32[512]{0:T(512)}, u32[]{:S(2)}) copy-start(f32[512]{0:T(512)} %param.7) | copy-start | bytes 6148
  14.8 28.7 %copy-start.17 = (f32[512]{0:T(512)S(1)}, f32[512]{0:T(512)}, u32[]{:S(2)}) copy-start(f32[512]{0:T(512)} %param.6) | copy-start | bytes 6148
  14.8 31.0 %collective-permute-start.8 = (bf16[496,512]{1,0:T(8,128)(2,1)S(1)}, bf16[496,512]{1,0:T(8,128)(2,1)S(1)}, u32[]{:S(2)}, u32[]{:S(2)}) collective-permute-start(bf16[496,512]{1,0:T(8,128)(2,1)S(1)} %shard_map.58.refs_0_), channel_id=1, source_target_pairs={{0,8},{8,0},{16,24},{24,16},{1,9},{9,1},{17,25},{25,17},{2,10},{10... | collective-permute-start | bytes 1523720 | tf_op jit(solution)/shard_map/ppermute | solution.py:29
  16.3 30.3 %collective-permute-start.9 = (bf16[496,512]{1,0:T(8,128)(2,1)S(1)}, bf16[496,512]{1,0:T(8,128)(2,1)S(1)}, u32[]{:S(2)}, u32[]{:S(2)}) collective-permute-start(bf16[496,512]{1,0:T(8,128)(2,1)S(1)} %shard_map.58.refs_0_), channel_id=1, source_target_pairs={{0,16},{8,24},{16,0},{24,8},{1,17},{9,25},{17,1},{25,9},{2,18},{10... | collective-permute-start | bytes 1523720 | tf_op jit(solution)/shard_map/ppermute | solution.py:29
  17.9 29.6 %collective-permute-start.10 = (bf16[496,512]{1,0:T(8,128)(2,1)S(1)}, bf16[496,512]{1,0:T(8,128)(2,1)S(1)}, u32[]{:S(2)}, u32[]{:S(2)}) collective-permute-start(bf16[496,512]{1,0:T(8,128)(2,1)S(1)} %shard_map.58.refs_0_), channel_id=1, source_target_pairs={{0,24},{8,16},{16,8},{24,0},{1,25},{9,17},{17,9},{25,1},{2,26},{10... | collective-permute-start | bytes 1523720 | tf_op jit(solution)/shard_map/ppermute | solution.py:29
  31.0 4.6 %copy-start.11 = (bf16[27,16,512]{2,1,0:T(8,128)(2,1)}, bf16[27,16,512]{2,1,0:T(8,128)(2,1)S(1)}, u32[]{:S(2)}) copy-start(bf16[27,16,512]{2,1,0:T(8,128)(2,1)S(1)} %collective-permute-done.2.refs_1_) | copy-start | bytes 1327108
  35.6 20.2 %collective-permute-start.11 = (bf16[27,16,512]{2,1,0:T(8,128)(2,1)}, bf16[27,16,512]{2,1,0:T(8,128)(2,1)}, u32[]{:S(2)}, u32[]{:S(2)}) collective-permute-start(bf16[27,16,512]{2,1,0:T(8,128)(2,1)} %collective-permute-done.3.refs_2_), channel_id=1, source_target_pairs={{2,0},{3,1},{4,6},{5,7},{10,8},{11,9},{12,14},{13,15},{18,16},{19,... | collective-permute-start | bytes 1327112 | tf_op jit(solution)/shard_map/ppermute | solution.py:408
  40.0 15.9 %collective-permute-start.12 = (bf16[27,16,512]{2,1,0:T(8,128)(2,1)}, bf16[27,16,512]{2,1,0:T(8,128)(2,1)}, u32[]{:S(2)}, u32[]{:S(2)}) collective-permute-start(bf16[27,16,512]{2,1,0:T(8,128)(2,1)} %bitcast.12.refs_0_), channel_id=1, source_target_pairs={{2,4},{3,5},{4,2},{5,3},{10,12},{11,13},{12,10},{13,11},{18,20},{1... | collective-permute-start | bytes 1327112 | tf_op jit(solution)/shard_map/ppermute | solution.py:409
  43.4 4.8 %copy-start.4 = (bf16[496,512]{1,0:T(8,128)(2,1)S(1)}, bf16[496,512]{1,0:T(8,128)(2,1)}, u32[]{:S(2)}) copy-start(bf16[496,512]{1,0:T(8,128)(2,1)} %copy-done.3) | copy-start | bytes 1523716
  43.5 1.1 %copy-start.12 = (bf16[27,16,512]{2,1,0:T(8,128)(2,1)S(1)}, bf16[27,16,512]{2,1,0:T(8,128)(2,1)}, u32[]{:S(2)}) copy-start(bf16[27,16,512]{2,1,0:T(8,128)(2,1)} %copy-done.11) | copy-start | bytes 1327108
  48.2 1.0 %copy-start.6 = (bf16[496,512]{1,0:T(8,128)(2,1)S(1)}, bf16[496,512]{1,0:T(8,128)(2,1)}, u32[]{:S(2)}) copy-start(bf16[496,512]{1,0:T(8,128)(2,1)} %copy-done.5) | copy-start | bytes 1523716
  49.2 1.0 %copy-start.8 = (bf16[496,512]{1,0:T(8,128)(2,1)S(1)}, bf16[496,512]{1,0:T(8,128)(2,1)}, u32[]{:S(2)}) copy-start(bf16[496,512]{1,0:T(8,128)(2,1)} %copy-done.7) | copy-start | bytes 1523716
  50.3 1.0 %copy-start.10 = (bf16[496,512]{1,0:T(8,128)(2,1)S(1)}, bf16[496,512]{1,0:T(8,128)(2,1)}, u32[]{:S(2)}) copy-start(bf16[496,512]{1,0:T(8,128)(2,1)} %copy-done.9) | copy-start | bytes 1523716
  54.5 1.3 %copy-start.1 = (bf16[6,320,512]{2,1,0:T(8,128)(2,1)}, bf16[6,320,512]{2,1,0:T(8,128)(2,1)S(1)}, u32[]{:S(2)}) copy-start(bf16[6,320,512]{2,1,0:T(8,128)(2,1)S(1)} %get-tuple-element.51.odd_ref) | copy-start | bytes 5898244
  55.8 3.7 %collective-permute-start.13 = (bf16[81,16,512]{2,1,0:T(8,128)(2,1)S(1)}, bf16[81,16,512]{2,1,0:T(8,128)(2,1)}, u32[]{:S(2)}, u32[]{:S(2)}) collective-permute-start(bf16[81,16,512]{2,1,0:T(8,128)(2,1)S(1)} %shard_map.57.refs_0_), channel_id=1, source_target_pairs={{0,1},{1,0},{2,3},{3,2},{4,5},{5,4},{6,7},{7,6},{8,9},{9,8},{10,11... | collective-permute-start | bytes 3981320 | tf_op jit(solution)/shard_map/ppermute | solution.py:425
  59.0 7.8 %collective-permute-start.14 = (bf16[27,16,512]{2,1,0:T(8,128)(2,1)}, bf16[27,16,512]{2,1,0:T(8,128)(2,1)}, u32[]{:S(2)}, u32[]{:S(2)}) collective-permute-start(bf16[27,16,512]{2,1,0:T(8,128)(2,1)} %shard_map.61.refs_2_), channel_id=1, source_target_pairs={{0,1},{1,0},{2,3},{3,2},{4,5},{5,4},{6,7},{7,6},{8,9},{9,8},{10,11... | collective-permute-start | bytes 1327112 | tf_op jit(solution)/shard_map/ppermute | solution.py:446
  59.6 1.5 %copy-start.2 = (bf16[6,320,512]{2,1,0:T(8,128)(2,1)S(1)}, bf16[6,320,512]{2,1,0:T(8,128)(2,1)}, u32[]{:S(2)}) copy-start(bf16[6,320,512]{2,1,0:T(8,128)(2,1)} %copy-done.1) | copy-start | bytes 5898244
  61.8 5.0 %copy-start.15 = (f32[1,128]{1,0:T(1,128)S(1)}, f32[1,128]{1,0:T(1,128)}, u32[]{:S(2)}) copy-start(f32[1,128]{1,0:T(1,128)} %shard_map.60.bias_ref) | copy-start | bytes 1540
  72.0 4.5 %collective-permute-start.15 = (bf16[2,160,128]{2,1,0:T(8,128)(2,1)S(1)}, bf16[2,160,128]{2,1,0:T(8,128)(2,1)S(1)}, u32[]{:S(2)}, u32[]{:S(2)}) collective-permute-start(bf16[2,160,128]{2,1,0:T(8,128)(2,1)S(1)} %get-tuple-element.62), channel_id=1, source_target_pairs={{0,8},{8,0},{16,24},{24,16},{1,9},{9,1},{17,25},{25,17},{2,10},{10... | collective-permute-start | bytes 245768 | tf_op jit(solution)/shard_map/ppermute | solution.py:450
  73.5 4.4 %collective-permute-start.16 = (bf16[2,160,128]{2,1,0:T(8,128)(2,1)S(1)}, bf16[2,160,128]{2,1,0:T(8,128)(2,1)S(1)}, u32[]{:S(2)}, u32[]{:S(2)}) collective-permute-start(bf16[2,160,128]{2,1,0:T(8,128)(2,1)S(1)} %get-tuple-element.63), channel_id=1, source_target_pairs={{0,16},{8,24},{16,0},{24,8},{1,17},{9,25},{17,1},{25,9},{2,18},{10... | collective-permute-start | bytes 245768 | tf_op jit(solution)/shard_map/ppermute | solution.py:450
  75.0 5.3 %collective-permute-start.17 = (bf16[2,160,128]{2,1,0:T(8,128)(2,1)S(1)}, bf16[2,160,128]{2,1,0:T(8,128)(2,1)S(1)}, u32[]{:S(2)}, u32[]{:S(2)}) collective-permute-start(bf16[2,160,128]{2,1,0:T(8,128)(2,1)S(1)} %get-tuple-element.64), channel_id=1, source_target_pairs={{0,24},{8,16},{16,8},{24,0},{1,25},{9,17},{17,9},{25,1},{2,26},{10... | collective-permute-start | bytes 245768 | tf_op jit(solution)/shard_map/ppermute | solution.py:450
  (4 other events, 3.1 us)

commit v7 on v3

--- a/solution.py
+++ b/solution.py
@@ -37,11 +37,12 @@
     return lax.optimization_barrier((block, *others))[0]
 
 
-def local_kernel(x_ref, stats_ref, top_ref, bottom_ref, payload_ref):
+def local_kernel(core_ref, x_ref, stats_ref, inner_ref, outer_ref, payload_ref):
     frames, rows, cols, channels = x_ref.shape
     entries = frames * rows * cols
-    top_ref[...] = x_ref[:, 0:1]
-    bottom_ref[...] = x_ref[:, rows - 1 : rows]
+    inner = (rows - 1) * (1 - core_ref[0])
+    inner_ref[...] = x_ref[:, pl.ds(inner, 1)]
+    outer_ref[...] = x_ref[:, pl.ds(rows - 1 - inner, 1)]
     for f in range(frames):
         start = (f * (rows + 2) + 1) * cols
         payload_ref[start : start + rows * cols, :] = x_ref[f].reshape(rows * cols, channels)
@@ -62,7 +63,7 @@
         stats_ref[1:2, lanes] = jnp.sum(total, axis=0, keepdims=True)
 
 
-def local(latents):
+def local(core, latents):
     frames, rows, cols, channels = latents.shape
     edge = jax.ShapeDtypeStruct((frames, 1, cols, channels), jnp.bfloat16)
     return pl.pallas_call(
@@ -73,10 +74,10 @@
             edge,
             jax.ShapeDtypeStruct((frames * (rows + 2) * cols + 16, channels), jnp.bfloat16),
         ),
-        in_specs=[whole],
+        in_specs=[scalars, whole],
         out_specs=(whole,) * 4,
-        compiler_params=params(8),
-    )(latents)
+        compiler_params=params(2),
+    )(core, latents)
 
 
 def merge(parts, entries):
@@ -85,21 +86,21 @@
     return jnp.stack([mean, sum(part[1] for part in parts) + apart])
 
 
-def pack_kernel(frames, rows, cols, edge_ref, stats_ref, above_ref, below_ref, _, out_ref):
+def pack_kernel(frames, rows, cols, edge_ref, stats_ref, sibling_ref, facing_ref, _, out_ref):
     count = frames * rows * cols
     for f in range(frames):
         first = f * rows * cols
         last = first + (rows - 1) * cols
-        for start, rim_ref, edge, mirror in (
-            (first, above_ref, 0, first + 2 * cols),
-            (last, below_ref, 1, last - 2 * cols),
-        ):
-
+        for start, edge, mirror in ((first, 0, first + 2 * cols), (last, 1, last - 2 * cols)):
             @pl.when(edge_ref[edge] == 0)
             def _():
-                out_ref[start : start + cols, :] = rim_ref[f, 0]
-
-            @pl.when(edge_ref[edge] != 0)
+                out_ref[start : start + cols, :] = sibling_ref[f, 0]
+
+            @pl.when(edge_ref[edge] == 1)
+            def _():
+                out_ref[start : start + cols, :] = facing_ref[f, 0]
+
+            @pl.when(edge_ref[edge] == 2)
             def _():
                 out_ref[start : start + cols, :] = out_ref[mirror : mirror + cols, :]
 
@@ -114,15 +115,15 @@
     out_ref[count:, :] = jnp.concatenate(terms, axis=0).astype(jnp.bfloat16)
 
 
-def pack(edges, stats, above, below, payload, frames, rows, cols):
+def pack(edges, stats, sibling, facing, payload, frames, rows, cols):
     return pl.pallas_call(
         functools.partial(pack_kernel, frames, rows, cols),
         out_shape=jax.ShapeDtypeStruct(payload.shape, jnp.bfloat16),
         in_specs=[scalars] + [whole] * 4,
         out_specs=whole,
         input_output_aliases={4: 0},
-        compiler_params=params(8),
-    )(edges, stats, above, below, payload)
+        compiler_params=params(2),
+    )(edges, stats, sibling, facing, payload)
 
 
 def held_kernel(in_ref, out_ref):
@@ -133,9 +134,10 @@
     return pl.pallas_call(
         held_kernel,
         out_shape=jax.ShapeDtypeStruct(block.shape, block.dtype),
-        in_specs=[pl.BlockSpec(memory_space=pl.ANY)],
-        out_specs=pl.BlockSpec(memory_space=pl.ANY),
+        in_specs=[whole],
+        out_specs=whole,
         input_output_aliases={0: 0},
+        compiler_params=params(1),
         cost_estimate=pl.CostEstimate(flops=10**10, bytes_accessed=0, transcendentals=0),
     )(block)
 
@@ -156,8 +158,8 @@
         out_shape=jax.ShapeDtypeStruct(one.shape, one.dtype),
         in_specs=[scalars] + [whole] * 2,
         out_specs=whole,
-        compiler_params=params(8),
-        cost_estimate=pl.CostEstimate(flops=10**10, bytes_accessed=one.size, transcendentals=0),
+        compiler_params=params(2),
+        cost_estimate=pl.CostEstimate(flops=0, bytes_accessed=one.size, transcendentals=0),
     )(which, one, other)
 
 
@@ -237,7 +239,7 @@
             pltpu.VMEM((2, (cols + 2) * frames, LANES), jnp.float32),
             pltpu.VMEM((3, channels), jnp.float32),
         ],
-        compiler_params=params(24),
+        compiler_params=params(4),
         cost_estimate=pl.CostEstimate(
             flops=10 * frames * rows * cols * channels,
             bytes_accessed=6 * frames * rows * cols * channels,
@@ -321,7 +323,7 @@
             pltpu.VMEM((2, rows * per_row, 2 * width), jnp.float32),
             pltpu.VMEM((frames, positions, 2 * width), jnp.bfloat16),
         ],
-        compiler_params=params(32),
+        compiler_params=params(10),
         cost_estimate=pl.CostEstimate(
             flops=2 * rows * per_row * channels * width,
             bytes_accessed=2 * channels * width,
@@ -345,7 +347,7 @@
         out_shape=jax.ShapeDtypeStruct((held, positions, width * len(pieces)), jnp.bfloat16),
         in_specs=[scalars] + [whole] * len(pieces),
         out_specs=whole,
-        compiler_params=params(8),
+        compiler_params=params(2),
     )(groups, *pieces)
 
 
@@ -359,16 +361,20 @@
     weight = conv_weight.transpose(0, 1, 2, 4, 3)
     weight = weight.reshape((-1,) + weight.shape[3:])
 
-    stats, top, bottom, payload = local(latents)
-    above = lax.ppermute(bottom, "rows", [(i, i + 1) for i in range(strips - 1)])
-    below = lax.ppermute(top, "rows", [(i + 1, i) for i in range(strips - 1)])
-
+    core = strip % CORES
+    stats, inner, outer, payload = local(core[None], latents)
+    sibling = lax.ppermute(inner, "rows", flip("rows", 1))
+    facing = [(i, i + 1) for i in range(1, strips - 1, CORES)]
+    facing = lax.ppermute(outer, "rows", facing + [(b, a) for a, b in facing])
+
+    width = channels // group_count
+    bias = lax.dynamic_slice_in_dim(conv_bias, group * width, width)[None]
     entries = held * row_count * col_count
     if is_line:
+        weight = after(weight, sibling, facing)
+        first, second = exchange(weight, "rows", [CORES, 2 * CORES])
         chips = range(CORES, strips, CORES)
         stats = merge([stats] + exchange(stats, "rows", chips), entries)
-        weight = after(weight, stats, above, below)
-        first, second = exchange(weight, "rows", [CORES, 2 * CORES])
         stats = merge([stats] + exchange(stats, "rows", [1]), 4 * entries)
         entries *= strips
     else:
@@ -386,8 +392,10 @@
         third_ends = lax.ppermute(second, "rows", ends)
         third_middle = lax.ppermute(weight, "rows", middle)
 
-    edges = jnp.stack([strip == 0, strip == strips - 1]).astype(jnp.int32)
-    payload = pack(edges, stats, above, below, payload, held, row_count + 2, col_count)
+    above = jnp.where(strip == 0, 2, 1 - core)
+    below = jnp.where(strip == strips - 1, 2, core)
+    edges = jnp.stack([above, below]).astype(jnp.int32)
+    payload = pack(edges, stats, sibling, facing, payload, held, row_count + 2, col_count)
     strip_pieces = [payload] + exchange(payload, "frames", range(1, group_count))
     groups = jnp.stack([group ^ d for d in range(group_count)]).astype(jnp.int32)
     affine = jnp.stack([norm_gain, norm_bias])
@@ -397,8 +405,6 @@
         groups * held, affine, strip_pieces, held, row_count + 2, col_count, entries
     )
 
-    width = channels // group_count
-    bias = lax.dynamic_slice_in_dim(conv_bias, group * width, width)[None]
     if is_line:
         near += [lax.ppermute(piece, "rows", flip("rows", 1)) for piece in near]
         slots = jnp.stack([strip, strip ^ 2, strip ^ 1, strip ^ 3]) % 4
@@ -409,9 +415,9 @@
         slots = jnp.zeros((1,), jnp.int32)
         half, other_half = slots, slots + 1
     convolved = functools.partial(
-        convolve, groups * held, slots, even=even, odd=odd, bias=bias, frames=held * group_count
+        convolve, groups * held, slots, even=even, odd=odd, frames=held * group_count
     )
-    done = convolved(half, pieces=near)[0]
+    done = convolved(half, bias=bias, pieces=near)[0]
     if is_line:
         third_ends, third_middle, done = lax.optimization_barrier((third_ends, third_middle, done))
         chip = strip // CORES
@@ -419,7 +425,7 @@
         third = pick(at_end, third_ends, third_middle)
         far.append(third)
         far += [lax.ppermute(piece, "rows", flip("rows", 1)) for piece in far]
-    parts = convolved(other_half, pieces=far, other=done)
+    parts = convolved(other_half, bias=bias, pieces=far, other=done)
     parts = [parts[0]] + [
         lax.ppermute(parts[d], "frames", flip("frames", d)) for d in range(1, group_count)
     ]

time: 70.9 us -> 66.6 us (0.939)
  starting transfers between devices: 24.5 us -> 21.2 us
  waiting for transfers between devices: 29.7 us -> 28.9 us
  local copies, waits for them, and re-layouts: 1.86 us -> 1.08 us
    ppermute x2, starting transfers between devices: 2.57 us -> 0.66 us  [the longest x1 0.65 us: body(): facing = lax.ppermute(outer, 'rows', facing + [(b, a) for a, b in facing])]
    ppermute x9, starting transfers between devices: 15.7 us -> 13.9 us  [exchange(): return [lax.ppermute(block, axis, flip(axis, d)) for d in distances]]
    ppermute x1, waiting for transfers between devices: 1.17 us -> 0.01 us  [body(): third_ends = lax.ppermute(second, 'rows', ends)]
    ppermute x9, waiting for transfers between devices: 21.8 us -> 22.7 us  [exchange(): return [lax.ppermute(block, axis, flip(axis, d)) for d in distances]]
    unnamed x14 -> x10, local copies, waits for them, and re-layouts: 1.78 us -> 1.01 us
  transfers between devices with their start and end apart: 20 -> 20, of which waited for: 10 -> 8; matrix products, arithmetic and copies ran while one was open for 1% -> 1% of each run, Pallas kernels for 12% -> 12%
where the time goes in v7:
time: 66.6 us; the launch traced here: 65.5 us
  waiting for transfers between devices  28.9 us (43%)
  starting transfers between devices  21.2 us (32%)
  Pallas kernels  13.8 us (21%)
  local copies, waits for them, and re-layouts  1.08 us (2%)
    ppermute x9, waiting for transfers between devices, exchange(): return [lax.ppermute(block, axis, flip(axis, d)) for d in distances]  22.7 us
    ppermute x9, starting transfers between devices, exchange(): return [lax.ppermute(block, axis, flip(axis, d)) for d in distances]  13.9 us
    pallas_call x2, Pallas kernels, convolve(): pl.pallas_call(functools.partial(conv_kernel, len(pieces), other is not N...  8.28 us
    ppermute x3, waiting for transfers between devices, body(): lax.ppermute(parts[d], 'frames', flip('frames', d))  4.76 us
    ppermute x3, starting transfers between devices, body(): lax.ppermute(parts[d], 'frames', flip('frames', d))  3.57 us
    pallas_call x1, Pallas kernels, activate(): pl.pallas_call(functools.partial(activate_kernel, held, rows, entries), o...  3.32 us
    ppermute x2, waiting for transfers between devices, body(): far += [lax.ppermute(piece, 'rows', flip('rows', 1)) for piece in far]  1.42 us
  transfers between devices with their start and end apart: 20, of which 8 were waited for; matrix products, arithmetic and copies ran while one was open for 1% of the time, Pallas kernels for 12%

profile of v7, /device:TPU:0, one launch (start us, length us, event | category | flops | bytes accessed | tf_op | source)
XLA Modules:
  0.0 65.5 jit_solution(4270441672342448030)
XLA Ops:
  0.0 1.0 %copy-done.2 = bf16[2,4,40,512]{3,2,1,0:T(8,128)(2,1)S(1)} copy-done((bf16[2,4,40,512]{3,2,1,0:T(8,128)(2,1)S(1)}, bf16[2,4,40,512]{3,2,1,0:T(8,128)(2,1)}, u32[]{:S(2)}) %copy-start.2) | copy-done | bytes 327704
  1.0 0.2 shard_map.55
  1.2 3.1 %collective-permute-start.4 = (f32[2,512]{1,0:T(2,128)S(1)}, f32[2,512]{1,0:T(2,128)S(1)}, u32[]{:S(2)}, u32[]{:S(2)}) collective-permute-start(f32[2,512]{1,0:T(2,128)S(1)} %get-tuple-element.34), channel_id=1, source_target_pairs={{0,2},{1,3},{2,0},{3,1},{4,6},{5,7},{6,4},{7,5},{8,10},{9,11},{10,... | collective-permute-start | bytes 12296 | tf_op jit(solution)/shard_map/ppermute | solution.py:29
  4.3 2.6 %collective-permute-start.5 = (f32[2,512]{1,0:T(2,128)S(1)}, f32[2,512]{1,0:T(2,128)S(1)}, u32[]{:S(2)}, u32[]{:S(2)}) collective-permute-start(f32[2,512]{1,0:T(2,128)S(1)} %get-tuple-element.34), channel_id=1, source_target_pairs={{0,4},{1,5},{2,6},{3,7},{4,0},{5,1},{6,2},{7,3},{8,12},{9,13},{10,... | collective-permute-start | bytes 12296 | tf_op jit(solution)/shard_map/ppermute | solution.py:29
  6.9 0.7 collective-permute-start.1
  7.5 1.2 %collective-permute-done.5 = f32[2,512]{1,0:T(2,128)S(1)} collective-permute-done((f32[2,512]{1,0:T(2,128)S(1)}, f32[2,512]{1,0:T(2,128)S(1)}, u32[]{:S(2)}, u32[]{:S(2)}) %collective-permute-start.5) | collective-permute-done | bytes 4128 | tf_op jit(solution)/shard_map/ppermute | solution.py:29
  8.8 3.5 %collective-permute-done.6 = f32[2,512]{1,0:T(2,128)S(1)} collective-permute-done((f32[2,512]{1,0:T(2,128)S(1)}, f32[2,512]{1,0:T(2,128)S(1)}, u32[]{:S(2)}, u32[]{:S(2)}) %collective-permute-start.6) | collective-permute-done | bytes 4128 | tf_op jit(solution)/shard_map/ppermute | solution.py:29
  12.4 1.1 %collective-permute-start.2 = (bf16[27,16,512]{2,1,0:T(8,128)(2,1)}, bf16[27,16,512]{2,1,0:T(8,128)(2,1)S(1)}, u32[]{:S(2)}, u32[]{:S(2)}) collective-permute-start(bf16[27,16,512]{2,1,0:T(8,128)(2,1)} %bitcast.21), channel_id=1, source_target_pairs={{0,2},{1,3},{2,0},{3,1},{4,6},{5,7},{6,4},{7,5},{8,10},{9,11},{10,... | collective-permute-start | bytes 1327112 | tf_op jit(solution)/shard_map/ppermute | solution.py:29
  13.5 3.5 %collective-permute-start.3 = (bf16[27,16,512]{2,1,0:T(8,128)(2,1)}, bf16[27,16,512]{2,1,0:T(8,128)(2,1)S(1)}, u32[]{:S(2)}, u32[]{:S(2)}) collective-permute-start(bf16[27,16,512]{2,1,0:T(8,128)(2,1)} %bitcast.22), channel_id=1, source_target_pairs={{0,4},{1,5},{2,6},{3,7},{4,0},{5,1},{6,2},{7,3},{8,12},{9,13},{10,... | collective-permute-start | bytes 1327112 | tf_op jit(solution)/shard_map/ppermute | solution.py:29
  17.1 0.7 %shard_map.56.refs_0_ = bf16[496,512]{1,0:T(8,128)(2,1)S(1)} custom-call(s32[2]{0:T(128)S(1)} %pad_add_fusion.1.edge_ref, f32[2,512]{1,0:T(2,128)S(1)} %pad_maximum_fusion.2.stats_ref, bf16[2,1,40,512]{3,2,1,0:T(8,128)(2,1)S(1)} %collective-permute-done.sibling_ref, ...), custom_call_target="tpu_custom_call", output_to_operand_aliasing={{}: (4, {})} | custom-call | tf_op jit(solution)/shard_map/pallas_call | solution.py:119
  17.8 2.5 %collective-permute-start.10 = (bf16[496,512]{1,0:T(8,128)(2,1)S(1)}, bf16[496,512]{1,0:T(8,128)(2,1)S(1)}, u32[]{:S(2)}, u32[]{:S(2)}) collective-permute-start(bf16[496,512]{1,0:T(8,128)(2,1)S(1)} %shard_map.56.refs_0_), channel_id=1, source_target_pairs={{0,24},{8,16},{16,8},{24,0},{1,25},{9,17},{17,9},{25,1},{2,26},{10... | collective-permute-start | bytes 1523720 | tf_op jit(solution)/shard_map/ppermute | solution.py:29
  20.3 0.5 collective-permute-start.8
  20.8 0.5 collective-permute-start.9
  21.4 13.5 %collective-permute-done.2.refs_1_ = bf16[27,16,512]{2,1,0:T(8,128)(2,1)S(1)} collective-permute-done((bf16[27,16,512]{2,1,0:T(8,128)(2,1)}, bf16[27,16,512]{2,1,0:T(8,128)(2,1)S(1)}, u32[]{:S(2)}, u32[]{:S(2)}) %collective-permute-start.2) | collective-permute-done | bytes 442400 | tf_op jit(solution)/shard_map/ppermute | solution.py:29
  34.9 1.3 %collective-permute-start.11 = (bf16[27,16,512]{2,1,0:T(8,128)(2,1)S(1)}, bf16[27,16,512]{2,1,0:T(8,128)(2,1)S(1)}, u32[]{:S(2)}, u32[]{:S(2)}) collective-permute-start(bf16[27,16,512]{2,1,0:T(8,128)(2,1)S(1)} %shard_map.57.refs_0_), channel_id=1, source_target_pairs={{2,0},{3,1},{4,6},{5,7},{10,8},{11,9},{12,14},{13,15},{18,16},{19,... | collective-permute-start | bytes 1327112 | tf_op jit(solution)/shard_map/ppermute | solution.py:392
  36.2 0.7 %collective-permute-start.12 = (bf16[27,16,512]{2,1,0:T(8,128)(2,1)S(1)}, bf16[27,16,512]{2,1,0:T(8,128)(2,1)S(1)}, u32[]{:S(2)}, u32[]{:S(2)}) collective-permute-start(bf16[27,16,512]{2,1,0:T(8,128)(2,1)S(1)} %bitcast.23), channel_id=1, source_target_pairs={{2,4},{3,5},{4,2},{5,3},{10,12},{11,13},{12,10},{13,11},{18,20},{1... | collective-permute-start | bytes 1327112 | tf_op jit(solution)/shard_map/ppermute | solution.py:393
  36.9 4.4 %collective-permute-done.8.refs_1_ = bf16[496,512]{1,0:T(8,128)(2,1)S(1)} collective-permute-done((bf16[496,512]{1,0:T(8,128)(2,1)S(1)}, bf16[496,512]{1,0:T(8,128)(2,1)S(1)}, u32[]{:S(2)}, u32[]{:S(2)}) %collective-permute-start.8) | collective-permute-done | bytes 507936 | tf_op jit(solution)/shard_map/ppermute | solution.py:29
  41.3 0.5 collective-permute-start.14
  41.9 0.1 and_select_fusion.slot_ref
  42.0 0.1 broadcast_multiply_fusion
  42.2 3.3 %shard_map.58 = (bf16[6,336,512]{2,1,0:T(8,128)(2,1)S(1)}, bf16[6,320,512]{2,1,0:T(8,128)(2,1)S(1)}) custom-call(s32[4]{0:T(128)S(1)} %get-tuple-element.55.place_ref, f32[2,512]{1,0:T(2,128)S(1)} %pad_maximum_fusion.affine_ref, bf16[496,512]{1,0:T(8,128)(2,1)S(1)} %shard_map.56.refs_0_, bf16[496,512]{1,0:T(8,128)(2,1)S(1)} %collective-permute-done.8.refs_1_, ...), custom_call_target="tpu_custom_call" | custom-call | flops 9830400 | bytes 5898240 | tf_op jit(solution)/shard_map/pallas_call | solution.py:230
  45.5 4.2 %shard_map.59.refs_4_ = bf16[8,160,128]{2,1,0:T(8,128)(2,1)S(1)} custom-call(s32[4]{0:T(128)S(1)} %get-tuple-element.55.place_ref, s32[4]{0:T(128)S(1)} %and_select_fusion.slot_ref, s32[1]{0:T(128)} %bitcast.8.half_ref, bf16[6,336,512]{2,1,0:T(8,128)(2,1)S(1)} %get-tuple-element.41.even_ref, bf16[6,320,512]{2,1,0:T(8,128)(2,1)S(1)} %get-tuple-element.42.odd_ref, ...), custom_call_target="tpu_custom_call" | custom-call | flops 83886080 | bytes 65536 | tf_op jit(solution)/shard_map/pallas_call | solution.py:316
  49.8 0.6 collective-permute-start.16
  50.3 1.4 %collective-permute-done.16.refs_3_ = bf16[27,16,512]{2,1,0:T(8,128)(2,1)S(1)} collective-permute-done((bf16[27,16,512]{2,1,0:T(8,128)(2,1)S(1)}, bf16[27,16,512]{2,1,0:T(8,128)(2,1)S(1)}, u32[]{:S(2)}, u32[]{:S(2)}) %collective-permute-start.16) | collective-permute-done | bytes 442400 | tf_op jit(solution)/shard_map/ppermute | solution.py:427
  51.8 4.1 %shard_map.61 = (bf16[2,160,128]{2,1,0:T(8,128)(2,1)S(1)}, bf16[2,160,128]{2,1,0:T(8,128)(2,1)S(1)}, bf16[2,160,128]{2,1,0:T(8,128)(2,1)S(1)}, bf16[2,160,128]{2,1,0:T(8,128)(2,1)S(1)}) custom-call(s32[4]{0:T(128)S(1)} %get-tuple-element.55.place_ref, s32[4]{0:T(128)S(1)} %and_select_fusion.slot_ref, s32[1]{0:T(128)S(6)} %sub.43.half_ref, ...), custom_call_target="tpu_custom_call" | custom-call | flops 83886080 | bytes 65536 | tf_op jit(solution)/shard_map/pallas_call | solution.py:316
  55.9 1.6 %collective-permute-start.17 = (bf16[2,160,128]{2,1,0:T(8,128)(2,1)S(1)}, bf16[2,160,128]{2,1,0:T(8,128)(2,1)S(1)}, u32[]{:S(2)}, u32[]{:S(2)}) collective-permute-start(bf16[2,160,128]{2,1,0:T(8,128)(2,1)S(1)} %get-tuple-element.50), channel_id=1, source_target_pairs={{0,8},{8,0},{16,24},{24,16},{1,9},{9,1},{17,25},{25,17},{2,10},{10... | collective-permute-start | bytes 245768 | tf_op jit(solution)/shard_map/ppermute | solution.py:430
  57.4 1.4 %collective-permute-start.18 = (bf16[2,160,128]{2,1,0:T(8,128)(2,1)S(1)}, bf16[2,160,128]{2,1,0:T(8,128)(2,1)S(1)}, u32[]{:S(2)}, u32[]{:S(2)}) collective-permute-start(bf16[2,160,128]{2,1,0:T(8,128)(2,1)S(1)} %get-tuple-element.51), channel_id=1, source_target_pairs={{0,16},{8,24},{16,0},{24,8},{1,17},{9,25},{17,1},{25,9},{2,18},{10... | collective-permute-start | bytes 245768 | tf_op jit(solution)/shard_map/ppermute | solution.py:430
  58.9 0.6 collective-permute-start.19
  59.4 1.2 %collective-permute-done.17.refs_1_ = bf16[2,160,128]{2,1,0:T(8,128)(2,1)S(1)} collective-permute-done((bf16[2,160,128]{2,1,0:T(8,128)(2,1)S(1)}, bf16[2,160,128]{2,1,0:T(8,128)(2,1)S(1)}, u32[]{:S(2)}, u32[]{:S(2)}) %collective-permute-start.17) | collective-permute-done | bytes 81952 | tf_op jit(solution)/shard_map/ppermute | solution.py:430
  60.7 1.9 %collective-permute-done.18.refs_2_ = bf16[2,160,128]{2,1,0:T(8,128)(2,1)S(1)} collective-permute-done((bf16[2,160,128]{2,1,0:T(8,128)(2,1)S(1)}, bf16[2,160,128]{2,1,0:T(8,128)(2,1)S(1)}, u32[]{:S(2)}, u32[]{:S(2)}) %collective-permute-start.18) | collective-permute-done | bytes 81952 | tf_op jit(solution)/shard_map/ppermute | solution.py:430
  62.6 1.6 %collective-permute-done.19.refs_3_ = bf16[2,160,128]{2,1,0:T(8,128)(2,1)S(1)} collective-permute-done((bf16[2,160,128]{2,1,0:T(8,128)(2,1)S(1)}, bf16[2,160,128]{2,1,0:T(8,128)(2,1)S(1)}, u32[]{:S(2)}, u32[]{:S(2)}) %collective-permute-start.19) | collective-permute-done | bytes 81952 | tf_op jit(solution)/shard_map/ppermute | solution.py:430
  64.2 1.3 %shard_map.62 = bf16[2,160,512]{2,1,0:T(8,128)(2,1)} custom-call(s32[4]{0:T(128)S(1)} %get-tuple-element.56.place_ref, bf16[2,160,128]{2,1,0:T(8,128)(2,1)S(1)} %get-tuple-element.49.refs_0_, bf16[2,160,128]{2,1,0:T(8,128)(2,1)S(1)} %collective-permute-done.17.refs_1_, bf16[2,160,128]{2,1,0:T(8,128)(2,1)S(1)} %collective-permute-done.18.refs_2_, ...), custom_call_target="tpu_custom_call" | custom-call | tf_op jit(solution)/shard_map/pallas_call | solution.py:345
  (35 shorter events, 0.5 us)
Async XLA Ops:
  0.0 41.8 %copy-start = (f32[512]{0:T(512)S(1)}, f32[512]{0:T(512)}, u32[]{:S(2)}) copy-start(f32[512]{0:T(512)} %param.9) | copy-start | bytes 6148
  0.0 1.0 %copy-start.2 = (bf16[2,4,40,512]{3,2,1,0:T(8,128)(2,1)S(1)}, bf16[2,4,40,512]{3,2,1,0:T(8,128)(2,1)}, u32[]{:S(2)}) copy-start(bf16[2,4,40,512]{3,2,1,0:T(8,128)(2,1)} %x_ref.1) | copy-start | bytes 983044
  1.2 6.4 %collective-permute-start.4 = (f32[2,512]{1,0:T(2,128)S(1)}, f32[2,512]{1,0:T(2,128)S(1)}, u32[]{:S(2)}, u32[]{:S(2)}) collective-permute-start(f32[2,512]{1,0:T(2,128)S(1)} %get-tuple-element.34), channel_id=1, source_target_pairs={{0,2},{1,3},{2,0},{3,1},{4,6},{5,7},{6,4},{7,5},{8,10},{9,11},{10,... | collective-permute-start | bytes 12296 | tf_op jit(solution)/shard_map/ppermute | solution.py:29
  4.3 4.5 %collective-permute-start.5 = (f32[2,512]{1,0:T(2,128)S(1)}, f32[2,512]{1,0:T(2,128)S(1)}, u32[]{:S(2)}, u32[]{:S(2)}) collective-permute-start(f32[2,512]{1,0:T(2,128)S(1)} %get-tuple-element.34), channel_id=1, source_target_pairs={{0,4},{1,5},{2,6},{3,7},{4,0},{5,1},{6,2},{7,3},{8,12},{9,13},{10,... | collective-permute-start | bytes 12296 | tf_op jit(solution)/shard_map/ppermute | solution.py:29
  6.9 5.4 %collective-permute-start.6 = (f32[2,512]{1,0:T(2,128)S(1)}, f32[2,512]{1,0:T(2,128)S(1)}, u32[]{:S(2)}, u32[]{:S(2)}) collective-permute-start(f32[2,512]{1,0:T(2,128)S(1)} %get-tuple-element.34), channel_id=1, source_target_pairs={{0,6},{1,7},{2,4},{3,5},{4,2},{5,3},{6,0},{7,1},{8,14},{9,15},{10,... | collective-permute-start | bytes 12296 | tf_op jit(solution)/shard_map/ppermute | solution.py:29
  6.9 5.5 %collective-permute-start = (bf16[2,1,40,512]{3,2,1,0:T(8,128)(2,1)S(1)}, bf16[2,1,40,512]{3,2,1,0:T(8,128)(2,1)S(1)}, u32[]{:S(2)}, u32[]{:S(2)}) collective-permute-start(bf16[2,1,40,512]{3,2,1,0:T(8,128)(2,1)S(1)} %get-tuple-element.29), channel_id=1, source_target_pairs={{0,1},{1,0},{2,3},{3,2},{4,5},{5,4},{6,7},{7,6},{8,9},{9,8},{10,11... | collective-permute-start | bytes 245768 | tf_op jit(solution)/shard_map/ppermute | solution.py:366
  6.9 5.5 %collective-permute-start.1 = (bf16[2,1,40,512]{3,2,1,0:T(8,128)(2,1)S(1)}, bf16[2,1,40,512]{3,2,1,0:T(8,128)(2,1)S(1)}, u32[]{:S(2)}, u32[]{:S(2)}) collective-permute-start(bf16[2,1,40,512]{3,2,1,0:T(8,128)(2,1)S(1)} %get-tuple-element.30), channel_id=1, source_target_pairs={{1,2},{3,4},{5,6},{2,1},{4,3},{6,5},{9,10},{11,12},{13,14},{10,9},... | collective-permute-start | bytes 245768 | tf_op jit(solution)/shard_map/ppermute | solution.py:368
  12.3 4.8 %collective-permute-start.7 = (f32[2,512]{1,0:T(2,128)S(1)}, f32[2,512]{1,0:T(2,128)S(1)}, u32[]{:S(2)}, u32[]{:S(2)}) collective-permute-start(f32[2,512]{1,0:T(2,128)S(1)} %pad_maximum_fusion.1), channel_id=1, source_target_pairs={{0,1},{1,0},{2,3},{3,2},{4,5},{5,4},{6,7},{7,6},{8,9},{9,8},{10,11... | collective-permute-start | bytes 12296 | tf_op jit(solution)/shard_map/ppermute | solution.py:29
  12.4 22.5 %collective-permute-start.2 = (bf16[27,16,512]{2,1,0:T(8,128)(2,1)}, bf16[27,16,512]{2,1,0:T(8,128)(2,1)S(1)}, u32[]{:S(2)}, u32[]{:S(2)}) collective-permute-start(bf16[27,16,512]{2,1,0:T(8,128)(2,1)} %bitcast.21), channel_id=1, source_target_pairs={{0,2},{1,3},{2,0},{3,1},{4,6},{5,7},{6,4},{7,5},{8,10},{9,11},{10,... | collective-permute-start | bytes 1327112 | tf_op jit(solution)/shard_map/ppermute | solution.py:29
  13.5 21.4 %collective-permute-start.3 = (bf16[27,16,512]{2,1,0:T(8,128)(2,1)}, bf16[27,16,512]{2,1,0:T(8,128)(2,1)S(1)}, u32[]{:S(2)}, u32[]{:S(2)}) collective-permute-start(bf16[27,16,512]{2,1,0:T(8,128)(2,1)} %bitcast.22), channel_id=1, source_target_pairs={{0,4},{1,5},{2,6},{3,7},{4,0},{5,1},{6,2},{7,3},{8,12},{9,13},{10,... | collective-permute-start | bytes 1327112 | tf_op jit(solution)/shard_map/ppermute | solution.py:29
  17.8 18.4 %copy-start.1 = (bf16[3,3,3,512,16]{3,4,2,1,0:T(8,128)(2,1)S(1)}, bf16[3,3,3,512,16]{3,4,2,1,0:T(8,128)(2,1)}, u32[]{:S(2)}) copy-start(bf16[3,3,3,512,16]{3,4,2,1,0:T(8,128)(2,1)} %param.8) | copy-start | bytes 1327108
  17.8 24.3 %copy-start.3 = (f32[512]{0:T(512)S(1)}, f32[512]{0:T(512)}, u32[]{:S(2)}) copy-start(f32[512]{0:T(512)} %param.7) | copy-start | bytes 6148
  17.8 24.3 %copy-start.4 = (f32[512]{0:T(512)S(1)}, f32[512]{0:T(512)}, u32[]{:S(2)}) copy-start(f32[512]{0:T(512)} %param.6) | copy-start | bytes 6148
  17.8 19.1 %collective-permute-start.10 = (bf16[496,512]{1,0:T(8,128)(2,1)S(1)}, bf16[496,512]{1,0:T(8,128)(2,1)S(1)}, u32[]{:S(2)}, u32[]{:S(2)}) collective-permute-start(bf16[496,512]{1,0:T(8,128)(2,1)S(1)} %shard_map.56.refs_0_), channel_id=1, source_target_pairs={{0,24},{8,16},{16,8},{24,0},{1,25},{9,17},{17,9},{25,1},{2,26},{10... | collective-permute-start | bytes 1523720 | tf_op jit(solution)/shard_map/ppermute | solution.py:29
  20.3 21.0 %collective-permute-start.8 = (bf16[496,512]{1,0:T(8,128)(2,1)S(1)}, bf16[496,512]{1,0:T(8,128)(2,1)S(1)}, u32[]{:S(2)}, u32[]{:S(2)}) collective-permute-start(bf16[496,512]{1,0:T(8,128)(2,1)S(1)} %shard_map.56.refs_0_), channel_id=1, source_target_pairs={{0,8},{8,0},{16,24},{24,16},{1,9},{9,1},{17,25},{25,17},{2,10},{10... | collective-permute-start | bytes 1523720 | tf_op jit(solution)/shard_map/ppermute | solution.py:29
  20.8 20.5 %collective-permute-start.9 = (bf16[496,512]{1,0:T(8,128)(2,1)S(1)}, bf16[496,512]{1,0:T(8,128)(2,1)S(1)}, u32[]{:S(2)}, u32[]{:S(2)}) collective-permute-start(bf16[496,512]{1,0:T(8,128)(2,1)S(1)} %shard_map.56.refs_0_), channel_id=1, source_target_pairs={{0,16},{8,24},{16,0},{24,8},{1,17},{9,25},{17,1},{25,9},{2,18},{10... | collective-permute-start | bytes 1523720 | tf_op jit(solution)/shard_map/ppermute | solution.py:29
  34.9 14.8 %collective-permute-start.11 = (bf16[27,16,512]{2,1,0:T(8,128)(2,1)S(1)}, bf16[27,16,512]{2,1,0:T(8,128)(2,1)S(1)}, u32[]{:S(2)}, u32[]{:S(2)}) collective-permute-start(bf16[27,16,512]{2,1,0:T(8,128)(2,1)S(1)} %shard_map.57.refs_0_), channel_id=1, source_target_pairs={{2,0},{3,1},{4,6},{5,7},{10,8},{11,9},{12,14},{13,15},{18,16},{19,... | collective-permute-start | bytes 1327112 | tf_op jit(solution)/shard_map/ppermute | solution.py:392
  36.2 13.5 %collective-permute-start.12 = (bf16[27,16,512]{2,1,0:T(8,128)(2,1)S(1)}, bf16[27,16,512]{2,1,0:T(8,128)(2,1)S(1)}, u32[]{:S(2)}, u32[]{:S(2)}) collective-permute-start(bf16[27,16,512]{2,1,0:T(8,128)(2,1)S(1)} %bitcast.23), channel_id=1, source_target_pairs={{2,4},{3,5},{4,2},{5,3},{10,12},{11,13},{12,10},{13,11},{18,20},{1... | collective-permute-start | bytes 1327112 | tf_op jit(solution)/shard_map/ppermute | solution.py:393
  41.3 4.2 %collective-permute-start.13 = (bf16[27,16,512]{2,1,0:T(8,128)(2,1)S(1)}, bf16[27,16,512]{2,1,0:T(8,128)(2,1)S(1)}, u32[]{:S(2)}, u32[]{:S(2)}) collective-permute-start(bf16[27,16,512]{2,1,0:T(8,128)(2,1)S(1)} %bitcast.24), channel_id=1, source_target_pairs={{0,1},{1,0},{2,3},{3,2},{4,5},{5,4},{6,7},{7,6},{8,9},{9,8},{10,11... | collective-permute-start | bytes 1327112 | tf_op jit(solution)/shard_map/ppermute | solution.py:409
  41.3 4.2 %collective-permute-start.14 = (bf16[27,16,512]{2,1,0:T(8,128)(2,1)S(1)}, bf16[27,16,512]{2,1,0:T(8,128)(2,1)S(1)}, u32[]{:S(2)}, u32[]{:S(2)}) collective-permute-start(bf16[27,16,512]{2,1,0:T(8,128)(2,1)S(1)} %collective-permute-done.2.refs_1_), channel_id=1, source_target_pairs={{0,1},{1,0},{2,3},{3,2},{4,5},{5,4},{6,7},{7,6},{8,9},{9,8},{10,11... | collective-permute-start | bytes 1327112 | tf_op jit(solution)/shard_map/ppermute | solution.py:409
  42.1 8.2 %collective-permute-start.15 = (bf16[27,16,512]{2,1,0:T(8,128)(2,1)S(1)}, bf16[27,16,512]{2,1,0:T(8,128)(2,1)S(1)}, u32[]{:S(2)}, u32[]{:S(2)}) collective-permute-start(bf16[27,16,512]{2,1,0:T(8,128)(2,1)S(1)} %shard_map.57.refs_0_), channel_id=1, source_target_pairs={{0,1},{1,0},{2,3},{3,2},{4,5},{5,4},{6,7},{7,6},{8,9},{9,8},{10,11... | collective-permute-start | bytes 1327112 | tf_op jit(solution)/shard_map/ppermute | solution.py:427
  49.8 2.0 %collective-permute-start.16 = (bf16[27,16,512]{2,1,0:T(8,128)(2,1)S(1)}, bf16[27,16,512]{2,1,0:T(8,128)(2,1)S(1)}, u32[]{:S(2)}, u32[]{:S(2)}) collective-permute-start(bf16[27,16,512]{2,1,0:T(8,128)(2,1)S(1)} %shard_map.60.refs_1_), channel_id=1, source_target_pairs={{0,1},{1,0},{2,3},{3,2},{4,5},{5,4},{6,7},{7,6},{8,9},{9,8},{10,11... | collective-permute-start | bytes 1327112 | tf_op jit(solution)/shard_map/ppermute | solution.py:427
  55.9 4.8 %collective-permute-start.17 = (bf16[2,160,128]{2,1,0:T(8,128)(2,1)S(1)}, bf16[2,160,128]{2,1,0:T(8,128)(2,1)S(1)}, u32[]{:S(2)}, u32[]{:S(2)}) collective-permute-start(bf16[2,160,128]{2,1,0:T(8,128)(2,1)S(1)} %get-tuple-element.50), channel_id=1, source_target_pairs={{0,8},{8,0},{16,24},{24,16},{1,9},{9,1},{17,25},{25,17},{2,10},{10... | collective-permute-start | bytes 245768 | tf_op jit(solution)/shard_map/ppermute | solution.py:430
  57.4 5.2 %collective-permute-start.18 = (bf16[2,160,128]{2,1,0:T(8,128)(2,1)S(1)}, bf16[2,160,128]{2,1,0:T(8,128)(2,1)S(1)}, u32[]{:S(2)}, u32[]{:S(2)}) collective-permute-start(bf16[2,160,128]{2,1,0:T(8,128)(2,1)S(1)} %get-tuple-element.51), channel_id=1, source_target_pairs={{0,16},{8,24},{16,0},{24,8},{1,17},{9,25},{17,1},{25,9},{2,18},{10... | collective-permute-start | bytes 245768 | tf_op jit(solution)/shard_map/ppermute | solution.py:430
  58.9 5.3 %collective-permute-start.19 = (bf16[2,160,128]{2,1,0:T(8,128)(2,1)S(1)}, bf16[2,160,128]{2,1,0:T(8,128)(2,1)S(1)}, u32[]{:S(2)}, u32[]{:S(2)}) collective-permute-start(bf16[2,160,128]{2,1,0:T(8,128)(2,1)S(1)} %get-tuple-element.52), channel_id=1, source_target_pairs={{0,24},{8,16},{16,8},{24,0},{1,25},{9,17},{17,9},{25,1},{2,26},{10... | collective-permute-start | bytes 245768 | tf_op jit(solution)/shard_map/ppermute | solution.py:430

commit v8 on v7

--- a/solution.py
+++ b/solution.py
@@ -373,10 +373,9 @@
     if is_line:
         weight = after(weight, sibling, facing)
         first, second = exchange(weight, "rows", [CORES, 2 * CORES])
-        chips = range(CORES, strips, CORES)
-        stats = merge([stats] + exchange(stats, "rows", chips), entries)
-        stats = merge([stats] + exchange(stats, "rows", [1]), 4 * entries)
-        entries *= strips
+        for distance in (1, CORES, 2 * CORES):
+            stats = merge([stats] + exchange(stats, "rows", [distance]), entries)
+            entries *= 2
     else:
         distance = 1
         while distance < strips:
@@ -396,13 +395,15 @@
     below = jnp.where(strip == strips - 1, 2, core)
     edges = jnp.stack([above, below]).astype(jnp.int32)
     payload = pack(edges, stats, sibling, facing, payload, held, row_count + 2, col_count)
-    strip_pieces = [payload] + exchange(payload, "frames", range(1, group_count))
+    distances = [0] + list(reversed(range(1, group_count)))
+    strip_pieces = [payload] + exchange(payload, "frames", distances[1:])
     groups = jnp.stack([group ^ d for d in range(group_count)]).astype(jnp.int32)
     affine = jnp.stack([norm_gain, norm_bias])
     if is_line:
         near, strip_pieces, far = lax.optimization_barrier(([weight, first], strip_pieces, [second]))
+    places = jnp.stack([group ^ d for d in distances]).astype(jnp.int32) * held
     even, odd = activate(
-        groups * held, affine, strip_pieces, held, row_count + 2, col_count, entries
+        places, affine, strip_pieces, held, row_count + 2, col_count, entries
     )
 
     if is_line:

time: 66.6 us -> 64.8 us (0.973)
  starting transfers between devices: 21.2 us -> 19.6 us
    ppermute x9 -> x8, starting transfers between devices: 13.9 us -> 12.6 us  [exchange(): return [lax.ppermute(block, axis, flip(axis, d)) for d in distances]]
    ppermute x9 -> x8, waiting for transfers between devices: 22.7 us -> 21.9 us  [exchange(): return [lax.ppermute(block, axis, flip(axis, d)) for d in distances]]
  transfers between devices with their start and end apart: 20 -> 19, of which waited for: 8 -> 12; matrix products, arithmetic and copies ran while one was open for 1% -> 1% of each run, Pallas kernels for 12% -> 13%
where the time goes in v8:
time: 64.8 us; the launch traced here: 63.9 us
  waiting for transfers between devices  28.8 us (44%)
  starting transfers between devices  19.6 us (30%)
  Pallas kernels  13.8 us (21%)
  local copies, waits for them, and re-layouts  1.08 us (2%)
    ppermute x8, waiting for transfers between devices, exchange(): return [lax.ppermute(block, axis, flip(axis, d)) for d in distances]  21.9 us
    ppermute x8, starting transfers between devices, exchange(): return [lax.ppermute(block, axis, flip(axis, d)) for d in distances]  12.6 us
    pallas_call x2, Pallas kernels, convolve(): pl.pallas_call(functools.partial(conv_kernel, len(pieces), other is not N...  8.27 us
    ppermute x3, waiting for transfers between devices, body(): lax.ppermute(parts[d], 'frames', flip('frames', d))  4.86 us
    ppermute x3, starting transfers between devices, body(): lax.ppermute(parts[d], 'frames', flip('frames', d))  3.55 us
    pallas_call x1, Pallas kernels, activate(): pl.pallas_call(functools.partial(activate_kernel, held, rows, entries), o...  3.32 us
    ppermute x2, waiting for transfers between devices, body(): far += [lax.ppermute(piece, 'rows', flip('rows', 1)) for piece in far]  1.69 us
    pallas_call x1, Pallas kernels, place(): pl.pallas_call(place_kernel, out_shape=jax.ShapeDtypeStruct((held, positi...  1.32 us
  transfers between devices with their start and end apart: 19, of which 12 were waited for; matrix products, arithmetic and copies ran while one was open for 1% of the time, Pallas kernels for 13%

profile of v8, /device:TPU:0, one launch (start us, length us, event | category | flops | bytes accessed | tf_op | source)
XLA Modules:
  0.0 63.9 jit_solution(3790946961138703824)
XLA Ops:
  0.0 1.0 %copy-done.2 = bf16[2,4,40,512]{3,2,1,0:T(8,128)(2,1)S(1)} copy-done((bf16[2,4,40,512]{3,2,1,0:T(8,128)(2,1)S(1)}, bf16[2,4,40,512]{3,2,1,0:T(8,128)(2,1)}, u32[]{:S(2)}) %copy-start.2) | copy-done | bytes 327704
  1.0 0.2 shard_map.55
  1.2 0.5 collective-permute-start.4
  1.8 0.7 %collective-permute-start.1 = (bf16[2,1,40,512]{3,2,1,0:T(8,128)(2,1)S(1)}, bf16[2,1,40,512]{3,2,1,0:T(8,128)(2,1)S(1)}, u32[]{:S(2)}, u32[]{:S(2)}) collective-permute-start(bf16[2,1,40,512]{3,2,1,0:T(8,128)(2,1)S(1)} %get-tuple-element.30), channel_id=1, source_target_pairs={{1,2},{3,4},{5,6},{2,1},{4,3},{6,5},{9,10},{11,12},{13,14},{10,9},... | collective-permute-start | bytes 245768 | tf_op jit(solution)/shard_map/ppermute | solution.py:368
  2.5 4.3 %collective-permute-start.5 = (f32[2,512]{1,0:T(2,128)S(1)}, f32[2,512]{1,0:T(2,128)S(1)}, u32[]{:S(2)}, u32[]{:S(2)}) collective-permute-start(f32[2,512]{1,0:T(2,128)S(1)} %pad_maximum_fusion.1), channel_id=1, source_target_pairs={{0,2},{1,3},{2,0},{3,1},{4,6},{5,7},{6,4},{7,5},{8,10},{9,11},{10,... | collective-permute-start | bytes 12296 | tf_op jit(solution)/shard_map/ppermute | solution.py:29
  6.9 2.2 %collective-permute-done.5 = f32[2,512]{1,0:T(2,128)S(1)} collective-permute-done((f32[2,512]{1,0:T(2,128)S(1)}, f32[2,512]{1,0:T(2,128)S(1)}, u32[]{:S(2)}, u32[]{:S(2)}) %collective-permute-start.5) | collective-permute-done | bytes 4128 | tf_op jit(solution)/shard_map/ppermute | solution.py:29
  9.2 2.8 %collective-permute-start.6 = (f32[2,512]{1,0:T(2,128)S(1)}, f32[2,512]{1,0:T(2,128)S(1)}, u32[]{:S(2)}, u32[]{:S(2)}) collective-permute-start(f32[2,512]{1,0:T(2,128)S(1)} %pad_maximum_fusion.2), channel_id=1, source_target_pairs={{0,4},{1,5},{2,6},{3,7},{4,0},{5,1},{6,2},{7,3},{8,12},{9,13},{10,... | collective-permute-start | bytes 12296 | tf_op jit(solution)/shard_map/ppermute | solution.py:29
  11.9 1.3 %collective-permute-start.2 = (bf16[27,16,512]{2,1,0:T(8,128)(2,1)}, bf16[27,16,512]{2,1,0:T(8,128)(2,1)S(1)}, u32[]{:S(2)}, u32[]{:S(2)}) collective-permute-start(bf16[27,16,512]{2,1,0:T(8,128)(2,1)} %bitcast.21), channel_id=1, source_target_pairs={{0,2},{1,3},{2,0},{3,1},{4,6},{5,7},{6,4},{7,5},{8,10},{9,11},{10,... | collective-permute-start | bytes 1327112 | tf_op jit(solution)/shard_map/ppermute | solution.py:29
  13.3 0.2 collective-permute-start.3
  13.5 0.2 collective-permute-done.6
  13.8 0.7 %shard_map.56.refs_0_ = bf16[496,512]{1,0:T(8,128)(2,1)S(1)} custom-call(s32[2]{0:T(128)S(1)} %pad_add_fusion.1.edge_ref, f32[2,512]{1,0:T(2,128)S(1)} %pad_maximum_fusion.3.stats_ref, bf16[2,1,40,512]{3,2,1,0:T(8,128)(2,1)S(1)} %collective-permute-done.sibling_ref, ...), custom_call_target="tpu_custom_call", output_to_operand_aliasing={{}: (4, {})} | custom-call | tf_op jit(solution)/shard_map/pallas_call | solution.py:119
  14.5 2.6 %collective-permute-start.7 = (bf16[496,512]{1,0:T(8,128)(2,1)S(1)}, bf16[496,512]{1,0:T(8,128)(2,1)S(1)}, u32[]{:S(2)}, u32[]{:S(2)}) collective-permute-start(bf16[496,512]{1,0:T(8,128)(2,1)S(1)} %shard_map.56.refs_0_), channel_id=1, source_target_pairs={{0,24},{8,16},{16,8},{24,0},{1,25},{9,17},{17,9},{25,1},{2,26},{10... | collective-permute-start | bytes 1523720 | tf_op jit(solution)/shard_map/ppermute | solution.py:29
  17.1 0.5 collective-permute-start.8
  17.6 0.4 collective-permute-start.9
  18.0 13.5 %collective-permute-done.2.refs_1_ = bf16[27,16,512]{2,1,0:T(8,128)(2,1)S(1)} collective-permute-done((bf16[27,16,512]{2,1,0:T(8,128)(2,1)}, bf16[27,16,512]{2,1,0:T(8,128)(2,1)S(1)}, u32[]{:S(2)}, u32[]{:S(2)}) %collective-permute-start.2) | collective-permute-done | bytes 442400 | tf_op jit(solution)/shard_map/ppermute | solution.py:29
  31.6 4.0 %collective-permute-done.3.in_ref = bf16[27,16,512]{2,1,0:T(8,128)(2,1)S(1)} collective-permute-done((bf16[27,16,512]{2,1,0:T(8,128)(2,1)}, bf16[27,16,512]{2,1,0:T(8,128)(2,1)S(1)}, u32[]{:S(2)}, u32[]{:S(2)}) %collective-permute-start.3) | collective-permute-done | bytes 442400 | tf_op jit(solution)/shard_map/ppermute | solution.py:29
  35.5 1.3 %collective-permute-start.10 = (bf16[27,16,512]{2,1,0:T(8,128)(2,1)S(1)}, bf16[27,16,512]{2,1,0:T(8,128)(2,1)S(1)}, u32[]{:S(2)}, u32[]{:S(2)}) collective-permute-start(bf16[27,16,512]{2,1,0:T(8,128)(2,1)S(1)} %shard_map.57.refs_0_), channel_id=1, source_target_pairs={{2,0},{3,1},{4,6},{5,7},{10,8},{11,9},{12,14},{13,15},{18,16},{19,... | collective-permute-start | bytes 1327112 | tf_op jit(solution)/shard_map/ppermute | solution.py:391
  36.8 0.7 %collective-permute-start.11 = (bf16[27,16,512]{2,1,0:T(8,128)(2,1)S(1)}, bf16[27,16,512]{2,1,0:T(8,128)(2,1)S(1)}, u32[]{:S(2)}, u32[]{:S(2)}) collective-permute-start(bf16[27,16,512]{2,1,0:T(8,128)(2,1)S(1)} %bitcast.23), channel_id=1, source_target_pairs={{2,4},{3,5},{4,2},{5,3},{10,12},{11,13},{12,10},{13,11},{18,20},{1... | collective-permute-start | bytes 1327112 | tf_op jit(solution)/shard_map/ppermute | solution.py:392
  37.5 1.8 %collective-permute-done.8.refs_2_ = bf16[496,512]{1,0:T(8,128)(2,1)S(1)} collective-permute-done((bf16[496,512]{1,0:T(8,128)(2,1)S(1)}, bf16[496,512]{1,0:T(8,128)(2,1)S(1)}, u32[]{:S(2)}, u32[]{:S(2)}) %collective-permute-start.8) | collective-permute-done | bytes 507936 | tf_op jit(solution)/shard_map/ppermute | solution.py:29
  39.4 0.5 collective-permute-start.13
  40.2 3.3 %shard_map.58 = (bf16[6,336,512]{2,1,0:T(8,128)(2,1)S(1)}, bf16[6,320,512]{2,1,0:T(8,128)(2,1)S(1)}) custom-call(s32[4]{0:T(128)S(1)} %add_multiply_fusion.3.place_ref, f32[2,512]{1,0:T(2,128)S(1)} %pad_maximum_fusion.affine_ref, bf16[496,512]{1,0:T(8,128)(2,1)S(1)} %shard_map.56.refs_0_, bf16[496,512]{1,0:T(8,128)(2,1)S(1)} %collective-permute-done.7.refs_1_, ...), custom_call_target="tpu_custom_call" | custom-call | flops 9830400 | bytes 5898240 | tf_op jit(solution)/shard_map/pallas_call | solution.py:230
  43.6 4.2 %shard_map.59.refs_4_ = bf16[8,160,128]{2,1,0:T(8,128)(2,1)S(1)} custom-call(s32[4]{0:T(128)S(1)} %get-tuple-element.57.place_ref, s32[4]{0:T(128)S(1)} %and_select_fusion.slot_ref, s32[1]{0:T(128)} %bitcast.8.half_ref, bf16[6,336,512]{2,1,0:T(8,128)(2,1)S(1)} %get-tuple-element.41.even_ref, bf16[6,320,512]{2,1,0:T(8,128)(2,1)S(1)} %get-tuple-element.42.odd_ref, ...), custom_call_target="tpu_custom_call" | custom-call | flops 83886080 | bytes 65536 | tf_op jit(solution)/shard_map/pallas_call | solution.py:316
  47.7 0.4 collective-permute-done.10.one_ref
  48.4 1.7 %collective-permute-done.15.refs_3_ = bf16[27,16,512]{2,1,0:T(8,128)(2,1)S(1)} collective-permute-done((bf16[27,16,512]{2,1,0:T(8,128)(2,1)S(1)}, bf16[27,16,512]{2,1,0:T(8,128)(2,1)S(1)}, u32[]{:S(2)}, u32[]{:S(2)}) %collective-permute-start.15) | collective-permute-done | bytes 442400 | tf_op jit(solution)/shard_map/ppermute | solution.py:428
  50.1 4.1 %shard_map.61 = (bf16[2,160,128]{2,1,0:T(8,128)(2,1)S(1)}, bf16[2,160,128]{2,1,0:T(8,128)(2,1)S(1)}, bf16[2,160,128]{2,1,0:T(8,128)(2,1)S(1)}, bf16[2,160,128]{2,1,0:T(8,128)(2,1)S(1)}) custom-call(s32[4]{0:T(128)S(1)} %get-tuple-element.57.place_ref, s32[4]{0:T(128)S(1)} %and_select_fusion.slot_ref, s32[1]{0:T(128)S(6)} %sub.45.half_ref, ...), custom_call_target="tpu_custom_call" | custom-call | flops 83886080 | bytes 65536 | tf_op jit(solution)/shard_map/pallas_call | solution.py:316
  54.2 1.6 %collective-permute-start.16 = (bf16[2,160,128]{2,1,0:T(8,128)(2,1)S(1)}, bf16[2,160,128]{2,1,0:T(8,128)(2,1)S(1)}, u32[]{:S(2)}, u32[]{:S(2)}) collective-permute-start(bf16[2,160,128]{2,1,0:T(8,128)(2,1)S(1)} %get-tuple-element.50), channel_id=1, source_target_pairs={{0,8},{8,0},{16,24},{24,16},{1,9},{9,1},{17,25},{25,17},{2,10},{10... | collective-permute-start | bytes 245768 | tf_op jit(solution)/shard_map/ppermute | solution.py:431
  55.8 1.5 %collective-permute-start.17 = (bf16[2,160,128]{2,1,0:T(8,128)(2,1)S(1)}, bf16[2,160,128]{2,1,0:T(8,128)(2,1)S(1)}, u32[]{:S(2)}, u32[]{:S(2)}) collective-permute-start(bf16[2,160,128]{2,1,0:T(8,128)(2,1)S(1)} %get-tuple-element.51), channel_id=1, source_target_pairs={{0,16},{8,24},{16,0},{24,8},{1,17},{9,25},{17,1},{25,9},{2,18},{10... | collective-permute-start | bytes 245768 | tf_op jit(solution)/shard_map/ppermute | solution.py:431
  57.3 0.5 collective-permute-start.18
  57.8 1.0 %collective-permute-done.16.refs_1_ = bf16[2,160,128]{2,1,0:T(8,128)(2,1)S(1)} collective-permute-done((bf16[2,160,128]{2,1,0:T(8,128)(2,1)S(1)}, bf16[2,160,128]{2,1,0:T(8,128)(2,1)S(1)}, u32[]{:S(2)}, u32[]{:S(2)}) %collective-permute-start.16) | collective-permute-done | bytes 81952 | tf_op jit(solution)/shard_map/ppermute | solution.py:431
  58.8 2.3 %collective-permute-done.17.refs_2_ = bf16[2,160,128]{2,1,0:T(8,128)(2,1)S(1)} collective-permute-done((bf16[2,160,128]{2,1,0:T(8,128)(2,1)S(1)}, bf16[2,160,128]{2,1,0:T(8,128)(2,1)S(1)}, u32[]{:S(2)}, u32[]{:S(2)}) %collective-permute-start.17) | collective-permute-done | bytes 81952 | tf_op jit(solution)/shard_map/ppermute | solution.py:431
  61.0 1.6 %collective-permute-done.18.refs_3_ = bf16[2,160,128]{2,1,0:T(8,128)(2,1)S(1)} collective-permute-done((bf16[2,160,128]{2,1,0:T(8,128)(2,1)S(1)}, bf16[2,160,128]{2,1,0:T(8,128)(2,1)S(1)}, u32[]{:S(2)}, u32[]{:S(2)}) %collective-permute-start.18) | collective-permute-done | bytes 81952 | tf_op jit(solution)/shard_map/ppermute | solution.py:431
  62.6 1.3 %shard_map.62 = bf16[2,160,512]{2,1,0:T(8,128)(2,1)} custom-call(s32[4]{0:T(128)S(1)} %get-tuple-element.58.place_ref, bf16[2,160,128]{2,1,0:T(8,128)(2,1)S(1)} %get-tuple-element.49.refs_0_, bf16[2,160,128]{2,1,0:T(8,128)(2,1)S(1)} %collective-permute-done.16.refs_1_, bf16[2,160,128]{2,1,0:T(8,128)(2,1)S(1)} %collective-permute-done.17.refs_2_, ...), custom_call_target="tpu_custom_call" | custom-call | tf_op jit(solution)/shard_map/pallas_call | solution.py:345
  (36 shorter events, 1.0 us)
Async XLA Ops:
  0.0 13.5 %copy-start = (f32[512]{0:T(512)S(1)}, f32[512]{0:T(512)}, u32[]{:S(2)}) copy-start(f32[512]{0:T(512)} %param.9) | copy-start | bytes 6148
  0.0 1.0 %copy-start.2 = (bf16[2,4,40,512]{3,2,1,0:T(8,128)(2,1)S(1)}, bf16[2,4,40,512]{3,2,1,0:T(8,128)(2,1)}, u32[]{:S(2)}) copy-start(bf16[2,4,40,512]{3,2,1,0:T(8,128)(2,1)} %x_ref.1) | copy-start | bytes 983044
  1.2 1.3 %collective-permute-start.4 = (f32[2,512]{1,0:T(2,128)S(1)}, f32[2,512]{1,0:T(2,128)S(1)}, u32[]{:S(2)}, u32[]{:S(2)}) collective-permute-start(f32[2,512]{1,0:T(2,128)S(1)} %get-tuple-element.34), channel_id=1, source_target_pairs={{0,1},{1,0},{2,3},{3,2},{4,5},{5,4},{6,7},{7,6},{8,9},{9,8},{10,11... | collective-permute-start | bytes 12296 | tf_op jit(solution)/shard_map/ppermute | solution.py:29
  1.7 10.2 %collective-permute-start = (bf16[2,1,40,512]{3,2,1,0:T(8,128)(2,1)S(1)}, bf16[2,1,40,512]{3,2,1,0:T(8,128)(2,1)S(1)}, u32[]{:S(2)}, u32[]{:S(2)}) collective-permute-start(bf16[2,1,40,512]{3,2,1,0:T(8,128)(2,1)S(1)} %get-tuple-element.29), channel_id=1, source_target_pairs={{0,1},{1,0},{2,3},{3,2},{4,5},{5,4},{6,7},{7,6},{8,9},{9,8},{10,11... | collective-permute-start | bytes 245768 | tf_op jit(solution)/shard_map/ppermute | solution.py:366
  1.8 10.2 %collective-permute-start.1 = (bf16[2,1,40,512]{3,2,1,0:T(8,128)(2,1)S(1)}, bf16[2,1,40,512]{3,2,1,0:T(8,128)(2,1)S(1)}, u32[]{:S(2)}, u32[]{:S(2)}) collective-permute-start(bf16[2,1,40,512]{3,2,1,0:T(8,128)(2,1)S(1)} %get-tuple-element.30), channel_id=1, source_target_pairs={{1,2},{3,4},{5,6},{2,1},{4,3},{6,5},{9,10},{11,12},{13,14},{10,9},... | collective-permute-start | bytes 245768 | tf_op jit(solution)/shard_map/ppermute | solution.py:368
  2.5 6.6 %collective-permute-start.5 = (f32[2,512]{1,0:T(2,128)S(1)}, f32[2,512]{1,0:T(2,128)S(1)}, u32[]{:S(2)}, u32[]{:S(2)}) collective-permute-start(f32[2,512]{1,0:T(2,128)S(1)} %pad_maximum_fusion.1), channel_id=1, source_target_pairs={{0,2},{1,3},{2,0},{3,1},{4,6},{5,7},{6,4},{7,5},{8,10},{9,11},{10,... | collective-permute-start | bytes 12296 | tf_op jit(solution)/shard_map/ppermute | solution.py:29
  9.2 4.6 %collective-permute-start.6 = (f32[2,512]{1,0:T(2,128)S(1)}, f32[2,512]{1,0:T(2,128)S(1)}, u32[]{:S(2)}, u32[]{:S(2)}) collective-permute-start(f32[2,512]{1,0:T(2,128)S(1)} %pad_maximum_fusion.2), channel_id=1, source_target_pairs={{0,4},{1,5},{2,6},{3,7},{4,0},{5,1},{6,2},{7,3},{8,12},{9,13},{10,... | collective-permute-start | bytes 12296 | tf_op jit(solution)/shard_map/ppermute | solution.py:29
  11.9 19.6 %collective-permute-start.2 = (bf16[27,16,512]{2,1,0:T(8,128)(2,1)}, bf16[27,16,512]{2,1,0:T(8,128)(2,1)S(1)}, u32[]{:S(2)}, u32[]{:S(2)}) collective-permute-start(bf16[27,16,512]{2,1,0:T(8,128)(2,1)} %bitcast.21), channel_id=1, source_target_pairs={{0,2},{1,3},{2,0},{3,1},{4,6},{5,7},{6,4},{7,5},{8,10},{9,11},{10,... | collective-permute-start | bytes 1327112 | tf_op jit(solution)/shard_map/ppermute | solution.py:29
  13.3 22.3 %collective-permute-start.3 = (bf16[27,16,512]{2,1,0:T(8,128)(2,1)}, bf16[27,16,512]{2,1,0:T(8,128)(2,1)S(1)}, u32[]{:S(2)}, u32[]{:S(2)}) collective-permute-start(bf16[27,16,512]{2,1,0:T(8,128)(2,1)} %bitcast.22), channel_id=1, source_target_pairs={{0,4},{1,5},{2,6},{3,7},{4,0},{5,1},{6,2},{7,3},{8,12},{9,13},{10,... | collective-permute-start | bytes 1327112 | tf_op jit(solution)/shard_map/ppermute | solution.py:29
  14.4 22.4 %copy-start.1 = (bf16[3,3,3,512,16]{3,4,2,1,0:T(8,128)(2,1)S(1)}, bf16[3,3,3,512,16]{3,4,2,1,0:T(8,128)(2,1)}, u32[]{:S(2)}) copy-start(bf16[3,3,3,512,16]{3,4,2,1,0:T(8,128)(2,1)} %param.8) | copy-start | bytes 1327108
  14.4 25.7 %copy-start.3 = (f32[512]{0:T(512)S(1)}, f32[512]{0:T(512)}, u32[]{:S(2)}) copy-start(f32[512]{0:T(512)} %param.7) | copy-start | bytes 6148
  14.4 25.7 %copy-start.4 = (f32[512]{0:T(512)S(1)}, f32[512]{0:T(512)}, u32[]{:S(2)}) copy-start(f32[512]{0:T(512)} %param.6) | copy-start | bytes 6148
  14.5 23.1 %collective-permute-start.7 = (bf16[496,512]{1,0:T(8,128)(2,1)S(1)}, bf16[496,512]{1,0:T(8,128)(2,1)S(1)}, u32[]{:S(2)}, u32[]{:S(2)}) collective-permute-start(bf16[496,512]{1,0:T(8,128)(2,1)S(1)} %shard_map.56.refs_0_), channel_id=1, source_target_pairs={{0,24},{8,16},{16,8},{24,0},{1,25},{9,17},{17,9},{25,1},{2,26},{10... | collective-permute-start | bytes 1523720 | tf_op jit(solution)/shard_map/ppermute | solution.py:29
  17.1 22.2 %collective-permute-start.8 = (bf16[496,512]{1,0:T(8,128)(2,1)S(1)}, bf16[496,512]{1,0:T(8,128)(2,1)S(1)}, u32[]{:S(2)}, u32[]{:S(2)}) collective-permute-start(bf16[496,512]{1,0:T(8,128)(2,1)S(1)} %shard_map.56.refs_0_), channel_id=1, source_target_pairs={{0,16},{8,24},{16,0},{24,8},{1,17},{9,25},{17,1},{25,9},{2,18},{10... | collective-permute-start | bytes 1523720 | tf_op jit(solution)/shard_map/ppermute | solution.py:29
  17.6 21.8 %collective-permute-start.9 = (bf16[496,512]{1,0:T(8,128)(2,1)S(1)}, bf16[496,512]{1,0:T(8,128)(2,1)S(1)}, u32[]{:S(2)}, u32[]{:S(2)}) collective-permute-start(bf16[496,512]{1,0:T(8,128)(2,1)S(1)} %shard_map.56.refs_0_), channel_id=1, source_target_pairs={{0,8},{8,0},{16,24},{24,16},{1,9},{9,1},{17,25},{25,17},{2,10},{10... | collective-permute-start | bytes 1523720 | tf_op jit(solution)/shard_map/ppermute | solution.py:29
  35.5 12.6 %collective-permute-start.10 = (bf16[27,16,512]{2,1,0:T(8,128)(2,1)S(1)}, bf16[27,16,512]{2,1,0:T(8,128)(2,1)S(1)}, u32[]{:S(2)}, u32[]{:S(2)}) collective-permute-start(bf16[27,16,512]{2,1,0:T(8,128)(2,1)S(1)} %shard_map.57.refs_0_), channel_id=1, source_target_pairs={{2,0},{3,1},{4,6},{5,7},{10,8},{11,9},{12,14},{13,15},{18,16},{19,... | collective-permute-start | bytes 1327112 | tf_op jit(solution)/shard_map/ppermute | solution.py:391
  36.8 11.3 %collective-permute-start.11 = (bf16[27,16,512]{2,1,0:T(8,128)(2,1)S(1)}, bf16[27,16,512]{2,1,0:T(8,128)(2,1)S(1)}, u32[]{:S(2)}, u32[]{:S(2)}) collective-permute-start(bf16[27,16,512]{2,1,0:T(8,128)(2,1)S(1)} %bitcast.23), channel_id=1, source_target_pairs={{2,4},{3,5},{4,2},{5,3},{10,12},{11,13},{12,10},{13,11},{18,20},{1... | collective-permute-start | bytes 1327112 | tf_op jit(solution)/shard_map/ppermute | solution.py:392
  39.4 4.2 %collective-permute-start.12 = (bf16[27,16,512]{2,1,0:T(8,128)(2,1)S(1)}, bf16[27,16,512]{2,1,0:T(8,128)(2,1)S(1)}, u32[]{:S(2)}, u32[]{:S(2)}) collective-permute-start(bf16[27,16,512]{2,1,0:T(8,128)(2,1)S(1)} %bitcast.24), channel_id=1, source_target_pairs={{0,1},{1,0},{2,3},{3,2},{4,5},{5,4},{6,7},{7,6},{8,9},{9,8},{10,11... | collective-permute-start | bytes 1327112 | tf_op jit(solution)/shard_map/ppermute | solution.py:410
  39.4 4.2 %collective-permute-start.13 = (bf16[27,16,512]{2,1,0:T(8,128)(2,1)S(1)}, bf16[27,16,512]{2,1,0:T(8,128)(2,1)S(1)}, u32[]{:S(2)}, u32[]{:S(2)}) collective-permute-start(bf16[27,16,512]{2,1,0:T(8,128)(2,1)S(1)} %collective-permute-done.2.refs_1_), channel_id=1, source_target_pairs={{0,1},{1,0},{2,3},{3,2},{4,5},{5,4},{6,7},{7,6},{8,9},{9,8},{10,11... | collective-permute-start | bytes 1327112 | tf_op jit(solution)/shard_map/ppermute | solution.py:410
  40.2 8.2 %collective-permute-start.14 = (bf16[27,16,512]{2,1,0:T(8,128)(2,1)S(1)}, bf16[27,16,512]{2,1,0:T(8,128)(2,1)S(1)}, u32[]{:S(2)}, u32[]{:S(2)}) collective-permute-start(bf16[27,16,512]{2,1,0:T(8,128)(2,1)S(1)} %shard_map.57.refs_0_), channel_id=1, source_target_pairs={{0,1},{1,0},{2,3},{3,2},{4,5},{5,4},{6,7},{7,6},{8,9},{9,8},{10,11... | collective-permute-start | bytes 1327112 | tf_op jit(solution)/shard_map/ppermute | solution.py:428
  48.2 1.9 %collective-permute-start.15 = (bf16[27,16,512]{2,1,0:T(8,128)(2,1)S(1)}, bf16[27,16,512]{2,1,0:T(8,128)(2,1)S(1)}, u32[]{:S(2)}, u32[]{:S(2)}) collective-permute-start(bf16[27,16,512]{2,1,0:T(8,128)(2,1)S(1)} %shard_map.60.refs_1_), channel_id=1, source_target_pairs={{0,1},{1,0},{2,3},{3,2},{4,5},{5,4},{6,7},{7,6},{8,9},{9,8},{10,11... | collective-permute-start | bytes 1327112 | tf_op jit(solution)/shard_map/ppermute | solution.py:428
  54.2 4.6 %collective-permute-start.16 = (bf16[2,160,128]{2,1,0:T(8,128)(2,1)S(1)}, bf16[2,160,128]{2,1,0:T(8,128)(2,1)S(1)}, u32[]{:S(2)}, u32[]{:S(2)}) collective-permute-start(bf16[2,160,128]{2,1,0:T(8,128)(2,1)S(1)} %get-tuple-element.50), channel_id=1, source_target_pairs={{0,8},{8,0},{16,24},{24,16},{1,9},{9,1},{17,25},{25,17},{2,10},{10... | collective-permute-start | bytes 245768 | tf_op jit(solution)/shard_map/ppermute | solution.py:431
  55.8 5.3 %collective-permute-start.17 = (bf16[2,160,128]{2,1,0:T(8,128)(2,1)S(1)}, bf16[2,160,128]{2,1,0:T(8,128)(2,1)S(1)}, u32[]{:S(2)}, u32[]{:S(2)}) collective-permute-start(bf16[2,160,128]{2,1,0:T(8,128)(2,1)S(1)} %get-tuple-element.51), channel_id=1, source_target_pairs={{0,16},{8,24},{16,0},{24,8},{1,17},{9,25},{17,1},{25,9},{2,18},{10... | collective-permute-start | bytes 245768 | tf_op jit(solution)/shard_map/ppermute | solution.py:431
  57.3 5.3 %collective-permute-start.18 = (bf16[2,160,128]{2,1,0:T(8,128)(2,1)S(1)}, bf16[2,160,128]{2,1,0:T(8,128)(2,1)S(1)}, u32[]{:S(2)}, u32[]{:S(2)}) collective-permute-start(bf16[2,160,128]{2,1,0:T(8,128)(2,1)S(1)} %get-tuple-element.52), channel_id=1, source_target_pairs={{0,24},{8,16},{16,8},{24,0},{1,25},{9,17},{17,9},{25,1},{2,26},{10... | collective-permute-start | bytes 245768 | tf_op jit(solution)/shard_map/ppermute | solution.py:431

commit v9 on v8

--- a/solution.py
+++ b/solution.py
@@ -372,7 +372,7 @@
     entries = held * row_count * col_count
     if is_line:
         weight = after(weight, sibling, facing)
-        first, second = exchange(weight, "rows", [CORES, 2 * CORES])
+        second = lax.ppermute(weight, "rows", flip("rows", 2 * CORES))
         for distance in (1, CORES, 2 * CORES):
             stats = merge([stats] + exchange(stats, "rows", [distance]), entries)
             entries *= 2
@@ -384,17 +384,19 @@
             distance *= 2
 
     if is_line:
-        weight, first, second = lax.optimization_barrier((weight, first, second))
+        last, second = lax.optimization_barrier((weight, second))
         second = hold(second)
         ends = chip_pairs([(1, 0), (2, 3)])
         middle = chip_pairs([(1, 2), (2, 1)])
         third_ends = lax.ppermute(second, "rows", ends)
-        third_middle = lax.ppermute(weight, "rows", middle)
+        third_middle = lax.ppermute(last, "rows", middle)
 
     above = jnp.where(strip == 0, 2, 1 - core)
     below = jnp.where(strip == strips - 1, 2, core)
     edges = jnp.stack([above, below]).astype(jnp.int32)
     payload = pack(edges, stats, sibling, facing, payload, held, row_count + 2, col_count)
+    if is_line:
+        first = lax.ppermute(after(weight, payload), "rows", flip("rows", CORES))
     distances = [0] + list(reversed(range(1, group_count)))
     strip_pieces = [payload] + exchange(payload, "frames", distances[1:])
     groups = jnp.stack([group ^ d for d in range(group_count)]).astype(jnp.int32)

time: 64.8 us -> 64.4 us (level)
    ppermute x8 -> x6, waiting for transfers between devices: 21.9 us -> 4.88 us  [exchange(): return [lax.ppermute(block, axis, flip(axis, d)) for d in distances]]
    ppermute x1 -> x3, waiting for transfers between devices: 0.01 us -> 16.6 us  [the longest x1 15.2 us: body(): second = lax.ppermute(weight, 'rows', flip('rows', 2 * CORES))]
    ppermute x8 -> x6, starting transfers between devices: 12.6 us -> 11.1 us  [exchange(): return [lax.ppermute(block, axis, flip(axis, d)) for d in distances]]
    ppermute x1 -> x3, starting transfers between devices: 0.69 us -> 2.2 us  [the longest x1 1.3 us: body(): first = lax.ppermute(after(weight, payload), 'rows', flip('rows', CORES))]
where the time goes in v9:
time: 64.4 us; the launch traced here: 63.5 us
  waiting for transfers between devices  28.3 us (44%)
  starting transfers between devices  19.7 us (31%)
  Pallas kernels  13.8 us (21%)
  local copies, waits for them, and re-layouts  1.08 us (2%)
    ppermute x1, waiting for transfers between devices, body(): second = lax.ppermute(weight, 'rows', flip('rows', 2 * CORES))  15.2 us
    ppermute x6, starting transfers between devices, exchange(): return [lax.ppermute(block, axis, flip(axis, d)) for d in distances]  11.1 us
    pallas_call x2, Pallas kernels, convolve(): pl.pallas_call(functools.partial(conv_kernel, len(pieces), other is not N...  8.28 us
    ppermute x6, waiting for transfers between devices, exchange(): return [lax.ppermute(block, axis, flip(axis, d)) for d in distances]  4.88 us
    ppermute x3, waiting for transfers between devices, body(): lax.ppermute(parts[d], 'frames', flip('frames', d))  4.85 us
    ppermute x3, starting transfers between devices, body(): lax.ppermute(parts[d], 'frames', flip('frames', d))  3.55 us
    pallas_call x1, Pallas kernels, activate(): pl.pallas_call(functools.partial(activate_kernel, held, rows, entries), o...  3.32 us
    ppermute x2, waiting for transfers between devices, body(): far += [lax.ppermute(piece, 'rows', flip('rows', 1)) for piece in far]  1.64 us
  transfers between devices with their start and end apart: 19, of which 12 were waited for; matrix products, arithmetic and copies ran while one was open for 1% of the time, Pallas kernels for 13%

profile of v9, /device:TPU:0, one launch (start us, length us, event | category | flops | bytes accessed | tf_op | source)
XLA Modules:
  0.0 63.5 jit_solution(9967800064433225078)
XLA Ops:
  0.0 1.0 %copy-done.2 = bf16[2,4,40,512]{3,2,1,0:T(8,128)(2,1)S(1)} copy-done((bf16[2,4,40,512]{3,2,1,0:T(8,128)(2,1)S(1)}, bf16[2,4,40,512]{3,2,1,0:T(8,128)(2,1)}, u32[]{:S(2)}) %copy-start.2) | copy-done | bytes 327704
  1.2 0.5 collective-permute-start.2
  1.8 0.7 %collective-permute-start.1 = (bf16[2,1,40,512]{3,2,1,0:T(8,128)(2,1)S(1)}, bf16[2,1,40,512]{3,2,1,0:T(8,128)(2,1)S(1)}, u32[]{:S(2)}, u32[]{:S(2)}) collective-permute-start(bf16[2,1,40,512]{3,2,1,0:T(8,128)(2,1)S(1)} %get-tuple-element.30), channel_id=1, source_target_pairs={{1,2},{3,4},{5,6},{2,1},{4,3},{6,5},{9,10},{11,12},{13,14},{10,9},... | collective-permute-start | bytes 245768 | tf_op jit(solution)/shard_map/ppermute | solution.py:368
  2.5 4.3 %collective-permute-start.3 = (f32[2,512]{1,0:T(2,128)S(1)}, f32[2,512]{1,0:T(2,128)S(1)}, u32[]{:S(2)}, u32[]{:S(2)}) collective-permute-start(f32[2,512]{1,0:T(2,128)S(1)} %pad_maximum_fusion.1), channel_id=1, source_target_pairs={{0,2},{1,3},{2,0},{3,1},{4,6},{5,7},{6,4},{7,5},{8,10},{9,11},{10,... | collective-permute-start | bytes 12296 | tf_op jit(solution)/shard_map/ppermute | solution.py:29
  6.9 2.2 %collective-permute-done.3 = f32[2,512]{1,0:T(2,128)S(1)} collective-permute-done((f32[2,512]{1,0:T(2,128)S(1)}, f32[2,512]{1,0:T(2,128)S(1)}, u32[]{:S(2)}, u32[]{:S(2)}) %collective-permute-start.3) | collective-permute-done | bytes 4128 | tf_op jit(solution)/shard_map/ppermute | solution.py:29
  9.2 2.8 %collective-permute-start.4 = (f32[2,512]{1,0:T(2,128)S(1)}, f32[2,512]{1,0:T(2,128)S(1)}, u32[]{:S(2)}, u32[]{:S(2)}) collective-permute-start(f32[2,512]{1,0:T(2,128)S(1)} %pad_maximum_fusion.2), channel_id=1, source_target_pairs={{0,4},{1,5},{2,6},{3,7},{4,0},{5,1},{6,2},{7,3},{8,12},{9,13},{10,... | collective-permute-start | bytes 12296 | tf_op jit(solution)/shard_map/ppermute | solution.py:29
  11.9 0.2 collective-permute-start.9
  12.2 1.5 %collective-permute-done.4 = f32[2,512]{1,0:T(2,128)S(1)} collective-permute-done((f32[2,512]{1,0:T(2,128)S(1)}, f32[2,512]{1,0:T(2,128)S(1)}, u32[]{:S(2)}, u32[]{:S(2)}) %collective-permute-start.4) | collective-permute-done | bytes 4128 | tf_op jit(solution)/shard_map/ppermute | solution.py:29
  13.8 0.7 %shard_map.56.refs_0_ = bf16[496,512]{1,0:T(8,128)(2,1)S(1)} custom-call(s32[2]{0:T(128)S(1)} %pad_add_fusion.1.edge_ref, f32[2,512]{1,0:T(2,128)S(1)} %pad_maximum_fusion.3.stats_ref, bf16[2,1,40,512]{3,2,1,0:T(8,128)(2,1)S(1)} %collective-permute-done.sibling_ref, ...), custom_call_target="tpu_custom_call", output_to_operand_aliasing={{}: (4, {})} | custom-call | tf_op jit(solution)/shard_map/pallas_call | solution.py:119
  14.5 2.6 %collective-permute-start.6 = (bf16[496,512]{1,0:T(8,128)(2,1)S(1)}, bf16[496,512]{1,0:T(8,128)(2,1)S(1)}, u32[]{:S(2)}, u32[]{:S(2)}) collective-permute-start(bf16[496,512]{1,0:T(8,128)(2,1)S(1)} %shard_map.56.refs_0_), channel_id=1, source_target_pairs={{0,24},{8,16},{16,8},{24,0},{1,25},{9,17},{17,9},{25,1},{2,26},{10... | collective-permute-start | bytes 1523720 | tf_op jit(solution)/shard_map/ppermute | solution.py:29
  17.1 0.5 collective-permute-start.7
  17.6 0.4 collective-permute-start.8
  18.0 1.3 %collective-permute-start.5 = (bf16[27,16,512]{2,1,0:T(8,128)(2,1)}, bf16[27,16,512]{2,1,0:T(8,128)(2,1)S(1)}, u32[]{:S(2)}, u32[]{:S(2)}) collective-permute-start(bf16[27,16,512]{2,1,0:T(8,128)(2,1)} %bitcast.22), channel_id=1, source_target_pairs={{0,2},{1,3},{2,0},{3,1},{4,6},{5,7},{6,4},{7,5},{8,10},{9,11},{10,... | collective-permute-start | bytes 1327112 | tf_op jit(solution)/shard_map/ppermute | solution.py:399
  19.3 15.2 %collective-permute-done.9.in_ref = bf16[27,16,512]{2,1,0:T(8,128)(2,1)S(1)} collective-permute-done((bf16[27,16,512]{2,1,0:T(8,128)(2,1)}, bf16[27,16,512]{2,1,0:T(8,128)(2,1)S(1)}, u32[]{:S(2)}, u32[]{:S(2)}) %collective-permute-start.9) | collective-permute-done | bytes 442400 | tf_op jit(solution)/shard_map/ppermute | solution.py:375
  34.6 1.3 %collective-permute-start.10 = (bf16[27,16,512]{2,1,0:T(8,128)(2,1)S(1)}, bf16[27,16,512]{2,1,0:T(8,128)(2,1)S(1)}, u32[]{:S(2)}, u32[]{:S(2)}) collective-permute-start(bf16[27,16,512]{2,1,0:T(8,128)(2,1)S(1)} %shard_map.57.refs_0_), channel_id=1, source_target_pairs={{2,0},{3,1},{4,6},{5,7},{10,8},{11,9},{12,14},{13,15},{18,16},{19,... | collective-permute-start | bytes 1327112 | tf_op jit(solution)/shard_map/ppermute | solution.py:391
  35.9 1.3 %collective-permute-done.5.refs_1_ = bf16[27,16,512]{2,1,0:T(8,128)(2,1)S(1)} collective-permute-done((bf16[27,16,512]{2,1,0:T(8,128)(2,1)}, bf16[27,16,512]{2,1,0:T(8,128)(2,1)S(1)}, u32[]{:S(2)}, u32[]{:S(2)}) %collective-permute-start.5) | collective-permute-done | bytes 442400 | tf_op jit(solution)/shard_map/ppermute | solution.py:399
  37.2 0.7 %collective-permute-start.11 = (bf16[27,16,512]{2,1,0:T(8,128)(2,1)S(1)}, bf16[27,16,512]{2,1,0:T(8,128)(2,1)S(1)}, u32[]{:S(2)}, u32[]{:S(2)}) collective-permute-start(bf16[27,16,512]{2,1,0:T(8,128)(2,1)S(1)} %bitcast.23), channel_id=1, source_target_pairs={{2,4},{3,5},{4,2},{5,3},{10,12},{11,13},{12,10},{13,11},{18,20},{1... | collective-permute-start | bytes 1327112 | tf_op jit(solution)/shard_map/ppermute | solution.py:392
  37.9 1.0 %collective-permute-done.7.refs_2_ = bf16[496,512]{1,0:T(8,128)(2,1)S(1)} collective-permute-done((bf16[496,512]{1,0:T(8,128)(2,1)S(1)}, bf16[496,512]{1,0:T(8,128)(2,1)S(1)}, u32[]{:S(2)}, u32[]{:S(2)}) %collective-permute-start.7) | collective-permute-done | bytes 507936 | tf_op jit(solution)/shard_map/ppermute | solution.py:29
  39.0 0.5 collective-permute-start.13
  39.8 3.3 %shard_map.58 = (bf16[6,336,512]{2,1,0:T(8,128)(2,1)S(1)}, bf16[6,320,512]{2,1,0:T(8,128)(2,1)S(1)}) custom-call(s32[4]{0:T(128)S(1)} %add_multiply_fusion.3.place_ref, f32[2,512]{1,0:T(2,128)S(1)} %pad_maximum_fusion.affine_ref, bf16[496,512]{1,0:T(8,128)(2,1)S(1)} %shard_map.56.refs_0_, bf16[496,512]{1,0:T(8,128)(2,1)S(1)} %collective-permute-done.6.refs_1_, ...), custom_call_target="tpu_custom_call" | custom-call | flops 9830400 | bytes 5898240 | tf_op jit(solution)/shard_map/pallas_call | solution.py:230
  43.2 4.2 %shard_map.59.refs_4_ = bf16[8,160,128]{2,1,0:T(8,128)(2,1)S(1)} custom-call(s32[4]{0:T(128)S(1)} %get-tuple-element.57.place_ref, s32[4]{0:T(128)S(1)} %and_select_fusion.slot_ref, s32[1]{0:T(128)} %bitcast.8.half_ref, bf16[6,336,512]{2,1,0:T(8,128)(2,1)S(1)} %get-tuple-element.40.even_ref, bf16[6,320,512]{2,1,0:T(8,128)(2,1)S(1)} %get-tuple-element.41.odd_ref, ...), custom_call_target="tpu_custom_call" | custom-call | flops 83886080 | bytes 65536 | tf_op jit(solution)/shard_map/pallas_call | solution.py:316
  47.4 0.4 collective-permute-done.10.one_ref
  47.8 0.2 collective-permute-start.15
  48.0 1.6 %collective-permute-done.15.refs_3_ = bf16[27,16,512]{2,1,0:T(8,128)(2,1)S(1)} collective-permute-done((bf16[27,16,512]{2,1,0:T(8,128)(2,1)S(1)}, bf16[27,16,512]{2,1,0:T(8,128)(2,1)S(1)}, u32[]{:S(2)}, u32[]{:S(2)}) %collective-permute-start.15) | collective-permute-done | bytes 442400 | tf_op jit(solution)/shard_map/ppermute | solution.py:430
  49.6 4.1 %shard_map.61 = (bf16[2,160,128]{2,1,0:T(8,128)(2,1)S(1)}, bf16[2,160,128]{2,1,0:T(8,128)(2,1)S(1)}, bf16[2,160,128]{2,1,0:T(8,128)(2,1)S(1)}, bf16[2,160,128]{2,1,0:T(8,128)(2,1)S(1)}) custom-call(s32[4]{0:T(128)S(1)} %get-tuple-element.57.place_ref, s32[4]{0:T(128)S(1)} %and_select_fusion.slot_ref, s32[1]{0:T(128)S(6)} %sub.45.half_ref, ...), custom_call_target="tpu_custom_call" | custom-call | flops 83886080 | bytes 65536 | tf_op jit(solution)/shard_map/pallas_call | solution.py:316
  53.8 1.5 %collective-permute-start.16 = (bf16[2,160,128]{2,1,0:T(8,128)(2,1)S(1)}, bf16[2,160,128]{2,1,0:T(8,128)(2,1)S(1)}, u32[]{:S(2)}, u32[]{:S(2)}) collective-permute-start(bf16[2,160,128]{2,1,0:T(8,128)(2,1)S(1)} %get-tuple-element.50), channel_id=1, source_target_pairs={{0,8},{8,0},{16,24},{24,16},{1,9},{9,1},{17,25},{25,17},{2,10},{10... | collective-permute-start | bytes 245768 | tf_op jit(solution)/shard_map/ppermute | solution.py:433
  55.3 1.5 %collective-permute-start.17 = (bf16[2,160,128]{2,1,0:T(8,128)(2,1)S(1)}, bf16[2,160,128]{2,1,0:T(8,128)(2,1)S(1)}, u32[]{:S(2)}, u32[]{:S(2)}) collective-permute-start(bf16[2,160,128]{2,1,0:T(8,128)(2,1)S(1)} %get-tuple-element.51), channel_id=1, source_target_pairs={{0,16},{8,24},{16,0},{24,8},{1,17},{9,25},{17,1},{25,9},{2,18},{10... | collective-permute-start | bytes 245768 | tf_op jit(solution)/shard_map/ppermute | solution.py:433
  56.8 0.5 collective-permute-start.18
  57.3 1.0 %collective-permute-done.16.refs_1_ = bf16[2,160,128]{2,1,0:T(8,128)(2,1)S(1)} collective-permute-done((bf16[2,160,128]{2,1,0:T(8,128)(2,1)S(1)}, bf16[2,160,128]{2,1,0:T(8,128)(2,1)S(1)}, u32[]{:S(2)}, u32[]{:S(2)}) %collective-permute-start.16) | collective-permute-done | bytes 81952 | tf_op jit(solution)/shard_map/ppermute | solution.py:433
  58.3 2.2 %collective-permute-done.17.refs_2_ = bf16[2,160,128]{2,1,0:T(8,128)(2,1)S(1)} collective-permute-done((bf16[2,160,128]{2,1,0:T(8,128)(2,1)S(1)}, bf16[2,160,128]{2,1,0:T(8,128)(2,1)S(1)}, u32[]{:S(2)}, u32[]{:S(2)}) %collective-permute-start.17) | collective-permute-done | bytes 81952 | tf_op jit(solution)/shard_map/ppermute | solution.py:433
  60.6 1.6 %collective-permute-done.18.refs_3_ = bf16[2,160,128]{2,1,0:T(8,128)(2,1)S(1)} collective-permute-done((bf16[2,160,128]{2,1,0:T(8,128)(2,1)S(1)}, bf16[2,160,128]{2,1,0:T(8,128)(2,1)S(1)}, u32[]{:S(2)}, u32[]{:S(2)}) %collective-permute-start.18) | collective-permute-done | bytes 81952 | tf_op jit(solution)/shard_map/ppermute | solution.py:433
  62.2 1.3 %shard_map.62 = bf16[2,160,512]{2,1,0:T(8,128)(2,1)} custom-call(s32[4]{0:T(128)S(1)} %get-tuple-element.58.place_ref, bf16[2,160,128]{2,1,0:T(8,128)(2,1)S(1)} %get-tuple-element.49.refs_0_, bf16[2,160,128]{2,1,0:T(8,128)(2,1)S(1)} %collective-permute-done.16.refs_1_, bf16[2,160,128]{2,1,0:T(8,128)(2,1)S(1)} %collective-permute-done.17.refs_2_, ...), custom_call_target="tpu_custom_call" | custom-call | tf_op jit(solution)/shard_map/pallas_call | solution.py:345
  (36 shorter events, 1.0 us)
Async XLA Ops:
  0.0 12.2 %copy-start = (f32[512]{0:T(512)S(1)}, f32[512]{0:T(512)}, u32[]{:S(2)}) copy-start(f32[512]{0:T(512)} %param.9) | copy-start | bytes 6148
  0.0 1.0 %copy-start.2 = (bf16[2,4,40,512]{3,2,1,0:T(8,128)(2,1)S(1)}, bf16[2,4,40,512]{3,2,1,0:T(8,128)(2,1)}, u32[]{:S(2)}) copy-start(bf16[2,4,40,512]{3,2,1,0:T(8,128)(2,1)} %x_ref.1) | copy-start | bytes 983044
  1.2 1.3 %collective-permute-start.2 = (f32[2,512]{1,0:T(2,128)S(1)}, f32[2,512]{1,0:T(2,128)S(1)}, u32[]{:S(2)}, u32[]{:S(2)}) collective-permute-start(f32[2,512]{1,0:T(2,128)S(1)} %get-tuple-element.32), channel_id=1, source_target_pairs={{0,1},{1,0},{2,3},{3,2},{4,5},{5,4},{6,7},{7,6},{8,9},{9,8},{10,11... | collective-permute-start | bytes 12296 | tf_op jit(solution)/shard_map/ppermute | solution.py:29
  1.7 10.2 %collective-permute-start = (bf16[2,1,40,512]{3,2,1,0:T(8,128)(2,1)S(1)}, bf16[2,1,40,512]{3,2,1,0:T(8,128)(2,1)S(1)}, u32[]{:S(2)}, u32[]{:S(2)}) collective-permute-start(bf16[2,1,40,512]{3,2,1,0:T(8,128)(2,1)S(1)} %get-tuple-element.29), channel_id=1, source_target_pairs={{0,1},{1,0},{2,3},{3,2},{4,5},{5,4},{6,7},{7,6},{8,9},{9,8},{10,11... | collective-permute-start | bytes 245768 | tf_op jit(solution)/shard_map/ppermute | solution.py:366
  1.8 10.2 %collective-permute-start.1 = (bf16[2,1,40,512]{3,2,1,0:T(8,128)(2,1)S(1)}, bf16[2,1,40,512]{3,2,1,0:T(8,128)(2,1)S(1)}, u32[]{:S(2)}, u32[]{:S(2)}) collective-permute-start(bf16[2,1,40,512]{3,2,1,0:T(8,128)(2,1)S(1)} %get-tuple-element.30), channel_id=1, source_target_pairs={{1,2},{3,4},{5,6},{2,1},{4,3},{6,5},{9,10},{11,12},{13,14},{10,9},... | collective-permute-start | bytes 245768 | tf_op jit(solution)/shard_map/ppermute | solution.py:368
  2.5 6.6 %collective-permute-start.3 = (f32[2,512]{1,0:T(2,128)S(1)}, f32[2,512]{1,0:T(2,128)S(1)}, u32[]{:S(2)}, u32[]{:S(2)}) collective-permute-start(f32[2,512]{1,0:T(2,128)S(1)} %pad_maximum_fusion.1), channel_id=1, source_target_pairs={{0,2},{1,3},{2,0},{3,1},{4,6},{5,7},{6,4},{7,5},{8,10},{9,11},{10,... | collective-permute-start | bytes 12296 | tf_op jit(solution)/shard_map/ppermute | solution.py:29
  9.2 4.6 %collective-permute-start.4 = (f32[2,512]{1,0:T(2,128)S(1)}, f32[2,512]{1,0:T(2,128)S(1)}, u32[]{:S(2)}, u32[]{:S(2)}) collective-permute-start(f32[2,512]{1,0:T(2,128)S(1)} %pad_maximum_fusion.2), channel_id=1, source_target_pairs={{0,4},{1,5},{2,6},{3,7},{4,0},{5,1},{6,2},{7,3},{8,12},{9,13},{10,... | collective-permute-start | bytes 12296 | tf_op jit(solution)/shard_map/ppermute | solution.py:29
  11.9 22.6 %collective-permute-start.9 = (bf16[27,16,512]{2,1,0:T(8,128)(2,1)}, bf16[27,16,512]{2,1,0:T(8,128)(2,1)S(1)}, u32[]{:S(2)}, u32[]{:S(2)}) collective-permute-start(bf16[27,16,512]{2,1,0:T(8,128)(2,1)} %bitcast.21), channel_id=1, source_target_pairs={{0,4},{1,5},{2,6},{3,7},{4,0},{5,1},{6,2},{7,3},{8,12},{9,13},{10,... | collective-permute-start | bytes 1327112 | tf_op jit(solution)/shard_map/ppermute | solution.py:375
  14.4 22.8 %copy-start.1 = (bf16[3,3,3,512,16]{3,4,2,1,0:T(8,128)(2,1)S(1)}, bf16[3,3,3,512,16]{3,4,2,1,0:T(8,128)(2,1)}, u32[]{:S(2)}) copy-start(bf16[3,3,3,512,16]{3,4,2,1,0:T(8,128)(2,1)} %param.8) | copy-start | bytes 1327108
  14.4 25.3 %copy-start.3 = (f32[512]{0:T(512)S(1)}, f32[512]{0:T(512)}, u32[]{:S(2)}) copy-start(f32[512]{0:T(512)} %param.7) | copy-start | bytes 6148
  14.4 25.3 %copy-start.4 = (f32[512]{0:T(512)S(1)}, f32[512]{0:T(512)}, u32[]{:S(2)}) copy-start(f32[512]{0:T(512)} %param.6) | copy-start | bytes 6148
  14.5 23.4 %collective-permute-start.6 = (bf16[496,512]{1,0:T(8,128)(2,1)S(1)}, bf16[496,512]{1,0:T(8,128)(2,1)S(1)}, u32[]{:S(2)}, u32[]{:S(2)}) collective-permute-start(bf16[496,512]{1,0:T(8,128)(2,1)S(1)} %shard_map.56.refs_0_), channel_id=1, source_target_pairs={{0,24},{8,16},{16,8},{24,0},{1,25},{9,17},{17,9},{25,1},{2,26},{10... | collective-permute-start | bytes 1523720 | tf_op jit(solution)/shard_map/ppermute | solution.py:29
  17.1 21.8 %collective-permute-start.7 = (bf16[496,512]{1,0:T(8,128)(2,1)S(1)}, bf16[496,512]{1,0:T(8,128)(2,1)S(1)}, u32[]{:S(2)}, u32[]{:S(2)}) collective-permute-start(bf16[496,512]{1,0:T(8,128)(2,1)S(1)} %shard_map.56.refs_0_), channel_id=1, source_target_pairs={{0,16},{8,24},{16,0},{24,8},{1,17},{9,25},{17,1},{25,9},{2,18},{10... | collective-permute-start | bytes 1523720 | tf_op jit(solution)/shard_map/ppermute | solution.py:29
  17.6 21.4 %collective-permute-start.8 = (bf16[496,512]{1,0:T(8,128)(2,1)S(1)}, bf16[496,512]{1,0:T(8,128)(2,1)S(1)}, u32[]{:S(2)}, u32[]{:S(2)}) collective-permute-start(bf16[496,512]{1,0:T(8,128)(2,1)S(1)} %shard_map.56.refs_0_), channel_id=1, source_target_pairs={{0,8},{8,0},{16,24},{24,16},{1,9},{9,1},{17,25},{25,17},{2,10},{10... | collective-permute-start | bytes 1523720 | tf_op jit(solution)/shard_map/ppermute | solution.py:29
  18.0 19.2 %collective-permute-start.5 = (bf16[27,16,512]{2,1,0:T(8,128)(2,1)}, bf16[27,16,512]{2,1,0:T(8,128)(2,1)S(1)}, u32[]{:S(2)}, u32[]{:S(2)}) collective-permute-start(bf16[27,16,512]{2,1,0:T(8,128)(2,1)} %bitcast.22), channel_id=1, source_target_pairs={{0,2},{1,3},{2,0},{3,1},{4,6},{5,7},{6,4},{7,5},{8,10},{9,11},{10,... | collective-permute-start | bytes 1327112 | tf_op jit(solution)/shard_map/ppermute | solution.py:399
  34.6 13.2 %collective-permute-start.10 = (bf16[27,16,512]{2,1,0:T(8,128)(2,1)S(1)}, bf16[27,16,512]{2,1,0:T(8,128)(2,1)S(1)}, u32[]{:S(2)}, u32[]{:S(2)}) collective-permute-start(bf16[27,16,512]{2,1,0:T(8,128)(2,1)S(1)} %shard_map.57.refs_0_), channel_id=1, source_target_pairs={{2,0},{3,1},{4,6},{5,7},{10,8},{11,9},{12,14},{13,15},{18,16},{19,... | collective-permute-start | bytes 1327112 | tf_op jit(solution)/shard_map/ppermute | solution.py:391
  37.2 10.5 %collective-permute-start.11 = (bf16[27,16,512]{2,1,0:T(8,128)(2,1)S(1)}, bf16[27,16,512]{2,1,0:T(8,128)(2,1)S(1)}, u32[]{:S(2)}, u32[]{:S(2)}) collective-permute-start(bf16[27,16,512]{2,1,0:T(8,128)(2,1)S(1)} %bitcast.23), channel_id=1, source_target_pairs={{2,4},{3,5},{4,2},{5,3},{10,12},{11,13},{12,10},{13,11},{18,20},{1... | collective-permute-start | bytes 1327112 | tf_op jit(solution)/shard_map/ppermute | solution.py:392
  39.0 4.2 %collective-permute-start.12 = (bf16[27,16,512]{2,1,0:T(8,128)(2,1)S(1)}, bf16[27,16,512]{2,1,0:T(8,128)(2,1)S(1)}, u32[]{:S(2)}, u32[]{:S(2)}) collective-permute-start(bf16[27,16,512]{2,1,0:T(8,128)(2,1)S(1)} %bitcast.24), channel_id=1, source_target_pairs={{0,1},{1,0},{2,3},{3,2},{4,5},{5,4},{6,7},{7,6},{8,9},{9,8},{10,11... | collective-permute-start | bytes 1327112 | tf_op jit(solution)/shard_map/ppermute | solution.py:412
  39.0 4.2 %collective-permute-start.13 = (bf16[27,16,512]{2,1,0:T(8,128)(2,1)S(1)}, bf16[27,16,512]{2,1,0:T(8,128)(2,1)S(1)}, u32[]{:S(2)}, u32[]{:S(2)}) collective-permute-start(bf16[27,16,512]{2,1,0:T(8,128)(2,1)S(1)} %collective-permute-done.5.refs_1_), channel_id=1, source_target_pairs={{0,1},{1,0},{2,3},{3,2},{4,5},{5,4},{6,7},{7,6},{8,9},{9,8},{10,11... | collective-permute-start | bytes 1327112 | tf_op jit(solution)/shard_map/ppermute | solution.py:412
  39.8 8.2 %collective-permute-start.14 = (bf16[27,16,512]{2,1,0:T(8,128)(2,1)S(1)}, bf16[27,16,512]{2,1,0:T(8,128)(2,1)S(1)}, u32[]{:S(2)}, u32[]{:S(2)}) collective-permute-start(bf16[27,16,512]{2,1,0:T(8,128)(2,1)S(1)} %shard_map.57.refs_0_), channel_id=1, source_target_pairs={{0,1},{1,0},{2,3},{3,2},{4,5},{5,4},{6,7},{7,6},{8,9},{9,8},{10,11... | collective-permute-start | bytes 1327112 | tf_op jit(solution)/shard_map/ppermute | solution.py:430
  47.8 1.9 %collective-permute-start.15 = (bf16[27,16,512]{2,1,0:T(8,128)(2,1)S(1)}, bf16[27,16,512]{2,1,0:T(8,128)(2,1)S(1)}, u32[]{:S(2)}, u32[]{:S(2)}) collective-permute-start(bf16[27,16,512]{2,1,0:T(8,128)(2,1)S(1)} %shard_map.60.refs_1_), channel_id=1, source_target_pairs={{0,1},{1,0},{2,3},{3,2},{4,5},{5,4},{6,7},{7,6},{8,9},{9,8},{10,11... | collective-permute-start | bytes 1327112 | tf_op jit(solution)/shard_map/ppermute | solution.py:430
  53.8 4.6 %collective-permute-start.16 = (bf16[2,160,128]{2,1,0:T(8,128)(2,1)S(1)}, bf16[2,160,128]{2,1,0:T(8,128)(2,1)S(1)}, u32[]{:S(2)}, u32[]{:S(2)}) collective-permute-start(bf16[2,160,128]{2,1,0:T(8,128)(2,1)S(1)} %get-tuple-element.50), channel_id=1, source_target_pairs={{0,8},{8,0},{16,24},{24,16},{1,9},{9,1},{17,25},{25,17},{2,10},{10... | collective-permute-start | bytes 245768 | tf_op jit(solution)/shard_map/ppermute | solution.py:433
  55.3 5.3 %collective-permute-start.17 = (bf16[2,160,128]{2,1,0:T(8,128)(2,1)S(1)}, bf16[2,160,128]{2,1,0:T(8,128)(2,1)S(1)}, u32[]{:S(2)}, u32[]{:S(2)}) collective-permute-start(bf16[2,160,128]{2,1,0:T(8,128)(2,1)S(1)} %get-tuple-element.51), channel_id=1, source_target_pairs={{0,16},{8,24},{16,0},{24,8},{1,17},{9,25},{17,1},{25,9},{2,18},{10... | collective-permute-start | bytes 245768 | tf_op jit(solution)/shard_map/ppermute | solution.py:433
  56.8 5.3 %collective-permute-start.18 = (bf16[2,160,128]{2,1,0:T(8,128)(2,1)S(1)}, bf16[2,160,128]{2,1,0:T(8,128)(2,1)S(1)}, u32[]{:S(2)}, u32[]{:S(2)}) collective-permute-start(bf16[2,160,128]{2,1,0:T(8,128)(2,1)S(1)} %get-tuple-element.52), channel_id=1, source_target_pairs={{0,24},{8,16},{16,8},{24,0},{1,25},{9,17},{17,9},{25,1},{2,26},{10... | collective-permute-start | bytes 245768 | tf_op jit(solution)/shard_map/ppermute | solution.py:433

commit v10 on v9

--- a/solution.py
+++ b/solution.py
@@ -86,8 +86,9 @@
     return jnp.stack([mean, sum(part[1] for part in parts) + apart])
 
 
-def pack_kernel(frames, rows, cols, edge_ref, stats_ref, sibling_ref, facing_ref, _, out_ref):
+def pack_kernel(frames, rows, cols, edge_ref, stats_ref, sibling_ref, facing_ref, payload_ref, out_ref):
     count = frames * rows * cols
+    out_ref[...] = payload_ref[...]
     for f in range(frames):
         first = f * rows * cols
         last = first + (rows - 1) * cols
@@ -121,13 +122,12 @@
         out_shape=jax.ShapeDtypeStruct(payload.shape, jnp.bfloat16),
         in_specs=[scalars] + [whole] * 4,
         out_specs=whole,
-        input_output_aliases={4: 0},
         compiler_params=params(2),
     )(edges, stats, sibling, facing, payload)
 
 
 def held_kernel(in_ref, out_ref):
-    pass
+    out_ref[...] = in_ref[...]
 
 
 def hold(block):
@@ -136,7 +136,6 @@
         out_shape=jax.ShapeDtypeStruct(block.shape, block.dtype),
         in_specs=[whole],
         out_specs=whole,
-        input_output_aliases={0: 0},
         compiler_params=params(1),
         cost_estimate=pl.CostEstimate(flops=10**10, bytes_accessed=0, transcendentals=0),
     )(block)

time: 64.4 us -> 64.4 us (level)
  no operation moved by 1% of the time
where the time goes in v10:
time: 64.4 us; the launch traced here: 63.5 us
  waiting for transfers between devices  28.4 us (44%)
  starting transfers between devices  19.7 us (31%)
  Pallas kernels  13.9 us (22%)
  local copies, waits for them, and re-layouts  1.08 us (2%)
    ppermute x1, waiting for transfers between devices, body(): second = lax.ppermute(weight, 'rows', flip('rows', 2 * CORES))  15.2 us
    ppermute x6, starting transfers between devices, exchange(): return [lax.ppermute(block, axis, flip(axis, d)) for d in distances]  11.1 us
    pallas_call x2, Pallas kernels, convolve(): pl.pallas_call(functools.partial(conv_kernel, len(pieces), other is not N...  8.27 us
    ppermute x6, waiting for transfers between devices, exchange(): return [lax.ppermute(block, axis, flip(axis, d)) for d in distances]  4.88 us
    ppermute x3, waiting for transfers between devices, body(): lax.ppermute(parts[d], 'frames', flip('frames', d))  4.87 us
    ppermute x3, starting transfers between devices, body(): lax.ppermute(parts[d], 'frames', flip('frames', d))  3.55 us
    pallas_call x1, Pallas kernels, activate(): pl.pallas_call(functools.partial(activate_kernel, held, rows, entries), o...  3.32 us
    ppermute x2, waiting for transfers between devices, body(): far += [lax.ppermute(piece, 'rows', flip('rows', 1)) for piece in far]  1.66 us
  transfers between devices with their start and end apart: 19, of which 12 were waited for; matrix products, arithmetic and copies ran while one was open for 1% of the time, Pallas kernels for 13%

profile of v10, /device:TPU:0, one launch (start us, length us, event | category | flops | bytes accessed | tf_op | source)
XLA Modules:
  0.0 63.5 jit_solution(4601664601960552464)
XLA Ops:
  0.0 1.0 %copy-done.2 = bf16[2,4,40,512]{3,2,1,0:T(8,128)(2,1)S(1)} copy-done((bf16[2,4,40,512]{3,2,1,0:T(8,128)(2,1)S(1)}, bf16[2,4,40,512]{3,2,1,0:T(8,128)(2,1)}, u32[]{:S(2)}) %copy-start.2) | copy-done | bytes 327704
  1.2 0.5 collective-permute-start.2
  1.8 0.7 %collective-permute-start.1 = (bf16[2,1,40,512]{3,2,1,0:T(8,128)(2,1)S(1)}, bf16[2,1,40,512]{3,2,1,0:T(8,128)(2,1)S(1)}, u32[]{:S(2)}, u32[]{:S(2)}) collective-permute-start(bf16[2,1,40,512]{3,2,1,0:T(8,128)(2,1)S(1)} %get-tuple-element.30), channel_id=1, source_target_pairs={{1,2},{3,4},{5,6},{2,1},{4,3},{6,5},{9,10},{11,12},{13,14},{10,9},... | collective-permute-start | bytes 245768 | tf_op jit(solution)/shard_map/ppermute | solution.py:367
  2.5 4.3 %collective-permute-start.3 = (f32[2,512]{1,0:T(2,128)S(1)}, f32[2,512]{1,0:T(2,128)S(1)}, u32[]{:S(2)}, u32[]{:S(2)}) collective-permute-start(f32[2,512]{1,0:T(2,128)S(1)} %pad_maximum_fusion.1), channel_id=1, source_target_pairs={{0,2},{1,3},{2,0},{3,1},{4,6},{5,7},{6,4},{7,5},{8,10},{9,11},{10,... | collective-permute-start | bytes 12296 | tf_op jit(solution)/shard_map/ppermute | solution.py:29
  6.9 2.2 %collective-permute-done.3 = f32[2,512]{1,0:T(2,128)S(1)} collective-permute-done((f32[2,512]{1,0:T(2,128)S(1)}, f32[2,512]{1,0:T(2,128)S(1)}, u32[]{:S(2)}, u32[]{:S(2)}) %collective-permute-start.3) | collective-permute-done | bytes 4128 | tf_op jit(solution)/shard_map/ppermute | solution.py:29
  9.2 2.8 %collective-permute-start.4 = (f32[2,512]{1,0:T(2,128)S(1)}, f32[2,512]{1,0:T(2,128)S(1)}, u32[]{:S(2)}, u32[]{:S(2)}) collective-permute-start(f32[2,512]{1,0:T(2,128)S(1)} %pad_maximum_fusion.2), channel_id=1, source_target_pairs={{0,4},{1,5},{2,6},{3,7},{4,0},{5,1},{6,2},{7,3},{8,12},{9,13},{10,... | collective-permute-start | bytes 12296 | tf_op jit(solution)/shard_map/ppermute | solution.py:29
  11.9 0.2 collective-permute-start.9
  12.2 1.5 %collective-permute-done.4 = f32[2,512]{1,0:T(2,128)S(1)} collective-permute-done((f32[2,512]{1,0:T(2,128)S(1)}, f32[2,512]{1,0:T(2,128)S(1)}, u32[]{:S(2)}, u32[]{:S(2)}) %collective-permute-start.4) | collective-permute-done | bytes 4128 | tf_op jit(solution)/shard_map/ppermute | solution.py:29
  13.8 0.7 %shard_map.56.refs_0_ = bf16[496,512]{1,0:T(8,128)(2,1)S(1)} custom-call(s32[2]{0:T(128)S(1)} %pad_add_fusion.1.edge_ref, f32[2,512]{1,0:T(2,128)S(1)} %pad_maximum_fusion.3.stats_ref, bf16[2,1,40,512]{3,2,1,0:T(8,128)(2,1)S(1)} %collective-permute-done.sibling_ref, bf16[2,1,40,512]{3,2,1,0:T(8,128)(2,1)S(1)} %collective-permute-done.1.facing_ref, ...), custom_call_target="tpu_custom_call" | custom-call | tf_op jit(solution)/shard_map/pallas_call | solution.py:120
  14.5 2.6 %collective-permute-start.6 = (bf16[496,512]{1,0:T(8,128)(2,1)S(1)}, bf16[496,512]{1,0:T(8,128)(2,1)S(1)}, u32[]{:S(2)}, u32[]{:S(2)}) collective-permute-start(bf16[496,512]{1,0:T(8,128)(2,1)S(1)} %shard_map.56.refs_0_), channel_id=1, source_target_pairs={{0,24},{8,16},{16,8},{24,0},{1,25},{9,17},{17,9},{25,1},{2,26},{10... | collective-permute-start | bytes 1523720 | tf_op jit(solution)/shard_map/ppermute | solution.py:29
  17.1 0.5 collective-permute-start.7
  17.6 0.4 collective-permute-start.8
  18.0 1.3 %collective-permute-start.5 = (bf16[27,16,512]{2,1,0:T(8,128)(2,1)}, bf16[27,16,512]{2,1,0:T(8,128)(2,1)S(1)}, u32[]{:S(2)}, u32[]{:S(2)}) collective-permute-start(bf16[27,16,512]{2,1,0:T(8,128)(2,1)} %bitcast.22), channel_id=1, source_target_pairs={{0,2},{1,3},{2,0},{3,1},{4,6},{5,7},{6,4},{7,5},{8,10},{9,11},{10,... | collective-permute-start | bytes 1327112 | tf_op jit(solution)/shard_map/ppermute | solution.py:398
  19.3 15.2 %collective-permute-done.9.in_ref = bf16[27,16,512]{2,1,0:T(8,128)(2,1)S(1)} collective-permute-done((bf16[27,16,512]{2,1,0:T(8,128)(2,1)}, bf16[27,16,512]{2,1,0:T(8,128)(2,1)S(1)}, u32[]{:S(2)}, u32[]{:S(2)}) %collective-permute-start.9) | collective-permute-done | bytes 442400 | tf_op jit(solution)/shard_map/ppermute | solution.py:374
  34.6 1.3 %collective-permute-start.10 = (bf16[27,16,512]{2,1,0:T(8,128)(2,1)S(1)}, bf16[27,16,512]{2,1,0:T(8,128)(2,1)S(1)}, u32[]{:S(2)}, u32[]{:S(2)}) collective-permute-start(bf16[27,16,512]{2,1,0:T(8,128)(2,1)S(1)} %shard_map.57.refs_0_), channel_id=1, source_target_pairs={{2,0},{3,1},{4,6},{5,7},{10,8},{11,9},{12,14},{13,15},{18,16},{19,... | collective-permute-start | bytes 1327112 | tf_op jit(solution)/shard_map/ppermute | solution.py:390
  35.9 1.3 %collective-permute-done.5.refs_1_ = bf16[27,16,512]{2,1,0:T(8,128)(2,1)S(1)} collective-permute-done((bf16[27,16,512]{2,1,0:T(8,128)(2,1)}, bf16[27,16,512]{2,1,0:T(8,128)(2,1)S(1)}, u32[]{:S(2)}, u32[]{:S(2)}) %collective-permute-start.5) | collective-permute-done | bytes 442400 | tf_op jit(solution)/shard_map/ppermute | solution.py:398
  37.2 0.7 %collective-permute-start.11 = (bf16[27,16,512]{2,1,0:T(8,128)(2,1)S(1)}, bf16[27,16,512]{2,1,0:T(8,128)(2,1)S(1)}, u32[]{:S(2)}, u32[]{:S(2)}) collective-permute-start(bf16[27,16,512]{2,1,0:T(8,128)(2,1)S(1)} %bitcast.23), channel_id=1, source_target_pairs={{2,4},{3,5},{4,2},{5,3},{10,12},{11,13},{12,10},{13,11},{18,20},{1... | collective-permute-start | bytes 1327112 | tf_op jit(solution)/shard_map/ppermute | solution.py:391
  37.9 1.0 %collective-permute-done.7.refs_2_ = bf16[496,512]{1,0:T(8,128)(2,1)S(1)} collective-permute-done((bf16[496,512]{1,0:T(8,128)(2,1)S(1)}, bf16[496,512]{1,0:T(8,128)(2,1)S(1)}, u32[]{:S(2)}, u32[]{:S(2)}) %collective-permute-start.7) | collective-permute-done | bytes 507936 | tf_op jit(solution)/shard_map/ppermute | solution.py:29
  39.0 0.5 collective-permute-start.13
  39.9 3.3 %shard_map.58 = (bf16[6,336,512]{2,1,0:T(8,128)(2,1)S(1)}, bf16[6,320,512]{2,1,0:T(8,128)(2,1)S(1)}) custom-call(s32[4]{0:T(128)S(1)} %add_multiply_fusion.3.place_ref, f32[2,512]{1,0:T(2,128)S(1)} %pad_maximum_fusion.affine_ref, bf16[496,512]{1,0:T(8,128)(2,1)S(1)} %shard_map.56.refs_0_, bf16[496,512]{1,0:T(8,128)(2,1)S(1)} %collective-permute-done.6.refs_1_, ...), custom_call_target="tpu_custom_call" | custom-call | flops 9830400 | bytes 5898240 | tf_op jit(solution)/shard_map/pallas_call | solution.py:229
  43.2 4.2 %shard_map.59.refs_4_ = bf16[8,160,128]{2,1,0:T(8,128)(2,1)S(1)} custom-call(s32[4]{0:T(128)S(1)} %get-tuple-element.57.place_ref, s32[4]{0:T(128)S(1)} %and_select_fusion.slot_ref, s32[1]{0:T(128)} %bitcast.8.half_ref, bf16[6,336,512]{2,1,0:T(8,128)(2,1)S(1)} %get-tuple-element.40.even_ref, bf16[6,320,512]{2,1,0:T(8,128)(2,1)S(1)} %get-tuple-element.41.odd_ref, ...), custom_call_target="tpu_custom_call" | custom-call | flops 83886080 | bytes 65536 | tf_op jit(solution)/shard_map/pallas_call | solution.py:315
  47.4 0.4 collective-permute-done.10.one_ref
  47.8 0.2 collective-permute-start.15
  48.0 1.7 %collective-permute-done.15.refs_3_ = bf16[27,16,512]{2,1,0:T(8,128)(2,1)S(1)} collective-permute-done((bf16[27,16,512]{2,1,0:T(8,128)(2,1)S(1)}, bf16[27,16,512]{2,1,0:T(8,128)(2,1)S(1)}, u32[]{:S(2)}, u32[]{:S(2)}) %collective-permute-start.15) | collective-permute-done | bytes 442400 | tf_op jit(solution)/shard_map/ppermute | solution.py:429
  49.7 4.1 %shard_map.61 = (bf16[2,160,128]{2,1,0:T(8,128)(2,1)S(1)}, bf16[2,160,128]{2,1,0:T(8,128)(2,1)S(1)}, bf16[2,160,128]{2,1,0:T(8,128)(2,1)S(1)}, bf16[2,160,128]{2,1,0:T(8,128)(2,1)S(1)}) custom-call(s32[4]{0:T(128)S(1)} %get-tuple-element.57.place_ref, s32[4]{0:T(128)S(1)} %and_select_fusion.slot_ref, s32[1]{0:T(128)S(6)} %sub.45.half_ref, ...), custom_call_target="tpu_custom_call" | custom-call | flops 83886080 | bytes 65536 | tf_op jit(solution)/shard_map/pallas_call | solution.py:315
  53.8 1.6 %collective-permute-start.16 = (bf16[2,160,128]{2,1,0:T(8,128)(2,1)S(1)}, bf16[2,160,128]{2,1,0:T(8,128)(2,1)S(1)}, u32[]{:S(2)}, u32[]{:S(2)}) collective-permute-start(bf16[2,160,128]{2,1,0:T(8,128)(2,1)S(1)} %get-tuple-element.50), channel_id=1, source_target_pairs={{0,8},{8,0},{16,24},{24,16},{1,9},{9,1},{17,25},{25,17},{2,10},{10... | collective-permute-start | bytes 245768 | tf_op jit(solution)/shard_map/ppermute | solution.py:432
  55.4 1.5 %collective-permute-start.17 = (bf16[2,160,128]{2,1,0:T(8,128)(2,1)S(1)}, bf16[2,160,128]{2,1,0:T(8,128)(2,1)S(1)}, u32[]{:S(2)}, u32[]{:S(2)}) collective-permute-start(bf16[2,160,128]{2,1,0:T(8,128)(2,1)S(1)} %get-tuple-element.51), channel_id=1, source_target_pairs={{0,16},{8,24},{16,0},{24,8},{1,17},{9,25},{17,1},{25,9},{2,18},{10... | collective-permute-start | bytes 245768 | tf_op jit(solution)/shard_map/ppermute | solution.py:432
  56.9 0.5 collective-permute-start.18
  57.3 1.0 %collective-permute-done.16.refs_1_ = bf16[2,160,128]{2,1,0:T(8,128)(2,1)S(1)} collective-permute-done((bf16[2,160,128]{2,1,0:T(8,128)(2,1)S(1)}, bf16[2,160,128]{2,1,0:T(8,128)(2,1)S(1)}, u32[]{:S(2)}, u32[]{:S(2)}) %collective-permute-start.16) | collective-permute-done | bytes 81952 | tf_op jit(solution)/shard_map/ppermute | solution.py:432
  58.4 2.3 %collective-permute-done.17.refs_2_ = bf16[2,160,128]{2,1,0:T(8,128)(2,1)S(1)} collective-permute-done((bf16[2,160,128]{2,1,0:T(8,128)(2,1)S(1)}, bf16[2,160,128]{2,1,0:T(8,128)(2,1)S(1)}, u32[]{:S(2)}, u32[]{:S(2)}) %collective-permute-start.17) | collective-permute-done | bytes 81952 | tf_op jit(solution)/shard_map/ppermute | solution.py:432
  60.6 1.6 %collective-permute-done.18.refs_3_ = bf16[2,160,128]{2,1,0:T(8,128)(2,1)S(1)} collective-permute-done((bf16[2,160,128]{2,1,0:T(8,128)(2,1)S(1)}, bf16[2,160,128]{2,1,0:T(8,128)(2,1)S(1)}, u32[]{:S(2)}, u32[]{:S(2)}) %collective-permute-start.18) | collective-permute-done | bytes 81952 | tf_op jit(solution)/shard_map/ppermute | solution.py:432
  62.2 1.3 %shard_map.62 = bf16[2,160,512]{2,1,0:T(8,128)(2,1)} custom-call(s32[4]{0:T(128)S(1)} %get-tuple-element.58.place_ref, bf16[2,160,128]{2,1,0:T(8,128)(2,1)S(1)} %get-tuple-element.49.refs_0_, bf16[2,160,128]{2,1,0:T(8,128)(2,1)S(1)} %collective-permute-done.16.refs_1_, bf16[2,160,128]{2,1,0:T(8,128)(2,1)S(1)} %collective-permute-done.17.refs_2_, ...), custom_call_target="tpu_custom_call" | custom-call | tf_op jit(solution)/shard_map/pallas_call | solution.py:344
  (36 shorter events, 1.1 us)
Async XLA Ops:
  0.0 12.2 %copy-start = (f32[512]{0:T(512)S(1)}, f32[512]{0:T(512)}, u32[]{:S(2)}) copy-start(f32[512]{0:T(512)} %param.9) | copy-start | bytes 6148
  0.0 1.0 %copy-start.2 = (bf16[2,4,40,512]{3,2,1,0:T(8,128)(2,1)S(1)}, bf16[2,4,40,512]{3,2,1,0:T(8,128)(2,1)}, u32[]{:S(2)}) copy-start(bf16[2,4,40,512]{3,2,1,0:T(8,128)(2,1)} %x_ref.1) | copy-start | bytes 983044
  1.2 1.3 %collective-permute-start.2 = (f32[2,512]{1,0:T(2,128)S(1)}, f32[2,512]{1,0:T(2,128)S(1)}, u32[]{:S(2)}, u32[]{:S(2)}) collective-permute-start(f32[2,512]{1,0:T(2,128)S(1)} %get-tuple-element.32), channel_id=1, source_target_pairs={{0,1},{1,0},{2,3},{3,2},{4,5},{5,4},{6,7},{7,6},{8,9},{9,8},{10,11... | collective-permute-start | bytes 12296 | tf_op jit(solution)/shard_map/ppermute | solution.py:29
  1.7 10.2 %collective-permute-start = (bf16[2,1,40,512]{3,2,1,0:T(8,128)(2,1)S(1)}, bf16[2,1,40,512]{3,2,1,0:T(8,128)(2,1)S(1)}, u32[]{:S(2)}, u32[]{:S(2)}) collective-permute-start(bf16[2,1,40,512]{3,2,1,0:T(8,128)(2,1)S(1)} %get-tuple-element.29), channel_id=1, source_target_pairs={{0,1},{1,0},{2,3},{3,2},{4,5},{5,4},{6,7},{7,6},{8,9},{9,8},{10,11... | collective-permute-start | bytes 245768 | tf_op jit(solution)/shard_map/ppermute | solution.py:365
  1.8 10.2 %collective-permute-start.1 = (bf16[2,1,40,512]{3,2,1,0:T(8,128)(2,1)S(1)}, bf16[2,1,40,512]{3,2,1,0:T(8,128)(2,1)S(1)}, u32[]{:S(2)}, u32[]{:S(2)}) collective-permute-start(bf16[2,1,40,512]{3,2,1,0:T(8,128)(2,1)S(1)} %get-tuple-element.30), channel_id=1, source_target_pairs={{1,2},{3,4},{5,6},{2,1},{4,3},{6,5},{9,10},{11,12},{13,14},{10,9},... | collective-permute-start | bytes 245768 | tf_op jit(solution)/shard_map/ppermute | solution.py:367
  2.5 6.6 %collective-permute-start.3 = (f32[2,512]{1,0:T(2,128)S(1)}, f32[2,512]{1,0:T(2,128)S(1)}, u32[]{:S(2)}, u32[]{:S(2)}) collective-permute-start(f32[2,512]{1,0:T(2,128)S(1)} %pad_maximum_fusion.1), channel_id=1, source_target_pairs={{0,2},{1,3},{2,0},{3,1},{4,6},{5,7},{6,4},{7,5},{8,10},{9,11},{10,... | collective-permute-start | bytes 12296 | tf_op jit(solution)/shard_map/ppermute | solution.py:29
  9.2 4.6 %collective-permute-start.4 = (f32[2,512]{1,0:T(2,128)S(1)}, f32[2,512]{1,0:T(2,128)S(1)}, u32[]{:S(2)}, u32[]{:S(2)}) collective-permute-start(f32[2,512]{1,0:T(2,128)S(1)} %pad_maximum_fusion.2), channel_id=1, source_target_pairs={{0,4},{1,5},{2,6},{3,7},{4,0},{5,1},{6,2},{7,3},{8,12},{9,13},{10,... | collective-permute-start | bytes 12296 | tf_op jit(solution)/shard_map/ppermute | solution.py:29
  11.9 22.6 %collective-permute-start.9 = (bf16[27,16,512]{2,1,0:T(8,128)(2,1)}, bf16[27,16,512]{2,1,0:T(8,128)(2,1)S(1)}, u32[]{:S(2)}, u32[]{:S(2)}) collective-permute-start(bf16[27,16,512]{2,1,0:T(8,128)(2,1)} %bitcast.21), channel_id=1, source_target_pairs={{0,4},{1,5},{2,6},{3,7},{4,0},{5,1},{6,2},{7,3},{8,12},{9,13},{10,... | collective-permute-start | bytes 1327112 | tf_op jit(solution)/shard_map/ppermute | solution.py:374
  14.4 22.8 %copy-start.1 = (bf16[3,3,3,512,16]{3,4,2,1,0:T(8,128)(2,1)S(1)}, bf16[3,3,3,512,16]{3,4,2,1,0:T(8,128)(2,1)}, u32[]{:S(2)}) copy-start(bf16[3,3,3,512,16]{3,4,2,1,0:T(8,128)(2,1)} %param.8) | copy-start | bytes 1327108
  14.5 25.3 %copy-start.3 = (f32[512]{0:T(512)S(1)}, f32[512]{0:T(512)}, u32[]{:S(2)}) copy-start(f32[512]{0:T(512)} %param.7) | copy-start | bytes 6148
  14.5 25.3 %copy-start.4 = (f32[512]{0:T(512)S(1)}, f32[512]{0:T(512)}, u32[]{:S(2)}) copy-start(f32[512]{0:T(512)} %param.6) | copy-start | bytes 6148
  14.5 23.4 %collective-permute-start.6 = (bf16[496,512]{1,0:T(8,128)(2,1)S(1)}, bf16[496,512]{1,0:T(8,128)(2,1)S(1)}, u32[]{:S(2)}, u32[]{:S(2)}) collective-permute-start(bf16[496,512]{1,0:T(8,128)(2,1)S(1)} %shard_map.56.refs_0_), channel_id=1, source_target_pairs={{0,24},{8,16},{16,8},{24,0},{1,25},{9,17},{17,9},{25,1},{2,26},{10... | collective-permute-start | bytes 1523720 | tf_op jit(solution)/shard_map/ppermute | solution.py:29
  17.1 21.8 %collective-permute-start.7 = (bf16[496,512]{1,0:T(8,128)(2,1)S(1)}, bf16[496,512]{1,0:T(8,128)(2,1)S(1)}, u32[]{:S(2)}, u32[]{:S(2)}) collective-permute-start(bf16[496,512]{1,0:T(8,128)(2,1)S(1)} %shard_map.56.refs_0_), channel_id=1, source_target_pairs={{0,16},{8,24},{16,0},{24,8},{1,17},{9,25},{17,1},{25,9},{2,18},{10... | collective-permute-start | bytes 1523720 | tf_op jit(solution)/shard_map/ppermute | solution.py:29
  17.6 21.4 %collective-permute-start.8 = (bf16[496,512]{1,0:T(8,128)(2,1)S(1)}, bf16[496,512]{1,0:T(8,128)(2,1)S(1)}, u32[]{:S(2)}, u32[]{:S(2)}) collective-permute-start(bf16[496,512]{1,0:T(8,128)(2,1)S(1)} %shard_map.56.refs_0_), channel_id=1, source_target_pairs={{0,8},{8,0},{16,24},{24,16},{1,9},{9,1},{17,25},{25,17},{2,10},{10... | collective-permute-start | bytes 1523720 | tf_op jit(solution)/shard_map/ppermute | solution.py:29
  18.0 19.2 %collective-permute-start.5 = (bf16[27,16,512]{2,1,0:T(8,128)(2,1)}, bf16[27,16,512]{2,1,0:T(8,128)(2,1)S(1)}, u32[]{:S(2)}, u32[]{:S(2)}) collective-permute-start(bf16[27,16,512]{2,1,0:T(8,128)(2,1)} %bitcast.22), channel_id=1, source_target_pairs={{0,2},{1,3},{2,0},{3,1},{4,6},{5,7},{6,4},{7,5},{8,10},{9,11},{10,... | collective-permute-start | bytes 1327112 | tf_op jit(solution)/shard_map/ppermute | solution.py:398
  34.6 13.2 %collective-permute-start.10 = (bf16[27,16,512]{2,1,0:T(8,128)(2,1)S(1)}, bf16[27,16,512]{2,1,0:T(8,128)(2,1)S(1)}, u32[]{:S(2)}, u32[]{:S(2)}) collective-permute-start(bf16[27,16,512]{2,1,0:T(8,128)(2,1)S(1)} %shard_map.57.refs_0_), channel_id=1, source_target_pairs={{2,0},{3,1},{4,6},{5,7},{10,8},{11,9},{12,14},{13,15},{18,16},{19,... | collective-permute-start | bytes 1327112 | tf_op jit(solution)/shard_map/ppermute | solution.py:390
  37.2 10.5 %collective-permute-start.11 = (bf16[27,16,512]{2,1,0:T(8,128)(2,1)S(1)}, bf16[27,16,512]{2,1,0:T(8,128)(2,1)S(1)}, u32[]{:S(2)}, u32[]{:S(2)}) collective-permute-start(bf16[27,16,512]{2,1,0:T(8,128)(2,1)S(1)} %bitcast.23), channel_id=1, source_target_pairs={{2,4},{3,5},{4,2},{5,3},{10,12},{11,13},{12,10},{13,11},{18,20},{1... | collective-permute-start | bytes 1327112 | tf_op jit(solution)/shard_map/ppermute | solution.py:391
  39.0 4.2 %collective-permute-start.12 = (bf16[27,16,512]{2,1,0:T(8,128)(2,1)S(1)}, bf16[27,16,512]{2,1,0:T(8,128)(2,1)S(1)}, u32[]{:S(2)}, u32[]{:S(2)}) collective-permute-start(bf16[27,16,512]{2,1,0:T(8,128)(2,1)S(1)} %bitcast.24), channel_id=1, source_target_pairs={{0,1},{1,0},{2,3},{3,2},{4,5},{5,4},{6,7},{7,6},{8,9},{9,8},{10,11... | collective-permute-start | bytes 1327112 | tf_op jit(solution)/shard_map/ppermute | solution.py:411
  39.0 4.2 %collective-permute-start.13 = (bf16[27,16,512]{2,1,0:T(8,128)(2,1)S(1)}, bf16[27,16,512]{2,1,0:T(8,128)(2,1)S(1)}, u32[]{:S(2)}, u32[]{:S(2)}) collective-permute-start(bf16[27,16,512]{2,1,0:T(8,128)(2,1)S(1)} %collective-permute-done.5.refs_1_), channel_id=1, source_target_pairs={{0,1},{1,0},{2,3},{3,2},{4,5},{5,4},{6,7},{7,6},{8,9},{9,8},{10,11... | collective-permute-start | bytes 1327112 | tf_op jit(solution)/shard_map/ppermute | solution.py:411
  39.8 8.2 %collective-permute-start.14 = (bf16[27,16,512]{2,1,0:T(8,128)(2,1)S(1)}, bf16[27,16,512]{2,1,0:T(8,128)(2,1)S(1)}, u32[]{:S(2)}, u32[]{:S(2)}) collective-permute-start(bf16[27,16,512]{2,1,0:T(8,128)(2,1)S(1)} %shard_map.57.refs_0_), channel_id=1, source_target_pairs={{0,1},{1,0},{2,3},{3,2},{4,5},{5,4},{6,7},{7,6},{8,9},{9,8},{10,11... | collective-permute-start | bytes 1327112 | tf_op jit(solution)/shard_map/ppermute | solution.py:429
  47.8 1.9 %collective-permute-start.15 = (bf16[27,16,512]{2,1,0:T(8,128)(2,1)S(1)}, bf16[27,16,512]{2,1,0:T(8,128)(2,1)S(1)}, u32[]{:S(2)}, u32[]{:S(2)}) collective-permute-start(bf16[27,16,512]{2,1,0:T(8,128)(2,1)S(1)} %shard_map.60.refs_1_), channel_id=1, source_target_pairs={{0,1},{1,0},{2,3},{3,2},{4,5},{5,4},{6,7},{7,6},{8,9},{9,8},{10,11... | collective-permute-start | bytes 1327112 | tf_op jit(solution)/shard_map/ppermute | solution.py:429
  53.8 4.6 %collective-permute-start.16 = (bf16[2,160,128]{2,1,0:T(8,128)(2,1)S(1)}, bf16[2,160,128]{2,1,0:T(8,128)(2,1)S(1)}, u32[]{:S(2)}, u32[]{:S(2)}) collective-permute-start(bf16[2,160,128]{2,1,0:T(8,128)(2,1)S(1)} %get-tuple-element.50), channel_id=1, source_target_pairs={{0,8},{8,0},{16,24},{24,16},{1,9},{9,1},{17,25},{25,17},{2,10},{10... | collective-permute-start | bytes 245768 | tf_op jit(solution)/shard_map/ppermute | solution.py:432
  55.4 5.3 %collective-permute-start.17 = (bf16[2,160,128]{2,1,0:T(8,128)(2,1)S(1)}, bf16[2,160,128]{2,1,0:T(8,128)(2,1)S(1)}, u32[]{:S(2)}, u32[]{:S(2)}) collective-permute-start(bf16[2,160,128]{2,1,0:T(8,128)(2,1)S(1)} %get-tuple-element.51), channel_id=1, source_target_pairs={{0,16},{8,24},{16,0},{24,8},{1,17},{9,25},{17,1},{25,9},{2,18},{10... | collective-permute-start | bytes 245768 | tf_op jit(solution)/shard_map/ppermute | solution.py:432
  56.9 5.3 %collective-permute-start.18 = (bf16[2,160,128]{2,1,0:T(8,128)(2,1)S(1)}, bf16[2,160,128]{2,1,0:T(8,128)(2,1)S(1)}, u32[]{:S(2)}, u32[]{:S(2)}) collective-permute-start(bf16[2,160,128]{2,1,0:T(8,128)(2,1)S(1)} %get-tuple-element.52), channel_id=1, source_target_pairs={{0,24},{8,16},{16,8},{24,0},{1,25},{9,17},{17,9},{25,1},{2,26},{10... | collective-permute-start | bytes 245768 | tf_op jit(solution)/shard_map/ppermute | solution.py:432
